TPU v7x, 32 devices: a whole 2x2x4 slice. The times are simulated.
32 devices in a mesh: groups: 2 (over y), shot: 4 (over z), freq: 4 (over x, core).
Axes of the slice: x: 2, y: 2, z: 4, core: 2. Of those that a mesh axis runs over, the one named last changes fastest.
Arguments:
- source_field: bfloat16 [4, 4096, 16, 2, 128], P('freq', ('groups', 'shot')), parts along dimension 1, may hold values from -6 to 6
- receiver_field: bfloat16 [4, 4096, 16, 2, 128], P('freq', ('groups', 'shot')), parts along dimension 1, may hold values from -6 to 6
- operator: bfloat16 [4, 32, 3, 2, 128, 128], P('freq', 'groups'), parts along dimension 1, may hold values from -0.21875 to 0.21875
- band_offsets: int32 [32, 3], P('groups'), parts along dimension 0, may hold values from -2 to 4, as said below
- survey_tiles: int32 [128, 2], P('groups'), parts along dimension 0, may hold values from 0 to 15, as said below
- survey_data: bfloat16 [4, 128, 2, 128, 128], P('freq', ('groups', 'shot')), parts along dimension 1, may hold values from -0.1875 to 0.1875
Outputs:
- image: float32 [2, 4096, 128], P(None, ('groups', 'shot', 'freq')), parts along dimension 1
There are 2 independent parts, one for each index of `groups`. A program takes and returns all parts, laid end to end along the dimension named above; each array names one. Nothing has to cross between parts.
Inputs may be any that keep to these rules, and one draw needn't show every extreme that they name: `band_offsets`: in each row the offsets rise strictly; band k of row block i acts on cell block (i + offset) mod 16. `survey_tiles`: tile t has source block t div (4), so each source block has 4 tiles; the receiver blocks of one source block's tiles differ.
All inputs are finite; a program needn't handle non-finite values.
Results may differ from a plain program's by a relative error of at most 0.005.
Values may be sent and summed in bfloat16 or wider, within the bound.
No kernel may reach another device: no remote copies, remote signals or barrier semaphores. Data moves between devices by JAX's collectives and lax.ppermute only.
A program may use at most 256 MiB of HBM per device.

v0:
```python
import functools
import math

import jax
import jax.numpy as jnp
from jax import lax
from jax.experimental import pallas as pl
from jax.experimental.pallas import tpu as pltpu
from jax.sharding import PartitionSpec as P

NR = 2048
HEAD_LIMIT = 60
SMALL = pl.CostEstimate(flops=1000, bytes_accessed=1000, transcendentals=0)


def extrapolate(wavefield, operator, columns):
    row_count, blocks_x, components, block_size = wavefield.shape
    bands = columns.shape[1]
    real_part = operator[:, :, 0]
    imag_part = operator[:, :, 1]
    upper_rows = jnp.concatenate([real_part, imag_part], -1)
    lower_rows = jnp.concatenate([-imag_part, real_part], -1)
    real_block = jnp.concatenate([upper_rows, lower_rows], -2)
    real_block = real_block.reshape(blocks_x, bands, 2 * block_size, 2, block_size)
    chosen = jnp.take(wavefield, columns, axis=1).reshape(
        row_count, blocks_x, bands, 2 * block_size
    )
    result = jnp.einsum("sikc,ikcoy->soiy", chosen, real_block, preferred_element_type=jnp.float32)
    return result.astype(jnp.bfloat16)


def to_owners(wavefield, shot_count, own_cells):
    row_count = wavefield.shape[0]
    return wavefield.reshape(row_count, 2, shot_count, own_cells)


def to_tiles(wavefield, shot_count, own_cells):
    row_count, components, blocks_x, block_size = wavefield.shape
    if own_cells >= block_size:
        return to_owners(wavefield, shot_count, own_cells)
    factor = block_size // own_cells
    copies = jnp.broadcast_to(
        wavefield[:, :, :, None, :], (row_count, components, blocks_x, factor, block_size)
    )
    return copies.reshape(row_count, components, shot_count, block_size)


def data_product(source_cells, data_shard, survey_tiles, block_size, own_cells):
    source_count = source_cells.shape[0]
    receiver_blocks = NR // block_size
    blocks = source_cells.reshape(source_count // block_size, block_size, 2 * own_cells)
    block_ids = jnp.arange(receiver_blocks, dtype=jnp.int32)
    chosen = jnp.take(blocks, survey_tiles[:, 0], axis=0)
    products = jnp.einsum(
        "ncsr,nsk->ncrk",
        lax.all_gather(data_shard, "shot", axis=0, tiled=True),
        chosen,
        preferred_element_type=jnp.float32,
    )
    real_part = products[:, 0, :, :own_cells] - products[:, 1, :, own_cells:]
    imag_part = products[:, 0, :, own_cells:] + products[:, 1, :, :own_cells]
    contribution = jnp.concatenate([real_part, imag_part], -1)
    onehot = (survey_tiles[:, 1][:, None] == block_ids[None, :]).astype(jnp.float32)
    summed = jnp.einsum("nq,nrk->qrk", onehot, contribution, precision=lax.Precision.HIGHEST)
    return summed.reshape(NR, 2, own_cells).astype(jnp.bfloat16)


def image_tile(product, receiver_tile, block_size):
    row_count, components, own_cells = product.shape
    tiles_here = max(own_cells // block_size, 1)
    inner_cells = own_cells // tiles_here
    left = product.reshape(row_count, 2, tiles_here, inner_cells)
    right = receiver_tile.reshape(row_count, 2, tiles_here, block_size)
    turned = jnp.stack([-right[:, 1], right[:, 0]], 1)
    both = jnp.stack([right, turned], 1)
    result = jnp.einsum("rctx,rocty->otxy", left, both, preferred_element_type=jnp.float32)
    return result.reshape(2, own_cells, block_size)


def general_body(source_field, receiver_field, operator, band_offsets, survey_tiles, survey_data):
    shot_count = lax.axis_size("shot")
    freq_local = source_field.shape[0]
    blocks_x = source_field.shape[2]
    block_size = source_field.shape[4]
    own_cells = blocks_x * block_size // shot_count
    block_rows = jnp.arange(blocks_x, dtype=jnp.int32)[:, None]
    columns = (block_rows + band_offsets) % blocks_x
    source_next = extrapolate(source_field[0], operator[0], columns)
    receiver_next = extrapolate(receiver_field[0], operator[0], columns)
    source_send = to_owners(source_next, shot_count, own_cells)
    receiver_send = to_tiles(receiver_next, shot_count, own_cells)
    source_cells = lax.all_to_all(source_send, "shot", split_axis=2, concat_axis=0, tiled=True)
    receiver_tile = lax.all_to_all(receiver_send, "shot", split_axis=2, concat_axis=0, tiled=True)
    source_cells = source_cells.reshape(source_cells.shape[0], 2 * own_cells)
    product = data_product(source_cells, survey_data[0], survey_tiles, block_size, own_cells)
    receiver_tile = receiver_tile.reshape(receiver_tile.shape[0], 2, -1)
    image_sum = image_tile(product, receiver_tile, block_size)
    total_freqs = freq_local * lax.axis_size("freq")
    scaled = image_sum * (1.0 / math.sqrt(2.0 * NR * total_freqs))
    return lax.psum_scatter(scaled, "freq", scatter_dimension=1, tiled=True)


INNER = [4, 8, 6, 10, 15, 5, 9, 7, 11]
HEAD = 3
OUTER = [0, 12, 2, 14, 1, 13, 3]
FIRST = 5
OUTER_FIRST = 4


def outer_place(slot):
    return jnp.where(slot < FIRST, jnp.minimum(slot, OUTER_FIRST - 1), jnp.minimum(slot - 1, len(OUTER) - 1))


def params(limit=24):
    return pltpu.CompilerParams(vmem_limit_bytes=limit * 1024 * 1024)


def extrapolate_kernel(order, columns, field, operator, *refs, sizes, rows, blocks, chunk, listed):
    stage, apart = refs[-2:]
    outs = refs[-2 - len(sizes):-2]
    step = pl.program_id(0)
    lines = 2 * blocks
    bands = operator.shape[1]

    @pl.when(step == 0)
    def _():
        if listed:
            wanted = [columns[order[n // bands], n % bands] for n in range(sum(sizes) * bands)]
        else:
            wanted = list(range(blocks))

        def split(n, carry):
            start = pl.multiple_of(n * (chunk * lines), chunk * lines)
            stage[...] = field[pl.ds(start, chunk * lines), :].astype(jnp.float32)
            to = pl.ds(pl.multiple_of(n * chunk, chunk), chunk)
            for slot, block in enumerate(wanted):
                for part in range(2):
                    picked = stage[pl.ds(2 * block + part, chunk, stride=lines), :]
                    apart[slot, to, part * 128:(part + 1) * 128] = picked.astype(jnp.bfloat16)
            return carry

        lax.fori_loop(0, rows // chunk, split, 0)

    block = order[step]
    inputs = []
    weights = []
    for band in range(bands):
        inputs.append(apart[step * bands + band if listed else columns[block, band]])
        real = operator[0, band, 0]
        imag = operator[0, band, 1]
        weights.append(jnp.concatenate([real, imag], 1))
        weights.append(jnp.concatenate([-imag, real], 1))
    result = jnp.dot(
        jnp.concatenate(inputs, 1), jnp.concatenate(weights, 0), preferred_element_type=jnp.float32
    ).astype(jnp.bfloat16)
    first = 0
    for out, count in zip(outs, sizes):
        if len(sizes) == 1:
            out[0] = result
        else:
            @pl.when((step >= first) & (step < first + count))
            def _(out=out):
                out[0] = result
        first += count


def extrapolate_blocks(field, operator, columns, sets, listed=False, after=(), limit=24):
    rows, blocks, _, size = field.shape
    bands = columns.shape[1]
    width = 2 * size
    chunk = 32
    sizes = [len(one) for one in sets]
    order = jnp.array(sum(sets, []), jnp.int32)
    firsts = [sum(sizes[:n]) for n in range(len(sizes))]
    flat = field.reshape(rows * blocks * 2, size)

    def out_spec(first, count):
        return pl.BlockSpec((1, rows, width), lambda j, o, c: (jnp.clip(j - first, 0, count - 1), 0, 0))

    return pl.pallas_call(
        functools.partial(
            extrapolate_kernel, sizes=sizes, rows=rows, blocks=blocks, chunk=chunk, listed=listed
        ),
        grid_spec=pltpu.PrefetchScalarGridSpec(
            num_scalar_prefetch=2,
            grid=(sum(sizes),),
            in_specs=[
                pl.BlockSpec(flat.shape, lambda j, o, c: (0, 0)),
                pl.BlockSpec((1, bands, 2, size, size), lambda j, o, c: (o[j], 0, 0, 0, 0)),
            ]
            + [pl.BlockSpec(memory_space=pl.ANY)] * len(after),
            out_specs=[out_spec(*one) for one in zip(firsts, sizes)],
            scratch_shapes=[
                pltpu.VMEM((chunk * blocks * 2, size), jnp.float32),
                pltpu.VMEM((sum(sizes) * bands if listed else blocks, rows, width), jnp.bfloat16),
            ],
        ),
        out_shape=[jax.ShapeDtypeStruct((n, rows, width), jnp.bfloat16) for n in sizes],
        compiler_params=params(limit),
        cost_estimate=SMALL,
        name="extrapolate",
    )(order, columns, flat, operator, *after)


def product_kernel(near_ids, far_ids, inner, near_in, near_out, far_in, far_out, near_data, far_data, out, turned, total):
    size = near_data.shape[2]
    tiles = near_data.shape[0]
    sources = near_in.shape[1] // size
    per_source = tiles // sources

    @pl.when(pl.program_id(0) == 0)
    def _():
        for side, data in enumerate((near_data, far_data)):
            for tile in range(tiles):
                for part in range(2):
                    turned[side * tiles + tile, :, part * size:(part + 1) * size] = data[tile, part].T

    total[...] = jnp.zeros_like(total)
    sides = ((near_in, near_out, near_ids), (far_in, far_out, far_ids))
    for side, (field_in, field_out, ids) in enumerate(sides):
        for source in range(sources):
            lines = slice(source * size, (source + 1) * size)
            upper = jnp.where(inner[0] > 0, field_in[0, lines, :], field_out[0, lines, :])
            lower = jnp.concatenate([-upper[:, size:], upper[:, :size]], 1)
            both = jnp.concatenate([upper, lower], 0)
            first = side * tiles + source * per_source
            left = turned[first:first + per_source].reshape(per_source * size, 2 * size)
            result = jnp.dot(left, both, preferred_element_type=jnp.float32)
            for tile in range(per_source):
                total[ids[source * per_source + tile]] += result[tile * size:(tile + 1) * size]
    for block in range(total.shape[0]):
        out[0, :, block * size:(block + 1) * size] = total[block].T.astype(jnp.bfloat16)


def part_spec(shape, first, begin, count, is_inner):
    def index(j, a, b, inner):
        place = first + j if is_inner else outer_place(first + j)
        place = jnp.clip(place - begin, 0, count - 1)
        return jnp.where((inner[0] > 0) == is_inner, place, 0), 0, 0

    return pl.BlockSpec(shape, index)


def product_blocks(near_in, near_out, far_in, far_out, near_data, far_data, near_ids, far_ids, inner):
    blocks, rows, width = near_in.shape
    tiles, _, size, _ = near_data.shape
    receivers = NR // size
    shape = (1, rows, width)
    data_spec = pl.BlockSpec(near_data.shape, lambda j, a, b, i: (0, 0, 0, 0))
    return pl.pallas_call(
        product_kernel,
        grid_spec=pltpu.PrefetchScalarGridSpec(
            num_scalar_prefetch=3,
            grid=(blocks,),
            in_specs=[part_spec(shape, 0, 0, len(INNER), True), part_spec(shape, 0, 0, len(OUTER), False)] * 2
            + [data_spec, data_spec],
            out_specs=pl.BlockSpec((1, width, NR), lambda j, a, b, i: (j, 0, 0)),
            scratch_shapes=[
                pltpu.VMEM((2 * tiles, size, width), jnp.bfloat16),
                pltpu.VMEM((receivers, size, width), jnp.float32),
            ],
        ),
        out_shape=jax.ShapeDtypeStruct((blocks, width, NR), jnp.bfloat16),
        compiler_params=params(),
        cost_estimate=SMALL,
        name="product",
    )(near_ids, far_ids, inner, near_in, near_out, far_in, far_out, near_data, far_data)


def image_kernel(places, unused, inner, *refs, first, begins, size):
    out = refs[-1]
    slot = first + pl.program_id(0)
    parts = refs[len(begins):]
    both = None
    for n, piece in enumerate(begins):
        field = parts[0][0]
        for part, (begin, is_inner) in zip(parts[1:], piece[1:]):
            chosen = (inner[0] > 0) & (slot >= begin) if is_inner else inner[0] == 0
            field = jnp.where(chosen, part[0], field)
        parts = parts[len(piece):]
        term = jnp.dot(refs[n][0], field, preferred_element_type=jnp.float32)
        both = term if both is None else both + term
    real = both[:size, :size] + both[size:, size:]
    imag = both[size:, :size] - both[:size, size:]
    if len(parts) > 1:
        real += parts[0][0, 0]
        imag += parts[0][0, 1]
    out[0, 0] = real
    out[0, 1] = imag


def image_blocks(product, first, count, pieces, inner, before=None):
    _, rows, width = pieces[0][1][0][0].shape
    size = width // 2
    image_spec = pl.BlockSpec((1, 2, size, size), lambda j, o, u, i: (j, 0, 0, 0))
    specs = [
        pl.BlockSpec((1, width, rows), lambda j, o, u, i, n=n: (first + j, 0, o[n])) for n in range(len(pieces))
    ]
    values = [product] * len(pieces)
    begins = []
    for _, parts in pieces:
        inners = [True] * (len(parts) - 1) + [False]
        for (field, begin), is_inner in zip(parts, inners):
            specs.append(part_spec((1, rows, width), first, begin, field.shape[0], is_inner))
            values.append(field)
        begins.append([(begin, is_inner) for (_, begin), is_inner in zip(parts, inners)])
    if before is not None:
        specs.append(image_spec)
        values.append(before)
    places = jnp.stack([shot for shot, _ in pieces])
    return pl.pallas_call(
        functools.partial(image_kernel, first=first, begins=begins, size=size),
        grid_spec=pltpu.PrefetchScalarGridSpec(
            num_scalar_prefetch=3, grid=(count,), in_specs=specs, out_specs=image_spec
        ),
        out_shape=jax.ShapeDtypeStruct((count, 2, size, size), jnp.float32),
        compiler_params=params(),
        cost_estimate=SMALL,
        name="image",
    )(places, places, inner, *values)


def following(value, *earlier):
    return lax.optimization_barrier((value,) + earlier)[0]


def hand(value, *pairs):
    return lax.ppermute(value, "shot", pairs)


def send_sum(value, pairs):
    pairs = [(4 * a + b, 4 * c + d) for (a, b), (c, d) in pairs]
    return lax.ppermute(value.astype(jnp.bfloat16), ("shot", "freq"), pairs).astype(jnp.float32)


def sum_images(one, two, shot, freq):
    left = shot < 2
    shots = range(4)
    even = freq % 2 == 0
    low = freq < 2
    last = one[4:]
    one = one[:4]
    keep = jnp.where(even, jnp.concatenate([one, last]), jnp.concatenate([two, last]))
    send = jnp.where(even, jnp.concatenate([two, last]), jnp.concatenate([one, last]))
    image = keep + send_sum(send, [((s, f), (s, f ^ 1)) for s in shots for f in range(4)])
    keep = jnp.where(low, image[:2], image[2:4])
    send = jnp.where(low, image[2:4], image[:2])
    last = image[4] + send_sum(image[4], [((s, 1), (s, 3)) for s in (1, 2)])
    image = keep + send_sum(send, [((s, f), (s, f ^ 2)) for s in shots for f in range(4)])
    keep = jnp.where(left, image[0], image[1])
    send = jnp.where(left, image[1], image[0])
    image = keep + send_sum(send, [((s, f), (3 - s, f)) for s in shots for f in range(4) if (s, f) != (0, 3)])
    last = send_sum(last, [((1, 3), (3, 3))]) + send_sum(last, [((2, 3), (3, 3))])
    return jnp.where((shot == 3) & (freq == 3), last, image)


def split_body(source_field, receiver_field, operator, band_offsets, survey_tiles, survey_data):
    blocks = source_field.shape[2]
    tiles = survey_data.shape[1]
    shot = lax.axis_index("shot")
    freq = lax.axis_index("freq")
    inner = ((shot == 1) | (shot == 2)).astype(jnp.int32)[None]
    columns = (jnp.arange(blocks, dtype=jnp.int32)[:, None] + band_offsets) % blocks
    make = functools.partial(extrapolate_blocks, operator=operator[0], columns=columns)
    inward = ((0, 1), (3, 2))
    outward = ((1, 0), (2, 3))
    middle = ((1, 2), (2, 1))
    ends = ((0, 3), (3, 0))
    beyond = ((1, 3), (2, 0))

    far_data = hand(survey_data[0], *inward, *outward)
    (r_head,) = make(receiver_field[0], sets=[INNER[:HEAD]], listed=True, limit=HEAD_LIMIT)
    r_3_head = hand(r_head, *middle)
    r_1_head = hand(r_head, *inward)
    r_inner, r_outer = make(receiver_field[0], sets=[INNER[HEAD:], OUTER], after=(r_head,))
    r_1_out = hand(following(r_outer, far_data), *outward)
    r_3_in = hand(r_inner, *middle)
    r_1_in = hand(r_inner, *inward)
    s_inner, s_outer = make(source_field[0], sets=[INNER, OUTER], after=(r_outer, r_3_head, r_1_head))
    s_out = hand(s_outer, *outward)
    s_in = hand(s_inner, *inward)
    forward_head = hand(following(r_1_head, r_3_in), *middle)
    r_3_out = hand(following(r_outer, r_1_out), *ends)
    forward = hand(r_1_in, *middle)
    beyond_1 = hand(following(r_outer, s_out, forward_head)[:OUTER_FIRST], *beyond)
    beyond_2 = hand(r_outer[OUTER_FIRST:], *beyond)

    ids = survey_tiles[:, 1]
    near_ids = lax.dynamic_slice_in_dim(ids, shot * tiles, tiles)
    far_ids = lax.dynamic_slice_in_dim(ids, (shot ^ 1) * tiles, tiles)
    product = product_blocks(
        s_inner, s_outer, s_in, s_out, survey_data[0], far_data, near_ids, far_ids, inner
    )
    early = [
        (shot, [(r_head, 0), (r_inner, HEAD), (r_outer, 0)]),
        (shot ^ 1, [(r_1_head, 0), (r_1_in, HEAD), (r_1_out, 0)]),
        (shot ^ 3, [(r_3_head, 0), (r_3_in, HEAD), (r_3_out, 0)]),
    ]
    forwarded = [(forward_head, 0), (forward, HEAD)]
    one = image_blocks(product, 0, FIRST, early, inner)
    two = image_blocks(product, FIRST, len(INNER) - FIRST, early, inner)
    one = image_blocks(product, 0, FIRST, [(shot ^ 2, forwarded + [(beyond_1, 0)])], inner, one)
    two = image_blocks(
        product, FIRST, len(INNER) - FIRST, [(shot ^ 2, forwarded + [(beyond_2, OUTER_FIRST)])], inner,
        following(two, one),
    )
    image = sum_images(one, two, shot, freq)
    total_freqs = source_field.shape[0] * lax.axis_size("freq")
    return image * (1.0 / math.sqrt(2.0 * NR * total_freqs))


def body(source_field, *rest):
    fits = (
        lax.axis_size("shot") == 4
        and lax.axis_size("freq") == 4
        and source_field.shape[1:] == (512, 16, 2, 128)
    )
    return (split_body if fits else general_body)(source_field, *rest)


def solution(mesh):
    return jax.shard_map(
        body,
        mesh=mesh,
        in_specs=(
            P("freq", ("groups", "shot"), None, None, None),
            P("freq", ("groups", "shot"), None, None, None),
            P("freq", "groups", None, None, None, None),
            P("groups", None),
            P("groups", None),
            P("freq", ("groups", "shot"), None, None, None),
        ),
        out_specs=P(None, ("groups", "shot", "freq"), None),
        check_vma=False,
    )
```

profile of v0, /device:TPU:0, one launch (start us, length us, event | category | flops | bytes accessed | tf_op | source)
XLA Modules:
  0.0 227.2 jit_solution(2953936143876089012)
XLA Ops:
  0.0 3.0 %collective-permute-start.4 = (bf16[16,2,128,128]{3,2,1,0:T(8,128)(2,1)}, bf16[16,2,128,128]{3,2,1,0:T(8,128)(2,1)}, u32[]{:S(2)}, u32[]{:S(2)}) collective-permute-start(bf16[16,2,128,128]{3,2,1,0:T(8,128)(2,1)} %bitcast.33), channel_id=1, source_target_pairs={{0,4},{12,8},{4,0},{8,12},{1,5},{13,9},{5,1},{9,13},{2,6},{14,10},... | collective-permute-start | bytes 3145736 | tf_op jit(solution)/shard_map/ppermute | solution.py:328
  4.4 9.2 %extrapolate.3.refs_0_.refs_3_ = bf16[3,512,256]{2,1,0:T(8,128)(2,1)} custom-call(s32[3]{0:T(128)} %constant.50.clone.order, s32[16,3]{1,0:T(8,128)} %add_select_fusion.columns, bf16[16384,128]{1,0:T(8,128)(2,1)} %bitcast.30, bf16[16,3,2,128,128]{4,3,2,1,0:T(8,128)(2,1)} %bitcast.27), custom_call_target="tpu_custom_call" | custom-call | flops 1000 | bytes 1000 | tf_op jit(solution)/shard_map/extrapolate/pallas_call | solution.py:180
  13.6 1.9 collective-permute-start.1
  16.3 1.9 copy-done
  18.2 2.2 copy-done.2
  21.5 11.5 %extrapolate.4 = (bf16[6,512,256]{2,1,0:T(8,128)(2,1)S(1)}, bf16[7,512,256]{2,1,0:T(8,128)(2,1)S(1)}) custom-call(s32[13]{0:T(128)S(1)} %copy-done.21, s32[16,3]{1,0:T(8,128)S(1)} %copy-done.19, bf16[16384,128]{1,0:T(8,128)(2,1)S(1)} %bitcast.31, bf16[16,3,2,128,128]{4,3,2,1,0:T(8,128)(2,1)S(1)} %bitcast.28, bf16[3,512,256]{2,1,0:T(8,128)(2,1)S(1)} %copy-done.3), custom_call_target="tpu_custom_call" | custom-call | flops 1000 | bytes 1000 | tf_op jit(solution)/shard_map/extrapolate/pallas_call | solution.py:180
  33.0 1.3 collective-permute-start.10
  35.1 10.1 %collective-permute-start.7 = (bf16[6,512,256]{2,1,0:T(8,128)(2,1)S(1)}, bf16[6,512,256]{2,1,0:T(8,128)(2,1)}, u32[]{:S(2)}, u32[]{:S(2)}) collective-permute-start(bf16[6,512,256]{2,1,0:T(8,128)(2,1)S(1)} %get-tuple-element.17.refs_4_), channel_id=1, source_target_pairs={{0,4},{12,8},{1,5},{13,9},{2,6},{14,10},{3,7},{15,11},{16,20},{28,... | collective-permute-start | bytes 4718600 | tf_op jit(solution)/shard_map/ppermute | solution.py:328
  45.3 14.7 %extrapolate.5 = (bf16[9,512,256]{2,1,0:T(8,128)(2,1)}, bf16[7,512,256]{2,1,0:T(8,128)(2,1)S(1)}) custom-call(s32[16]{0:T(128)S(1)} %copy-done.20, s32[16,3]{1,0:T(8,128)S(1)} %copy-done.19, bf16[16384,128]{1,0:T(8,128)(2,1)S(1)} %bitcast.32, bf16[16,3,2,128,128]{4,3,2,1,0:T(8,128)(2,1)S(1)} %bitcast.29, ...), custom_call_target="tpu_custom_call" | custom-call | flops 1000 | bytes 1000 | tf_op jit(solution)/shard_map/extrapolate/pallas_call | solution.py:180
  60.0 1.3 collective-permute-start.3
  62.5 6.2 %collective-permute-start.2 = (bf16[9,512,256]{2,1,0:T(8,128)(2,1)}, bf16[9,512,256]{2,1,0:T(8,128)(2,1)}, u32[]{:S(2)}, u32[]{:S(2)}) collective-permute-start(bf16[9,512,256]{2,1,0:T(8,128)(2,1)} %get-tuple-element.15.near_in), channel_id=1, source_target_pairs={{0,4},{12,8},{1,5},{13,9},{2,6},{14,10},{3,7},{15,11},{16,20},{28,... | collective-permute-start | bytes 7077896 | tf_op jit(solution)/shard_map/ppermute | solution.py:328
  69.5 9.5 %collective-permute-done.10.refs_8_ = bf16[7,512,256]{2,1,0:T(8,128)(2,1)S(1)} collective-permute-done((bf16[7,512,256]{2,1,0:T(8,128)(2,1)S(1)}, bf16[7,512,256]{2,1,0:T(8,128)(2,1)S(1)}, u32[]{:S(2)}, u32[]{:S(2)}) %collective-permute-start.10) | collective-permute-done | bytes 1835040 | tf_op jit(solution)/shard_map/ppermute | solution.py:328
  78.9 4.9 %collective-permute-start.11 = (bf16[7,512,256]{2,1,0:T(8,128)(2,1)S(1)}, bf16[7,512,256]{2,1,0:T(8,128)(2,1)}, u32[]{:S(2)}, u32[]{:S(2)}) collective-permute-start(bf16[7,512,256]{2,1,0:T(8,128)(2,1)S(1)} %get-tuple-element.21.refs_0_.refs_5_), channel_id=1, source_target_pairs={{0,12},{12,0},{1,13},{13,1},{2,14},{14,2},{3,15},{15,3},{16,28},{2... | collective-permute-start | bytes 5505032 | tf_op jit(solution)/shard_map/ppermute | solution.py:328
  83.8 1.8 collective-permute-start.8
  86.5 30.2 %collective-permute-done.3.far_out = bf16[7,512,256]{2,1,0:T(8,128)(2,1)S(1)} collective-permute-done((bf16[7,512,256]{2,1,0:T(8,128)(2,1)S(1)}, bf16[7,512,256]{2,1,0:T(8,128)(2,1)S(1)}, u32[]{:S(2)}, u32[]{:S(2)}) %collective-permute-start.3) | collective-permute-done | bytes 1835040 | tf_op jit(solution)/shard_map/ppermute | solution.py:328
  121.3 1.3 collective-permute-start.12
  122.8 6.7 %collective-permute-done.2.far_in = bf16[9,512,256]{2,1,0:T(8,128)(2,1)} collective-permute-done((bf16[9,512,256]{2,1,0:T(8,128)(2,1)}, bf16[9,512,256]{2,1,0:T(8,128)(2,1)}, u32[]{:S(2)}, u32[]{:S(2)}) %collective-permute-start.2) | collective-permute-done | bytes 2359328 | tf_op jit(solution)/shard_map/ppermute | solution.py:328
  129.6 1.5 copy-done.15
  131.1 1.5 copy-done.17
  133.8 14.6 %product.1.refs_0_.refs_1_.refs_2_ = bf16[9,256,2048]{2,1,0:T(8,128)(2,1)S(1)} custom-call(s32[16]{0:T(128)S(1)} %get-tuple-element.24.near_ids, s32[16]{0:T(128)S(1)} %get-tuple-element.23.far_ids, s32[1]{0:T(128)} %bitcast.1.inner, bf16[9,512,256]{2,1,0:T(8,128)(2,1)} %get-tuple-element.15.near_in, bf16[7,512,256]{2,1,0:T(8,128)(2,1)S(1)} %copy-done.15, ...), custom_call_target="tpu_custom_call" | custom-call | flops 1000 | bytes 1000 | tf_op jit(solution)/shard_map/product/pallas_call | solution.py:250
  148.4 20.8 %collective-permute-done.11.refs_11_ = bf16[7,512,256]{2,1,0:T(8,128)(2,1)} collective-permute-done((bf16[7,512,256]{2,1,0:T(8,128)(2,1)S(1)}, bf16[7,512,256]{2,1,0:T(8,128)(2,1)}, u32[]{:S(2)}, u32[]{:S(2)}) %collective-permute-start.11) | collective-permute-done | bytes 1835040 | tf_op jit(solution)/shard_map/ppermute | solution.py:328
  169.3 4.1 %image.6.refs_4_ = f32[4,2,128,128]{3,2,1,0:T(8,128)S(1)} custom-call(s32[3]{0:T(128)S(1)} %pad_add_fusion.places.unused, s32[3]{0:T(128)S(1)} %pad_add_fusion.places.unused, s32[1]{0:T(128)} %bitcast.1.inner, bf16[9,256,2048]{2,1,0:T(8,128)(2,1)S(1)} %product.1.refs_0_.refs_1_.refs_2_, bf16[9,256,2048]{2,1,0:T(8,128)(2,1)S(1)} %product.1.refs_0_.refs_1_.refs_2_, ...), custom_call_target="tpu_custom_call" | custom-call | flops 1000 | bytes 1000 | tf_op jit(solution)/shard_map/image/pallas_call | solution.py:311
  173.4 4.7 %image.4.refs_4_ = f32[5,2,128,128]{3,2,1,0:T(8,128)S(1)} custom-call(s32[3]{0:T(128)S(1)} %pad_add_fusion.places.unused, s32[3]{0:T(128)S(1)} %pad_add_fusion.places.unused, s32[1]{0:T(128)} %bitcast.1.inner, bf16[9,256,2048]{2,1,0:T(8,128)(2,1)S(1)} %product.1.refs_0_.refs_1_.refs_2_, bf16[9,256,2048]{2,1,0:T(8,128)(2,1)S(1)} %product.1.refs_0_.refs_1_.refs_2_, ...), custom_call_target="tpu_custom_call" | custom-call | flops 1000 | bytes 1000 | tf_op jit(solution)/shard_map/image/pallas_call | solution.py:311
  178.1 15.0 %collective-permute-done.9.refs_3_ = bf16[4,512,256]{2,1,0:T(8,128)(2,1)} collective-permute-done((bf16[4,512,256]{2,1,0:T(8,128)(2,1)}, bf16[4,512,256]{2,1,0:T(8,128)(2,1)}, u32[]{:S(2)}, u32[]{:S(2)}) %collective-permute-start.9) | collective-permute-done | bytes 1048608 | tf_op jit(solution)/shard_map/ppermute | solution.py:328
  193.1 3.2 %image.5 = f32[5,2,128,128]{3,2,1,0:T(8,128)S(1)} custom-call(s32[1]{0:T(128)} %bitcast.places.unused, s32[1]{0:T(128)} %bitcast.places.unused, s32[1]{0:T(128)} %bitcast.1.inner, bf16[9,256,2048]{2,1,0:T(8,128)(2,1)S(1)} %product.1.refs_0_.refs_1_.refs_2_, bf16[3,512,256]{2,1,0:T(8,128)(2,1)S(1)} %copy-done.13, ...), custom_call_target="tpu_custom_call" | custom-call | flops 1000 | bytes 1000 | tf_op jit(solution)/shard_map/image/pallas_call | solution.py:311
  196.3 11.1 %collective-permute-done.12.refs_3_ = bf16[3,512,256]{2,1,0:T(8,128)(2,1)} collective-permute-done((bf16[3,512,256]{2,1,0:T(8,128)(2,1)}, bf16[3,512,256]{2,1,0:T(8,128)(2,1)}, u32[]{:S(2)}, u32[]{:S(2)}) %collective-permute-start.12) | collective-permute-done | bytes 786464 | tf_op jit(solution)/shard_map/ppermute | solution.py:328
  207.4 2.9 %image.7 = f32[4,2,128,128]{3,2,1,0:T(8,128)S(1)} custom-call(s32[1]{0:T(128)} %bitcast.places.unused, s32[1]{0:T(128)} %bitcast.places.unused, s32[1]{0:T(128)} %bitcast.1.inner, bf16[9,256,2048]{2,1,0:T(8,128)(2,1)S(1)} %product.1.refs_0_.refs_1_.refs_2_, bf16[3,512,256]{2,1,0:T(8,128)(2,1)S(1)} %copy-done.13, ...), custom_call_target="tpu_custom_call" | custom-call | flops 1000 | bytes 1000 | tf_op jit(solution)/shard_map/image/pallas_call | solution.py:311
  210.4 1.6 collective-permute-done.13
  212.8 1.6 collective-permute-start.17
  215.8 2.7 %collective-permute-done.17 = bf16[2,2,128,128]{3,2,1,0:T(8,128)(2,1)S(1)} collective-permute-done((bf16[2,2,128,128]{3,2,1,0:T(8,128)(2,1)S(1)}, bf16[2,2,128,128]{3,2,1,0:T(8,128)(2,1)S(1)}, u32[]{:S(2)}, u32[]{:S(2)}) %collective-permute-start.17) | collective-permute-done | bytes 131104 | tf_op jit(solution)/shard_map/ppermute | solution.py:333
  218.5 4.3 %collective-permute-start.18 = (bf16[2,128,128]{2,1,0:T(8,128)(2,1)S(1)}, bf16[2,128,128]{2,1,0:T(8,128)(2,1)S(1)}, u32[]{:S(2)}, u32[]{:S(2)}) collective-permute-start(bf16[2,128,128]{2,1,0:T(8,128)(2,1)S(1)} %fusion.3), channel_id=1, source_target_pairs={{0,12},{1,13},{2,14},{4,8},{5,9},{6,10},{7,11},{8,4},{9,5},{10,6},... | collective-permute-start | bytes 196616 | tf_op jit(solution)/shard_map/ppermute | solution.py:333
  222.8 3.6 %collective-permute-done.18 = bf16[2,128,128]{2,1,0:T(8,128)(2,1)S(1)} collective-permute-done((bf16[2,128,128]{2,1,0:T(8,128)(2,1)S(1)}, bf16[2,128,128]{2,1,0:T(8,128)(2,1)S(1)}, u32[]{:S(2)}, u32[]{:S(2)}) %collective-permute-start.18) | collective-permute-done | bytes 65568 | tf_op jit(solution)/shard_map/ppermute | solution.py:333
  (76 shorter events, 15.9 us)
Async XLA Ops:
  0.0 33.0 %collective-permute-start.4 = (bf16[16,2,128,128]{3,2,1,0:T(8,128)(2,1)}, bf16[16,2,128,128]{3,2,1,0:T(8,128)(2,1)}, u32[]{:S(2)}, u32[]{:S(2)}) collective-permute-start(bf16[16,2,128,128]{3,2,1,0:T(8,128)(2,1)} %bitcast.33), channel_id=1, source_target_pairs={{0,4},{12,8},{4,0},{8,12},{1,5},{13,9},{5,1},{9,13},{2,6},{14,10},... | collective-permute-start | bytes 3145736 | tf_op jit(solution)/shard_map/ppermute | solution.py:328
  4.4 11.9 %copy-start.21 = (s32[13]{0:T(128)S(1)}, s32[13]{0:T(128)}, u32[]{:S(2)}) copy-start(s32[13]{0:T(128)} %constant.51.clone.order) | copy-start | bytes 160
  4.4 40.8 %copy-start.20 = (s32[16]{0:T(128)S(1)}, s32[16]{0:T(128)}, u32[]{:S(2)}) copy-start(s32[16]{0:T(128)} %constant.52.clone.order) | copy-start | bytes 196
  13.6 31.7 %collective-permute-start.1 = (bf16[3,512,256]{2,1,0:T(8,128)(2,1)}, bf16[3,512,256]{2,1,0:T(8,128)(2,1)S(1)}, u32[]{:S(2)}, u32[]{:S(2)}) collective-permute-start(bf16[3,512,256]{2,1,0:T(8,128)(2,1)} %extrapolate.3.refs_0_.refs_3_), channel_id=1, source_target_pairs={{0,4},{12,8},{1,5},{13,9},{2,6},{14,10},{3,7},{15,11},{16,20},{28,... | collective-permute-start | bytes 2359304 | tf_op jit(solution)/shard_map/ppermute | solution.py:328
  15.5 29.7 %collective-permute-start = (bf16[3,512,256]{2,1,0:T(8,128)(2,1)}, bf16[3,512,256]{2,1,0:T(8,128)(2,1)S(1)}, u32[]{:S(2)}, u32[]{:S(2)}) collective-permute-start(bf16[3,512,256]{2,1,0:T(8,128)(2,1)} %extrapolate.3.refs_0_.refs_3_), channel_id=1, source_target_pairs={{4,8},{8,4},{5,9},{9,5},{6,10},{10,6},{7,11},{11,7},{20,24},{24,20... | collective-permute-start | bytes 2359304 | tf_op jit(solution)/shard_map/ppermute | solution.py:328
  21.5 23.8 %copy-start.1 = (bf16[1,16,3,2,128,128]{5,4,3,2,1,0:T(8,128)(2,1)S(1)}, bf16[1,16,3,2,128,128]{5,4,3,2,1,0:T(8,128)(2,1)}, u32[]{:S(2)}) copy-start(bf16[1,16,3,2,128,128]{5,4,3,2,1,0:T(8,128)(2,1)} %param.11) | copy-start | bytes 9437188
  21.5 23.8 %copy-start.11 = (bf16[1,512,16,2,128]{4,3,2,1,0:T(2,128)(2,1)S(1)}, bf16[1,512,16,2,128]{4,3,2,1,0:T(2,128)(2,1)}, u32[]{:S(2)}) copy-start(bf16[1,512,16,2,128]{4,3,2,1,0:T(2,128)(2,1)} %param.9) | copy-start | bytes 12582916
  33.0 27.0 %copy-start.7 = (bf16[6,512,256]{2,1,0:T(8,128)(2,1)}, bf16[6,512,256]{2,1,0:T(8,128)(2,1)S(1)}, u32[]{:S(2)}) copy-start(bf16[6,512,256]{2,1,0:T(8,128)(2,1)S(1)} %get-tuple-element.17.refs_4_) | copy-start | bytes 4718596
  33.0 45.9 %collective-permute-start.10 = (bf16[7,512,256]{2,1,0:T(8,128)(2,1)S(1)}, bf16[7,512,256]{2,1,0:T(8,128)(2,1)S(1)}, u32[]{:S(2)}, u32[]{:S(2)}) collective-permute-start(bf16[7,512,256]{2,1,0:T(8,128)(2,1)S(1)} %get-tuple-element.21.refs_0_.refs_5_), channel_id=1, source_target_pairs={{4,0},{8,12},{5,1},{9,13},{6,2},{10,14},{7,3},{11,15},{20,16},{24,... | collective-permute-start | bytes 5505032 | tf_op jit(solution)/shard_map/ppermute | solution.py:328
  34.3 34.4 %collective-permute-start.5 = (bf16[6,512,256]{2,1,0:T(8,128)(2,1)S(1)}, bf16[6,512,256]{2,1,0:T(8,128)(2,1)S(1)}, u32[]{:S(2)}, u32[]{:S(2)}) collective-permute-start(bf16[6,512,256]{2,1,0:T(8,128)(2,1)S(1)} %get-tuple-element.17.refs_4_), channel_id=1, source_target_pairs={{4,8},{8,4},{5,9},{9,5},{6,10},{10,6},{7,11},{11,7},{20,24},{24,20... | collective-permute-start | bytes 4718600 | tf_op jit(solution)/shard_map/ppermute | solution.py:328
  35.1 48.7 %collective-permute-start.7 = (bf16[6,512,256]{2,1,0:T(8,128)(2,1)S(1)}, bf16[6,512,256]{2,1,0:T(8,128)(2,1)}, u32[]{:S(2)}, u32[]{:S(2)}) collective-permute-start(bf16[6,512,256]{2,1,0:T(8,128)(2,1)S(1)} %get-tuple-element.17.refs_4_), channel_id=1, source_target_pairs={{0,4},{12,8},{1,5},{13,9},{2,6},{14,10},{3,7},{15,11},{16,20},{28,... | collective-permute-start | bytes 4718600 | tf_op jit(solution)/shard_map/ppermute | solution.py:328
  60.0 56.8 %collective-permute-start.3 = (bf16[7,512,256]{2,1,0:T(8,128)(2,1)S(1)}, bf16[7,512,256]{2,1,0:T(8,128)(2,1)S(1)}, u32[]{:S(2)}, u32[]{:S(2)}) collective-permute-start(bf16[7,512,256]{2,1,0:T(8,128)(2,1)S(1)} %get-tuple-element.16.near_out), channel_id=1, source_target_pairs={{4,0},{8,12},{5,1},{9,13},{6,2},{10,14},{7,3},{11,15},{20,16},{24,... | collective-permute-start | bytes 5505032 | tf_op jit(solution)/shard_map/ppermute | solution.py:328
  62.5 60.1 %copy-start.22 = (s32[64,2]{0,1:T(2,128)S(1)}, s32[64,2]{0,1:T(2,128)}, u32[]{:S(2)}) copy-start(s32[64,2]{0,1:T(2,128)} %param.13) | copy-start | bytes 1540
  62.5 67.0 %collective-permute-start.2 = (bf16[9,512,256]{2,1,0:T(8,128)(2,1)}, bf16[9,512,256]{2,1,0:T(8,128)(2,1)}, u32[]{:S(2)}, u32[]{:S(2)}) collective-permute-start(bf16[9,512,256]{2,1,0:T(8,128)(2,1)} %get-tuple-element.15.near_in), channel_id=1, source_target_pairs={{0,4},{12,8},{1,5},{13,9},{2,6},{14,10},{3,7},{15,11},{16,20},{28,... | collective-permute-start | bytes 7077896 | tf_op jit(solution)/shard_map/ppermute | solution.py:328
  68.7 52.6 %copy-start.9 = (bf16[6,512,256]{2,1,0:T(8,128)(2,1)}, bf16[6,512,256]{2,1,0:T(8,128)(2,1)S(1)}, u32[]{:S(2)}) copy-start(bf16[6,512,256]{2,1,0:T(8,128)(2,1)S(1)} %collective-permute-done.5.refs_10_) | copy-start | bytes 4718596
  68.8 16.9 %collective-permute-start.6 = (bf16[3,512,256]{2,1,0:T(8,128)(2,1)S(1)}, bf16[3,512,256]{2,1,0:T(8,128)(2,1)S(1)}, u32[]{:S(2)}, u32[]{:S(2)}) collective-permute-start(bf16[3,512,256]{2,1,0:T(8,128)(2,1)S(1)} %collective-permute-done.1.refs_2_.refs_6_), channel_id=1, source_target_pairs={{4,8},{8,4},{5,9},{9,5},{6,10},{10,6},{7,11},{11,7},{20,24},{24,20... | collective-permute-start | bytes 2359304 | tf_op jit(solution)/shard_map/ppermute | solution.py:328
  78.9 42.4 %copy-start.5 = (bf16[7,512,256]{2,1,0:T(8,128)(2,1)}, bf16[7,512,256]{2,1,0:T(8,128)(2,1)S(1)}, u32[]{:S(2)}) copy-start(bf16[7,512,256]{2,1,0:T(8,128)(2,1)S(1)} %collective-permute-done.10.refs_8_) | copy-start | bytes 5505028
  78.9 90.3 %collective-permute-start.11 = (bf16[7,512,256]{2,1,0:T(8,128)(2,1)S(1)}, bf16[7,512,256]{2,1,0:T(8,128)(2,1)}, u32[]{:S(2)}, u32[]{:S(2)}) collective-permute-start(bf16[7,512,256]{2,1,0:T(8,128)(2,1)S(1)} %get-tuple-element.21.refs_0_.refs_5_), channel_id=1, source_target_pairs={{0,12},{12,0},{1,13},{13,1},{2,14},{14,2},{3,15},{15,3},{16,28},{2... | collective-permute-start | bytes 5505032 | tf_op jit(solution)/shard_map/ppermute | solution.py:328
  83.8 94.3 %collective-permute-start.8 = (bf16[6,512,256]{2,1,0:T(8,128)(2,1)}, bf16[6,512,256]{2,1,0:T(8,128)(2,1)}, u32[]{:S(2)}, u32[]{:S(2)}) collective-permute-start(bf16[6,512,256]{2,1,0:T(8,128)(2,1)} %collective-permute-done.7.refs_7_), channel_id=1, source_target_pairs={{4,8},{8,4},{5,9},{9,5},{6,10},{10,6},{7,11},{11,7},{20,24},{24,20... | collective-permute-start | bytes 4718600 | tf_op jit(solution)/shard_map/ppermute | solution.py:328
  119.0 74.1 %collective-permute-start.9 = (bf16[4,512,256]{2,1,0:T(8,128)(2,1)}, bf16[4,512,256]{2,1,0:T(8,128)(2,1)}, u32[]{:S(2)}, u32[]{:S(2)}) collective-permute-start(bf16[4,512,256]{2,1,0:T(8,128)(2,1)} %slice.35), channel_id=1, source_target_pairs={{4,12},{8,0},{5,13},{9,1},{6,14},{10,2},{7,15},{11,3},{20,28},{24,... | collective-permute-start | bytes 3145736 | tf_op jit(solution)/shard_map/ppermute | solution.py:328
  121.3 86.1 %collective-permute-start.12 = (bf16[3,512,256]{2,1,0:T(8,128)(2,1)}, bf16[3,512,256]{2,1,0:T(8,128)(2,1)}, u32[]{:S(2)}, u32[]{:S(2)}) collective-permute-start(bf16[3,512,256]{2,1,0:T(8,128)(2,1)} %slice.36), channel_id=1, source_target_pairs={{4,12},{8,0},{5,13},{9,1},{6,14},{10,2},{7,15},{11,3},{20,28},{24,... | collective-permute-start | bytes 2359304 | tf_op jit(solution)/shard_map/ppermute | solution.py:328
  133.8 35.4 %copy-start.4 = (bf16[3,512,256]{2,1,0:T(8,128)(2,1)S(1)}, bf16[3,512,256]{2,1,0:T(8,128)(2,1)}, u32[]{:S(2)}) copy-start(bf16[3,512,256]{2,1,0:T(8,128)(2,1)} %extrapolate.3.refs_0_.refs_3_) | copy-start | bytes 2359300
  133.8 35.4 %copy-start.6 = (bf16[7,512,256]{2,1,0:T(8,128)(2,1)S(1)}, bf16[7,512,256]{2,1,0:T(8,128)(2,1)}, u32[]{:S(2)}) copy-start(bf16[7,512,256]{2,1,0:T(8,128)(2,1)} %copy-done.5) | copy-start | bytes 5505028
  133.8 35.5 %copy-start.8 = (bf16[6,512,256]{2,1,0:T(8,128)(2,1)S(1)}, bf16[6,512,256]{2,1,0:T(8,128)(2,1)}, u32[]{:S(2)}) copy-start(bf16[6,512,256]{2,1,0:T(8,128)(2,1)} %copy-done.7) | copy-start | bytes 4718596
  133.8 35.5 %copy-start.10 = (bf16[6,512,256]{2,1,0:T(8,128)(2,1)S(1)}, bf16[6,512,256]{2,1,0:T(8,128)(2,1)}, u32[]{:S(2)}) copy-start(bf16[6,512,256]{2,1,0:T(8,128)(2,1)} %copy-done.9) | copy-start | bytes 4718596
  173.4 19.7 %copy-start.13 = (bf16[3,512,256]{2,1,0:T(8,128)(2,1)S(1)}, bf16[3,512,256]{2,1,0:T(8,128)(2,1)}, u32[]{:S(2)}) copy-start(bf16[3,512,256]{2,1,0:T(8,128)(2,1)} %copy-done.12) | copy-start | bytes 2359300
  210.3 1.7 collective-permute-start.13
  212.1 2.3 %collective-permute-start.14 = (bf16[2,128,128]{2,1,0:T(8,128)(2,1)S(1)}, bf16[2,128,128]{2,1,0:T(8,128)(2,1)S(1)}, u32[]{:S(2)}, u32[]{:S(2)}) collective-permute-start(bf16[2,128,128]{2,1,0:T(8,128)(2,1)S(1)} %fusion.2), channel_id=1, source_target_pairs={{5,7},{9,11},{21,23},{25,27}} | collective-permute-start | bytes 196616 | tf_op jit(solution)/shard_map/ppermute | solution.py:333
  212.8 5.6 %collective-permute-start.17 = (bf16[2,2,128,128]{3,2,1,0:T(8,128)(2,1)S(1)}, bf16[2,2,128,128]{3,2,1,0:T(8,128)(2,1)S(1)}, u32[]{:S(2)}, u32[]{:S(2)}) collective-permute-start(bf16[2,2,128,128]{3,2,1,0:T(8,128)(2,1)S(1)} %select_convert_fusion.1), channel_id=1, source_target_pairs={{0,2},{1,3},{2,0},{3,1},{4,6},{5,7},{6,4},{7,5},{8,10},{9,11},{10,... | collective-permute-start | bytes 393224 | tf_op jit(solution)/shard_map/ppermute | solution.py:333
  214.4 8.4 %collective-permute-start.15 = (bf16[2,128,128]{2,1,0:T(8,128)(2,1)S(1)}, bf16[2,128,128]{2,1,0:T(8,128)(2,1)S(1)}, u32[]{:S(2)}, u32[]{:S(2)}) collective-permute-start(bf16[2,128,128]{2,1,0:T(8,128)(2,1)S(1)} %add_convert_fusion), channel_id=1, source_target_pairs={{7,15},{23,31}} | collective-permute-start | bytes 196616 | tf_op jit(solution)/shard_map/ppermute | solution.py:333
  215.1 7.7 %collective-permute-start.16 = (bf16[2,128,128]{2,1,0:T(8,128)(2,1)S(1)}, bf16[2,128,128]{2,1,0:T(8,128)(2,1)S(1)}, u32[]{:S(2)}, u32[]{:S(2)}) collective-permute-start(bf16[2,128,128]{2,1,0:T(8,128)(2,1)S(1)} %add_convert_fusion), channel_id=1, source_target_pairs={{11,15},{27,31}} | collective-permute-start | bytes 196616 | tf_op jit(solution)/shard_map/ppermute | solution.py:333
  218.5 8.0 %collective-permute-start.18 = (bf16[2,128,128]{2,1,0:T(8,128)(2,1)S(1)}, bf16[2,128,128]{2,1,0:T(8,128)(2,1)S(1)}, u32[]{:S(2)}, u32[]{:S(2)}) collective-permute-start(bf16[2,128,128]{2,1,0:T(8,128)(2,1)S(1)} %fusion.3), channel_id=1, source_target_pairs={{0,12},{1,13},{2,14},{4,8},{5,9},{6,10},{7,11},{8,4},{9,5},{10,6},... | collective-permute-start | bytes 196616 | tf_op jit(solution)/shard_map/ppermute | solution.py:333
  (10 other events, 24.7 us)
where the time goes:
time: 228 us; the launch traced here: 227 us
  waiting for transfers between devices  101 us (44%)
  Pallas kernels  64.9 us (28%)
  starting transfers between devices  43.3 us (19%)
  local copies, waits for them, and re-layouts  15.7 us (7%)
    ppermute x13, waiting for transfers between devices, hand(): return lax.ppermute(value, 'shot', pairs)  93.3 us
    pallas_call x3, Pallas kernels, extrapolate_blocks(): pl.pallas_call(functools.partial(extrapolate_kernel, sizes=sizes, rows=ro...  35.4 us
    ppermute x13, starting transfers between devices, hand(): return lax.ppermute(value, 'shot', pairs)  35.4 us
    pallas_call x4, Pallas kernels, image_blocks(): pl.pallas_call(functools.partial(image_kernel, first=first, begins=begins...  14.9 us
    pallas_call x1, Pallas kernels, product_blocks(): pl.pallas_call(product_kernel, grid_spec=pltpu.PrefetchScalarGridSpec(num...  14.6 us
    unnamed x47, local copies, waits for them, and re-layouts  13.6 us
    ppermute x6, waiting for transfers between devices, send_sum(): lax.ppermute(value.astype(jnp.bfloat16), ('shot', 'freq'), pairs)  7.93 us
    ppermute x6, starting transfers between devices, send_sum(): lax.ppermute(value.astype(jnp.bfloat16), ('shot', 'freq'), pairs)  7.89 us
  transfers between devices with their start and end apart: 19, of which 9 were waited for; matrix products, arithmetic and copies ran while one was open for 2% of the time, Pallas kernels for 27%

commit v1 on v0

--- a/solution.py
+++ b/solution.py
@@ -9,7 +9,6 @@
 from jax.sharding import PartitionSpec as P
 
 NR = 2048
-HEAD_LIMIT = 60
 SMALL = pl.CostEstimate(flops=1000, bytes_accessed=1000, transcendentals=0)
 
 
@@ -115,43 +114,65 @@
     return pltpu.CompilerParams(vmem_limit_bytes=limit * 1024 * 1024)
 
 
-def extrapolate_kernel(order, columns, field, operator, *refs, sizes, rows, blocks, chunk, listed):
-    stage, apart = refs[-2:]
-    outs = refs[-2 - len(sizes):-2]
+def extrapolate_kernel(order, offsets, field, operator, *refs, sets, rows, blocks, parts, listed):
+    stage, apart, lines, weights, field_sems, weight_sems = refs[-6:]
+    outs = refs[:-6]
+    sizes = [len(one) for one in sets]
     step = pl.program_id(0)
-    lines = 2 * blocks
     bands = operator.shape[1]
+    pitch = 2 * blocks + 1
+    chunk = stage.shape[0] // pitch
+    part_lines = lines.shape[0] // parts
+
+    def column(block, band):
+        return lax.rem(block + offsets[band, block] + blocks, blocks)
+
+    def field_copy(part):
+        here = pl.ds(part * part_lines, part_lines)
+        return pltpu.make_async_copy(field.at[here], lines.at[here], field_sems.at[part])
+
+    def weight_copy(n, block):
+        return pltpu.make_async_copy(operator.at[block], weights.at[n], weight_sems.at[n])
 
     @pl.when(step == 0)
     def _():
+        for part in range(parts):
+            field_copy(part).start()
+        for n, block in enumerate(sum(sets, [])):
+            weight_copy(n, block).start()
         if listed:
-            wanted = [columns[order[n // bands], n % bands] for n in range(sum(sizes) * bands)]
+            wanted = [column(block, band) for block in sum(sets, []) for band in range(bands)]
         else:
             wanted = list(range(blocks))
 
         def split(n, carry):
-            start = pl.multiple_of(n * (chunk * lines), chunk * lines)
-            stage[...] = field[pl.ds(start, chunk * lines), :].astype(jnp.float32)
+            for row in range(chunk):
+                here = pl.ds(pl.multiple_of((n * chunk + row) * 2 * blocks, 2 * blocks), 2 * blocks)
+                stage[pl.ds(row * pitch, 2 * blocks), :] = lines[here, :].astype(jnp.float32)
             to = pl.ds(pl.multiple_of(n * chunk, chunk), chunk)
             for slot, block in enumerate(wanted):
-                for part in range(2):
-                    picked = stage[pl.ds(2 * block + part, chunk, stride=lines), :]
-                    apart[slot, to, part * 128:(part + 1) * 128] = picked.astype(jnp.bfloat16)
+                for half in range(2):
+                    picked = stage[pl.ds(2 * block + half, chunk, stride=pitch), :]
+                    apart[slot, to, half * 128:(half + 1) * 128] = picked.astype(jnp.bfloat16)
             return carry
 
-        lax.fori_loop(0, rows // chunk, split, 0)
+        steps = rows // chunk // parts
+        for part in range(parts):
+            field_copy(part).wait()
+            lax.fori_loop(part * steps, (part + 1) * steps, split, 0)
 
     block = order[step]
+    weight_copy(step, block).wait()
     inputs = []
-    weights = []
+    factors = []
     for band in range(bands):
-        inputs.append(apart[step * bands + band if listed else columns[block, band]])
-        real = operator[0, band, 0]
-        imag = operator[0, band, 1]
-        weights.append(jnp.concatenate([real, imag], 1))
-        weights.append(jnp.concatenate([-imag, real], 1))
+        inputs.append(apart[step * bands + band if listed else column(block, band)])
+        real = weights[step, band, 0]
+        imag = weights[step, band, 1]
+        factors.append(jnp.concatenate([real, imag], 1))
+        factors.append(jnp.concatenate([-imag, real], 1))
     result = jnp.dot(
-        jnp.concatenate(inputs, 1), jnp.concatenate(weights, 0), preferred_element_type=jnp.float32
+        jnp.concatenate(inputs, 1), jnp.concatenate(factors, 0), preferred_element_type=jnp.float32
     ).astype(jnp.bfloat16)
     first = 0
     for out, count in zip(outs, sizes):
@@ -164,12 +185,14 @@
         first += count
 
 
-def extrapolate_blocks(field, operator, columns, sets, listed=False, after=(), limit=24):
+def extrapolate_blocks(field, operator, offsets, sets, listed=False, limit=60):
     rows, blocks, _, size = field.shape
-    bands = columns.shape[1]
+    bands = offsets.shape[0]
     width = 2 * size
     chunk = 32
+    parts = 4
     sizes = [len(one) for one in sets]
+    count = sum(sizes)
     order = jnp.array(sum(sets, []), jnp.int32)
     firsts = [sum(sizes[:n]) for n in range(len(sizes))]
     flat = field.reshape(rows * blocks * 2, size)
@@ -179,27 +202,27 @@
 
     return pl.pallas_call(
         functools.partial(
-            extrapolate_kernel, sizes=sizes, rows=rows, blocks=blocks, chunk=chunk, listed=listed
+            extrapolate_kernel, sets=sets, rows=rows, blocks=blocks, parts=parts, listed=listed
         ),
         grid_spec=pltpu.PrefetchScalarGridSpec(
             num_scalar_prefetch=2,
-            grid=(sum(sizes),),
-            in_specs=[
-                pl.BlockSpec(flat.shape, lambda j, o, c: (0, 0)),
-                pl.BlockSpec((1, bands, 2, size, size), lambda j, o, c: (o[j], 0, 0, 0, 0)),
-            ]
-            + [pl.BlockSpec(memory_space=pl.ANY)] * len(after),
+            grid=(count,),
+            in_specs=[pl.BlockSpec(memory_space=pltpu.HBM)] * 2,
             out_specs=[out_spec(*one) for one in zip(firsts, sizes)],
             scratch_shapes=[
-                pltpu.VMEM((chunk * blocks * 2, size), jnp.float32),
-                pltpu.VMEM((sum(sizes) * bands if listed else blocks, rows, width), jnp.bfloat16),
+                pltpu.VMEM((chunk * (2 * blocks + 1), size), jnp.float32),
+                pltpu.VMEM((count * bands if listed else blocks, rows, width), jnp.bfloat16),
+                pltpu.VMEM(flat.shape, jnp.bfloat16),
+                pltpu.VMEM((count,) + operator.shape[1:], jnp.bfloat16),
+                pltpu.SemaphoreType.DMA((parts,)),
+                pltpu.SemaphoreType.DMA((count,)),
             ],
         ),
         out_shape=[jax.ShapeDtypeStruct((n, rows, width), jnp.bfloat16) for n in sizes],
         compiler_params=params(limit),
         cost_estimate=SMALL,
         name="extrapolate",
-    )(order, columns, flat, operator, *after)
+    )(order, offsets, flat, operator)
 
 
 def product_kernel(near_ids, far_ids, inner, near_in, near_out, far_in, far_out, near_data, far_data, out, turned, total):
@@ -355,13 +378,12 @@
 
 
 def split_body(source_field, receiver_field, operator, band_offsets, survey_tiles, survey_data):
-    blocks = source_field.shape[2]
     tiles = survey_data.shape[1]
     shot = lax.axis_index("shot")
     freq = lax.axis_index("freq")
     inner = ((shot == 1) | (shot == 2)).astype(jnp.int32)[None]
-    columns = (jnp.arange(blocks, dtype=jnp.int32)[:, None] + band_offsets) % blocks
-    make = functools.partial(extrapolate_blocks, operator=operator[0], columns=columns)
+    offsets = band_offsets.T
+    make = functools.partial(extrapolate_blocks, operator=operator[0])
     inward = ((0, 1), (3, 2))
     outward = ((1, 0), (2, 3))
     middle = ((1, 2), (2, 1))
@@ -369,19 +391,21 @@
     beyond = ((1, 3), (2, 0))
 
     far_data = hand(survey_data[0], *inward, *outward)
-    (r_head,) = make(receiver_field[0], sets=[INNER[:HEAD]], listed=True, limit=HEAD_LIMIT)
+    (r_head,) = make(receiver_field[0], offsets=offsets, sets=[INNER[:HEAD]], listed=True)
+    r_1_head = hand(r_head, *inward)
     r_3_head = hand(r_head, *middle)
-    r_1_head = hand(r_head, *inward)
-    r_inner, r_outer = make(receiver_field[0], sets=[INNER[HEAD:], OUTER], after=(r_head,))
-    r_1_out = hand(following(r_outer, far_data), *outward)
+    r_inner, r_outer = make(receiver_field[0], offsets=following(offsets, r_head), sets=[INNER[HEAD:], OUTER])
     r_3_in = hand(r_inner, *middle)
     r_1_in = hand(r_inner, *inward)
-    s_inner, s_outer = make(source_field[0], sets=[INNER, OUTER], after=(r_outer, r_3_head, r_1_head))
+    r_1_out = hand(following(r_outer, far_data, r_3_head), *outward)
+    s_inner, s_outer = make(
+        source_field[0], offsets=following(offsets, r_outer, r_3_head, r_1_head), sets=[INNER, OUTER]
+    )
     s_out = hand(s_outer, *outward)
     s_in = hand(s_inner, *inward)
     forward_head = hand(following(r_1_head, r_3_in), *middle)
-    r_3_out = hand(following(r_outer, r_1_out), *ends)
-    forward = hand(r_1_in, *middle)
+    r_3_out = hand(r_outer, *ends)
+    forward = hand(following(r_1_in, r_1_out), *middle)
     beyond_1 = hand(following(r_outer, s_out, forward_head)[:OUTER_FIRST], *beyond)
     beyond_2 = hand(r_outer[OUTER_FIRST:], *beyond)
 

time: 228 us -> 219 us (0.961)
  Pallas kernels: 64.9 us -> 60.9 us
  starting transfers between devices: 43.3 us -> 39.3 us
  waiting for transfers between devices: 101 us -> 105 us
  local copies, waits for them, and re-layouts: 15.7 us -> 12 us
    pallas_call x3, Pallas kernels: 35.4 us -> 31.4 us  [extrapolate_blocks(): pl.pallas_call(functools.partial(extrapolate_kernel, sets=sets, rows=rows...]
    ppermute x13, starting transfers between devices: 35.4 us -> 31.4 us  [hand(): return lax.ppermute(value, 'shot', pairs)]
    ppermute x13, waiting for transfers between devices: 93.3 us -> 97 us  [hand(): return lax.ppermute(value, 'shot', pairs)]
    unnamed x47 -> x30, local copies, waits for them, and re-layouts: 13.6 us -> 9.86 us
  transfers between devices with their start and end apart: 19 -> 19, of which waited for: 9 -> 10; matrix products, arithmetic and copies ran while one was open for 2% -> 1% of each run, Pallas kernels for 27% -> 27%
where the time goes in v1:
time: 219 us
  waiting for transfers between devices  105 us (48%)
  Pallas kernels  60.9 us (28%)
  starting transfers between devices  39.3 us (18%)
  local copies, waits for them, and re-layouts  12 us (5%)
    ppermute x13, waiting for transfers between devices, hand(): return lax.ppermute(value, 'shot', pairs)  97 us
    pallas_call x3, Pallas kernels, extrapolate_blocks(): pl.pallas_call(functools.partial(extrapolate_kernel, sets=sets, rows=rows...  31.4 us
    ppermute x13, starting transfers between devices, hand(): return lax.ppermute(value, 'shot', pairs)  31.4 us
    pallas_call x4, Pallas kernels, image_blocks(): pl.pallas_call(functools.partial(image_kernel, first=first, begins=begins...  15 us
    pallas_call x1, Pallas kernels, product_blocks(): pl.pallas_call(product_kernel, grid_spec=pltpu.PrefetchScalarGridSpec(num...  14.5 us
    unnamed x30, local copies, waits for them, and re-layouts  9.86 us
    ppermute x6, waiting for transfers between devices, send_sum(): lax.ppermute(value.astype(jnp.bfloat16), ('shot', 'freq'), pairs)  7.94 us
    ppermute x6, starting transfers between devices, send_sum(): lax.ppermute(value.astype(jnp.bfloat16), ('shot', 'freq'), pairs)  7.89 us
  transfers between devices with their start and end apart: 19, of which 10 were waited for; matrix products, arithmetic and copies ran while one was open for 1% of the time, Pallas kernels for 27%

profile of v1, /device:TPU:0, one launch (start us, length us, event | category | flops | bytes accessed | tf_op | source)
XLA Modules:
  0.0 218.6 jit_solution(17750531211930922590)
XLA Ops:
  0.0 3.0 %collective-permute-start.4 = (bf16[16,2,128,128]{3,2,1,0:T(8,128)(2,1)}, bf16[16,2,128,128]{3,2,1,0:T(8,128)(2,1)}, u32[]{:S(2)}, u32[]{:S(2)}) collective-permute-start(bf16[16,2,128,128]{3,2,1,0:T(8,128)(2,1)} %bitcast.28), channel_id=1, source_target_pairs={{0,4},{12,8},{4,0},{8,12},{1,5},{13,9},{5,1},{9,13},{2,6},{14,10},... | collective-permute-start | bytes 3145736 | tf_op jit(solution)/shard_map/ppermute | solution.py:351
  3.0 5.5 %extrapolate.3.refs_3_ = bf16[3,512,256]{2,1,0:T(8,128)(2,1)} custom-call(s32[3]{0:T(128)} %constant.38.clone.order, s32[3,16]{1,0:T(4,128)} %bitcast.36, bf16[16384,128]{1,0:T(8,128)(2,1)} %bitcast.33, bf16[16,3,2,128,128]{4,3,2,1,0:T(8,128)(2,1)} %bitcast.30), custom_call_target="tpu_custom_call" | custom-call | flops 1000 | bytes 1000 | tf_op jit(solution)/shard_map/extrapolate/pallas_call | solution.py:203
  9.2 6.3 %collective-permute-start.1 = (bf16[3,512,256]{2,1,0:T(8,128)(2,1)}, bf16[3,512,256]{2,1,0:T(8,128)(2,1)S(1)}, u32[]{:S(2)}, u32[]{:S(2)}) collective-permute-start(bf16[3,512,256]{2,1,0:T(8,128)(2,1)} %extrapolate.3.refs_3_), channel_id=1, source_target_pairs={{0,4},{12,8},{1,5},{13,9},{2,6},{14,10},{3,7},{15,11},{16,20},{28,... | collective-permute-start | bytes 2359304 | tf_op jit(solution)/shard_map/ppermute | solution.py:351
  15.5 12.0 %extrapolate.4 = (bf16[6,512,256]{2,1,0:T(8,128)(2,1)}, bf16[7,512,256]{2,1,0:T(8,128)(2,1)}) custom-call(s32[13]{0:T(128)} %constant.39.clone.order, s32[3,16]{1,0:T(4,128)} %bitcast.37, bf16[16384,128]{1,0:T(8,128)(2,1)} %bitcast.34, bf16[16,3,2,128,128]{4,3,2,1,0:T(8,128)(2,1)} %bitcast.31), custom_call_target="tpu_custom_call" | custom-call | flops 1000 | bytes 1000 | tf_op jit(solution)/shard_map/extrapolate/pallas_call | solution.py:203
  27.6 1.9 collective-permute-start.5
  29.4 1.4 collective-permute-start.7
  31.7 1.3 collective-permute-start.8
  33.0 10.7 %collective-permute-done.1.refs_6_ = bf16[3,512,256]{2,1,0:T(8,128)(2,1)S(1)} collective-permute-done((bf16[3,512,256]{2,1,0:T(8,128)(2,1)}, bf16[3,512,256]{2,1,0:T(8,128)(2,1)S(1)}, u32[]{:S(2)}, u32[]{:S(2)}) %collective-permute-start.1) | collective-permute-done | bytes 786464 | tf_op jit(solution)/shard_map/ppermute | solution.py:351
  44.7 13.9 %extrapolate.5 = (bf16[9,512,256]{2,1,0:T(8,128)(2,1)}, bf16[7,512,256]{2,1,0:T(8,128)(2,1)}) custom-call(s32[16]{0:T(128)} %constant.40.clone.order, s32[3,16]{1,0:T(4,128)} %bitcast.38, bf16[16384,128]{1,0:T(8,128)(2,1)} %bitcast.35, bf16[16,3,2,128,128]{4,3,2,1,0:T(8,128)(2,1)} %bitcast.32), custom_call_target="tpu_custom_call" | custom-call | flops 1000 | bytes 1000 | tf_op jit(solution)/shard_map/extrapolate/pallas_call | solution.py:203
  58.6 1.3 collective-permute-start.3
  59.9 6.1 %collective-permute-start.2 = (bf16[9,512,256]{2,1,0:T(8,128)(2,1)}, bf16[9,512,256]{2,1,0:T(8,128)(2,1)}, u32[]{:S(2)}, u32[]{:S(2)}) collective-permute-start(bf16[9,512,256]{2,1,0:T(8,128)(2,1)} %get-tuple-element.19.near_in), channel_id=1, source_target_pairs={{0,4},{12,8},{1,5},{13,9},{2,6},{14,10},{3,7},{15,11},{16,20},{28,... | collective-permute-start | bytes 7077896 | tf_op jit(solution)/shard_map/ppermute | solution.py:351
  66.7 10.7 %collective-permute-done.7.refs_7_ = bf16[6,512,256]{2,1,0:T(8,128)(2,1)S(1)} collective-permute-done((bf16[6,512,256]{2,1,0:T(8,128)(2,1)}, bf16[6,512,256]{2,1,0:T(8,128)(2,1)S(1)}, u32[]{:S(2)}, u32[]{:S(2)}) %collective-permute-start.7) | collective-permute-done | bytes 1572896 | tf_op jit(solution)/shard_map/ppermute | solution.py:351
  77.5 4.4 %collective-permute-start.11 = (bf16[7,512,256]{2,1,0:T(8,128)(2,1)S(1)}, bf16[7,512,256]{2,1,0:T(8,128)(2,1)}, u32[]{:S(2)}, u32[]{:S(2)}) collective-permute-start(bf16[7,512,256]{2,1,0:T(8,128)(2,1)S(1)} %copy-done), channel_id=1, source_target_pairs={{0,12},{12,0},{1,13},{13,1},{2,14},{14,2},{3,15},{15,3},{16,28},{2... | collective-permute-start | bytes 5505032 | tf_op jit(solution)/shard_map/ppermute | solution.py:351
  81.9 1.8 collective-permute-start.9
  84.6 29.5 %collective-permute-done.3.far_out = bf16[7,512,256]{2,1,0:T(8,128)(2,1)S(1)} collective-permute-done((bf16[7,512,256]{2,1,0:T(8,128)(2,1)}, bf16[7,512,256]{2,1,0:T(8,128)(2,1)S(1)}, u32[]{:S(2)}, u32[]{:S(2)}) %collective-permute-start.3) | collective-permute-done | bytes 1835040 | tf_op jit(solution)/shard_map/ppermute | solution.py:351
  120.1 7.9 %collective-permute-done.2.far_in = bf16[9,512,256]{2,1,0:T(8,128)(2,1)} collective-permute-done((bf16[9,512,256]{2,1,0:T(8,128)(2,1)}, bf16[9,512,256]{2,1,0:T(8,128)(2,1)}, u32[]{:S(2)}, u32[]{:S(2)}) %collective-permute-start.2) | collective-permute-done | bytes 2359328 | tf_op jit(solution)/shard_map/ppermute | solution.py:351
  128.0 1.7 copy-done.9
  129.7 1.5 copy-done.10
  131.2 1.5 copy-done.12
  133.9 14.5 %product.1.refs_0_.refs_1_.refs_2_ = bf16[9,256,2048]{2,1,0:T(8,128)(2,1)S(1)} custom-call(s32[16]{0:T(128)S(1)} %get-tuple-element.28.near_ids, s32[16]{0:T(128)S(1)} %get-tuple-element.27.far_ids, s32[1]{0:T(128)} %bitcast.1.inner, bf16[9,512,256]{2,1,0:T(8,128)(2,1)S(1)} %copy-done.9, bf16[7,512,256]{2,1,0:T(8,128)(2,1)S(1)} %copy-done.10, ...), custom_call_target="tpu_custom_call" | custom-call | flops 1000 | bytes 1000 | tf_op jit(solution)/shard_map/product/pallas_call | solution.py:273
  148.4 20.8 %collective-permute-done.11.refs_11_ = bf16[7,512,256]{2,1,0:T(8,128)(2,1)} collective-permute-done((bf16[7,512,256]{2,1,0:T(8,128)(2,1)S(1)}, bf16[7,512,256]{2,1,0:T(8,128)(2,1)}, u32[]{:S(2)}, u32[]{:S(2)}) %collective-permute-start.11) | collective-permute-done | bytes 1835040 | tf_op jit(solution)/shard_map/ppermute | solution.py:351
  169.3 4.2 %image.6.refs_4_ = f32[4,2,128,128]{3,2,1,0:T(8,128)S(1)} custom-call(s32[3]{0:T(128)S(1)} %pad_add_fusion.places.unused, s32[3]{0:T(128)S(1)} %pad_add_fusion.places.unused, s32[1]{0:T(128)} %bitcast.1.inner, bf16[9,256,2048]{2,1,0:T(8,128)(2,1)S(1)} %product.1.refs_0_.refs_1_.refs_2_, bf16[9,256,2048]{2,1,0:T(8,128)(2,1)S(1)} %product.1.refs_0_.refs_1_.refs_2_, ...), custom_call_target="tpu_custom_call" | custom-call | flops 1000 | bytes 1000 | tf_op jit(solution)/shard_map/image/pallas_call | solution.py:334
  173.5 4.7 %image.4.refs_4_ = f32[5,2,128,128]{3,2,1,0:T(8,128)S(1)} custom-call(s32[3]{0:T(128)S(1)} %pad_add_fusion.places.unused, s32[3]{0:T(128)S(1)} %pad_add_fusion.places.unused, s32[1]{0:T(128)} %bitcast.1.inner, bf16[9,256,2048]{2,1,0:T(8,128)(2,1)S(1)} %product.1.refs_0_.refs_1_.refs_2_, bf16[9,256,2048]{2,1,0:T(8,128)(2,1)S(1)} %product.1.refs_0_.refs_1_.refs_2_, ...), custom_call_target="tpu_custom_call" | custom-call | flops 1000 | bytes 1000 | tf_op jit(solution)/shard_map/image/pallas_call | solution.py:334
  178.2 6.7 %collective-permute-done.10.refs_3_ = bf16[4,512,256]{2,1,0:T(8,128)(2,1)} collective-permute-done((bf16[4,512,256]{2,1,0:T(8,128)(2,1)}, bf16[4,512,256]{2,1,0:T(8,128)(2,1)}, u32[]{:S(2)}, u32[]{:S(2)}) %collective-permute-start.10) | collective-permute-done | bytes 1048608 | tf_op jit(solution)/shard_map/ppermute | solution.py:351
  184.9 3.2 %image.5 = f32[5,2,128,128]{3,2,1,0:T(8,128)S(1)} custom-call(s32[1]{0:T(128)} %bitcast.places.unused, s32[1]{0:T(128)} %bitcast.places.unused, s32[1]{0:T(128)} %bitcast.1.inner, bf16[9,256,2048]{2,1,0:T(8,128)(2,1)S(1)} %product.1.refs_0_.refs_1_.refs_2_, bf16[3,512,256]{2,1,0:T(8,128)(2,1)S(1)} %copy-done.4, ...), custom_call_target="tpu_custom_call" | custom-call | flops 1000 | bytes 1000 | tf_op jit(solution)/shard_map/image/pallas_call | solution.py:334
  188.1 10.6 %collective-permute-done.12.refs_3_ = bf16[3,512,256]{2,1,0:T(8,128)(2,1)} collective-permute-done((bf16[3,512,256]{2,1,0:T(8,128)(2,1)}, bf16[3,512,256]{2,1,0:T(8,128)(2,1)}, u32[]{:S(2)}, u32[]{:S(2)}) %collective-permute-start.12) | collective-permute-done | bytes 786464 | tf_op jit(solution)/shard_map/ppermute | solution.py:351
  198.8 2.9 %image.7 = f32[4,2,128,128]{3,2,1,0:T(8,128)S(1)} custom-call(s32[1]{0:T(128)} %bitcast.places.unused, s32[1]{0:T(128)} %bitcast.places.unused, s32[1]{0:T(128)} %bitcast.1.inner, bf16[9,256,2048]{2,1,0:T(8,128)(2,1)S(1)} %product.1.refs_0_.refs_1_.refs_2_, bf16[3,512,256]{2,1,0:T(8,128)(2,1)S(1)} %copy-done.4, ...), custom_call_target="tpu_custom_call" | custom-call | flops 1000 | bytes 1000 | tf_op jit(solution)/shard_map/image/pallas_call | solution.py:334
  201.8 1.6 collective-permute-done.13
  204.3 1.6 collective-permute-start.17
  207.2 2.7 %collective-permute-done.17 = bf16[2,2,128,128]{3,2,1,0:T(8,128)(2,1)S(1)} collective-permute-done((bf16[2,2,128,128]{3,2,1,0:T(8,128)(2,1)S(1)}, bf16[2,2,128,128]{3,2,1,0:T(8,128)(2,1)S(1)}, u32[]{:S(2)}, u32[]{:S(2)}) %collective-permute-start.17) | collective-permute-done | bytes 131104 | tf_op jit(solution)/shard_map/ppermute | solution.py:356
  209.9 4.3 %collective-permute-start.18 = (bf16[2,128,128]{2,1,0:T(8,128)(2,1)S(1)}, bf16[2,128,128]{2,1,0:T(8,128)(2,1)S(1)}, u32[]{:S(2)}, u32[]{:S(2)}) collective-permute-start(bf16[2,128,128]{2,1,0:T(8,128)(2,1)S(1)} %fusion.3), channel_id=1, source_target_pairs={{0,12},{1,13},{2,14},{4,8},{5,9},{6,10},{7,11},{8,4},{9,5},{10,6},... | collective-permute-start | bytes 196616 | tf_op jit(solution)/shard_map/ppermute | solution.py:356
  214.2 3.7 %collective-permute-done.18 = bf16[2,128,128]{2,1,0:T(8,128)(2,1)S(1)} collective-permute-done((bf16[2,128,128]{2,1,0:T(8,128)(2,1)S(1)}, bf16[2,128,128]{2,1,0:T(8,128)(2,1)S(1)}, u32[]{:S(2)}, u32[]{:S(2)}) %collective-permute-start.18) | collective-permute-done | bytes 65568 | tf_op jit(solution)/shard_map/ppermute | solution.py:356
  (58 shorter events, 14.4 us)
Async XLA Ops:
  0.0 31.7 %collective-permute-start.4 = (bf16[16,2,128,128]{3,2,1,0:T(8,128)(2,1)}, bf16[16,2,128,128]{3,2,1,0:T(8,128)(2,1)}, u32[]{:S(2)}, u32[]{:S(2)}) collective-permute-start(bf16[16,2,128,128]{3,2,1,0:T(8,128)(2,1)} %bitcast.28), channel_id=1, source_target_pairs={{0,4},{12,8},{4,0},{8,12},{1,5},{13,9},{5,1},{9,13},{2,6},{14,10},... | collective-permute-start | bytes 3145736 | tf_op jit(solution)/shard_map/ppermute | solution.py:351
  8.5 22.3 %collective-permute-start = (bf16[3,512,256]{2,1,0:T(8,128)(2,1)}, bf16[3,512,256]{2,1,0:T(8,128)(2,1)S(1)}, u32[]{:S(2)}, u32[]{:S(2)}) collective-permute-start(bf16[3,512,256]{2,1,0:T(8,128)(2,1)} %extrapolate.3.refs_3_), channel_id=1, source_target_pairs={{4,8},{8,4},{5,9},{9,5},{6,10},{10,6},{7,11},{11,7},{20,24},{24,20... | collective-permute-start | bytes 2359304 | tf_op jit(solution)/shard_map/ppermute | solution.py:351
  9.2 34.5 %collective-permute-start.1 = (bf16[3,512,256]{2,1,0:T(8,128)(2,1)}, bf16[3,512,256]{2,1,0:T(8,128)(2,1)S(1)}, u32[]{:S(2)}, u32[]{:S(2)}) collective-permute-start(bf16[3,512,256]{2,1,0:T(8,128)(2,1)} %extrapolate.3.refs_3_), channel_id=1, source_target_pairs={{0,4},{12,8},{1,5},{13,9},{2,6},{14,10},{3,7},{15,11},{16,20},{28,... | collective-permute-start | bytes 2359304 | tf_op jit(solution)/shard_map/ppermute | solution.py:351
  27.6 38.5 %collective-permute-start.5 = (bf16[6,512,256]{2,1,0:T(8,128)(2,1)}, bf16[6,512,256]{2,1,0:T(8,128)(2,1)}, u32[]{:S(2)}, u32[]{:S(2)}) collective-permute-start(bf16[6,512,256]{2,1,0:T(8,128)(2,1)} %get-tuple-element.21.refs_4_), channel_id=1, source_target_pairs={{4,8},{8,4},{5,9},{9,5},{6,10},{10,6},{7,11},{11,7},{20,24},{24,20... | collective-permute-start | bytes 4718600 | tf_op jit(solution)/shard_map/ppermute | solution.py:351
  29.4 48.0 %collective-permute-start.7 = (bf16[6,512,256]{2,1,0:T(8,128)(2,1)}, bf16[6,512,256]{2,1,0:T(8,128)(2,1)S(1)}, u32[]{:S(2)}, u32[]{:S(2)}) collective-permute-start(bf16[6,512,256]{2,1,0:T(8,128)(2,1)} %get-tuple-element.21.refs_4_), channel_id=1, source_target_pairs={{0,4},{12,8},{1,5},{13,9},{2,6},{14,10},{3,7},{15,11},{16,20},{28,... | collective-permute-start | bytes 4718600 | tf_op jit(solution)/shard_map/ppermute | solution.py:351
  31.7 50.1 %collective-permute-start.8 = (bf16[7,512,256]{2,1,0:T(8,128)(2,1)}, bf16[7,512,256]{2,1,0:T(8,128)(2,1)}, u32[]{:S(2)}, u32[]{:S(2)}) collective-permute-start(bf16[7,512,256]{2,1,0:T(8,128)(2,1)} %get-tuple-element.25.refs_5_), channel_id=1, source_target_pairs={{4,0},{8,12},{5,1},{9,13},{6,2},{10,14},{7,3},{11,15},{20,16},{24,... | collective-permute-start | bytes 5505032 | tf_op jit(solution)/shard_map/ppermute | solution.py:351
  43.8 0.9 copy-start.7
  44.7 32.8 %copy-start = (bf16[7,512,256]{2,1,0:T(8,128)(2,1)S(1)}, bf16[7,512,256]{2,1,0:T(8,128)(2,1)}, u32[]{:S(2)}) copy-start(bf16[7,512,256]{2,1,0:T(8,128)(2,1)} %get-tuple-element.25.refs_5_) | copy-start | bytes 5505028
  58.6 55.5 %collective-permute-start.3 = (bf16[7,512,256]{2,1,0:T(8,128)(2,1)}, bf16[7,512,256]{2,1,0:T(8,128)(2,1)S(1)}, u32[]{:S(2)}, u32[]{:S(2)}) collective-permute-start(bf16[7,512,256]{2,1,0:T(8,128)(2,1)} %get-tuple-element.20.near_out), channel_id=1, source_target_pairs={{4,0},{8,12},{5,1},{9,13},{6,2},{10,14},{7,3},{11,15},{20,16},{24,... | collective-permute-start | bytes 5505032 | tf_op jit(solution)/shard_map/ppermute | solution.py:351
  59.9 60.0 %copy-start.14 = (s32[64,2]{0,1:T(2,128)S(1)}, s32[64,2]{0,1:T(2,128)}, u32[]{:S(2)}) copy-start(s32[64,2]{0,1:T(2,128)} %param.13) | copy-start | bytes 1540
  59.9 68.1 %collective-permute-start.2 = (bf16[9,512,256]{2,1,0:T(8,128)(2,1)}, bf16[9,512,256]{2,1,0:T(8,128)(2,1)}, u32[]{:S(2)}, u32[]{:S(2)}) collective-permute-start(bf16[9,512,256]{2,1,0:T(8,128)(2,1)} %get-tuple-element.19.near_in), channel_id=1, source_target_pairs={{0,4},{12,8},{1,5},{13,9},{2,6},{14,10},{3,7},{15,11},{16,20},{28,... | collective-permute-start | bytes 7077896 | tf_op jit(solution)/shard_map/ppermute | solution.py:351
  66.0 17.6 %collective-permute-start.6 = (bf16[3,512,256]{2,1,0:T(8,128)(2,1)}, bf16[3,512,256]{2,1,0:T(8,128)(2,1)S(1)}, u32[]{:S(2)}, u32[]{:S(2)}) collective-permute-start(bf16[3,512,256]{2,1,0:T(8,128)(2,1)} %copy-done.7), channel_id=1, source_target_pairs={{4,8},{8,4},{5,9},{9,5},{6,10},{10,6},{7,11},{11,7},{20,24},{24,20... | collective-permute-start | bytes 2359304 | tf_op jit(solution)/shard_map/ppermute | solution.py:351
  77.5 91.8 %collective-permute-start.11 = (bf16[7,512,256]{2,1,0:T(8,128)(2,1)S(1)}, bf16[7,512,256]{2,1,0:T(8,128)(2,1)}, u32[]{:S(2)}, u32[]{:S(2)}) collective-permute-start(bf16[7,512,256]{2,1,0:T(8,128)(2,1)S(1)} %copy-done), channel_id=1, source_target_pairs={{0,12},{12,0},{1,13},{13,1},{2,14},{14,2},{3,15},{15,3},{16,28},{2... | collective-permute-start | bytes 5505032 | tf_op jit(solution)/shard_map/ppermute | solution.py:351
  81.9 103.0 %collective-permute-start.9 = (bf16[6,512,256]{2,1,0:T(8,128)(2,1)S(1)}, bf16[6,512,256]{2,1,0:T(8,128)(2,1)}, u32[]{:S(2)}, u32[]{:S(2)}) collective-permute-start(bf16[6,512,256]{2,1,0:T(8,128)(2,1)S(1)} %collective-permute-done.7.refs_7_), channel_id=1, source_target_pairs={{4,8},{8,4},{5,9},{9,5},{6,10},{10,6},{7,11},{11,7},{20,24},{24,20... | collective-permute-start | bytes 4718600 | tf_op jit(solution)/shard_map/ppermute | solution.py:351
  114.1 1.2 copy-start.11
  116.4 68.5 %collective-permute-start.10 = (bf16[4,512,256]{2,1,0:T(8,128)(2,1)}, bf16[4,512,256]{2,1,0:T(8,128)(2,1)}, u32[]{:S(2)}, u32[]{:S(2)}) collective-permute-start(bf16[4,512,256]{2,1,0:T(8,128)(2,1)} %slice.35), channel_id=1, source_target_pairs={{4,12},{8,0},{5,13},{9,1},{6,14},{10,2},{7,15},{11,3},{20,28},{24,... | collective-permute-start | bytes 3145736 | tf_op jit(solution)/shard_map/ppermute | solution.py:351
  118.6 80.2 %collective-permute-start.12 = (bf16[3,512,256]{2,1,0:T(8,128)(2,1)}, bf16[3,512,256]{2,1,0:T(8,128)(2,1)}, u32[]{:S(2)}, u32[]{:S(2)}) collective-permute-start(bf16[3,512,256]{2,1,0:T(8,128)(2,1)} %slice.36), channel_id=1, source_target_pairs={{4,12},{8,0},{5,13},{9,1},{6,14},{10,2},{7,15},{11,3},{20,28},{24,... | collective-permute-start | bytes 2359304 | tf_op jit(solution)/shard_map/ppermute | solution.py:351
  128.0 1.7 copy-start.9
  129.7 1.5 copy-start.10
  131.2 1.5 copy-start.12
  132.7 1.2 copy-start.13
  133.9 35.3 %copy-start.1 = (bf16[3,512,256]{2,1,0:T(8,128)(2,1)S(1)}, bf16[3,512,256]{2,1,0:T(8,128)(2,1)}, u32[]{:S(2)}) copy-start(bf16[3,512,256]{2,1,0:T(8,128)(2,1)} %extrapolate.3.refs_3_) | copy-start | bytes 2359300
  133.9 35.3 %copy-start.2 = (bf16[6,512,256]{2,1,0:T(8,128)(2,1)S(1)}, bf16[6,512,256]{2,1,0:T(8,128)(2,1)}, u32[]{:S(2)}) copy-start(bf16[6,512,256]{2,1,0:T(8,128)(2,1)} %get-tuple-element.21.refs_4_) | copy-start | bytes 4718596
  133.9 35.3 %copy-start.6 = (bf16[3,512,256]{2,1,0:T(8,128)(2,1)S(1)}, bf16[3,512,256]{2,1,0:T(8,128)(2,1)}, u32[]{:S(2)}) copy-start(bf16[3,512,256]{2,1,0:T(8,128)(2,1)} %copy-done.5) | copy-start | bytes 2359300
  133.9 35.3 %copy-start.8 = (bf16[3,512,256]{2,1,0:T(8,128)(2,1)S(1)}, bf16[3,512,256]{2,1,0:T(8,128)(2,1)}, u32[]{:S(2)}) copy-start(bf16[3,512,256]{2,1,0:T(8,128)(2,1)} %copy-done.7) | copy-start | bytes 2359300
  173.4 11.4 %copy-start.4 = (bf16[3,512,256]{2,1,0:T(8,128)(2,1)S(1)}, bf16[3,512,256]{2,1,0:T(8,128)(2,1)}, u32[]{:S(2)}) copy-start(bf16[3,512,256]{2,1,0:T(8,128)(2,1)} %copy-done.3) | copy-start | bytes 2359300
  201.7 1.7 collective-permute-start.13
  203.6 2.3 %collective-permute-start.14 = (bf16[2,128,128]{2,1,0:T(8,128)(2,1)S(1)}, bf16[2,128,128]{2,1,0:T(8,128)(2,1)S(1)}, u32[]{:S(2)}, u32[]{:S(2)}) collective-permute-start(bf16[2,128,128]{2,1,0:T(8,128)(2,1)S(1)} %fusion.2), channel_id=1, source_target_pairs={{5,7},{9,11},{21,23},{25,27}} | collective-permute-start | bytes 196616 | tf_op jit(solution)/shard_map/ppermute | solution.py:356
  204.3 5.6 %collective-permute-start.17 = (bf16[2,2,128,128]{3,2,1,0:T(8,128)(2,1)S(1)}, bf16[2,2,128,128]{3,2,1,0:T(8,128)(2,1)S(1)}, u32[]{:S(2)}, u32[]{:S(2)}) collective-permute-start(bf16[2,2,128,128]{3,2,1,0:T(8,128)(2,1)S(1)} %select_convert_fusion.1), channel_id=1, source_target_pairs={{0,2},{1,3},{2,0},{3,1},{4,6},{5,7},{6,4},{7,5},{8,10},{9,11},{10,... | collective-permute-start | bytes 393224 | tf_op jit(solution)/shard_map/ppermute | solution.py:356
  205.8 8.4 %collective-permute-start.15 = (bf16[2,128,128]{2,1,0:T(8,128)(2,1)S(1)}, bf16[2,128,128]{2,1,0:T(8,128)(2,1)S(1)}, u32[]{:S(2)}, u32[]{:S(2)}) collective-permute-start(bf16[2,128,128]{2,1,0:T(8,128)(2,1)S(1)} %add_convert_fusion), channel_id=1, source_target_pairs={{7,15},{23,31}} | collective-permute-start | bytes 196616 | tf_op jit(solution)/shard_map/ppermute | solution.py:356
  206.5 7.7 %collective-permute-start.16 = (bf16[2,128,128]{2,1,0:T(8,128)(2,1)S(1)}, bf16[2,128,128]{2,1,0:T(8,128)(2,1)S(1)}, u32[]{:S(2)}, u32[]{:S(2)}) collective-permute-start(bf16[2,128,128]{2,1,0:T(8,128)(2,1)S(1)} %add_convert_fusion), channel_id=1, source_target_pairs={{11,15},{27,31}} | collective-permute-start | bytes 196616 | tf_op jit(solution)/shard_map/ppermute | solution.py:356
  209.9 8.0 %collective-permute-start.18 = (bf16[2,128,128]{2,1,0:T(8,128)(2,1)S(1)}, bf16[2,128,128]{2,1,0:T(8,128)(2,1)S(1)}, u32[]{:S(2)}, u32[]{:S(2)}) collective-permute-start(bf16[2,128,128]{2,1,0:T(8,128)(2,1)S(1)} %fusion.3), channel_id=1, source_target_pairs={{0,12},{1,13},{2,14},{4,8},{5,9},{6,10},{7,11},{8,4},{9,5},{10,6},... | collective-permute-start | bytes 196616 | tf_op jit(solution)/shard_map/ppermute | solution.py:356
  (2 other events, 1.8 us)

commit v2 on v1

--- a/solution.py
+++ b/solution.py
@@ -100,10 +100,11 @@
 
 
 INNER = [4, 8, 6, 10, 15, 5, 9, 7, 11]
-HEAD = 3
+HEAD = 4
 OUTER = [0, 12, 2, 14, 1, 13, 3]
 FIRST = 5
 OUTER_FIRST = 4
+LATE = 4
 
 
 def outer_place(slot):
@@ -225,7 +226,9 @@
     )(order, offsets, flat, operator)
 
 
-def product_kernel(near_ids, far_ids, inner, near_in, near_out, far_in, far_out, near_data, far_data, out, turned, total):
+def product_kernel(
+    near_ids, far_ids, inner, near_in, near_out, far_in, far_out, near_data, data_in, data_out, out, turned, total
+):
     size = near_data.shape[2]
     tiles = near_data.shape[0]
     sources = near_in.shape[1] // size
@@ -233,10 +236,12 @@
 
     @pl.when(pl.program_id(0) == 0)
     def _():
-        for side, data in enumerate((near_data, far_data)):
-            for tile in range(tiles):
-                for part in range(2):
-                    turned[side * tiles + tile, :, part * size:(part + 1) * size] = data[tile, part].T
+        for tile in range(tiles):
+            for part in range(2):
+                columns = slice(part * size, (part + 1) * size)
+                far = jnp.where(inner[0] > 0, data_in[tile, part], data_out[tile, part])
+                turned[tile, :, columns] = near_data[tile, part].T
+                turned[tiles + tile, :, columns] = far.T
 
     total[...] = jnp.zeros_like(total)
     sides = ((near_in, near_out, near_ids), (far_in, far_out, far_ids))
@@ -264,7 +269,7 @@
     return pl.BlockSpec(shape, index)
 
 
-def product_blocks(near_in, near_out, far_in, far_out, near_data, far_data, near_ids, far_ids, inner):
+def product_blocks(near_in, near_out, far_in, far_out, near_data, data_in, data_out, near_ids, far_ids, inner):
     blocks, rows, width = near_in.shape
     tiles, _, size, _ = near_data.shape
     receivers = NR // size
@@ -276,7 +281,7 @@
             num_scalar_prefetch=3,
             grid=(blocks,),
             in_specs=[part_spec(shape, 0, 0, len(INNER), True), part_spec(shape, 0, 0, len(OUTER), False)] * 2
-            + [data_spec, data_spec],
+            + [data_spec] * 3,
             out_specs=pl.BlockSpec((1, width, NR), lambda j, a, b, i: (j, 0, 0)),
             scratch_shapes=[
                 pltpu.VMEM((2 * tiles, size, width), jnp.bfloat16),
@@ -287,7 +292,7 @@
         compiler_params=params(),
         cost_estimate=SMALL,
         name="product",
-    )(near_ids, far_ids, inner, near_in, near_out, far_in, far_out, near_data, far_data)
+    )(near_ids, far_ids, inner, near_in, near_out, far_in, far_out, near_data, data_in, data_out)
 
 
 def image_kernel(places, unused, inner, *refs, first, begins, size):
@@ -328,7 +333,7 @@
             values.append(field)
         begins.append([(begin, is_inner) for (_, begin), is_inner in zip(parts, inners)])
     if before is not None:
-        specs.append(image_spec)
+        specs.append(pl.BlockSpec((1, 2, size, size), lambda j, o, u, i: (first + j, 0, 0, 0)))
         values.append(before)
     places = jnp.stack([shot for shot, _ in pieces])
     return pl.pallas_call(
@@ -390,44 +395,43 @@
     ends = ((0, 3), (3, 0))
     beyond = ((1, 3), (2, 0))
 
-    far_data = hand(survey_data[0], *inward, *outward)
     (r_head,) = make(receiver_field[0], offsets=offsets, sets=[INNER[:HEAD]], listed=True)
+    r_3_head = hand(r_head, *middle)
     r_1_head = hand(r_head, *inward)
-    r_3_head = hand(r_head, *middle)
+    data_out = hand(survey_data[0], *outward)
     r_inner, r_outer = make(receiver_field[0], offsets=following(offsets, r_head), sets=[INNER[HEAD:], OUTER])
     r_3_in = hand(r_inner, *middle)
     r_1_in = hand(r_inner, *inward)
-    r_1_out = hand(following(r_outer, far_data, r_3_head), *outward)
-    s_inner, s_outer = make(
-        source_field[0], offsets=following(offsets, r_outer, r_3_head, r_1_head), sets=[INNER, OUTER]
-    )
+    r_1_out = hand(following(r_outer, r_3_head), *outward)
+    s_inner, s_outer = make(source_field[0], offsets=following(offsets, r_outer, data_out, r_1_head), sets=[INNER, OUTER])
     s_out = hand(s_outer, *outward)
-    s_in = hand(s_inner, *inward)
-    forward_head = hand(following(r_1_head, r_3_in), *middle)
-    r_3_out = hand(r_outer, *ends)
-    forward = hand(following(r_1_in, r_1_out), *middle)
-    beyond_1 = hand(following(r_outer, s_out, forward_head)[:OUTER_FIRST], *beyond)
-    beyond_2 = hand(r_outer[OUTER_FIRST:], *beyond)
+    s_in = hand(following(s_inner, r_1_in, r_3_in), *inward)
+    data_in = hand(following(survey_data[0], data_out), *inward)
+    forward_head = hand(r_1_head, *middle)
+    forward = hand(r_1_in, *middle)
+    r_3_out = hand(following(r_outer, r_1_out, data_in), *ends)
+    beyond_1 = hand(following(r_outer, s_out, forward_head)[:LATE], *beyond)
+    beyond_2 = hand(r_outer[LATE:], *beyond)
 
     ids = survey_tiles[:, 1]
     near_ids = lax.dynamic_slice_in_dim(ids, shot * tiles, tiles)
     far_ids = lax.dynamic_slice_in_dim(ids, (shot ^ 1) * tiles, tiles)
     product = product_blocks(
-        s_inner, s_outer, s_in, s_out, survey_data[0], far_data, near_ids, far_ids, inner
+        s_inner, s_outer, s_in, s_out, survey_data[0], data_in, data_out, near_ids, far_ids, inner
     )
     early = [
         (shot, [(r_head, 0), (r_inner, HEAD), (r_outer, 0)]),
         (shot ^ 1, [(r_1_head, 0), (r_1_in, HEAD), (r_1_out, 0)]),
         (shot ^ 3, [(r_3_head, 0), (r_3_in, HEAD), (r_3_out, 0)]),
     ]
-    forwarded = [(forward_head, 0), (forward, HEAD)]
-    one = image_blocks(product, 0, FIRST, early, inner)
-    two = image_blocks(product, FIRST, len(INNER) - FIRST, early, inner)
-    one = image_blocks(product, 0, FIRST, [(shot ^ 2, forwarded + [(beyond_1, 0)])], inner, one)
-    two = image_blocks(
-        product, FIRST, len(INNER) - FIRST, [(shot ^ 2, forwarded + [(beyond_2, OUTER_FIRST)])], inner,
-        following(two, one),
-    )
+    image = image_blocks(product, 0, len(INNER), early, inner)
+    most = image_blocks(product, 0, LATE + 1, [(shot ^ 2, [(forward_head, 0), (forward, HEAD), (beyond_1, 0)])], inner, image)
+    rest = image_blocks(
+        product, LATE + 1, len(INNER) - LATE - 1, [(shot ^ 2, [(forward_head, 0), (forward, HEAD), (beyond_2, LATE)])], inner,
+        following(image, most),
+    )
+    one = most[:FIRST]
+    two = jnp.concatenate([most[FIRST:], rest])
     image = sum_images(one, two, shot, freq)
     total_freqs = source_field.shape[0] * lax.axis_size("freq")
     return image * (1.0 / math.sqrt(2.0 * NR * total_freqs))

time: 219 us -> 225 us (1.027)
  waiting for transfers between devices: 105 us -> 110 us
  starting transfers between devices: 39.3 us -> 42.5 us
    ppermute x13 -> x14, waiting for transfers between devices: 97 us -> 102 us  [hand(): return lax.ppermute(value, 'shot', pairs)]
    ppermute x13 -> x14, starting transfers between devices: 31.4 us -> 35.3 us  [hand(): return lax.ppermute(value, 'shot', pairs)]
    unnamed x30 -> x32, local copies, waits for them, and re-layouts: 9.86 us -> 7.91 us
    pallas_call x4 -> x3, Pallas kernels: 15 us -> 13.6 us  [image_blocks(): pl.pallas_call(functools.partial(image_kernel, first=first, begins=begins...]
  transfers between devices with their start and end apart: 19 -> 20, of which waited for: 10 -> 12; matrix products, arithmetic and copies ran while one was open for 1% -> 1% of each run, Pallas kernels for 27% -> 23%
where the time goes in v2:
time: 225 us; the launch traced here: 224 us
  waiting for transfers between devices  110 us (49%)
  Pallas kernels  60.1 us (27%)
  starting transfers between devices  42.5 us (19%)
  local copies, waits for them, and re-layouts  10.1 us (4%)
    ppermute x14, waiting for transfers between devices, hand(): return lax.ppermute(value, 'shot', pairs)  102 us
    ppermute x14, starting transfers between devices, hand(): return lax.ppermute(value, 'shot', pairs)  35.3 us
    pallas_call x3, Pallas kernels, extrapolate_blocks(): pl.pallas_call(functools.partial(extrapolate_kernel, sets=sets, rows=rows...  31.3 us
    pallas_call x1, Pallas kernels, product_blocks(): pl.pallas_call(product_kernel, grid_spec=pltpu.PrefetchScalarGridSpec(num...  15.1 us
    pallas_call x3, Pallas kernels, image_blocks(): pl.pallas_call(functools.partial(image_kernel, first=first, begins=begins...  13.6 us
    ppermute x6, waiting for transfers between devices, send_sum(): lax.ppermute(value.astype(jnp.bfloat16), ('shot', 'freq'), pairs)  8.63 us
    unnamed x32, local copies, waits for them, and re-layouts  7.91 us
    ppermute x6, starting transfers between devices, send_sum(): lax.ppermute(value.astype(jnp.bfloat16), ('shot', 'freq'), pairs)  7.2 us
  transfers between devices with their start and end apart: 20, of which 12 were waited for; matrix products, arithmetic and copies ran while one was open for 1% of the time, Pallas kernels for 23%

profile of v2, /device:TPU:0, one launch (start us, length us, event | category | flops | bytes accessed | tf_op | source)
XLA Modules:
  0.0 224.4 jit_solution(4175812622850390813)
XLA Ops:
  0.0 6.1 %extrapolate.3.refs_3_ = bf16[4,512,256]{2,1,0:T(8,128)(2,1)} custom-call(s32[4]{0:T(128)} %constant.38.clone.order, s32[3,16]{1,0:T(4,128)} %bitcast.34, bf16[16384,128]{1,0:T(8,128)(2,1)} %bitcast.31, bf16[16,3,2,128,128]{4,3,2,1,0:T(8,128)(2,1)} %bitcast.28), custom_call_target="tpu_custom_call" | custom-call | flops 1000 | bytes 1000 | tf_op jit(solution)/shard_map/extrapolate/pallas_call | solution.py:204
  6.8 7.7 %collective-permute-start.1 = (bf16[4,512,256]{2,1,0:T(8,128)(2,1)}, bf16[4,512,256]{2,1,0:T(8,128)(2,1)S(1)}, u32[]{:S(2)}, u32[]{:S(2)}) collective-permute-start(bf16[4,512,256]{2,1,0:T(8,128)(2,1)} %extrapolate.3.refs_3_), channel_id=1, source_target_pairs={{0,4},{12,8},{1,5},{13,9},{2,6},{14,10},{3,7},{15,11},{16,20},{28,... | collective-permute-start | bytes 3145736 | tf_op jit(solution)/shard_map/ppermute | solution.py:356
  14.6 1.3 collective-permute-start
  15.9 11.4 %extrapolate.4 = (bf16[5,512,256]{2,1,0:T(8,128)(2,1)}, bf16[7,512,256]{2,1,0:T(8,128)(2,1)}) custom-call(s32[12]{0:T(128)} %constant.39.clone.order, s32[3,16]{1,0:T(4,128)} %bitcast.35, bf16[16384,128]{1,0:T(8,128)(2,1)} %bitcast.32, bf16[16,3,2,128,128]{4,3,2,1,0:T(8,128)(2,1)} %bitcast.29), custom_call_target="tpu_custom_call" | custom-call | flops 1000 | bytes 1000 | tf_op jit(solution)/shard_map/extrapolate/pallas_call | solution.py:204
  27.2 5.6 %collective-permute-start.2 = (bf16[5,512,256]{2,1,0:T(8,128)(2,1)}, bf16[5,512,256]{2,1,0:T(8,128)(2,1)S(1)}, u32[]{:S(2)}, u32[]{:S(2)}) collective-permute-start(bf16[5,512,256]{2,1,0:T(8,128)(2,1)} %get-tuple-element.22.refs_4_), channel_id=1, source_target_pairs={{0,4},{12,8},{1,5},{13,9},{2,6},{14,10},{3,7},{15,11},{16,20},{28,... | collective-permute-start | bytes 3932168 | tf_op jit(solution)/shard_map/ppermute | solution.py:356
  32.8 1.8 collective-permute-start.3
  36.9 1.5 collective-permute-done.1.refs_6_
  38.4 4.5 %collective-permute-done.data_out = bf16[16,2,128,128]{3,2,1,0:T(8,128)(2,1)} collective-permute-done((bf16[16,2,128,128]{3,2,1,0:T(8,128)(2,1)}, bf16[16,2,128,128]{3,2,1,0:T(8,128)(2,1)}, u32[]{:S(2)}, u32[]{:S(2)}) %collective-permute-start) | collective-permute-done | bytes 1048608 | tf_op jit(solution)/shard_map/ppermute | solution.py:356
  42.9 2.4 %collective-permute-start.6 = (bf16[16,2,128,128]{3,2,1,0:T(8,128)(2,1)}, bf16[16,2,128,128]{3,2,1,0:T(8,128)(2,1)}, u32[]{:S(2)}, u32[]{:S(2)}) collective-permute-start(bf16[16,2,128,128]{3,2,1,0:T(8,128)(2,1)} %bitcast.7.near_data), channel_id=1, source_target_pairs={{0,4},{12,8},{1,5},{13,9},{2,6},{14,10},{3,7},{15,11},{16,20},{28,... | collective-permute-start | bytes 3145736 | tf_op jit(solution)/shard_map/ppermute | solution.py:356
  45.3 13.9 %extrapolate.5 = (bf16[9,512,256]{2,1,0:T(8,128)(2,1)}, bf16[7,512,256]{2,1,0:T(8,128)(2,1)}) custom-call(s32[16]{0:T(128)} %constant.40.clone.order, s32[3,16]{1,0:T(4,128)} %bitcast.36, bf16[16384,128]{1,0:T(8,128)(2,1)} %bitcast.33, bf16[16,3,2,128,128]{4,3,2,1,0:T(8,128)(2,1)} %bitcast.30), custom_call_target="tpu_custom_call" | custom-call | flops 1000 | bytes 1000 | tf_op jit(solution)/shard_map/extrapolate/pallas_call | solution.py:204
  59.2 1.3 collective-permute-start.5
  60.5 6.0 %collective-permute-done.2.refs_7_ = bf16[5,512,256]{2,1,0:T(8,128)(2,1)S(1)} collective-permute-done((bf16[5,512,256]{2,1,0:T(8,128)(2,1)}, bf16[5,512,256]{2,1,0:T(8,128)(2,1)S(1)}, u32[]{:S(2)}, u32[]{:S(2)}) %collective-permute-start.2) | collective-permute-done | bytes 1310752 | tf_op jit(solution)/shard_map/ppermute | solution.py:356
  66.5 5.8 %collective-permute-start.4 = (bf16[9,512,256]{2,1,0:T(8,128)(2,1)}, bf16[9,512,256]{2,1,0:T(8,128)(2,1)}, u32[]{:S(2)}, u32[]{:S(2)}) collective-permute-start(bf16[9,512,256]{2,1,0:T(8,128)(2,1)} %get-tuple-element.23.near_in), channel_id=1, source_target_pairs={{0,4},{12,8},{1,5},{13,9},{2,6},{14,10},{3,7},{15,11},{16,20},{28,... | collective-permute-start | bytes 7077896 | tf_op jit(solution)/shard_map/ppermute | solution.py:356
  73.1 15.9 %collective-permute-done.6.data_in = bf16[16,2,128,128]{3,2,1,0:T(8,128)(2,1)} collective-permute-done((bf16[16,2,128,128]{3,2,1,0:T(8,128)(2,1)}, bf16[16,2,128,128]{3,2,1,0:T(8,128)(2,1)}, u32[]{:S(2)}, u32[]{:S(2)}) %collective-permute-start.6) | collective-permute-done | bytes 1048608 | tf_op jit(solution)/shard_map/ppermute | solution.py:356
  89.0 3.3 %collective-permute-start.12 = (bf16[7,512,256]{2,1,0:T(8,128)(2,1)S(1)}, bf16[7,512,256]{2,1,0:T(8,128)(2,1)}, u32[]{:S(2)}, u32[]{:S(2)}) collective-permute-start(bf16[7,512,256]{2,1,0:T(8,128)(2,1)S(1)} %copy-done), channel_id=1, source_target_pairs={{0,12},{12,0},{1,13},{13,1},{2,14},{14,2},{3,15},{15,3},{16,28},{2... | collective-permute-start | bytes 5505032 | tf_op jit(solution)/shard_map/ppermute | solution.py:356
  94.0 25.7 %collective-permute-done.5.far_out = bf16[7,512,256]{2,1,0:T(8,128)(2,1)S(1)} collective-permute-done((bf16[7,512,256]{2,1,0:T(8,128)(2,1)}, bf16[7,512,256]{2,1,0:T(8,128)(2,1)S(1)}, u32[]{:S(2)}, u32[]{:S(2)}) %collective-permute-start.5) | collective-permute-done | bytes 1835040 | tf_op jit(solution)/shard_map/ppermute | solution.py:356
  125.8 13.7 %collective-permute-done.4.far_in = bf16[9,512,256]{2,1,0:T(8,128)(2,1)} collective-permute-done((bf16[9,512,256]{2,1,0:T(8,128)(2,1)}, bf16[9,512,256]{2,1,0:T(8,128)(2,1)}, u32[]{:S(2)}, u32[]{:S(2)}) %collective-permute-start.4) | collective-permute-done | bytes 2359328 | tf_op jit(solution)/shard_map/ppermute | solution.py:356
  139.5 1.7 copy-done.4
  141.2 1.5 copy-done.5
  142.7 1.5 copy-done.7
  144.2 15.1 %product.1.refs_0_.refs_1_.refs_2_ = bf16[9,256,2048]{2,1,0:T(8,128)(2,1)S(1)} custom-call(s32[16]{0:T(128)S(1)} %get-tuple-element.30.near_ids, s32[16]{0:T(128)S(1)} %get-tuple-element.29.far_ids, s32[1]{0:T(128)} %bitcast.1.inner, bf16[9,512,256]{2,1,0:T(8,128)(2,1)S(1)} %copy-done.4, bf16[7,512,256]{2,1,0:T(8,128)(2,1)S(1)} %copy-done.5, ...), custom_call_target="tpu_custom_call" | custom-call | flops 1000 | bytes 1000 | tf_op jit(solution)/shard_map/product/pallas_call | solution.py:278
  159.4 19.9 %collective-permute-done.12.refs_11_ = bf16[7,512,256]{2,1,0:T(8,128)(2,1)} collective-permute-done((bf16[7,512,256]{2,1,0:T(8,128)(2,1)S(1)}, bf16[7,512,256]{2,1,0:T(8,128)(2,1)}, u32[]{:S(2)}, u32[]{:S(2)}) %collective-permute-start.12) | collective-permute-done | bytes 1835040 | tf_op jit(solution)/shard_map/ppermute | solution.py:356
  179.3 7.8 %image.3.refs_4_ = f32[9,2,128,128]{3,2,1,0:T(8,128)S(1)} custom-call(s32[3]{0:T(128)S(1)} %pad_add_fusion.places.unused, s32[3]{0:T(128)S(1)} %pad_add_fusion.places.unused, s32[1]{0:T(128)} %bitcast.1.inner, bf16[9,256,2048]{2,1,0:T(8,128)(2,1)S(1)} %product.1.refs_0_.refs_1_.refs_2_, bf16[9,256,2048]{2,1,0:T(8,128)(2,1)S(1)} %product.1.refs_0_.refs_1_.refs_2_, ...), custom_call_target="tpu_custom_call" | custom-call | flops 1000 | bytes 1000 | tf_op jit(solution)/shard_map/image/pallas_call | solution.py:339
  187.2 3.3 %collective-permute-done.9.refs_3_ = bf16[4,512,256]{2,1,0:T(8,128)(2,1)} collective-permute-done((bf16[4,512,256]{2,1,0:T(8,128)(2,1)}, bf16[4,512,256]{2,1,0:T(8,128)(2,1)}, u32[]{:S(2)}, u32[]{:S(2)}) %collective-permute-start.9) | collective-permute-done | bytes 1048608 | tf_op jit(solution)/shard_map/ppermute | solution.py:356
  190.5 3.0 %image.4 = f32[5,2,128,128]{3,2,1,0:T(8,128)S(1)} custom-call(s32[1]{0:T(128)} %bitcast.places.unused, s32[1]{0:T(128)} %bitcast.places.unused, s32[1]{0:T(128)} %bitcast.1.inner, bf16[9,256,2048]{2,1,0:T(8,128)(2,1)S(1)} %product.1.refs_0_.refs_1_.refs_2_, bf16[4,512,256]{2,1,0:T(8,128)(2,1)S(1)} %copy-done.3, ...), custom_call_target="tpu_custom_call" | custom-call | flops 1000 | bytes 1000 | tf_op jit(solution)/shard_map/image/pallas_call | solution.py:339
  193.6 11.1 %collective-permute-done.13.refs_3_ = bf16[3,512,256]{2,1,0:T(8,128)(2,1)} collective-permute-done((bf16[3,512,256]{2,1,0:T(8,128)(2,1)}, bf16[3,512,256]{2,1,0:T(8,128)(2,1)}, u32[]{:S(2)}, u32[]{:S(2)}) %collective-permute-start.13) | collective-permute-done | bytes 786464 | tf_op jit(solution)/shard_map/ppermute | solution.py:356
  204.7 2.7 %image.5 = f32[4,2,128,128]{3,2,1,0:T(8,128)S(1)} custom-call(s32[1]{0:T(128)} %bitcast.places.unused, s32[1]{0:T(128)} %bitcast.places.unused, s32[1]{0:T(128)} %bitcast.1.inner, bf16[9,256,2048]{2,1,0:T(8,128)(2,1)S(1)} %product.1.refs_0_.refs_1_.refs_2_, bf16[4,512,256]{2,1,0:T(8,128)(2,1)S(1)} %copy-done.3, ...), custom_call_target="tpu_custom_call" | custom-call | flops 1000 | bytes 1000 | tf_op jit(solution)/shard_map/image/pallas_call | solution.py:339
  207.6 1.6 collective-permute-done.14
  210.0 1.6 collective-permute-start.18
  213.0 2.7 %collective-permute-done.18 = bf16[2,2,128,128]{3,2,1,0:T(8,128)(2,1)S(1)} collective-permute-done((bf16[2,2,128,128]{3,2,1,0:T(8,128)(2,1)S(1)}, bf16[2,2,128,128]{3,2,1,0:T(8,128)(2,1)S(1)}, u32[]{:S(2)}, u32[]{:S(2)}) %collective-permute-start.18) | collective-permute-done | bytes 131104 | tf_op jit(solution)/shard_map/ppermute | solution.py:361
  215.7 3.6 %collective-permute-start.19 = (bf16[2,128,128]{2,1,0:T(8,128)(2,1)S(1)}, bf16[2,128,128]{2,1,0:T(8,128)(2,1)S(1)}, u32[]{:S(2)}, u32[]{:S(2)}) collective-permute-start(bf16[2,128,128]{2,1,0:T(8,128)(2,1)S(1)} %fusion.3), channel_id=1, source_target_pairs={{0,12},{1,13},{2,14},{4,8},{5,9},{6,10},{7,11},{8,4},{9,5},{10,6},... | collective-permute-start | bytes 196616 | tf_op jit(solution)/shard_map/ppermute | solution.py:361
  219.3 4.3 %collective-permute-done.19 = bf16[2,128,128]{2,1,0:T(8,128)(2,1)S(1)} collective-permute-done((bf16[2,128,128]{2,1,0:T(8,128)(2,1)S(1)}, bf16[2,128,128]{2,1,0:T(8,128)(2,1)S(1)}, u32[]{:S(2)}, u32[]{:S(2)}) %collective-permute-start.19) | collective-permute-done | bytes 65568 | tf_op jit(solution)/shard_map/ppermute | solution.py:361
  (61 shorter events, 14.6 us)
Async XLA Ops:
  6.1 28.6 %collective-permute-start.10 = (bf16[4,512,256]{2,1,0:T(8,128)(2,1)}, bf16[4,512,256]{2,1,0:T(8,128)(2,1)S(1)}, u32[]{:S(2)}, u32[]{:S(2)}) collective-permute-start(bf16[4,512,256]{2,1,0:T(8,128)(2,1)} %extrapolate.3.refs_3_), channel_id=1, source_target_pairs={{4,8},{8,4},{5,9},{9,5},{6,10},{10,6},{7,11},{11,7},{20,24},{24,20... | collective-permute-start | bytes 3145736 | tf_op jit(solution)/shard_map/ppermute | solution.py:356
  6.8 31.6 %collective-permute-start.1 = (bf16[4,512,256]{2,1,0:T(8,128)(2,1)}, bf16[4,512,256]{2,1,0:T(8,128)(2,1)S(1)}, u32[]{:S(2)}, u32[]{:S(2)}) collective-permute-start(bf16[4,512,256]{2,1,0:T(8,128)(2,1)} %extrapolate.3.refs_3_), channel_id=1, source_target_pairs={{0,4},{12,8},{1,5},{13,9},{2,6},{14,10},{3,7},{15,11},{16,20},{28,... | collective-permute-start | bytes 3145736 | tf_op jit(solution)/shard_map/ppermute | solution.py:356
  14.6 28.3 %collective-permute-start = (bf16[16,2,128,128]{3,2,1,0:T(8,128)(2,1)}, bf16[16,2,128,128]{3,2,1,0:T(8,128)(2,1)}, u32[]{:S(2)}, u32[]{:S(2)}) collective-permute-start(bf16[16,2,128,128]{3,2,1,0:T(8,128)(2,1)} %bitcast.7.near_data), channel_id=1, source_target_pairs={{4,0},{8,12},{5,1},{9,13},{6,2},{10,14},{7,3},{11,15},{20,16},{24,... | collective-permute-start | bytes 3145736 | tf_op jit(solution)/shard_map/ppermute | solution.py:356
  27.2 39.2 %collective-permute-start.2 = (bf16[5,512,256]{2,1,0:T(8,128)(2,1)}, bf16[5,512,256]{2,1,0:T(8,128)(2,1)S(1)}, u32[]{:S(2)}, u32[]{:S(2)}) collective-permute-start(bf16[5,512,256]{2,1,0:T(8,128)(2,1)} %get-tuple-element.22.refs_4_), channel_id=1, source_target_pairs={{0,4},{12,8},{1,5},{13,9},{2,6},{14,10},{3,7},{15,11},{16,20},{28,... | collective-permute-start | bytes 3932168 | tf_op jit(solution)/shard_map/ppermute | solution.py:356
  32.8 33.6 %collective-permute-start.3 = (bf16[5,512,256]{2,1,0:T(8,128)(2,1)}, bf16[5,512,256]{2,1,0:T(8,128)(2,1)}, u32[]{:S(2)}, u32[]{:S(2)}) collective-permute-start(bf16[5,512,256]{2,1,0:T(8,128)(2,1)} %get-tuple-element.22.refs_4_), channel_id=1, source_target_pairs={{4,8},{8,4},{5,9},{9,5},{6,10},{10,6},{7,11},{11,7},{20,24},{24,20... | collective-permute-start | bytes 3932168 | tf_op jit(solution)/shard_map/ppermute | solution.py:356
  35.6 53.3 %collective-permute-start.11 = (bf16[7,512,256]{2,1,0:T(8,128)(2,1)}, bf16[7,512,256]{2,1,0:T(8,128)(2,1)}, u32[]{:S(2)}, u32[]{:S(2)}) collective-permute-start(bf16[7,512,256]{2,1,0:T(8,128)(2,1)} %get-tuple-element.27.refs_5_), channel_id=1, source_target_pairs={{4,0},{8,12},{5,1},{9,13},{6,2},{10,14},{7,3},{11,15},{20,16},{24,... | collective-permute-start | bytes 5505032 | tf_op jit(solution)/shard_map/ppermute | solution.py:356
  38.4 6.9 %copy-start.13 = (bf16[4,512,256]{2,1,0:T(8,128)(2,1)}, bf16[4,512,256]{2,1,0:T(8,128)(2,1)S(1)}, u32[]{:S(2)}) copy-start(bf16[4,512,256]{2,1,0:T(8,128)(2,1)S(1)} %collective-permute-done.1.refs_6_) | copy-start | bytes 3145732
  42.9 46.1 %collective-permute-start.6 = (bf16[16,2,128,128]{3,2,1,0:T(8,128)(2,1)}, bf16[16,2,128,128]{3,2,1,0:T(8,128)(2,1)}, u32[]{:S(2)}, u32[]{:S(2)}) collective-permute-start(bf16[16,2,128,128]{3,2,1,0:T(8,128)(2,1)} %bitcast.7.near_data), channel_id=1, source_target_pairs={{0,4},{12,8},{1,5},{13,9},{2,6},{14,10},{3,7},{15,11},{16,20},{28,... | collective-permute-start | bytes 3145736 | tf_op jit(solution)/shard_map/ppermute | solution.py:356
  45.3 43.7 %copy-start = (bf16[7,512,256]{2,1,0:T(8,128)(2,1)S(1)}, bf16[7,512,256]{2,1,0:T(8,128)(2,1)}, u32[]{:S(2)}) copy-start(bf16[7,512,256]{2,1,0:T(8,128)(2,1)} %get-tuple-element.27.refs_5_) | copy-start | bytes 5505028
  59.2 60.5 %collective-permute-start.5 = (bf16[7,512,256]{2,1,0:T(8,128)(2,1)}, bf16[7,512,256]{2,1,0:T(8,128)(2,1)S(1)}, u32[]{:S(2)}, u32[]{:S(2)}) collective-permute-start(bf16[7,512,256]{2,1,0:T(8,128)(2,1)} %get-tuple-element.21.near_out), channel_id=1, source_target_pairs={{4,0},{8,12},{5,1},{9,13},{6,2},{10,14},{7,3},{11,15},{20,16},{24,... | collective-permute-start | bytes 5505032 | tf_op jit(solution)/shard_map/ppermute | solution.py:356
  66.5 22.5 %copy-start.9 = (bf16[5,512,256]{2,1,0:T(8,128)(2,1)}, bf16[5,512,256]{2,1,0:T(8,128)(2,1)S(1)}, u32[]{:S(2)}) copy-start(bf16[5,512,256]{2,1,0:T(8,128)(2,1)S(1)} %collective-permute-done.2.refs_7_) | copy-start | bytes 3932164
  66.5 59.1 %copy-start.15 = (s32[64,2]{0,1:T(2,128)S(1)}, s32[64,2]{0,1:T(2,128)}, u32[]{:S(2)}) copy-start(s32[64,2]{0,1:T(2,128)} %param.13) | copy-start | bytes 1540
  66.5 73.0 %collective-permute-start.4 = (bf16[9,512,256]{2,1,0:T(8,128)(2,1)}, bf16[9,512,256]{2,1,0:T(8,128)(2,1)}, u32[]{:S(2)}, u32[]{:S(2)}) collective-permute-start(bf16[9,512,256]{2,1,0:T(8,128)(2,1)} %get-tuple-element.23.near_in), channel_id=1, source_target_pairs={{0,4},{12,8},{1,5},{13,9},{2,6},{14,10},{3,7},{15,11},{16,20},{28,... | collective-permute-start | bytes 7077896 | tf_op jit(solution)/shard_map/ppermute | solution.py:356
  72.3 20.7 %collective-permute-start.7 = (bf16[4,512,256]{2,1,0:T(8,128)(2,1)}, bf16[4,512,256]{2,1,0:T(8,128)(2,1)S(1)}, u32[]{:S(2)}, u32[]{:S(2)}) collective-permute-start(bf16[4,512,256]{2,1,0:T(8,128)(2,1)} %copy-done.13), channel_id=1, source_target_pairs={{4,8},{8,4},{5,9},{9,5},{6,10},{10,6},{7,11},{11,7},{20,24},{24,20... | collective-permute-start | bytes 3145736 | tf_op jit(solution)/shard_map/ppermute | solution.py:356
  89.0 90.3 %collective-permute-start.12 = (bf16[7,512,256]{2,1,0:T(8,128)(2,1)S(1)}, bf16[7,512,256]{2,1,0:T(8,128)(2,1)}, u32[]{:S(2)}, u32[]{:S(2)}) collective-permute-start(bf16[7,512,256]{2,1,0:T(8,128)(2,1)S(1)} %copy-done), channel_id=1, source_target_pairs={{0,12},{12,0},{1,13},{13,1},{2,14},{14,2},{3,15},{15,3},{16,28},{2... | collective-permute-start | bytes 5505032 | tf_op jit(solution)/shard_map/ppermute | solution.py:356
  92.2 94.9 %collective-permute-start.8 = (bf16[5,512,256]{2,1,0:T(8,128)(2,1)}, bf16[5,512,256]{2,1,0:T(8,128)(2,1)S(1)}, u32[]{:S(2)}, u32[]{:S(2)}) collective-permute-start(bf16[5,512,256]{2,1,0:T(8,128)(2,1)} %copy-done.9), channel_id=1, source_target_pairs={{4,8},{8,4},{5,9},{9,5},{6,10},{10,6},{7,11},{11,7},{20,24},{24,20... | collective-permute-start | bytes 3932168 | tf_op jit(solution)/shard_map/ppermute | solution.py:356
  122.0 68.5 %collective-permute-start.9 = (bf16[4,512,256]{2,1,0:T(8,128)(2,1)}, bf16[4,512,256]{2,1,0:T(8,128)(2,1)}, u32[]{:S(2)}, u32[]{:S(2)}) collective-permute-start(bf16[4,512,256]{2,1,0:T(8,128)(2,1)} %slice.35), channel_id=1, source_target_pairs={{4,12},{8,0},{5,13},{9,1},{6,14},{10,2},{7,15},{11,3},{20,28},{24,... | collective-permute-start | bytes 3145736 | tf_op jit(solution)/shard_map/ppermute | solution.py:356
  124.3 80.4 %collective-permute-start.13 = (bf16[3,512,256]{2,1,0:T(8,128)(2,1)}, bf16[3,512,256]{2,1,0:T(8,128)(2,1)}, u32[]{:S(2)}, u32[]{:S(2)}) collective-permute-start(bf16[3,512,256]{2,1,0:T(8,128)(2,1)} %slice.36), channel_id=1, source_target_pairs={{4,12},{8,0},{5,13},{9,1},{6,14},{10,2},{7,15},{11,3},{20,28},{24,... | collective-permute-start | bytes 2359304 | tf_op jit(solution)/shard_map/ppermute | solution.py:356
  139.5 1.7 copy-start.4
  141.2 1.5 copy-start.5
  144.2 35.1 %copy-start.1 = (bf16[4,512,256]{2,1,0:T(8,128)(2,1)S(1)}, bf16[4,512,256]{2,1,0:T(8,128)(2,1)}, u32[]{:S(2)}) copy-start(bf16[4,512,256]{2,1,0:T(8,128)(2,1)} %extrapolate.3.refs_3_) | copy-start | bytes 3145732
  144.2 35.1 %copy-start.8 = (bf16[5,512,256]{2,1,0:T(8,128)(2,1)S(1)}, bf16[5,512,256]{2,1,0:T(8,128)(2,1)}, u32[]{:S(2)}) copy-start(bf16[5,512,256]{2,1,0:T(8,128)(2,1)} %get-tuple-element.22.refs_4_) | copy-start | bytes 3932164
  144.2 35.1 %copy-start.10 = (bf16[5,512,256]{2,1,0:T(8,128)(2,1)S(1)}, bf16[5,512,256]{2,1,0:T(8,128)(2,1)}, u32[]{:S(2)}) copy-start(bf16[5,512,256]{2,1,0:T(8,128)(2,1)} %copy-done.9) | copy-start | bytes 3932164
  144.2 35.1 %copy-start.12 = (bf16[4,512,256]{2,1,0:T(8,128)(2,1)S(1)}, bf16[4,512,256]{2,1,0:T(8,128)(2,1)}, u32[]{:S(2)}) copy-start(bf16[4,512,256]{2,1,0:T(8,128)(2,1)} %copy-done.11) | copy-start | bytes 3145732
  144.2 35.1 %copy-start.14 = (bf16[4,512,256]{2,1,0:T(8,128)(2,1)S(1)}, bf16[4,512,256]{2,1,0:T(8,128)(2,1)}, u32[]{:S(2)}) copy-start(bf16[4,512,256]{2,1,0:T(8,128)(2,1)} %copy-done.13) | copy-start | bytes 3145732
  159.4 31.1 %copy-start.3 = (bf16[4,512,256]{2,1,0:T(8,128)(2,1)S(1)}, bf16[4,512,256]{2,1,0:T(8,128)(2,1)}, u32[]{:S(2)}) copy-start(bf16[4,512,256]{2,1,0:T(8,128)(2,1)} %copy-done.2) | copy-start | bytes 3145732
  207.5 1.7 collective-permute-start.14
  209.3 2.3 %collective-permute-start.15 = (bf16[2,128,128]{2,1,0:T(8,128)(2,1)S(1)}, bf16[2,128,128]{2,1,0:T(8,128)(2,1)S(1)}, u32[]{:S(2)}, u32[]{:S(2)}) collective-permute-start(bf16[2,128,128]{2,1,0:T(8,128)(2,1)S(1)} %fusion.2), channel_id=1, source_target_pairs={{5,7},{9,11},{21,23},{25,27}} | collective-permute-start | bytes 196616 | tf_op jit(solution)/shard_map/ppermute | solution.py:361
  210.0 5.6 %collective-permute-start.18 = (bf16[2,2,128,128]{3,2,1,0:T(8,128)(2,1)S(1)}, bf16[2,2,128,128]{3,2,1,0:T(8,128)(2,1)S(1)}, u32[]{:S(2)}, u32[]{:S(2)}) collective-permute-start(bf16[2,2,128,128]{3,2,1,0:T(8,128)(2,1)S(1)} %select_convert_fusion.1), channel_id=1, source_target_pairs={{0,2},{1,3},{2,0},{3,1},{4,6},{5,7},{6,4},{7,5},{8,10},{9,11},{10,... | collective-permute-start | bytes 393224 | tf_op jit(solution)/shard_map/ppermute | solution.py:361
  211.6 7.7 %collective-permute-start.16 = (bf16[2,128,128]{2,1,0:T(8,128)(2,1)S(1)}, bf16[2,128,128]{2,1,0:T(8,128)(2,1)S(1)}, u32[]{:S(2)}, u32[]{:S(2)}) collective-permute-start(bf16[2,128,128]{2,1,0:T(8,128)(2,1)S(1)} %add_convert_fusion), channel_id=1, source_target_pairs={{7,15},{23,31}} | collective-permute-start | bytes 196616 | tf_op jit(solution)/shard_map/ppermute | solution.py:361
  212.3 7.0 %collective-permute-start.17 = (bf16[2,128,128]{2,1,0:T(8,128)(2,1)S(1)}, bf16[2,128,128]{2,1,0:T(8,128)(2,1)S(1)}, u32[]{:S(2)}, u32[]{:S(2)}) collective-permute-start(bf16[2,128,128]{2,1,0:T(8,128)(2,1)S(1)} %add_convert_fusion), channel_id=1, source_target_pairs={{11,15},{27,31}} | collective-permute-start | bytes 196616 | tf_op jit(solution)/shard_map/ppermute | solution.py:361
  215.7 8.0 %collective-permute-start.19 = (bf16[2,128,128]{2,1,0:T(8,128)(2,1)S(1)}, bf16[2,128,128]{2,1,0:T(8,128)(2,1)S(1)}, u32[]{:S(2)}, u32[]{:S(2)}) collective-permute-start(bf16[2,128,128]{2,1,0:T(8,128)(2,1)S(1)} %fusion.3), channel_id=1, source_target_pairs={{0,12},{1,13},{2,14},{4,8},{5,9},{6,10},{7,11},{8,4},{9,5},{10,6},... | collective-permute-start | bytes 196616 | tf_op jit(solution)/shard_map/ppermute | solution.py:361
  (4 other events, 4.7 us)

commit v3 on v1

--- a/solution.py
+++ b/solution.py
@@ -104,6 +104,7 @@
 OUTER = [0, 12, 2, 14, 1, 13, 3]
 FIRST = 5
 OUTER_FIRST = 4
+LATE = 5
 
 
 def outer_place(slot):
@@ -328,7 +329,7 @@
             values.append(field)
         begins.append([(begin, is_inner) for (_, begin), is_inner in zip(parts, inners)])
     if before is not None:
-        specs.append(image_spec)
+        specs.append(pl.BlockSpec((1, 2, size, size), lambda j, o, u, i: (first + j, 0, 0, 0)))
         values.append(before)
     places = jnp.stack([shot for shot, _ in pieces])
     return pl.pallas_call(
@@ -361,20 +362,29 @@
     shots = range(4)
     even = freq % 2 == 0
     low = freq < 2
-    last = one[4:]
-    one = one[:4]
-    keep = jnp.where(even, jnp.concatenate([one, last]), jnp.concatenate([two, last]))
-    send = jnp.where(even, jnp.concatenate([two, last]), jnp.concatenate([one, last]))
+    keep = jnp.where(even, one, two)
+    send = jnp.where(even, two, one)
     image = keep + send_sum(send, [((s, f), (s, f ^ 1)) for s in shots for f in range(4)])
-    keep = jnp.where(low, image[:2], image[2:4])
-    send = jnp.where(low, image[2:4], image[:2])
-    last = image[4] + send_sum(image[4], [((s, 1), (s, 3)) for s in (1, 2)])
-    image = keep + send_sum(send, [((s, f), (s, f ^ 2)) for s in shots for f in range(4)])
-    keep = jnp.where(left, image[0], image[1])
-    send = jnp.where(left, image[1], image[0])
-    image = keep + send_sum(send, [((s, f), (3 - s, f)) for s in shots for f in range(4) if (s, f) != (0, 3)])
-    last = send_sum(last, [((1, 3), (3, 3))]) + send_sum(last, [((2, 3), (3, 3))])
-    return jnp.where((shot == 3) & (freq == 3), last, image)
+    near = jnp.where(low, image[:2], image[2:])
+    far = jnp.where(low, image[2:], image[:2])
+
+    def pick(pair, own):
+        return jnp.where(left == own, pair[0], pair[1])
+
+    pairs = [(s, f) for s in shots for f in range(4)]
+    both = send_sum(pick(far, False), [((s, f), (3 - s, f ^ 2)) for s, f in pairs if (s, f) != (0, 1)])
+    across = send_sum(pick(near, False), [((s, f), (3 - s, f)) for s, f in pairs if (s, f) != (0, 3)])
+    along = send_sum(pick(far, True), [((s, f), (s, f ^ 2)) for s, f in pairs if (s, f) != (3, 1)])
+    return pick(near, True) + along + across + both
+
+
+def sum_cores(image):
+    return image + send_sum(image, [((s, f), (s, f + 1)) for s in (1, 2) for f in (0, 2)])
+
+
+def sum_last(image):
+    image = image + send_sum(image, [((s, 1), (s, 3)) for s in (1, 2)])
+    return send_sum(image, [((1, 3), (3, 3))]) + send_sum(image, [((2, 3), (3, 3))])
 
 
 def split_body(source_field, receiver_field, operator, band_offsets, survey_tiles, survey_data):
@@ -406,8 +416,8 @@
     forward_head = hand(following(r_1_head, r_3_in), *middle)
     r_3_out = hand(r_outer, *ends)
     forward = hand(following(r_1_in, r_1_out), *middle)
-    beyond_1 = hand(following(r_outer, s_out, forward_head)[:OUTER_FIRST], *beyond)
-    beyond_2 = hand(r_outer[OUTER_FIRST:], *beyond)
+    beyond_1 = hand(following(r_outer, s_out, forward_head)[:LATE], *beyond)
+    beyond_2 = hand(r_outer[LATE:], *beyond)
 
     ids = survey_tiles[:, 1]
     near_ids = lax.dynamic_slice_in_dim(ids, shot * tiles, tiles)
@@ -421,14 +431,15 @@
         (shot ^ 3, [(r_3_head, 0), (r_3_in, HEAD), (r_3_out, 0)]),
     ]
     forwarded = [(forward_head, 0), (forward, HEAD)]
-    one = image_blocks(product, 0, FIRST, early, inner)
-    two = image_blocks(product, FIRST, len(INNER) - FIRST, early, inner)
-    one = image_blocks(product, 0, FIRST, [(shot ^ 2, forwarded + [(beyond_1, 0)])], inner, one)
-    two = image_blocks(
-        product, FIRST, len(INNER) - FIRST, [(shot ^ 2, forwarded + [(beyond_2, OUTER_FIRST)])], inner,
-        following(two, one),
-    )
-    image = sum_images(one, two, shot, freq)
+    image = image_blocks(product, 0, len(INNER), early, inner)
+    most = image_blocks(product, 0, LATE + 1, [(shot ^ 2, forwarded + [(beyond_1, 0)])], inner, image)
+    last = sum_cores(most[FIRST - 1])
+    rest = image_blocks(
+        product, LATE + 1, len(INNER) - LATE - 1, [(shot ^ 2, forwarded + [(beyond_2, LATE)])], inner,
+        following(image, most, last),
+    )
+    image = sum_images(most[:FIRST - 1], jnp.concatenate([most[FIRST:], rest]), shot, freq)
+    image = jnp.where((shot == 3) & (freq == 3), sum_last(last), image)
     total_freqs = source_field.shape[0] * lax.axis_size("freq")
     return image * (1.0 / math.sqrt(2.0 * NR * total_freqs))
 

time: 219 us -> 230 us (1.050)
  starting transfers between devices: 39.3 us -> 47.5 us
  local copies, waits for them, and re-layouts: 12 us -> 20.1 us
  waiting for transfers between devices: 105 us -> 97.7 us
  other arithmetic: 1.05 us -> 3.39 us
    unnamed x30 -> x46, local copies, waits for them, and re-layouts: 9.86 us -> 18 us
    ppermute x6 -> x8, starting transfers between devices: 7.89 us -> 15 us  [send_sum(): lax.ppermute(value.astype(jnp.bfloat16), ('shot', 'freq'), pairs)]
    ppermute x13, waiting for transfers between devices: 97 us -> 91.9 us  [hand(): return lax.ppermute(value, 'shot', pairs)]
    convert_element_type x4 -> x5, other arithmetic: 0.14 us -> 2.46 us  [send_sum(): value.astype(jnp.bfloat16)]
    ppermute x6 -> x8, waiting for transfers between devices: 7.94 us -> 5.74 us  [send_sum(): lax.ppermute(value.astype(jnp.bfloat16), ('shot', 'freq'), pairs)]
    pallas_call x4 -> x3, Pallas kernels: 15 us -> 14.1 us  [image_blocks(): pl.pallas_call(functools.partial(image_kernel, first=first, begins=begins...]
  transfers between devices with their start and end apart: 19 -> 21, of which waited for: 10 -> 7; matrix products, arithmetic and copies ran while one was open for 1% -> 2% of each run, Pallas kernels for 27% -> 26%
where the time goes in v3:
time: 230 us; the launch traced here: 229 us
  waiting for transfers between devices  97.7 us (42%)
  Pallas kernels  59.7 us (26%)
  starting transfers between devices  47.5 us (21%)
  local copies, waits for them, and re-layouts  20.1 us (9%)
  other arithmetic  3.39 us (1%)
    ppermute x13, waiting for transfers between devices, hand(): return lax.ppermute(value, 'shot', pairs)  91.9 us
    ppermute x13, starting transfers between devices, hand(): return lax.ppermute(value, 'shot', pairs)  32.5 us
    pallas_call x3, Pallas kernels, extrapolate_blocks(): pl.pallas_call(functools.partial(extrapolate_kernel, sets=sets, rows=rows...  31.5 us
    unnamed x46, local copies, waits for them, and re-layouts  18 us
    ppermute x8, starting transfers between devices, send_sum(): lax.ppermute(value.astype(jnp.bfloat16), ('shot', 'freq'), pairs)  15 us
    pallas_call x3, Pallas kernels, image_blocks(): pl.pallas_call(functools.partial(image_kernel, first=first, begins=begins...  14.1 us
    pallas_call x1, Pallas kernels, product_blocks(): pl.pallas_call(product_kernel, grid_spec=pltpu.PrefetchScalarGridSpec(num...  14.1 us
    ppermute x8, waiting for transfers between devices, send_sum(): lax.ppermute(value.astype(jnp.bfloat16), ('shot', 'freq'), pairs)  5.74 us
  transfers between devices with their start and end apart: 21, of which 7 were waited for; matrix products, arithmetic and copies ran while one was open for 2% of the time, Pallas kernels for 26%

profile of v3, /device:TPU:0, one launch (start us, length us, event | category | flops | bytes accessed | tf_op | source)
XLA Modules:
  0.0 228.8 jit_solution(18084095404010337268)
XLA Ops:
  0.0 3.0 %collective-permute-start.4 = (bf16[16,2,128,128]{3,2,1,0:T(8,128)(2,1)}, bf16[16,2,128,128]{3,2,1,0:T(8,128)(2,1)S(1)}, u32[]{:S(2)}, u32[]{:S(2)}) collective-permute-start(bf16[16,2,128,128]{3,2,1,0:T(8,128)(2,1)} %bitcast.37), channel_id=1, source_target_pairs={{0,4},{12,8},{4,0},{8,12},{1,5},{13,9},{5,1},{9,13},{2,6},{14,10},... | collective-permute-start | bytes 3145736 | tf_op jit(solution)/shard_map/ppermute | solution.py:352
  3.0 5.5 %extrapolate.3.refs_3_ = bf16[3,512,256]{2,1,0:T(8,128)(2,1)} custom-call(s32[3]{0:T(128)} %constant.40.clone.order, s32[3,16]{1,0:T(4,128)} %bitcast.45, bf16[16384,128]{1,0:T(8,128)(2,1)} %bitcast.42, bf16[16,3,2,128,128]{4,3,2,1,0:T(8,128)(2,1)} %bitcast.39), custom_call_target="tpu_custom_call" | custom-call | flops 1000 | bytes 1000 | tf_op jit(solution)/shard_map/extrapolate/pallas_call | solution.py:204
  9.3 7.2 %collective-permute-start.1 = (bf16[3,512,256]{2,1,0:T(8,128)(2,1)}, bf16[3,512,256]{2,1,0:T(8,128)(2,1)}, u32[]{:S(2)}, u32[]{:S(2)}) collective-permute-start(bf16[3,512,256]{2,1,0:T(8,128)(2,1)} %extrapolate.3.refs_3_), channel_id=1, source_target_pairs={{0,4},{12,8},{1,5},{13,9},{2,6},{14,10},{3,7},{15,11},{16,20},{28,... | collective-permute-start | bytes 2359304 | tf_op jit(solution)/shard_map/ppermute | solution.py:352
  16.4 12.1 %extrapolate.4 = (bf16[6,512,256]{2,1,0:T(8,128)(2,1)}, bf16[7,512,256]{2,1,0:T(8,128)(2,1)}) custom-call(s32[13]{0:T(128)} %constant.41.clone.order, s32[3,16]{1,0:T(4,128)} %bitcast.46, bf16[16384,128]{1,0:T(8,128)(2,1)} %bitcast.43, bf16[16,3,2,128,128]{4,3,2,1,0:T(8,128)(2,1)} %bitcast.40), custom_call_target="tpu_custom_call" | custom-call | flops 1000 | bytes 1000 | tf_op jit(solution)/shard_map/extrapolate/pallas_call | solution.py:204
  29.3 2.7 %collective-permute-start.7 = (bf16[6,512,256]{2,1,0:T(8,128)(2,1)}, bf16[6,512,256]{2,1,0:T(8,128)(2,1)}, u32[]{:S(2)}, u32[]{:S(2)}) collective-permute-start(bf16[6,512,256]{2,1,0:T(8,128)(2,1)} %get-tuple-element.21.refs_4_), channel_id=1, source_target_pairs={{0,4},{12,8},{1,5},{13,9},{2,6},{14,10},{3,7},{15,11},{16,20},{28,... | collective-permute-start | bytes 4718600 | tf_op jit(solution)/shard_map/ppermute | solution.py:352
  35.2 8.5 %collective-permute-done.1.refs_6_ = bf16[3,512,256]{2,1,0:T(8,128)(2,1)} collective-permute-done((bf16[3,512,256]{2,1,0:T(8,128)(2,1)}, bf16[3,512,256]{2,1,0:T(8,128)(2,1)}, u32[]{:S(2)}, u32[]{:S(2)}) %collective-permute-start.1) | collective-permute-done | bytes 786464 | tf_op jit(solution)/shard_map/ppermute | solution.py:352
  43.8 13.9 %extrapolate.5 = (bf16[9,512,256]{2,1,0:T(8,128)(2,1)}, bf16[7,512,256]{2,1,0:T(8,128)(2,1)}) custom-call(s32[16]{0:T(128)} %constant.42.clone.order, s32[3,16]{1,0:T(4,128)} %bitcast.47, bf16[16384,128]{1,0:T(8,128)(2,1)} %bitcast.44, bf16[16,3,2,128,128]{4,3,2,1,0:T(8,128)(2,1)} %bitcast.41), custom_call_target="tpu_custom_call" | custom-call | flops 1000 | bytes 1000 | tf_op jit(solution)/shard_map/extrapolate/pallas_call | solution.py:204
  57.7 1.3 collective-permute-start.3
  59.0 6.1 %collective-permute-start.2 = (bf16[9,512,256]{2,1,0:T(8,128)(2,1)}, bf16[9,512,256]{2,1,0:T(8,128)(2,1)}, u32[]{:S(2)}, u32[]{:S(2)}) collective-permute-start(bf16[9,512,256]{2,1,0:T(8,128)(2,1)} %get-tuple-element.19.near_in), channel_id=1, source_target_pairs={{0,4},{12,8},{1,5},{13,9},{2,6},{14,10},{3,7},{15,11},{16,20},{28,... | collective-permute-start | bytes 7077896 | tf_op jit(solution)/shard_map/ppermute | solution.py:352
  67.0 10.5 %collective-permute-done.7.refs_7_ = bf16[6,512,256]{2,1,0:T(8,128)(2,1)} collective-permute-done((bf16[6,512,256]{2,1,0:T(8,128)(2,1)}, bf16[6,512,256]{2,1,0:T(8,128)(2,1)}, u32[]{:S(2)}, u32[]{:S(2)}) %collective-permute-start.7) | collective-permute-done | bytes 1572896 | tf_op jit(solution)/shard_map/ppermute | solution.py:352
  77.5 4.4 %collective-permute-start.11 = (bf16[7,512,256]{2,1,0:T(8,128)(2,1)S(1)}, bf16[7,512,256]{2,1,0:T(8,128)(2,1)}, u32[]{:S(2)}, u32[]{:S(2)}) collective-permute-start(bf16[7,512,256]{2,1,0:T(8,128)(2,1)S(1)} %copy-done.2), channel_id=1, source_target_pairs={{0,12},{12,0},{1,13},{13,1},{2,14},{14,2},{3,15},{15,3},{16,28},{2... | collective-permute-start | bytes 5505032 | tf_op jit(solution)/shard_map/ppermute | solution.py:352
  81.9 1.8 collective-permute-start.9
  84.6 31.7 %collective-permute-done.3.far_out = bf16[7,512,256]{2,1,0:T(8,128)(2,1)S(1)} collective-permute-done((bf16[7,512,256]{2,1,0:T(8,128)(2,1)}, bf16[7,512,256]{2,1,0:T(8,128)(2,1)S(1)}, u32[]{:S(2)}, u32[]{:S(2)}) %collective-permute-start.3) | collective-permute-done | bytes 1835040 | tf_op jit(solution)/shard_map/ppermute | solution.py:352
  116.3 1.3 copy-done.9
  122.4 5.6 %collective-permute-done.2.far_in = bf16[9,512,256]{2,1,0:T(8,128)(2,1)} collective-permute-done((bf16[9,512,256]{2,1,0:T(8,128)(2,1)}, bf16[9,512,256]{2,1,0:T(8,128)(2,1)}, u32[]{:S(2)}, u32[]{:S(2)}) %collective-permute-start.2) | collective-permute-done | bytes 2359328 | tf_op jit(solution)/shard_map/ppermute | solution.py:352
  128.0 1.7 copy-done.7
  129.7 1.5 copy-done.8
  131.2 1.5 copy-done.10
  135.2 14.1 %product.1.refs_0_.refs_1_.refs_2_ = bf16[9,256,2048]{2,1,0:T(8,128)(2,1)S(1)} custom-call(s32[16]{0:T(128)S(1)} %get-tuple-element.32.near_ids, s32[16]{0:T(128)S(1)} %get-tuple-element.31.far_ids, s32[1]{0:T(128)} %bitcast.1.inner, bf16[9,512,256]{2,1,0:T(8,128)(2,1)S(1)} %copy-done.7, bf16[7,512,256]{2,1,0:T(8,128)(2,1)S(1)} %copy-done.8, ...), custom_call_target="tpu_custom_call" | custom-call | flops 1000 | bytes 1000 | tf_op jit(solution)/shard_map/product/pallas_call | solution.py:274
  149.3 20.0 %collective-permute-done.11.refs_11_ = bf16[7,512,256]{2,1,0:T(8,128)(2,1)} collective-permute-done((bf16[7,512,256]{2,1,0:T(8,128)(2,1)S(1)}, bf16[7,512,256]{2,1,0:T(8,128)(2,1)}, u32[]{:S(2)}, u32[]{:S(2)}) %collective-permute-start.11) | collective-permute-done | bytes 1835040 | tf_op jit(solution)/shard_map/ppermute | solution.py:352
  169.3 8.0 %image.3.refs_4_ = f32[9,2,128,128]{3,2,1,0:T(8,128)S(1)} custom-call(s32[3]{0:T(128)S(1)} %pad_add_fusion.places.unused, s32[3]{0:T(128)S(1)} %pad_add_fusion.places.unused, s32[1]{0:T(128)} %bitcast.1.inner, bf16[9,256,2048]{2,1,0:T(8,128)(2,1)S(1)} %product.1.refs_0_.refs_1_.refs_2_, bf16[9,256,2048]{2,1,0:T(8,128)(2,1)S(1)} %product.1.refs_0_.refs_1_.refs_2_, ...), custom_call_target="tpu_custom_call" | custom-call | flops 1000 | bytes 1000 | tf_op jit(solution)/shard_map/image/pallas_call | solution.py:335
  177.3 15.6 %collective-permute-done.10.refs_3_ = bf16[5,512,256]{2,1,0:T(8,128)(2,1)} collective-permute-done((bf16[5,512,256]{2,1,0:T(8,128)(2,1)}, bf16[5,512,256]{2,1,0:T(8,128)(2,1)}, u32[]{:S(2)}, u32[]{:S(2)}) %collective-permute-start.10) | collective-permute-done | bytes 1310752 | tf_op jit(solution)/shard_map/ppermute | solution.py:352
  192.9 4.3 %image.4 = f32[6,2,128,128]{3,2,1,0:T(8,128)S(1)} custom-call(s32[1]{0:T(128)} %bitcast.places.unused, s32[1]{0:T(128)} %bitcast.places.unused, s32[1]{0:T(128)} %bitcast.1.inner, bf16[9,256,2048]{2,1,0:T(8,128)(2,1)S(1)} %product.1.refs_0_.refs_1_.refs_2_, bf16[3,512,256]{2,1,0:T(8,128)(2,1)S(1)} %copy-done.4, ...), custom_call_target="tpu_custom_call" | custom-call | flops 1000 | bytes 1000 | tf_op jit(solution)/shard_map/image/pallas_call | solution.py:335
  197.2 1.3 collective-permute-start.12
  198.5 1.5 fusion.8
  200.0 1.3 collective-permute-start.13
  202.2 3.7 %copy-done.1 = bf16[9,256,2048]{2,1,0:T(8,128)(2,1)S(1)} copy-done((bf16[9,256,2048]{2,1,0:T(8,128)(2,1)S(1)}, bf16[9,256,2048]{2,1,0:T(8,128)(2,1)}, u32[]{:S(2)}) %copy-start.1) | copy-done | bytes 9437208
  206.9 1.8 image.5
  211.3 4.5 %collective-permute-start.19 = (bf16[2,128,128]{2,1,0:T(8,128)(2,1)S(1)}, bf16[2,128,128]{2,1,0:T(8,128)(2,1)S(1)}, u32[]{:S(2)}, u32[]{:S(2)}) collective-permute-start(bf16[2,128,128]{2,1,0:T(8,128)(2,1)S(1)} %fusion.6), channel_id=1, source_target_pairs={{0,12},{1,13},{2,14},{4,8},{5,9},{6,10},{7,11},{8,4},{9,5},{10,6},... | collective-permute-start | bytes 196616 | tf_op jit(solution)/shard_map/ppermute | solution.py:357
  215.9 3.4 %collective-permute-start.18 = (bf16[2,128,128]{2,1,0:T(8,128)(2,1)S(1)}, bf16[2,128,128]{2,1,0:T(8,128)(2,1)S(1)}, u32[]{:S(2)}, u32[]{:S(2)}) collective-permute-start(bf16[2,128,128]{2,1,0:T(8,128)(2,1)S(1)} %get-tuple-element.29), channel_id=1, source_target_pairs={{0,2},{1,3},{2,0},{3,1},{4,6},{5,7},{6,4},{7,5},{8,10},{9,11},{10,... | collective-permute-start | bytes 196616 | tf_op jit(solution)/shard_map/ppermute | solution.py:357
  219.3 3.1 %collective-permute-start.20 = (bf16[2,128,128]{2,1,0:T(8,128)(2,1)S(1)}, bf16[2,128,128]{2,1,0:T(8,128)(2,1)S(1)}, u32[]{:S(2)}, u32[]{:S(2)}) collective-permute-start(bf16[2,128,128]{2,1,0:T(8,128)(2,1)S(1)} %get-tuple-element.30), channel_id=1, source_target_pairs={{0,14},{2,12},{3,13},{4,10},{5,11},{6,8},{7,9},{8,6},{9,7},{10,4},... | collective-permute-start | bytes 196616 | tf_op jit(solution)/shard_map/ppermute | solution.py:357
  222.4 5.7 %collective-permute-done.20 = bf16[2,128,128]{2,1,0:T(8,128)(2,1)S(1)} collective-permute-done((bf16[2,128,128]{2,1,0:T(8,128)(2,1)S(1)}, bf16[2,128,128]{2,1,0:T(8,128)(2,1)S(1)}, u32[]{:S(2)}, u32[]{:S(2)}) %collective-permute-start.20) | collective-permute-done | bytes 65568 | tf_op jit(solution)/shard_map/ppermute | solution.py:357
  (79 shorter events, 19.8 us)
Async XLA Ops:
  0.0 32.9 %collective-permute-start.4 = (bf16[16,2,128,128]{3,2,1,0:T(8,128)(2,1)}, bf16[16,2,128,128]{3,2,1,0:T(8,128)(2,1)S(1)}, u32[]{:S(2)}, u32[]{:S(2)}) collective-permute-start(bf16[16,2,128,128]{3,2,1,0:T(8,128)(2,1)} %bitcast.37), channel_id=1, source_target_pairs={{0,4},{12,8},{4,0},{8,12},{1,5},{13,9},{5,1},{9,13},{2,6},{14,10},... | collective-permute-start | bytes 3145736 | tf_op jit(solution)/shard_map/ppermute | solution.py:352
  8.5 23.5 %collective-permute-start = (bf16[3,512,256]{2,1,0:T(8,128)(2,1)}, bf16[3,512,256]{2,1,0:T(8,128)(2,1)S(1)}, u32[]{:S(2)}, u32[]{:S(2)}) collective-permute-start(bf16[3,512,256]{2,1,0:T(8,128)(2,1)} %extrapolate.3.refs_3_), channel_id=1, source_target_pairs={{4,8},{8,4},{5,9},{9,5},{6,10},{10,6},{7,11},{11,7},{20,24},{24,20... | collective-permute-start | bytes 2359304 | tf_op jit(solution)/shard_map/ppermute | solution.py:352
  9.3 34.5 %collective-permute-start.1 = (bf16[3,512,256]{2,1,0:T(8,128)(2,1)}, bf16[3,512,256]{2,1,0:T(8,128)(2,1)}, u32[]{:S(2)}, u32[]{:S(2)}) collective-permute-start(bf16[3,512,256]{2,1,0:T(8,128)(2,1)} %extrapolate.3.refs_3_), channel_id=1, source_target_pairs={{0,4},{12,8},{1,5},{13,9},{2,6},{14,10},{3,7},{15,11},{16,20},{28,... | collective-permute-start | bytes 2359304 | tf_op jit(solution)/shard_map/ppermute | solution.py:352
  28.5 36.6 %collective-permute-start.5 = (bf16[6,512,256]{2,1,0:T(8,128)(2,1)}, bf16[6,512,256]{2,1,0:T(8,128)(2,1)S(1)}, u32[]{:S(2)}, u32[]{:S(2)}) collective-permute-start(bf16[6,512,256]{2,1,0:T(8,128)(2,1)} %get-tuple-element.21.refs_4_), channel_id=1, source_target_pairs={{4,8},{8,4},{5,9},{9,5},{6,10},{10,6},{7,11},{11,7},{20,24},{24,20... | collective-permute-start | bytes 4718600 | tf_op jit(solution)/shard_map/ppermute | solution.py:352
  29.3 48.2 %collective-permute-start.7 = (bf16[6,512,256]{2,1,0:T(8,128)(2,1)}, bf16[6,512,256]{2,1,0:T(8,128)(2,1)}, u32[]{:S(2)}, u32[]{:S(2)}) collective-permute-start(bf16[6,512,256]{2,1,0:T(8,128)(2,1)} %get-tuple-element.21.refs_4_), channel_id=1, source_target_pairs={{0,4},{12,8},{1,5},{13,9},{2,6},{14,10},{3,7},{15,11},{16,20},{28,... | collective-permute-start | bytes 4718600 | tf_op jit(solution)/shard_map/ppermute | solution.py:352
  33.9 47.9 %collective-permute-start.8 = (bf16[7,512,256]{2,1,0:T(8,128)(2,1)}, bf16[7,512,256]{2,1,0:T(8,128)(2,1)}, u32[]{:S(2)}, u32[]{:S(2)}) collective-permute-start(bf16[7,512,256]{2,1,0:T(8,128)(2,1)} %get-tuple-element.25.refs_5_), channel_id=1, source_target_pairs={{4,0},{8,12},{5,1},{9,13},{6,2},{10,14},{7,3},{11,15},{20,16},{24,... | collective-permute-start | bytes 5505032 | tf_op jit(solution)/shard_map/ppermute | solution.py:352
  43.8 33.7 %copy-start.2 = (bf16[7,512,256]{2,1,0:T(8,128)(2,1)S(1)}, bf16[7,512,256]{2,1,0:T(8,128)(2,1)}, u32[]{:S(2)}) copy-start(bf16[7,512,256]{2,1,0:T(8,128)(2,1)} %get-tuple-element.25.refs_5_) | copy-start | bytes 5505028
  57.7 58.6 %collective-permute-start.3 = (bf16[7,512,256]{2,1,0:T(8,128)(2,1)}, bf16[7,512,256]{2,1,0:T(8,128)(2,1)S(1)}, u32[]{:S(2)}, u32[]{:S(2)}) collective-permute-start(bf16[7,512,256]{2,1,0:T(8,128)(2,1)} %get-tuple-element.20.near_out), channel_id=1, source_target_pairs={{4,0},{8,12},{5,1},{9,13},{6,2},{10,14},{7,3},{11,15},{20,16},{24,... | collective-permute-start | bytes 5505032 | tf_op jit(solution)/shard_map/ppermute | solution.py:352
  59.0 63.2 %copy-start.22 = (s32[64,2]{0,1:T(2,128)S(1)}, s32[64,2]{0,1:T(2,128)}, u32[]{:S(2)}) copy-start(s32[64,2]{0,1:T(2,128)} %param.13) | copy-start | bytes 1540
  59.0 69.0 %collective-permute-start.2 = (bf16[9,512,256]{2,1,0:T(8,128)(2,1)}, bf16[9,512,256]{2,1,0:T(8,128)(2,1)}, u32[]{:S(2)}, u32[]{:S(2)}) collective-permute-start(bf16[9,512,256]{2,1,0:T(8,128)(2,1)} %get-tuple-element.19.near_in), channel_id=1, source_target_pairs={{0,4},{12,8},{1,5},{13,9},{2,6},{14,10},{3,7},{15,11},{16,20},{28,... | collective-permute-start | bytes 7077896 | tf_op jit(solution)/shard_map/ppermute | solution.py:352
  66.3 17.4 %collective-permute-start.6 = (bf16[3,512,256]{2,1,0:T(8,128)(2,1)}, bf16[3,512,256]{2,1,0:T(8,128)(2,1)S(1)}, u32[]{:S(2)}, u32[]{:S(2)}) collective-permute-start(bf16[3,512,256]{2,1,0:T(8,128)(2,1)} %collective-permute-done.1.refs_6_), channel_id=1, source_target_pairs={{4,8},{8,4},{5,9},{9,5},{6,10},{10,6},{7,11},{11,7},{20,24},{24,20... | collective-permute-start | bytes 2359304 | tf_op jit(solution)/shard_map/ppermute | solution.py:352
  77.5 91.8 %collective-permute-start.11 = (bf16[7,512,256]{2,1,0:T(8,128)(2,1)S(1)}, bf16[7,512,256]{2,1,0:T(8,128)(2,1)}, u32[]{:S(2)}, u32[]{:S(2)}) collective-permute-start(bf16[7,512,256]{2,1,0:T(8,128)(2,1)S(1)} %copy-done.2), channel_id=1, source_target_pairs={{0,12},{12,0},{1,13},{13,1},{2,14},{14,2},{3,15},{15,3},{16,28},{2... | collective-permute-start | bytes 5505032 | tf_op jit(solution)/shard_map/ppermute | solution.py:352
  81.9 111.1 %collective-permute-start.9 = (bf16[6,512,256]{2,1,0:T(8,128)(2,1)}, bf16[6,512,256]{2,1,0:T(8,128)(2,1)}, u32[]{:S(2)}, u32[]{:S(2)}) collective-permute-start(bf16[6,512,256]{2,1,0:T(8,128)(2,1)} %collective-permute-done.7.refs_7_), channel_id=1, source_target_pairs={{4,8},{8,4},{5,9},{9,5},{6,10},{10,6},{7,11},{11,7},{20,24},{24,20... | collective-permute-start | bytes 4718600 | tf_op jit(solution)/shard_map/ppermute | solution.py:352
  118.8 74.1 %collective-permute-start.10 = (bf16[5,512,256]{2,1,0:T(8,128)(2,1)}, bf16[5,512,256]{2,1,0:T(8,128)(2,1)}, u32[]{:S(2)}, u32[]{:S(2)}) collective-permute-start(bf16[5,512,256]{2,1,0:T(8,128)(2,1)} %slice.43), channel_id=1, source_target_pairs={{4,12},{8,0},{5,13},{9,1},{6,14},{10,2},{7,15},{11,3},{20,28},{24,... | collective-permute-start | bytes 3932168 | tf_op jit(solution)/shard_map/ppermute | solution.py:352
  120.9 80.4 %collective-permute-start.16 = (bf16[2,512,256]{2,1,0:T(8,128)(2,1)}, bf16[2,512,256]{2,1,0:T(8,128)(2,1)S(1)}, u32[]{:S(2)}, u32[]{:S(2)}) collective-permute-start(bf16[2,512,256]{2,1,0:T(8,128)(2,1)} %slice.47), channel_id=1, source_target_pairs={{4,12},{8,0},{5,13},{9,1},{6,14},{10,2},{7,15},{11,3},{20,28},{24,... | collective-permute-start | bytes 1572872 | tf_op jit(solution)/shard_map/ppermute | solution.py:352
  135.1 34.1 %copy-start.6 = (bf16[3,512,256]{2,1,0:T(8,128)(2,1)S(1)}, bf16[3,512,256]{2,1,0:T(8,128)(2,1)}, u32[]{:S(2)}) copy-start(bf16[3,512,256]{2,1,0:T(8,128)(2,1)} %extrapolate.3.refs_3_) | copy-start | bytes 2359300
  135.1 34.1 %copy-start.11 = (bf16[6,512,256]{2,1,0:T(8,128)(2,1)S(1)}, bf16[6,512,256]{2,1,0:T(8,128)(2,1)}, u32[]{:S(2)}) copy-start(bf16[6,512,256]{2,1,0:T(8,128)(2,1)} %get-tuple-element.21.refs_4_) | copy-start | bytes 4718596
  135.1 34.1 %copy-start.13 = (bf16[6,512,256]{2,1,0:T(8,128)(2,1)S(1)}, bf16[6,512,256]{2,1,0:T(8,128)(2,1)}, u32[]{:S(2)}) copy-start(bf16[6,512,256]{2,1,0:T(8,128)(2,1)} %copy-done.12) | copy-start | bytes 4718596
  135.1 34.1 %copy-start.18 = (bf16[3,512,256]{2,1,0:T(8,128)(2,1)S(1)}, bf16[3,512,256]{2,1,0:T(8,128)(2,1)}, u32[]{:S(2)}) copy-start(bf16[3,512,256]{2,1,0:T(8,128)(2,1)} %copy-done.17) | copy-start | bytes 2359300
  149.2 43.7 %copy-start = (bf16[9,256,2048]{2,1,0:T(8,128)(2,1)}, bf16[9,256,2048]{2,1,0:T(8,128)(2,1)S(1)}, u32[]{:S(2)}) copy-start(bf16[9,256,2048]{2,1,0:T(8,128)(2,1)S(1)} %product.1.refs_0_.refs_1_.refs_2_) | copy-start | bytes 28311556
  149.2 43.7 %copy-start.4 = (bf16[3,512,256]{2,1,0:T(8,128)(2,1)S(1)}, bf16[3,512,256]{2,1,0:T(8,128)(2,1)}, u32[]{:S(2)}) copy-start(bf16[3,512,256]{2,1,0:T(8,128)(2,1)} %copy-done.3) | copy-start | bytes 2359300
  192.9 9.2 %copy-start.5 = (bf16[3,512,256]{2,1,0:T(8,128)(2,1)S(1)}, bf16[3,512,256]{2,1,0:T(8,128)(2,1)}, u32[]{:S(2)}) copy-start(bf16[3,512,256]{2,1,0:T(8,128)(2,1)} %copy-done.3) | copy-start | bytes 2359300
  197.2 1.3 collective-permute-start.12
  200.0 8.8 %collective-permute-start.13 = (bf16[2,128,128]{2,1,0:T(8,128)(2,1)S(1)}, bf16[2,128,128]{2,1,0:T(8,128)(2,1)}, u32[]{:S(2)}, u32[]{:S(2)}) collective-permute-start(bf16[2,128,128]{2,1,0:T(8,128)(2,1)S(1)} %get-tuple-element.27), channel_id=1, source_target_pairs={{5,7},{9,11},{21,23},{25,27}} | collective-permute-start | bytes 196616 | tf_op jit(solution)/shard_map/ppermute | solution.py:357
  202.2 3.7 %copy-start.1 = (bf16[9,256,2048]{2,1,0:T(8,128)(2,1)S(1)}, bf16[9,256,2048]{2,1,0:T(8,128)(2,1)}, u32[]{:S(2)}) copy-start(bf16[9,256,2048]{2,1,0:T(8,128)(2,1)} %copy-done) | copy-start | bytes 28311556
  206.9 2.0 copy-start.21
  208.8 2.3 %collective-permute-start.17 = (bf16[4,2,128,128]{3,2,1,0:T(8,128)(2,1)S(1)}, bf16[4,2,128,128]{3,2,1,0:T(8,128)(2,1)S(1)}, u32[]{:S(2)}, u32[]{:S(2)}) collective-permute-start(bf16[4,2,128,128]{3,2,1,0:T(8,128)(2,1)S(1)} %select_convert_fusion), channel_id=1, source_target_pairs={{0,1},{1,0},{2,3},{3,2},{4,5},{5,4},{6,7},{7,6},{8,9},{9,8},{10,11... | collective-permute-start | bytes 786440 | tf_op jit(solution)/shard_map/ppermute | solution.py:357
  209.8 12.6 %collective-permute-start.14 = (bf16[2,128,128]{2,1,0:T(8,128)(2,1)S(1)}, bf16[2,128,128]{2,1,0:T(8,128)(2,1)S(1)}, u32[]{:S(2)}, u32[]{:S(2)}) collective-permute-start(bf16[2,128,128]{2,1,0:T(8,128)(2,1)S(1)} %add_convert_fusion), channel_id=1, source_target_pairs={{7,15},{23,31}} | collective-permute-start | bytes 196616 | tf_op jit(solution)/shard_map/ppermute | solution.py:357
  210.4 11.9 %collective-permute-start.15 = (bf16[2,128,128]{2,1,0:T(8,128)(2,1)S(1)}, bf16[2,128,128]{2,1,0:T(8,128)(2,1)S(1)}, u32[]{:S(2)}, u32[]{:S(2)}) collective-permute-start(bf16[2,128,128]{2,1,0:T(8,128)(2,1)S(1)} %add_convert_fusion), channel_id=1, source_target_pairs={{11,15},{27,31}} | collective-permute-start | bytes 196616 | tf_op jit(solution)/shard_map/ppermute | solution.py:357
  211.3 11.1 %collective-permute-start.19 = (bf16[2,128,128]{2,1,0:T(8,128)(2,1)S(1)}, bf16[2,128,128]{2,1,0:T(8,128)(2,1)S(1)}, u32[]{:S(2)}, u32[]{:S(2)}) collective-permute-start(bf16[2,128,128]{2,1,0:T(8,128)(2,1)S(1)} %fusion.6), channel_id=1, source_target_pairs={{0,12},{1,13},{2,14},{4,8},{5,9},{6,10},{7,11},{8,4},{9,5},{10,6},... | collective-permute-start | bytes 196616 | tf_op jit(solution)/shard_map/ppermute | solution.py:357
  215.9 6.5 %collective-permute-start.18 = (bf16[2,128,128]{2,1,0:T(8,128)(2,1)S(1)}, bf16[2,128,128]{2,1,0:T(8,128)(2,1)S(1)}, u32[]{:S(2)}, u32[]{:S(2)}) collective-permute-start(bf16[2,128,128]{2,1,0:T(8,128)(2,1)S(1)} %get-tuple-element.29), channel_id=1, source_target_pairs={{0,2},{1,3},{2,0},{3,1},{4,6},{5,7},{6,4},{7,5},{8,10},{9,11},{10,... | collective-permute-start | bytes 196616 | tf_op jit(solution)/shard_map/ppermute | solution.py:357
  219.3 8.9 %collective-permute-start.20 = (bf16[2,128,128]{2,1,0:T(8,128)(2,1)S(1)}, bf16[2,128,128]{2,1,0:T(8,128)(2,1)S(1)}, u32[]{:S(2)}, u32[]{:S(2)}) collective-permute-start(bf16[2,128,128]{2,1,0:T(8,128)(2,1)S(1)} %get-tuple-element.30), channel_id=1, source_target_pairs={{0,14},{2,12},{3,13},{4,10},{5,11},{6,8},{7,9},{8,6},{9,7},{10,4},... | collective-permute-start | bytes 196616 | tf_op jit(solution)/shard_map/ppermute | solution.py:357
  (12 other events, 14.3 us)

commit v4 on v1

--- a/solution.py
+++ b/solution.py
@@ -104,6 +104,7 @@
 OUTER = [0, 12, 2, 14, 1, 13, 3]
 FIRST = 5
 OUTER_FIRST = 4
+LATE = 5
 
 
 def outer_place(slot):
@@ -114,7 +115,7 @@
     return pltpu.CompilerParams(vmem_limit_bytes=limit * 1024 * 1024)
 
 
-def extrapolate_kernel(order, offsets, field, operator, *refs, sets, rows, blocks, parts, listed):
+def extrapolate_kernel(order, offsets, inner, field, operator, *refs, sets, rows, blocks, parts, listed, swap):
     stage, apart, lines, weights, field_sems, weight_sems = refs[-6:]
     outs = refs[:-6]
     sizes = [len(one) for one in sets]
@@ -183,9 +184,13 @@
             def _(out=out):
                 out[0] = result
         first += count
-
-
-def extrapolate_blocks(field, operator, offsets, sets, listed=False, limit=60):
+    if swap:
+        @pl.when(jnp.where(inner[0] > 0, step >= sizes[0], step < sizes[1]))
+        def _():
+            outs[-1][0] = result
+
+
+def extrapolate_blocks(field, operator, offsets, inner, sets, listed=False, swap=False, limit=60):
     rows, blocks, _, size = field.shape
     bands = offsets.shape[0]
     width = 2 * size
@@ -198,17 +203,23 @@
     flat = field.reshape(rows * blocks * 2, size)
 
     def out_spec(first, count):
-        return pl.BlockSpec((1, rows, width), lambda j, o, c: (jnp.clip(j - first, 0, count - 1), 0, 0))
-
+        return pl.BlockSpec((1, rows, width), lambda j, o, c, i: (jnp.clip(j - first, 0, count - 1), 0, 0))
+
+    def swap_place(j, o, c, i):
+        return jnp.clip(j - jnp.where(i[0] > 0, sizes[0], 0), 0, sizes[1] - 1), 0, 0
+
+    out_specs = [out_spec(*one) for one in zip(firsts, sizes)]
+    if swap:
+        out_specs.append(pl.BlockSpec((1, rows, width), swap_place))
     return pl.pallas_call(
         functools.partial(
-            extrapolate_kernel, sets=sets, rows=rows, blocks=blocks, parts=parts, listed=listed
+            extrapolate_kernel, sets=sets, rows=rows, blocks=blocks, parts=parts, listed=listed, swap=swap
         ),
         grid_spec=pltpu.PrefetchScalarGridSpec(
-            num_scalar_prefetch=2,
+            num_scalar_prefetch=3,
             grid=(count,),
             in_specs=[pl.BlockSpec(memory_space=pltpu.HBM)] * 2,
-            out_specs=[out_spec(*one) for one in zip(firsts, sizes)],
+            out_specs=out_specs,
             scratch_shapes=[
                 pltpu.VMEM((chunk * (2 * blocks + 1), size), jnp.float32),
                 pltpu.VMEM((count * bands if listed else blocks, rows, width), jnp.bfloat16),
@@ -218,11 +229,11 @@
                 pltpu.SemaphoreType.DMA((count,)),
             ],
         ),
-        out_shape=[jax.ShapeDtypeStruct((n, rows, width), jnp.bfloat16) for n in sizes],
+        out_shape=[jax.ShapeDtypeStruct((n, rows, width), jnp.bfloat16) for n in sizes + sizes[1:] * swap],
         compiler_params=params(limit),
         cost_estimate=SMALL,
         name="extrapolate",
-    )(order, offsets, flat, operator)
+    )(order, offsets, inner, flat, operator)
 
 
 def product_kernel(near_ids, far_ids, inner, near_in, near_out, far_in, far_out, near_data, far_data, out, turned, total):
@@ -328,7 +339,7 @@
             values.append(field)
         begins.append([(begin, is_inner) for (_, begin), is_inner in zip(parts, inners)])
     if before is not None:
-        specs.append(image_spec)
+        specs.append(pl.BlockSpec((1, 2, size, size), lambda j, o, u, i: (first + j, 0, 0, 0)))
         values.append(before)
     places = jnp.stack([shot for shot, _ in pieces])
     return pl.pallas_call(
@@ -383,7 +394,7 @@
     freq = lax.axis_index("freq")
     inner = ((shot == 1) | (shot == 2)).astype(jnp.int32)[None]
     offsets = band_offsets.T
-    make = functools.partial(extrapolate_blocks, operator=operator[0])
+    make = functools.partial(extrapolate_blocks, operator=operator[0], inner=inner)
     inward = ((0, 1), (3, 2))
     outward = ((1, 0), (2, 3))
     middle = ((1, 2), (2, 1))
@@ -394,20 +405,21 @@
     (r_head,) = make(receiver_field[0], offsets=offsets, sets=[INNER[:HEAD]], listed=True)
     r_1_head = hand(r_head, *inward)
     r_3_head = hand(r_head, *middle)
-    r_inner, r_outer = make(receiver_field[0], offsets=following(offsets, r_head), sets=[INNER[HEAD:], OUTER])
+    r_inner, r_outer, r_swap = make(
+        receiver_field[0], offsets=following(offsets, r_head), sets=[INNER[HEAD:], OUTER], swap=True
+    )
     r_3_in = hand(r_inner, *middle)
-    r_1_in = hand(r_inner, *inward)
-    r_1_out = hand(following(r_outer, far_data, r_3_head), *outward)
+    r_1 = hand(following(r_swap, far_data, r_3_head), *inward, *outward)
     s_inner, s_outer = make(
         source_field[0], offsets=following(offsets, r_outer, r_3_head, r_1_head), sets=[INNER, OUTER]
     )
     s_out = hand(s_outer, *outward)
     s_in = hand(s_inner, *inward)
-    forward_head = hand(following(r_1_head, r_3_in), *middle)
-    r_3_out = hand(r_outer, *ends)
-    forward = hand(following(r_1_in, r_1_out), *middle)
-    beyond_1 = hand(following(r_outer, s_out, forward_head)[:OUTER_FIRST], *beyond)
-    beyond_2 = hand(r_outer[OUTER_FIRST:], *beyond)
+    forward_head = hand(r_1_head, *middle)
+    r_3_out = hand(following(r_outer, r_3_in), *ends)
+    forward = hand(r_1[:len(INNER) - HEAD], *middle)
+    beyond_1 = hand(following(r_outer, s_out, forward_head)[:LATE], *beyond)
+    beyond_2 = hand(r_outer[LATE:], *beyond)
 
     ids = survey_tiles[:, 1]
     near_ids = lax.dynamic_slice_in_dim(ids, shot * tiles, tiles)
@@ -417,17 +429,18 @@
     )
     early = [
         (shot, [(r_head, 0), (r_inner, HEAD), (r_outer, 0)]),
-        (shot ^ 1, [(r_1_head, 0), (r_1_in, HEAD), (r_1_out, 0)]),
+        (shot ^ 1, [(r_1_head, 0), (r_1, HEAD), (r_1, 0)]),
         (shot ^ 3, [(r_3_head, 0), (r_3_in, HEAD), (r_3_out, 0)]),
     ]
     forwarded = [(forward_head, 0), (forward, HEAD)]
-    one = image_blocks(product, 0, FIRST, early, inner)
-    two = image_blocks(product, FIRST, len(INNER) - FIRST, early, inner)
-    one = image_blocks(product, 0, FIRST, [(shot ^ 2, forwarded + [(beyond_1, 0)])], inner, one)
-    two = image_blocks(
-        product, FIRST, len(INNER) - FIRST, [(shot ^ 2, forwarded + [(beyond_2, OUTER_FIRST)])], inner,
-        following(two, one),
-    )
+    image = image_blocks(product, 0, len(INNER), early, inner)
+    most = image_blocks(product, 0, LATE + 1, [(shot ^ 2, forwarded + [(beyond_1, 0)])], inner, image)
+    rest = image_blocks(
+        product, LATE + 1, len(INNER) - LATE - 1, [(shot ^ 2, forwarded + [(beyond_2, LATE)])], inner,
+        following(image, most),
+    )
+    one = most[:FIRST]
+    two = jnp.concatenate([most[FIRST:], rest])
     image = sum_images(one, two, shot, freq)
     total_freqs = source_field.shape[0] * lax.axis_size("freq")
     return image * (1.0 / math.sqrt(2.0 * NR * total_freqs))

time: 219 us -> 222 us (1.014)
  waiting for transfers between devices: 105 us -> 108 us
    ppermute x13 -> x12, waiting for transfers between devices: 97 us -> 101 us  [hand(): return lax.ppermute(value, 'shot', pairs)]
    ppermute x13 -> x12, starting transfers between devices: 31.4 us -> 29.3 us  [hand(): return lax.ppermute(value, 'shot', pairs)]
    pallas_call x4 -> x3, Pallas kernels: 15 us -> 13.3 us  [image_blocks(): pl.pallas_call(functools.partial(image_kernel, first=first, begins=begins...]
    unnamed x30 -> x38, local copies, waits for them, and re-layouts: 9.86 us -> 10.2 us
  transfers between devices with their start and end apart: 19 -> 18, of which waited for: 10 -> 10; matrix products, arithmetic and copies ran while one was open for 1% -> 2% of each run, Pallas kernels for 27% -> 26%
where the time goes in v4:
time: 222 us; the launch traced here: 221 us
  waiting for transfers between devices  108 us (49%)
  Pallas kernels  59.2 us (27%)
  starting transfers between devices  37.3 us (17%)
  local copies, waits for them, and re-layouts  13.6 us (6%)
    ppermute x12, waiting for transfers between devices, hand(): return lax.ppermute(value, 'shot', pairs)  101 us
    pallas_call x3, Pallas kernels, extrapolate_blocks(): pl.pallas_call(functools.partial(extrapolate_kernel, sets=sets, rows=rows...  31.8 us
    ppermute x12, starting transfers between devices, hand(): return lax.ppermute(value, 'shot', pairs)  29.3 us
    pallas_call x1, Pallas kernels, product_blocks(): pl.pallas_call(product_kernel, grid_spec=pltpu.PrefetchScalarGridSpec(num...  14.1 us
    pallas_call x3, Pallas kernels, image_blocks(): pl.pallas_call(functools.partial(image_kernel, first=first, begins=begins...  13.3 us
    unnamed x38, local copies, waits for them, and re-layouts  10.2 us
    ppermute x6, starting transfers between devices, send_sum(): lax.ppermute(value.astype(jnp.bfloat16), ('shot', 'freq'), pairs)  8 us
    ppermute x6, waiting for transfers between devices, send_sum(): lax.ppermute(value.astype(jnp.bfloat16), ('shot', 'freq'), pairs)  7.82 us
  transfers between devices with their start and end apart: 18, of which 10 were waited for; matrix products, arithmetic and copies ran while one was open for 2% of the time, Pallas kernels for 26%

profile of v4, /device:TPU:0, one launch (start us, length us, event | category | flops | bytes accessed | tf_op | source)
XLA Modules:
  0.0 220.9 jit_solution(1878460256888959580)
XLA Ops:
  0.0 3.0 %collective-permute-start.4 = (bf16[16,2,128,128]{3,2,1,0:T(8,128)(2,1)}, bf16[16,2,128,128]{3,2,1,0:T(8,128)(2,1)S(1)}, u32[]{:S(2)}, u32[]{:S(2)}) collective-permute-start(bf16[16,2,128,128]{3,2,1,0:T(8,128)(2,1)} %bitcast.28), channel_id=1, source_target_pairs={{0,4},{12,8},{4,0},{8,12},{1,5},{13,9},{5,1},{9,13},{2,6},{14,10},... | collective-permute-start | bytes 3145736 | tf_op jit(solution)/shard_map/ppermute | solution.py:362
  3.0 5.5 %extrapolate.3.refs_3_ = bf16[3,512,256]{2,1,0:T(8,128)(2,1)} custom-call(s32[3]{0:T(128)} %constant.38.clone.order, s32[3,16]{1,0:T(4,128)} %bitcast.36, s32[1]{0:T(128)} %bitcast.1.inner, bf16[16384,128]{1,0:T(8,128)(2,1)} %bitcast.33, bf16[16,3,2,128,128]{4,3,2,1,0:T(8,128)(2,1)} %bitcast.30), custom_call_target="tpu_custom_call" | custom-call | flops 1000 | bytes 1000 | tf_op jit(solution)/shard_map/extrapolate/pallas_call | solution.py:214
  9.2 7.2 %collective-permute-start.1 = (bf16[3,512,256]{2,1,0:T(8,128)(2,1)}, bf16[3,512,256]{2,1,0:T(8,128)(2,1)}, u32[]{:S(2)}, u32[]{:S(2)}) collective-permute-start(bf16[3,512,256]{2,1,0:T(8,128)(2,1)} %extrapolate.3.refs_3_), channel_id=1, source_target_pairs={{0,4},{12,8},{1,5},{13,9},{2,6},{14,10},{3,7},{15,11},{16,20},{28,... | collective-permute-start | bytes 2359304 | tf_op jit(solution)/shard_map/ppermute | solution.py:362
  16.4 12.6 %extrapolate.4 = (bf16[6,512,256]{2,1,0:T(8,128)(2,1)}, bf16[7,512,256]{2,1,0:T(8,128)(2,1)}, bf16[7,512,256]{2,1,0:T(8,128)(2,1)}) custom-call(s32[13]{0:T(128)} %constant.39.clone.order, s32[3,16]{1,0:T(4,128)} %bitcast.37, s32[1]{0:T(128)} %bitcast.1.inner, bf16[16384,128]{1,0:T(8,128)(2,1)} %bitcast.34, bf16[16,3,2,128,128]{4,3,2,1,0:T(8,128)(2,1)} %bitcast.31), custom_call_target="tpu_custom_call" | custom-call | flops 1000 | bytes 1000 | tf_op jit(solution)/shard_map/extrapolate/pallas_call | solution.py:214
  31.6 1.6 collective-permute-start.6
  33.2 10.5 %collective-permute-done.1.refs_6_ = bf16[3,512,256]{2,1,0:T(8,128)(2,1)} collective-permute-done((bf16[3,512,256]{2,1,0:T(8,128)(2,1)}, bf16[3,512,256]{2,1,0:T(8,128)(2,1)}, u32[]{:S(2)}, u32[]{:S(2)}) %collective-permute-start.1) | collective-permute-done | bytes 786464 | tf_op jit(solution)/shard_map/ppermute | solution.py:362
  43.8 13.8 %extrapolate.5 = (bf16[9,512,256]{2,1,0:T(8,128)(2,1)}, bf16[7,512,256]{2,1,0:T(8,128)(2,1)}) custom-call(s32[16]{0:T(128)} %constant.40.clone.order, s32[3,16]{1,0:T(4,128)} %bitcast.38, s32[1]{0:T(128)} %bitcast.1.inner, bf16[16384,128]{1,0:T(8,128)(2,1)} %bitcast.35, bf16[16,3,2,128,128]{4,3,2,1,0:T(8,128)(2,1)} %bitcast.32), custom_call_target="tpu_custom_call" | custom-call | flops 1000 | bytes 1000 | tf_op jit(solution)/shard_map/extrapolate/pallas_call | solution.py:214
  57.6 1.4 collective-permute-start.3
  59.0 6.1 %collective-permute-start.2 = (bf16[9,512,256]{2,1,0:T(8,128)(2,1)}, bf16[9,512,256]{2,1,0:T(8,128)(2,1)}, u32[]{:S(2)}, u32[]{:S(2)}) collective-permute-start(bf16[9,512,256]{2,1,0:T(8,128)(2,1)} %get-tuple-element.19.near_in), channel_id=1, source_target_pairs={{0,4},{12,8},{1,5},{13,9},{2,6},{14,10},{3,7},{15,11},{16,20},{28,... | collective-permute-start | bytes 7077896 | tf_op jit(solution)/shard_map/ppermute | solution.py:362
  67.0 4.4 %collective-permute-start.10 = (bf16[7,512,256]{2,1,0:T(8,128)(2,1)}, bf16[7,512,256]{2,1,0:T(8,128)(2,1)}, u32[]{:S(2)}, u32[]{:S(2)}) collective-permute-start(bf16[7,512,256]{2,1,0:T(8,128)(2,1)} %get-tuple-element.25.refs_5_), channel_id=1, source_target_pairs={{0,12},{12,0},{1,13},{13,1},{2,14},{14,2},{3,15},{15,3},{16,28},{2... | collective-permute-start | bytes 5505032 | tf_op jit(solution)/shard_map/ppermute | solution.py:362
  71.3 11.7 %collective-permute-done.6.refs_7_.refs_8_ = bf16[7,512,256]{2,1,0:T(8,128)(2,1)S(1)} collective-permute-done((bf16[7,512,256]{2,1,0:T(8,128)(2,1)}, bf16[7,512,256]{2,1,0:T(8,128)(2,1)S(1)}, u32[]{:S(2)}, u32[]{:S(2)}) %collective-permute-start.6) | collective-permute-done | bytes 1835040 | tf_op jit(solution)/shard_map/ppermute | solution.py:362
  83.1 1.3 slice.54
  85.2 26.8 %collective-permute-done.3.far_out = bf16[7,512,256]{2,1,0:T(8,128)(2,1)S(1)} collective-permute-done((bf16[7,512,256]{2,1,0:T(8,128)(2,1)}, bf16[7,512,256]{2,1,0:T(8,128)(2,1)S(1)}, u32[]{:S(2)}, u32[]{:S(2)}) %collective-permute-start.3) | collective-permute-done | bytes 1835040 | tf_op jit(solution)/shard_map/ppermute | solution.py:362
  112.1 1.2 slice.45
  113.3 1.3 collective-permute-start.8
  115.5 1.3 collective-permute-start.11
  117.0 16.6 %collective-permute-done.2.far_in = bf16[9,512,256]{2,1,0:T(8,128)(2,1)} collective-permute-done((bf16[9,512,256]{2,1,0:T(8,128)(2,1)}, bf16[9,512,256]{2,1,0:T(8,128)(2,1)}, u32[]{:S(2)}, u32[]{:S(2)}) %collective-permute-start.2) | collective-permute-done | bytes 2359328 | tf_op jit(solution)/shard_map/ppermute | solution.py:362
  133.6 1.7 copy-done.5
  135.3 1.5 copy-done.6
  136.8 1.5 copy-done.8
  140.8 14.1 %product.1.refs_0_.refs_1_.refs_2_ = bf16[9,256,2048]{2,1,0:T(8,128)(2,1)S(1)} custom-call(s32[16]{0:T(128)S(1)} %get-tuple-element.30.near_ids, s32[16]{0:T(128)S(1)} %get-tuple-element.29.far_ids, s32[1]{0:T(128)} %bitcast.1.inner, bf16[9,512,256]{2,1,0:T(8,128)(2,1)S(1)} %copy-done.5, bf16[7,512,256]{2,1,0:T(8,128)(2,1)S(1)} %copy-done.6, ...), custom_call_target="tpu_custom_call" | custom-call | flops 1000 | bytes 1000 | tf_op jit(solution)/shard_map/product/pallas_call | solution.py:284
  154.9 20.0 %collective-permute-done.10.refs_11_ = bf16[7,512,256]{2,1,0:T(8,128)(2,1)} collective-permute-done((bf16[7,512,256]{2,1,0:T(8,128)(2,1)}, bf16[7,512,256]{2,1,0:T(8,128)(2,1)}, u32[]{:S(2)}, u32[]{:S(2)}) %collective-permute-start.10) | collective-permute-done | bytes 1835040 | tf_op jit(solution)/shard_map/ppermute | solution.py:362
  174.9 7.5 %image.3.refs_4_ = f32[9,2,128,128]{3,2,1,0:T(8,128)S(1)} custom-call(s32[3]{0:T(128)S(1)} %pad_add_fusion.places.unused, s32[3]{0:T(128)S(1)} %pad_add_fusion.places.unused, s32[1]{0:T(128)} %bitcast.1.inner, bf16[9,256,2048]{2,1,0:T(8,128)(2,1)S(1)} %product.1.refs_0_.refs_1_.refs_2_, bf16[9,256,2048]{2,1,0:T(8,128)(2,1)S(1)} %product.1.refs_0_.refs_1_.refs_2_, ...), custom_call_target="tpu_custom_call" | custom-call | flops 1000 | bytes 1000 | tf_op jit(solution)/shard_map/image/pallas_call | solution.py:345
  182.4 10.9 %collective-permute-done.8.refs_3_ = bf16[5,512,256]{2,1,0:T(8,128)(2,1)} collective-permute-done((bf16[5,512,256]{2,1,0:T(8,128)(2,1)}, bf16[5,512,256]{2,1,0:T(8,128)(2,1)}, u32[]{:S(2)}, u32[]{:S(2)}) %collective-permute-start.8) | collective-permute-done | bytes 1310752 | tf_op jit(solution)/shard_map/ppermute | solution.py:362
  193.2 4.0 %image.4 = f32[6,2,128,128]{3,2,1,0:T(8,128)S(1)} custom-call(s32[1]{0:T(128)} %bitcast.places.unused, s32[1]{0:T(128)} %bitcast.places.unused, s32[1]{0:T(128)} %bitcast.1.inner, bf16[9,256,2048]{2,1,0:T(8,128)(2,1)S(1)} %product.1.refs_0_.refs_1_.refs_2_, bf16[3,512,256]{2,1,0:T(8,128)(2,1)S(1)} %copy-done.3, ...), custom_call_target="tpu_custom_call" | custom-call | flops 1000 | bytes 1000 | tf_op jit(solution)/shard_map/image/pallas_call | solution.py:345
  197.3 4.0 %collective-permute-done.11.refs_3_ = bf16[2,512,256]{2,1,0:T(8,128)(2,1)} collective-permute-done((bf16[2,512,256]{2,1,0:T(8,128)(2,1)}, bf16[2,512,256]{2,1,0:T(8,128)(2,1)}, u32[]{:S(2)}, u32[]{:S(2)}) %collective-permute-start.11) | collective-permute-done | bytes 524320 | tf_op jit(solution)/shard_map/ppermute | solution.py:362
  201.2 1.8 image.5
  203.2 1.6 collective-permute-done.12
  206.6 1.6 collective-permute-start.16
  209.5 2.7 %collective-permute-done.16 = bf16[2,2,128,128]{3,2,1,0:T(8,128)(2,1)S(1)} collective-permute-done((bf16[2,2,128,128]{3,2,1,0:T(8,128)(2,1)S(1)}, bf16[2,2,128,128]{3,2,1,0:T(8,128)(2,1)S(1)}, u32[]{:S(2)}, u32[]{:S(2)}) %collective-permute-start.16) | collective-permute-done | bytes 131104 | tf_op jit(solution)/shard_map/ppermute | solution.py:367
  212.2 4.4 %collective-permute-start.17 = (bf16[2,128,128]{2,1,0:T(8,128)(2,1)S(1)}, bf16[2,128,128]{2,1,0:T(8,128)(2,1)S(1)}, u32[]{:S(2)}, u32[]{:S(2)}) collective-permute-start(bf16[2,128,128]{2,1,0:T(8,128)(2,1)S(1)} %fusion.3), channel_id=1, source_target_pairs={{0,12},{1,13},{2,14},{4,8},{5,9},{6,10},{7,11},{8,4},{9,5},{10,6},... | collective-permute-start | bytes 196616 | tf_op jit(solution)/shard_map/ppermute | solution.py:367
  216.7 3.5 %collective-permute-done.17 = bf16[2,128,128]{2,1,0:T(8,128)(2,1)S(1)} collective-permute-done((bf16[2,128,128]{2,1,0:T(8,128)(2,1)S(1)}, bf16[2,128,128]{2,1,0:T(8,128)(2,1)S(1)}, u32[]{:S(2)}, u32[]{:S(2)}) %collective-permute-start.17) | collective-permute-done | bytes 65568 | tf_op jit(solution)/shard_map/ppermute | solution.py:367
  (64 shorter events, 13.6 us)
Async XLA Ops:
  0.0 30.6 %collective-permute-start.4 = (bf16[16,2,128,128]{3,2,1,0:T(8,128)(2,1)}, bf16[16,2,128,128]{3,2,1,0:T(8,128)(2,1)S(1)}, u32[]{:S(2)}, u32[]{:S(2)}) collective-permute-start(bf16[16,2,128,128]{3,2,1,0:T(8,128)(2,1)} %bitcast.28), channel_id=1, source_target_pairs={{0,4},{12,8},{4,0},{8,12},{1,5},{13,9},{5,1},{9,13},{2,6},{14,10},... | collective-permute-start | bytes 3145736 | tf_op jit(solution)/shard_map/ppermute | solution.py:362
  8.5 21.2 %collective-permute-start = (bf16[3,512,256]{2,1,0:T(8,128)(2,1)}, bf16[3,512,256]{2,1,0:T(8,128)(2,1)S(1)}, u32[]{:S(2)}, u32[]{:S(2)}) collective-permute-start(bf16[3,512,256]{2,1,0:T(8,128)(2,1)} %extrapolate.3.refs_3_), channel_id=1, source_target_pairs={{4,8},{8,4},{5,9},{9,5},{6,10},{10,6},{7,11},{11,7},{20,24},{24,20... | collective-permute-start | bytes 2359304 | tf_op jit(solution)/shard_map/ppermute | solution.py:362
  9.2 34.5 %collective-permute-start.1 = (bf16[3,512,256]{2,1,0:T(8,128)(2,1)}, bf16[3,512,256]{2,1,0:T(8,128)(2,1)}, u32[]{:S(2)}, u32[]{:S(2)}) collective-permute-start(bf16[3,512,256]{2,1,0:T(8,128)(2,1)} %extrapolate.3.refs_3_), channel_id=1, source_target_pairs={{0,4},{12,8},{1,5},{13,9},{2,6},{14,10},{3,7},{15,11},{16,20},{28,... | collective-permute-start | bytes 2359304 | tf_op jit(solution)/shard_map/ppermute | solution.py:362
  29.0 36.8 %collective-permute-start.9 = (bf16[6,512,256]{2,1,0:T(8,128)(2,1)}, bf16[6,512,256]{2,1,0:T(8,128)(2,1)S(1)}, u32[]{:S(2)}, u32[]{:S(2)}) collective-permute-start(bf16[6,512,256]{2,1,0:T(8,128)(2,1)} %get-tuple-element.24.refs_4_), channel_id=1, source_target_pairs={{4,8},{8,4},{5,9},{9,5},{6,10},{10,6},{7,11},{11,7},{20,24},{24,20... | collective-permute-start | bytes 4718600 | tf_op jit(solution)/shard_map/ppermute | solution.py:362
  31.6 51.5 %collective-permute-start.6 = (bf16[7,512,256]{2,1,0:T(8,128)(2,1)}, bf16[7,512,256]{2,1,0:T(8,128)(2,1)S(1)}, u32[]{:S(2)}, u32[]{:S(2)}) collective-permute-start(bf16[7,512,256]{2,1,0:T(8,128)(2,1)} %get-tuple-element.22), channel_id=1, source_target_pairs={{0,4},{12,8},{4,0},{8,12},{1,5},{13,9},{5,1},{9,13},{2,6},{14,10},... | collective-permute-start | bytes 5505032 | tf_op jit(solution)/shard_map/ppermute | solution.py:362
  57.6 54.5 %copy-start = (bf16[7,512,256]{2,1,0:T(8,128)(2,1)S(1)}, bf16[7,512,256]{2,1,0:T(8,128)(2,1)}, u32[]{:S(2)}) copy-start(bf16[7,512,256]{2,1,0:T(8,128)(2,1)} %get-tuple-element.25.refs_5_) | copy-start | bytes 5505028
  57.6 54.5 %collective-permute-start.3 = (bf16[7,512,256]{2,1,0:T(8,128)(2,1)}, bf16[7,512,256]{2,1,0:T(8,128)(2,1)S(1)}, u32[]{:S(2)}, u32[]{:S(2)}) collective-permute-start(bf16[7,512,256]{2,1,0:T(8,128)(2,1)} %get-tuple-element.20.near_out), channel_id=1, source_target_pairs={{4,0},{8,12},{5,1},{9,13},{6,2},{10,14},{7,3},{11,15},{20,16},{24,... | collective-permute-start | bytes 5505032 | tf_op jit(solution)/shard_map/ppermute | solution.py:362
  59.0 74.6 %collective-permute-start.2 = (bf16[9,512,256]{2,1,0:T(8,128)(2,1)}, bf16[9,512,256]{2,1,0:T(8,128)(2,1)}, u32[]{:S(2)}, u32[]{:S(2)}) collective-permute-start(bf16[9,512,256]{2,1,0:T(8,128)(2,1)} %get-tuple-element.19.near_in), channel_id=1, source_target_pairs={{0,4},{12,8},{1,5},{13,9},{2,6},{14,10},{3,7},{15,11},{16,20},{28,... | collective-permute-start | bytes 7077896 | tf_op jit(solution)/shard_map/ppermute | solution.py:362
  65.1 20.1 %collective-permute-start.5 = (bf16[3,512,256]{2,1,0:T(8,128)(2,1)}, bf16[3,512,256]{2,1,0:T(8,128)(2,1)S(1)}, u32[]{:S(2)}, u32[]{:S(2)}) collective-permute-start(bf16[3,512,256]{2,1,0:T(8,128)(2,1)} %collective-permute-done.1.refs_6_), channel_id=1, source_target_pairs={{4,8},{8,4},{5,9},{9,5},{6,10},{10,6},{7,11},{11,7},{20,24},{24,20... | collective-permute-start | bytes 2359304 | tf_op jit(solution)/shard_map/ppermute | solution.py:362
  67.0 107.9 %collective-permute-start.10 = (bf16[7,512,256]{2,1,0:T(8,128)(2,1)}, bf16[7,512,256]{2,1,0:T(8,128)(2,1)}, u32[]{:S(2)}, u32[]{:S(2)}) collective-permute-start(bf16[7,512,256]{2,1,0:T(8,128)(2,1)} %get-tuple-element.25.refs_5_), channel_id=1, source_target_pairs={{0,12},{12,0},{1,13},{13,1},{2,14},{14,2},{3,15},{15,3},{16,28},{2... | collective-permute-start | bytes 5505032 | tf_op jit(solution)/shard_map/ppermute | solution.py:362
  84.3 32.5 %copy-start.18 = (s32[64,2]{0,1:T(2,128)S(1)}, s32[64,2]{0,1:T(2,128)}, u32[]{:S(2)}) copy-start(s32[64,2]{0,1:T(2,128)} %param.13) | copy-start | bytes 1540
  84.3 108.9 %collective-permute-start.7 = (bf16[6,512,256]{2,1,0:T(8,128)(2,1)}, bf16[6,512,256]{2,1,0:T(8,128)(2,1)S(1)}, u32[]{:S(2)}, u32[]{:S(2)}) collective-permute-start(bf16[6,512,256]{2,1,0:T(8,128)(2,1)} %slice.54), channel_id=1, source_target_pairs={{4,8},{8,4},{5,9},{9,5},{6,10},{10,6},{7,11},{11,7},{20,24},{24,20... | collective-permute-start | bytes 4718600 | tf_op jit(solution)/shard_map/ppermute | solution.py:362
  85.2 30.3 %copy-start.2 = (bf16[3,512,256]{2,1,0:T(8,128)(2,1)}, bf16[3,512,256]{2,1,0:T(8,128)(2,1)S(1)}, u32[]{:S(2)}) copy-start(bf16[3,512,256]{2,1,0:T(8,128)(2,1)S(1)} %collective-permute-done.5.refs_1_) | copy-start | bytes 2359300
  112.1 3.4 %copy-start.7 = (bf16[7,512,256]{2,1,0:T(8,128)(2,1)}, bf16[7,512,256]{2,1,0:T(8,128)(2,1)S(1)}, u32[]{:S(2)}) copy-start(bf16[7,512,256]{2,1,0:T(8,128)(2,1)S(1)} %collective-permute-done.3.far_out) | copy-start | bytes 5505028
  113.3 79.9 %collective-permute-start.8 = (bf16[5,512,256]{2,1,0:T(8,128)(2,1)}, bf16[5,512,256]{2,1,0:T(8,128)(2,1)}, u32[]{:S(2)}, u32[]{:S(2)}) collective-permute-start(bf16[5,512,256]{2,1,0:T(8,128)(2,1)} %slice.45), channel_id=1, source_target_pairs={{4,12},{8,0},{5,13},{9,1},{6,14},{10,2},{7,15},{11,3},{20,28},{24,... | collective-permute-start | bytes 3932168 | tf_op jit(solution)/shard_map/ppermute | solution.py:362
  115.5 85.7 %collective-permute-start.11 = (bf16[2,512,256]{2,1,0:T(8,128)(2,1)}, bf16[2,512,256]{2,1,0:T(8,128)(2,1)}, u32[]{:S(2)}, u32[]{:S(2)}) collective-permute-start(bf16[2,512,256]{2,1,0:T(8,128)(2,1)} %slice.47), channel_id=1, source_target_pairs={{4,12},{8,0},{5,13},{9,1},{6,14},{10,2},{7,15},{11,3},{20,28},{24,... | collective-permute-start | bytes 1572872 | tf_op jit(solution)/shard_map/ppermute | solution.py:362
  133.6 1.7 copy-start.5
  135.3 1.5 copy-start.6
  136.8 1.5 copy-start.8
  140.8 34.1 %copy-start.1 = (bf16[7,512,256]{2,1,0:T(8,128)(2,1)S(1)}, bf16[7,512,256]{2,1,0:T(8,128)(2,1)}, u32[]{:S(2)}) copy-start(bf16[7,512,256]{2,1,0:T(8,128)(2,1)} %get-tuple-element.25.refs_5_) | copy-start | bytes 5505028
  140.8 34.1 %copy-start.4 = (bf16[3,512,256]{2,1,0:T(8,128)(2,1)S(1)}, bf16[3,512,256]{2,1,0:T(8,128)(2,1)}, u32[]{:S(2)}) copy-start(bf16[3,512,256]{2,1,0:T(8,128)(2,1)} %extrapolate.3.refs_3_) | copy-start | bytes 2359300
  140.8 34.1 %copy-start.9 = (bf16[6,512,256]{2,1,0:T(8,128)(2,1)S(1)}, bf16[6,512,256]{2,1,0:T(8,128)(2,1)}, u32[]{:S(2)}) copy-start(bf16[6,512,256]{2,1,0:T(8,128)(2,1)} %get-tuple-element.24.refs_4_) | copy-start | bytes 4718596
  140.8 34.1 %copy-start.11 = (bf16[6,512,256]{2,1,0:T(8,128)(2,1)S(1)}, bf16[6,512,256]{2,1,0:T(8,128)(2,1)}, u32[]{:S(2)}) copy-start(bf16[6,512,256]{2,1,0:T(8,128)(2,1)} %copy-done.10) | copy-start | bytes 4718596
  140.8 34.1 %copy-start.16 = (bf16[3,512,256]{2,1,0:T(8,128)(2,1)S(1)}, bf16[3,512,256]{2,1,0:T(8,128)(2,1)}, u32[]{:S(2)}) copy-start(bf16[3,512,256]{2,1,0:T(8,128)(2,1)} %copy-done.15) | copy-start | bytes 2359300
  154.9 38.4 %copy-start.3 = (bf16[3,512,256]{2,1,0:T(8,128)(2,1)S(1)}, bf16[3,512,256]{2,1,0:T(8,128)(2,1)}, u32[]{:S(2)}) copy-start(bf16[3,512,256]{2,1,0:T(8,128)(2,1)} %copy-done.2) | copy-start | bytes 2359300
  197.3 5.8 %copy-start.17 = (f32[1,2,128,128]{3,2,1,0:T(8,128)}, f32[1,2,128,128]{3,2,1,0:T(8,128)S(1)}, u32[]{:S(2)}) copy-start(f32[1,2,128,128]{3,2,1,0:T(8,128)S(1)} %get-tuple-element.28) | copy-start | bytes 393220
  203.1 1.7 collective-permute-start.12
  205.9 2.3 %collective-permute-start.13 = (bf16[2,128,128]{2,1,0:T(8,128)(2,1)S(1)}, bf16[2,128,128]{2,1,0:T(8,128)(2,1)S(1)}, u32[]{:S(2)}, u32[]{:S(2)}) collective-permute-start(bf16[2,128,128]{2,1,0:T(8,128)(2,1)S(1)} %fusion.2), channel_id=1, source_target_pairs={{5,7},{9,11},{21,23},{25,27}} | collective-permute-start | bytes 196616 | tf_op jit(solution)/shard_map/ppermute | solution.py:367
  206.6 5.6 %collective-permute-start.16 = (bf16[2,2,128,128]{3,2,1,0:T(8,128)(2,1)S(1)}, bf16[2,2,128,128]{3,2,1,0:T(8,128)(2,1)S(1)}, u32[]{:S(2)}, u32[]{:S(2)}) collective-permute-start(bf16[2,2,128,128]{3,2,1,0:T(8,128)(2,1)S(1)} %select_convert_fusion.1), channel_id=1, source_target_pairs={{0,2},{1,3},{2,0},{3,1},{4,6},{5,7},{6,4},{7,5},{8,10},{9,11},{10,... | collective-permute-start | bytes 393224 | tf_op jit(solution)/shard_map/ppermute | solution.py:367
  208.1 8.5 %collective-permute-start.14 = (bf16[2,128,128]{2,1,0:T(8,128)(2,1)S(1)}, bf16[2,128,128]{2,1,0:T(8,128)(2,1)S(1)}, u32[]{:S(2)}, u32[]{:S(2)}) collective-permute-start(bf16[2,128,128]{2,1,0:T(8,128)(2,1)S(1)} %add_convert_fusion), channel_id=1, source_target_pairs={{7,15},{23,31}} | collective-permute-start | bytes 196616 | tf_op jit(solution)/shard_map/ppermute | solution.py:367
  208.8 7.8 %collective-permute-start.15 = (bf16[2,128,128]{2,1,0:T(8,128)(2,1)S(1)}, bf16[2,128,128]{2,1,0:T(8,128)(2,1)S(1)}, u32[]{:S(2)}, u32[]{:S(2)}) collective-permute-start(bf16[2,128,128]{2,1,0:T(8,128)(2,1)S(1)} %add_convert_fusion), channel_id=1, source_target_pairs={{11,15},{27,31}} | collective-permute-start | bytes 196616 | tf_op jit(solution)/shard_map/ppermute | solution.py:367
  212.2 8.0 %collective-permute-start.17 = (bf16[2,128,128]{2,1,0:T(8,128)(2,1)S(1)}, bf16[2,128,128]{2,1,0:T(8,128)(2,1)S(1)}, u32[]{:S(2)}, u32[]{:S(2)}) collective-permute-start(bf16[2,128,128]{2,1,0:T(8,128)(2,1)S(1)} %fusion.3), channel_id=1, source_target_pairs={{0,12},{1,13},{2,14},{4,8},{5,9},{6,10},{7,11},{8,4},{9,5},{10,6},... | collective-permute-start | bytes 196616 | tf_op jit(solution)/shard_map/ppermute | solution.py:367
  (5 other events, 5.5 us)

commit v5 on v4

--- a/solution.py
+++ b/solution.py
@@ -105,6 +105,7 @@
 FIRST = 5
 OUTER_FIRST = 4
 LATE = 5
+SWAP = len(INNER) - HEAD
 
 
 def outer_place(slot):
@@ -185,7 +186,7 @@
                 out[0] = result
         first += count
     if swap:
-        @pl.when(jnp.where(inner[0] > 0, step >= sizes[0], step < sizes[1]))
+        @pl.when(jnp.where(inner[0] > 0, (step >= sizes[0]) & (step < 2 * sizes[0]), step < sizes[0]))
         def _():
             outs[-1][0] = result
 
@@ -206,7 +207,7 @@
         return pl.BlockSpec((1, rows, width), lambda j, o, c, i: (jnp.clip(j - first, 0, count - 1), 0, 0))
 
     def swap_place(j, o, c, i):
-        return jnp.clip(j - jnp.where(i[0] > 0, sizes[0], 0), 0, sizes[1] - 1), 0, 0
+        return jnp.clip(j - jnp.where(i[0] > 0, sizes[0], 0), 0, sizes[0] - 1), 0, 0
 
     out_specs = [out_spec(*one) for one in zip(firsts, sizes)]
     if swap:
@@ -229,7 +230,7 @@
                 pltpu.SemaphoreType.DMA((count,)),
             ],
         ),
-        out_shape=[jax.ShapeDtypeStruct((n, rows, width), jnp.bfloat16) for n in sizes + sizes[1:] * swap],
+        out_shape=[jax.ShapeDtypeStruct((n, rows, width), jnp.bfloat16) for n in sizes + sizes[:1] * swap],
         compiler_params=params(limit),
         cost_estimate=SMALL,
         name="extrapolate",
@@ -309,8 +310,8 @@
     for n, piece in enumerate(begins):
         field = parts[0][0]
         for part, (begin, is_inner) in zip(parts[1:], piece[1:]):
-            chosen = (inner[0] > 0) & (slot >= begin) if is_inner else inner[0] == 0
-            field = jnp.where(chosen, part[0], field)
+            place = slot if is_inner else outer_place(slot)
+            field = jnp.where(((inner[0] > 0) == is_inner) & (place >= begin), part[0], field)
         parts = parts[len(piece):]
         term = jnp.dot(refs[n][0], field, preferred_element_type=jnp.float32)
         both = term if both is None else both + term
@@ -333,11 +334,10 @@
     values = [product] * len(pieces)
     begins = []
     for _, parts in pieces:
-        inners = [True] * (len(parts) - 1) + [False]
-        for (field, begin), is_inner in zip(parts, inners):
+        for field, begin, is_inner in parts:
             specs.append(part_spec((1, rows, width), first, begin, field.shape[0], is_inner))
             values.append(field)
-        begins.append([(begin, is_inner) for (_, begin), is_inner in zip(parts, inners)])
+        begins.append([(begin, is_inner) for _, begin, is_inner in parts])
     if before is not None:
         specs.append(pl.BlockSpec((1, 2, size, size), lambda j, o, u, i: (first + j, 0, 0, 0)))
         values.append(before)
@@ -416,10 +416,11 @@
     s_out = hand(s_outer, *outward)
     s_in = hand(s_inner, *inward)
     forward_head = hand(r_1_head, *middle)
-    r_3_out = hand(following(r_outer, r_3_in), *ends)
-    forward = hand(r_1[:len(INNER) - HEAD], *middle)
+    r_3_out = hand(following(r_outer, r_3_in, r_1), *ends)
+    r_1_rest = hand(r_outer[SWAP:], *outward)
+    forward = hand(r_1, *middle)
     beyond_1 = hand(following(r_outer, s_out, forward_head)[:LATE], *beyond)
-    beyond_2 = hand(r_outer[LATE:], *beyond)
+    beyond_2 = hand(following(r_outer, r_1_rest)[LATE:], *beyond)
 
     ids = survey_tiles[:, 1]
     near_ids = lax.dynamic_slice_in_dim(ids, shot * tiles, tiles)
@@ -428,15 +429,15 @@
         s_inner, s_outer, s_in, s_out, survey_data[0], far_data, near_ids, far_ids, inner
     )
     early = [
-        (shot, [(r_head, 0), (r_inner, HEAD), (r_outer, 0)]),
-        (shot ^ 1, [(r_1_head, 0), (r_1, HEAD), (r_1, 0)]),
-        (shot ^ 3, [(r_3_head, 0), (r_3_in, HEAD), (r_3_out, 0)]),
+        (shot, [(r_head, 0, True), (r_inner, HEAD, True), (r_outer, 0, False)]),
+        (shot ^ 1, [(r_1_head, 0, True), (r_1, HEAD, True), (r_1, 0, False), (r_1_rest, SWAP, False)]),
+        (shot ^ 3, [(r_3_head, 0, True), (r_3_in, HEAD, True), (r_3_out, 0, False)]),
     ]
-    forwarded = [(forward_head, 0), (forward, HEAD)]
+    forwarded = [(forward_head, 0, True), (forward, HEAD, True)]
     image = image_blocks(product, 0, len(INNER), early, inner)
-    most = image_blocks(product, 0, LATE + 1, [(shot ^ 2, forwarded + [(beyond_1, 0)])], inner, image)
+    most = image_blocks(product, 0, LATE + 1, [(shot ^ 2, forwarded + [(beyond_1, 0, False)])], inner, image)
     rest = image_blocks(
-        product, LATE + 1, len(INNER) - LATE - 1, [(shot ^ 2, forwarded + [(beyond_2, LATE)])], inner,
+        product, LATE + 1, len(INNER) - LATE - 1, [(shot ^ 2, forwarded + [(beyond_2, LATE, False)])], inner,
         following(image, most),
     )
     one = most[:FIRST]

time: 222 us -> 244 us (1.099)
  waiting for transfers between devices: 108 us -> 125 us
  starting transfers between devices: 37.3 us -> 40.1 us
    ppermute x12 -> x13, waiting for transfers between devices: 101 us -> 118 us  [hand(): return lax.ppermute(value, 'shot', pairs)]
    unnamed x38, local copies, waits for them, and re-layouts: 10.2 us -> 12.8 us
    ppermute x12 -> x13, starting transfers between devices: 29.3 us -> 31.4 us  [hand(): return lax.ppermute(value, 'shot', pairs)]
  transfers between devices with their start and end apart: 18 -> 19, of which waited for: 10 -> 7; matrix products, arithmetic and copies ran while one was open for 2% -> 1% of each run, Pallas kernels for 26% -> 24%
where the time goes in v5:
time: 244 us; the launch traced here: 241 us
  waiting for transfers between devices  125 us (51%)
  Pallas kernels  59.7 us (24%)
  starting transfers between devices  40.1 us (16%)
  local copies, waits for them, and re-layouts  15 us (6%)
    ppermute x13, waiting for transfers between devices, hand(): return lax.ppermute(value, 'shot', pairs)  118 us
    pallas_call x3, Pallas kernels, extrapolate_blocks(): pl.pallas_call(functools.partial(extrapolate_kernel, sets=sets, rows=rows...  32 us
    ppermute x13, starting transfers between devices, hand(): return lax.ppermute(value, 'shot', pairs)  31.4 us
    pallas_call x1, Pallas kernels, product_blocks(): pl.pallas_call(product_kernel, grid_spec=pltpu.PrefetchScalarGridSpec(num...  14.1 us
    pallas_call x3, Pallas kernels, image_blocks(): pl.pallas_call(functools.partial(image_kernel, first=first, begins=begins...  13.7 us
    unnamed x38, local copies, waits for them, and re-layouts  12.8 us
    ppermute x6, starting transfers between devices, send_sum(): lax.ppermute(value.astype(jnp.bfloat16), ('shot', 'freq'), pairs)  8.69 us
    ppermute x6, waiting for transfers between devices, send_sum(): lax.ppermute(value.astype(jnp.bfloat16), ('shot', 'freq'), pairs)  7.13 us
  transfers between devices with their start and end apart: 19, of which 7 were waited for; matrix products, arithmetic and copies ran while one was open for 1% of the time, Pallas kernels for 24%

profile of v5, /device:TPU:0, one launch (start us, length us, event | category | flops | bytes accessed | tf_op | source)
XLA Modules:
  0.0 241.2 jit_solution(4590462347616621237)
XLA Ops:
  0.0 3.0 %collective-permute-start.4 = (bf16[16,2,128,128]{3,2,1,0:T(8,128)(2,1)}, bf16[16,2,128,128]{3,2,1,0:T(8,128)(2,1)S(1)}, u32[]{:S(2)}, u32[]{:S(2)}) collective-permute-start(bf16[16,2,128,128]{3,2,1,0:T(8,128)(2,1)} %bitcast.28), channel_id=1, source_target_pairs={{0,4},{12,8},{4,0},{8,12},{1,5},{13,9},{5,1},{9,13},{2,6},{14,10},... | collective-permute-start | bytes 3145736 | tf_op jit(solution)/shard_map/ppermute | solution.py:362
  3.0 5.5 %extrapolate.3.refs_3_ = bf16[3,512,256]{2,1,0:T(8,128)(2,1)} custom-call(s32[3]{0:T(128)} %constant.38.clone.order, s32[3,16]{1,0:T(4,128)} %bitcast.36, s32[1]{0:T(128)} %bitcast.1.inner, bf16[16384,128]{1,0:T(8,128)(2,1)} %bitcast.33, bf16[16,3,2,128,128]{4,3,2,1,0:T(8,128)(2,1)} %bitcast.30), custom_call_target="tpu_custom_call" | custom-call | flops 1000 | bytes 1000 | tf_op jit(solution)/shard_map/extrapolate/pallas_call | solution.py:215
  9.2 6.3 %collective-permute-start.1 = (bf16[3,512,256]{2,1,0:T(8,128)(2,1)}, bf16[3,512,256]{2,1,0:T(8,128)(2,1)S(1)}, u32[]{:S(2)}, u32[]{:S(2)}) collective-permute-start(bf16[3,512,256]{2,1,0:T(8,128)(2,1)} %extrapolate.3.refs_3_), channel_id=1, source_target_pairs={{0,4},{12,8},{1,5},{13,9},{2,6},{14,10},{3,7},{15,11},{16,20},{28,... | collective-permute-start | bytes 2359304 | tf_op jit(solution)/shard_map/ppermute | solution.py:362
  15.6 12.5 %extrapolate.4 = (bf16[6,512,256]{2,1,0:T(8,128)(2,1)}, bf16[7,512,256]{2,1,0:T(8,128)(2,1)}, bf16[6,512,256]{2,1,0:T(8,128)(2,1)}) custom-call(s32[13]{0:T(128)} %constant.39.clone.order, s32[3,16]{1,0:T(4,128)} %bitcast.37, s32[1]{0:T(128)} %bitcast.1.inner, bf16[16384,128]{1,0:T(8,128)(2,1)} %bitcast.34, bf16[16,3,2,128,128]{4,3,2,1,0:T(8,128)(2,1)} %bitcast.31), custom_call_target="tpu_custom_call" | custom-call | flops 1000 | bytes 1000 | tf_op jit(solution)/shard_map/extrapolate/pallas_call | solution.py:215
  28.1 1.8 collective-permute-start.10
  31.8 1.5 collective-permute-start.6
  33.2 10.5 %collective-permute-done.1.refs_6_ = bf16[3,512,256]{2,1,0:T(8,128)(2,1)S(1)} collective-permute-done((bf16[3,512,256]{2,1,0:T(8,128)(2,1)}, bf16[3,512,256]{2,1,0:T(8,128)(2,1)S(1)}, u32[]{:S(2)}, u32[]{:S(2)}) %collective-permute-start.1) | collective-permute-done | bytes 786464 | tf_op jit(solution)/shard_map/ppermute | solution.py:362
  44.6 13.9 %extrapolate.5 = (bf16[9,512,256]{2,1,0:T(8,128)(2,1)}, bf16[7,512,256]{2,1,0:T(8,128)(2,1)}) custom-call(s32[16]{0:T(128)} %constant.40.clone.order, s32[3,16]{1,0:T(4,128)} %bitcast.38, s32[1]{0:T(128)} %bitcast.1.inner, bf16[16384,128]{1,0:T(8,128)(2,1)} %bitcast.35, bf16[16,3,2,128,128]{4,3,2,1,0:T(8,128)(2,1)} %bitcast.32), custom_call_target="tpu_custom_call" | custom-call | flops 1000 | bytes 1000 | tf_op jit(solution)/shard_map/extrapolate/pallas_call | solution.py:215
  58.6 1.3 collective-permute-start.3
  59.9 6.1 %collective-permute-start.2 = (bf16[9,512,256]{2,1,0:T(8,128)(2,1)}, bf16[9,512,256]{2,1,0:T(8,128)(2,1)}, u32[]{:S(2)}, u32[]{:S(2)}) collective-permute-start(bf16[9,512,256]{2,1,0:T(8,128)(2,1)} %get-tuple-element.20.near_in), channel_id=1, source_target_pairs={{0,4},{12,8},{1,5},{13,9},{2,6},{14,10},{3,7},{15,11},{16,20},{28,... | collective-permute-start | bytes 7077896 | tf_op jit(solution)/shard_map/ppermute | solution.py:362
  66.7 10.8 %collective-permute-done.6.refs_7_.refs_8_ = bf16[6,512,256]{2,1,0:T(8,128)(2,1)S(1)} collective-permute-done((bf16[6,512,256]{2,1,0:T(8,128)(2,1)}, bf16[6,512,256]{2,1,0:T(8,128)(2,1)S(1)}, u32[]{:S(2)}, u32[]{:S(2)}) %collective-permute-start.6) | collective-permute-done | bytes 1572896 | tf_op jit(solution)/shard_map/ppermute | solution.py:362
  77.5 4.4 %collective-permute-start.11 = (bf16[7,512,256]{2,1,0:T(8,128)(2,1)S(1)}, bf16[7,512,256]{2,1,0:T(8,128)(2,1)}, u32[]{:S(2)}, u32[]{:S(2)}) collective-permute-start(bf16[7,512,256]{2,1,0:T(8,128)(2,1)S(1)} %copy-done), channel_id=1, source_target_pairs={{0,12},{12,0},{1,13},{13,1},{2,14},{14,2},{3,15},{15,3},{16,28},{2... | collective-permute-start | bytes 5505032 | tf_op jit(solution)/shard_map/ppermute | solution.py:362
  81.8 1.8 collective-permute-start.7
  84.6 22.0 %collective-permute-done.3.far_out = bf16[7,512,256]{2,1,0:T(8,128)(2,1)S(1)} collective-permute-done((bf16[7,512,256]{2,1,0:T(8,128)(2,1)}, bf16[7,512,256]{2,1,0:T(8,128)(2,1)S(1)}, u32[]{:S(2)}, u32[]{:S(2)}) %collective-permute-start.3) | collective-permute-done | bytes 1835040 | tf_op jit(solution)/shard_map/ppermute | solution.py:362
  106.6 1.3 copy-done.6
  109.1 1.3 collective-permute-start.8
  110.4 1.3 collective-permute-start.9
  111.7 74.5 %collective-permute-done.9.refs_9_ = bf16[1,512,256]{2,1,0:T(8,128)(2,1)S(1)} collective-permute-done((bf16[1,512,256]{2,1,0:T(8,128)(2,1)S(1)}, bf16[1,512,256]{2,1,0:T(8,128)(2,1)S(1)}, u32[]{:S(2)}, u32[]{:S(2)}) %collective-permute-start.9) | collective-permute-done | bytes 262176 | tf_op jit(solution)/shard_map/ppermute | solution.py:362
  187.8 1.3 collective-permute-start.12
  189.3 1.7 copy-done.4
  190.9 1.5 copy-done.5
  192.4 1.5 copy-done.7
  193.9 1.2 copy-done.9
  196.4 14.1 %product.1.refs_0_.refs_1_.refs_2_ = bf16[9,256,2048]{2,1,0:T(8,128)(2,1)S(1)} custom-call(s32[16]{0:T(128)S(1)} %get-tuple-element.32.near_ids, s32[16]{0:T(128)S(1)} %get-tuple-element.31.far_ids, s32[1]{0:T(128)} %bitcast.1.inner, bf16[9,512,256]{2,1,0:T(8,128)(2,1)S(1)} %copy-done.4, bf16[7,512,256]{2,1,0:T(8,128)(2,1)S(1)} %copy-done.5, ...), custom_call_target="tpu_custom_call" | custom-call | flops 1000 | bytes 1000 | tf_op jit(solution)/shard_map/product/pallas_call | solution.py:285
  210.6 7.5 %image.3.refs_4_ = f32[9,2,128,128]{3,2,1,0:T(8,128)S(1)} custom-call(s32[3]{0:T(128)S(1)} %pad_add_fusion.places.unused, s32[3]{0:T(128)S(1)} %pad_add_fusion.places.unused, s32[1]{0:T(128)} %bitcast.1.inner, bf16[9,256,2048]{2,1,0:T(8,128)(2,1)S(1)} %product.1.refs_0_.refs_1_.refs_2_, bf16[9,256,2048]{2,1,0:T(8,128)(2,1)S(1)} %product.1.refs_0_.refs_1_.refs_2_, ...), custom_call_target="tpu_custom_call" | custom-call | flops 1000 | bytes 1000 | tf_op jit(solution)/shard_map/image/pallas_call | solution.py:345
  218.1 4.2 %image.4 = f32[6,2,128,128]{3,2,1,0:T(8,128)S(1)} custom-call(s32[1]{0:T(128)} %bitcast.places.unused, s32[1]{0:T(128)} %bitcast.places.unused, s32[1]{0:T(128)} %bitcast.1.inner, bf16[9,256,2048]{2,1,0:T(8,128)(2,1)S(1)} %product.1.refs_0_.refs_1_.refs_2_, bf16[3,512,256]{2,1,0:T(8,128)(2,1)S(1)} %copy-done.2, ...), custom_call_target="tpu_custom_call" | custom-call | flops 1000 | bytes 1000 | tf_op jit(solution)/shard_map/image/pallas_call | solution.py:345
  222.3 2.0 image.5
  224.5 1.6 collective-permute-done.13
  226.9 1.5 collective-permute-start.17
  229.8 2.7 %collective-permute-done.17 = bf16[2,2,128,128]{3,2,1,0:T(8,128)(2,1)S(1)} collective-permute-done((bf16[2,2,128,128]{3,2,1,0:T(8,128)(2,1)S(1)}, bf16[2,2,128,128]{3,2,1,0:T(8,128)(2,1)S(1)}, u32[]{:S(2)}, u32[]{:S(2)}) %collective-permute-start.17) | collective-permute-done | bytes 131104 | tf_op jit(solution)/shard_map/ppermute | solution.py:367
  232.6 5.1 %collective-permute-start.18 = (bf16[2,128,128]{2,1,0:T(8,128)(2,1)S(1)}, bf16[2,128,128]{2,1,0:T(8,128)(2,1)S(1)}, u32[]{:S(2)}, u32[]{:S(2)}) collective-permute-start(bf16[2,128,128]{2,1,0:T(8,128)(2,1)S(1)} %fusion.3), channel_id=1, source_target_pairs={{0,12},{1,13},{2,14},{4,8},{5,9},{6,10},{7,11},{8,4},{9,5},{10,6},... | collective-permute-start | bytes 196616 | tf_op jit(solution)/shard_map/ppermute | solution.py:367
  237.7 2.8 %collective-permute-done.18 = bf16[2,128,128]{2,1,0:T(8,128)(2,1)S(1)} collective-permute-done((bf16[2,128,128]{2,1,0:T(8,128)(2,1)S(1)}, bf16[2,128,128]{2,1,0:T(8,128)(2,1)S(1)}, u32[]{:S(2)}, u32[]{:S(2)}) %collective-permute-start.18) | collective-permute-done | bytes 65568 | tf_op jit(solution)/shard_map/ppermute | solution.py:367
  (66 shorter events, 12.3 us)
Async XLA Ops:
  0.0 30.8 %collective-permute-start.4 = (bf16[16,2,128,128]{3,2,1,0:T(8,128)(2,1)}, bf16[16,2,128,128]{3,2,1,0:T(8,128)(2,1)S(1)}, u32[]{:S(2)}, u32[]{:S(2)}) collective-permute-start(bf16[16,2,128,128]{3,2,1,0:T(8,128)(2,1)} %bitcast.28), channel_id=1, source_target_pairs={{0,4},{12,8},{4,0},{8,12},{1,5},{13,9},{5,1},{9,13},{2,6},{14,10},... | collective-permute-start | bytes 3145736 | tf_op jit(solution)/shard_map/ppermute | solution.py:362
  8.5 21.4 %collective-permute-start = (bf16[3,512,256]{2,1,0:T(8,128)(2,1)}, bf16[3,512,256]{2,1,0:T(8,128)(2,1)S(1)}, u32[]{:S(2)}, u32[]{:S(2)}) collective-permute-start(bf16[3,512,256]{2,1,0:T(8,128)(2,1)} %extrapolate.3.refs_3_), channel_id=1, source_target_pairs={{4,8},{8,4},{5,9},{9,5},{6,10},{10,6},{7,11},{11,7},{20,24},{24,20... | collective-permute-start | bytes 2359304 | tf_op jit(solution)/shard_map/ppermute | solution.py:362
  9.2 34.5 %collective-permute-start.1 = (bf16[3,512,256]{2,1,0:T(8,128)(2,1)}, bf16[3,512,256]{2,1,0:T(8,128)(2,1)S(1)}, u32[]{:S(2)}, u32[]{:S(2)}) collective-permute-start(bf16[3,512,256]{2,1,0:T(8,128)(2,1)} %extrapolate.3.refs_3_), channel_id=1, source_target_pairs={{0,4},{12,8},{1,5},{13,9},{2,6},{14,10},{3,7},{15,11},{16,20},{28,... | collective-permute-start | bytes 2359304 | tf_op jit(solution)/shard_map/ppermute | solution.py:362
  28.1 38.6 %collective-permute-start.10 = (bf16[6,512,256]{2,1,0:T(8,128)(2,1)}, bf16[6,512,256]{2,1,0:T(8,128)(2,1)}, u32[]{:S(2)}, u32[]{:S(2)}) collective-permute-start(bf16[6,512,256]{2,1,0:T(8,128)(2,1)} %get-tuple-element.25.refs_4_), channel_id=1, source_target_pairs={{4,8},{8,4},{5,9},{9,5},{6,10},{10,6},{7,11},{11,7},{20,24},{24,20... | collective-permute-start | bytes 4718600 | tf_op jit(solution)/shard_map/ppermute | solution.py:362
  31.8 45.7 %collective-permute-start.6 = (bf16[6,512,256]{2,1,0:T(8,128)(2,1)}, bf16[6,512,256]{2,1,0:T(8,128)(2,1)S(1)}, u32[]{:S(2)}, u32[]{:S(2)}) collective-permute-start(bf16[6,512,256]{2,1,0:T(8,128)(2,1)} %get-tuple-element.23), channel_id=1, source_target_pairs={{0,4},{12,8},{4,0},{8,12},{1,5},{13,9},{5,1},{9,13},{2,6},{14,10},... | collective-permute-start | bytes 4718600 | tf_op jit(solution)/shard_map/ppermute | solution.py:362
  44.6 32.8 %copy-start = (bf16[7,512,256]{2,1,0:T(8,128)(2,1)S(1)}, bf16[7,512,256]{2,1,0:T(8,128)(2,1)}, u32[]{:S(2)}) copy-start(bf16[7,512,256]{2,1,0:T(8,128)(2,1)} %get-tuple-element.27.refs_5_) | copy-start | bytes 5505028
  58.6 48.0 %collective-permute-start.3 = (bf16[7,512,256]{2,1,0:T(8,128)(2,1)}, bf16[7,512,256]{2,1,0:T(8,128)(2,1)S(1)}, u32[]{:S(2)}, u32[]{:S(2)}) collective-permute-start(bf16[7,512,256]{2,1,0:T(8,128)(2,1)} %get-tuple-element.21.near_out), channel_id=1, source_target_pairs={{4,0},{8,12},{5,1},{9,13},{6,2},{10,14},{7,3},{11,15},{20,16},{24,... | collective-permute-start | bytes 5505032 | tf_op jit(solution)/shard_map/ppermute | solution.py:362
  59.9 129.2 %copy-start.18 = (s32[64,2]{0,1:T(2,128)S(1)}, s32[64,2]{0,1:T(2,128)}, u32[]{:S(2)}) copy-start(s32[64,2]{0,1:T(2,128)} %param.13) | copy-start | bytes 1540
  59.9 129.4 %collective-permute-start.2 = (bf16[9,512,256]{2,1,0:T(8,128)(2,1)}, bf16[9,512,256]{2,1,0:T(8,128)(2,1)}, u32[]{:S(2)}, u32[]{:S(2)}) collective-permute-start(bf16[9,512,256]{2,1,0:T(8,128)(2,1)} %get-tuple-element.20.near_in), channel_id=1, source_target_pairs={{0,4},{12,8},{1,5},{13,9},{2,6},{14,10},{3,7},{15,11},{16,20},{28,... | collective-permute-start | bytes 7077896 | tf_op jit(solution)/shard_map/ppermute | solution.py:362
  66.0 17.7 %collective-permute-start.5 = (bf16[3,512,256]{2,1,0:T(8,128)(2,1)}, bf16[3,512,256]{2,1,0:T(8,128)(2,1)S(1)}, u32[]{:S(2)}, u32[]{:S(2)}) collective-permute-start(bf16[3,512,256]{2,1,0:T(8,128)(2,1)} %copy-done.14), channel_id=1, source_target_pairs={{4,8},{8,4},{5,9},{9,5},{6,10},{10,6},{7,11},{11,7},{20,24},{24,20... | collective-permute-start | bytes 2359304 | tf_op jit(solution)/shard_map/ppermute | solution.py:362
  77.5 133.0 %collective-permute-start.11 = (bf16[7,512,256]{2,1,0:T(8,128)(2,1)S(1)}, bf16[7,512,256]{2,1,0:T(8,128)(2,1)}, u32[]{:S(2)}, u32[]{:S(2)}) collective-permute-start(bf16[7,512,256]{2,1,0:T(8,128)(2,1)S(1)} %copy-done), channel_id=1, source_target_pairs={{0,12},{12,0},{1,13},{13,1},{2,14},{14,2},{3,15},{15,3},{16,28},{2... | collective-permute-start | bytes 5505032 | tf_op jit(solution)/shard_map/ppermute | solution.py:362
  81.8 136.2 %collective-permute-start.7 = (bf16[6,512,256]{2,1,0:T(8,128)(2,1)S(1)}, bf16[6,512,256]{2,1,0:T(8,128)(2,1)}, u32[]{:S(2)}, u32[]{:S(2)}) collective-permute-start(bf16[6,512,256]{2,1,0:T(8,128)(2,1)S(1)} %collective-permute-done.6.refs_7_.refs_8_), channel_id=1, source_target_pairs={{4,8},{8,4},{5,9},{9,5},{6,10},{10,6},{7,11},{11,7},{20,24},{24,20... | collective-permute-start | bytes 4718600 | tf_op jit(solution)/shard_map/ppermute | solution.py:362
  106.6 1.3 copy-start.6
  109.1 109.0 %collective-permute-start.8 = (bf16[5,512,256]{2,1,0:T(8,128)(2,1)}, bf16[5,512,256]{2,1,0:T(8,128)(2,1)}, u32[]{:S(2)}, u32[]{:S(2)}) collective-permute-start(bf16[5,512,256]{2,1,0:T(8,128)(2,1)} %slice.44), channel_id=1, source_target_pairs={{4,12},{8,0},{5,13},{9,1},{6,14},{10,2},{7,15},{11,3},{20,28},{24,... | collective-permute-start | bytes 3932168 | tf_op jit(solution)/shard_map/ppermute | solution.py:362
  110.4 75.8 %collective-permute-start.9 = (bf16[1,512,256]{2,1,0:T(8,128)(2,1)S(1)}, bf16[1,512,256]{2,1,0:T(8,128)(2,1)S(1)}, u32[]{:S(2)}, u32[]{:S(2)}) collective-permute-start(bf16[1,512,256]{2,1,0:T(8,128)(2,1)S(1)} %slice.45), channel_id=1, source_target_pairs={{4,0},{8,12},{5,1},{9,13},{6,2},{10,14},{7,3},{11,15},{20,16},{24,... | collective-permute-start | bytes 786440 | tf_op jit(solution)/shard_map/ppermute | solution.py:362
  187.8 34.6 %collective-permute-start.12 = (bf16[2,512,256]{2,1,0:T(8,128)(2,1)}, bf16[2,512,256]{2,1,0:T(8,128)(2,1)}, u32[]{:S(2)}, u32[]{:S(2)}) collective-permute-start(bf16[2,512,256]{2,1,0:T(8,128)(2,1)} %slice.47), channel_id=1, source_target_pairs={{4,12},{8,0},{5,13},{9,1},{6,14},{10,2},{7,15},{11,3},{20,28},{24,... | collective-permute-start | bytes 1572872 | tf_op jit(solution)/shard_map/ppermute | solution.py:362
  189.3 1.7 copy-start.4
  190.9 1.5 copy-start.5
  192.4 1.5 copy-start.7
  193.9 1.2 copy-start.9
  196.4 14.1 %copy-start.3 = (bf16[3,512,256]{2,1,0:T(8,128)(2,1)S(1)}, bf16[3,512,256]{2,1,0:T(8,128)(2,1)}, u32[]{:S(2)}) copy-start(bf16[3,512,256]{2,1,0:T(8,128)(2,1)} %extrapolate.3.refs_3_) | copy-start | bytes 2359300
  196.4 14.1 %copy-start.8 = (bf16[6,512,256]{2,1,0:T(8,128)(2,1)S(1)}, bf16[6,512,256]{2,1,0:T(8,128)(2,1)}, u32[]{:S(2)}) copy-start(bf16[6,512,256]{2,1,0:T(8,128)(2,1)} %get-tuple-element.25.refs_4_) | copy-start | bytes 4718596
  196.4 14.1 %copy-start.13 = (bf16[3,512,256]{2,1,0:T(8,128)(2,1)S(1)}, bf16[3,512,256]{2,1,0:T(8,128)(2,1)}, u32[]{:S(2)}) copy-start(bf16[3,512,256]{2,1,0:T(8,128)(2,1)} %copy-done.12) | copy-start | bytes 2359300
  196.4 14.2 %copy-start.15 = (bf16[3,512,256]{2,1,0:T(8,128)(2,1)S(1)}, bf16[3,512,256]{2,1,0:T(8,128)(2,1)}, u32[]{:S(2)}) copy-start(bf16[3,512,256]{2,1,0:T(8,128)(2,1)} %copy-done.14) | copy-start | bytes 2359300
  196.4 14.2 %copy-start.17 = (bf16[1,512,256]{2,1,0:T(8,128)(2,1)S(1)}, bf16[1,512,256]{2,1,0:T(8,128)(2,1)}, u32[]{:S(2)}) copy-start(bf16[1,512,256]{2,1,0:T(8,128)(2,1)} %copy-done.16) | copy-start | bytes 786436
  210.5 7.6 %copy-start.2 = (bf16[3,512,256]{2,1,0:T(8,128)(2,1)S(1)}, bf16[3,512,256]{2,1,0:T(8,128)(2,1)}, u32[]{:S(2)}) copy-start(bf16[3,512,256]{2,1,0:T(8,128)(2,1)} %copy-done.1) | copy-start | bytes 2359300
  224.4 1.7 collective-permute-start.13
  226.2 2.3 collective-permute-start.14
  226.9 5.6 %collective-permute-start.17 = (bf16[2,2,128,128]{3,2,1,0:T(8,128)(2,1)S(1)}, bf16[2,2,128,128]{3,2,1,0:T(8,128)(2,1)S(1)}, u32[]{:S(2)}, u32[]{:S(2)}) collective-permute-start(bf16[2,2,128,128]{3,2,1,0:T(8,128)(2,1)S(1)} %select_convert_fusion.1), channel_id=1, source_target_pairs={{0,2},{1,3},{2,0},{3,1},{4,6},{5,7},{6,4},{7,5},{8,10},{9,11},{10,... | collective-permute-start | bytes 393224 | tf_op jit(solution)/shard_map/ppermute | solution.py:367
  228.5 9.2 %collective-permute-start.15 = (bf16[2,128,128]{2,1,0:T(8,128)(2,1)S(1)}, bf16[2,128,128]{2,1,0:T(8,128)(2,1)S(1)}, u32[]{:S(2)}, u32[]{:S(2)}) collective-permute-start(bf16[2,128,128]{2,1,0:T(8,128)(2,1)S(1)} %add_convert_fusion), channel_id=1, source_target_pairs={{7,15},{23,31}} | collective-permute-start | bytes 196616 | tf_op jit(solution)/shard_map/ppermute | solution.py:367
  229.1 8.5 %collective-permute-start.16 = (bf16[2,128,128]{2,1,0:T(8,128)(2,1)S(1)}, bf16[2,128,128]{2,1,0:T(8,128)(2,1)S(1)}, u32[]{:S(2)}, u32[]{:S(2)}) collective-permute-start(bf16[2,128,128]{2,1,0:T(8,128)(2,1)S(1)} %add_convert_fusion), channel_id=1, source_target_pairs={{11,15},{27,31}} | collective-permute-start | bytes 196616 | tf_op jit(solution)/shard_map/ppermute | solution.py:367
  232.6 8.0 %collective-permute-start.18 = (bf16[2,128,128]{2,1,0:T(8,128)(2,1)S(1)}, bf16[2,128,128]{2,1,0:T(8,128)(2,1)S(1)}, u32[]{:S(2)}, u32[]{:S(2)}) collective-permute-start(bf16[2,128,128]{2,1,0:T(8,128)(2,1)S(1)} %fusion.3), channel_id=1, source_target_pairs={{0,12},{1,13},{2,14},{4,8},{5,9},{6,10},{7,11},{8,4},{9,5},{10,6},... | collective-permute-start | bytes 196616 | tf_op jit(solution)/shard_map/ppermute | solution.py:367
  (6 other events, 5.6 us)

commit v6 on v1

--- a/solution.py
+++ b/solution.py
@@ -104,6 +104,7 @@
 OUTER = [0, 12, 2, 14, 1, 13, 3]
 FIRST = 5
 OUTER_FIRST = 4
+LATE = 5
 
 
 def outer_place(slot):
@@ -328,7 +329,7 @@
             values.append(field)
         begins.append([(begin, is_inner) for (_, begin), is_inner in zip(parts, inners)])
     if before is not None:
-        specs.append(image_spec)
+        specs.append(pl.BlockSpec((1, 2, size, size), lambda j, o, u, i: (first + j, 0, 0, 0)))
         values.append(before)
     places = jnp.stack([shot for shot, _ in pieces])
     return pl.pallas_call(
@@ -399,15 +400,15 @@
     r_1_in = hand(r_inner, *inward)
     r_1_out = hand(following(r_outer, far_data, r_3_head), *outward)
     s_inner, s_outer = make(
-        source_field[0], offsets=following(offsets, r_outer, r_3_head, r_1_head), sets=[INNER, OUTER]
-    )
-    s_out = hand(s_outer, *outward)
+        source_field[0], offsets=following(offsets, r_outer, r_3_head), sets=[INNER, OUTER]
+    )
+    s_out = hand(following(s_outer, r_1_head), *outward)
     s_in = hand(s_inner, *inward)
     forward_head = hand(following(r_1_head, r_3_in), *middle)
     r_3_out = hand(r_outer, *ends)
     forward = hand(following(r_1_in, r_1_out), *middle)
-    beyond_1 = hand(following(r_outer, s_out, forward_head)[:OUTER_FIRST], *beyond)
-    beyond_2 = hand(r_outer[OUTER_FIRST:], *beyond)
+    beyond_1 = hand(following(r_outer, s_out, forward_head)[:LATE], *beyond)
+    beyond_2 = hand(r_outer[LATE:], *beyond)
 
     ids = survey_tiles[:, 1]
     near_ids = lax.dynamic_slice_in_dim(ids, shot * tiles, tiles)
@@ -421,13 +422,14 @@
         (shot ^ 3, [(r_3_head, 0), (r_3_in, HEAD), (r_3_out, 0)]),
     ]
     forwarded = [(forward_head, 0), (forward, HEAD)]
-    one = image_blocks(product, 0, FIRST, early, inner)
-    two = image_blocks(product, FIRST, len(INNER) - FIRST, early, inner)
-    one = image_blocks(product, 0, FIRST, [(shot ^ 2, forwarded + [(beyond_1, 0)])], inner, one)
-    two = image_blocks(
-        product, FIRST, len(INNER) - FIRST, [(shot ^ 2, forwarded + [(beyond_2, OUTER_FIRST)])], inner,
-        following(two, one),
-    )
+    image = image_blocks(product, 0, len(INNER), early, inner)
+    most = image_blocks(product, 0, LATE + 1, [(shot ^ 2, forwarded + [(beyond_1, 0)])], inner, image)
+    rest = image_blocks(
+        product, LATE + 1, len(INNER) - LATE - 1, [(shot ^ 2, forwarded + [(beyond_2, LATE)])], inner,
+        following(image, most),
+    )
+    one = most[:FIRST]
+    two = jnp.concatenate([most[FIRST:], rest])
     image = sum_images(one, two, shot, freq)
     total_freqs = source_field.shape[0] * lax.axis_size("freq")
     return image * (1.0 / math.sqrt(2.0 * NR * total_freqs))

time: 219 us -> 221 us (level)
    unnamed x30 -> x36, local copies, waits for them, and re-layouts: 9.86 us -> 11.2 us
    pallas_call x4 -> x3, Pallas kernels: 15 us -> 13.8 us  [image_blocks(): pl.pallas_call(functools.partial(image_kernel, first=first, begins=begins...]
  transfers between devices with their start and end apart: 19 -> 19, of which waited for: 10 -> 9; matrix products, arithmetic and copies ran while one was open for 1% -> 1% of each run, Pallas kernels for 27% -> 26%
where the time goes in v6:
time: 221 us; the launch traced here: 220 us
  waiting for transfers between devices  106 us (48%)
  Pallas kernels  59.3 us (27%)
  starting transfers between devices  39.5 us (18%)
  local copies, waits for them, and re-layouts  13.2 us (6%)
    ppermute x13, waiting for transfers between devices, hand(): return lax.ppermute(value, 'shot', pairs)  97.1 us
    ppermute x13, starting transfers between devices, hand(): return lax.ppermute(value, 'shot', pairs)  32.4 us
    pallas_call x3, Pallas kernels, extrapolate_blocks(): pl.pallas_call(functools.partial(extrapolate_kernel, sets=sets, rows=rows...  31.4 us
    pallas_call x1, Pallas kernels, product_blocks(): pl.pallas_call(product_kernel, grid_spec=pltpu.PrefetchScalarGridSpec(num...  14.1 us
    pallas_call x3, Pallas kernels, image_blocks(): pl.pallas_call(functools.partial(image_kernel, first=first, begins=begins...  13.8 us
    unnamed x36, local copies, waits for them, and re-layouts  11.2 us
    ppermute x6, waiting for transfers between devices, send_sum(): lax.ppermute(value.astype(jnp.bfloat16), ('shot', 'freq'), pairs)  8.75 us
    ppermute x6, starting transfers between devices, send_sum(): lax.ppermute(value.astype(jnp.bfloat16), ('shot', 'freq'), pairs)  7.08 us
  transfers between devices with their start and end apart: 19, of which 9 were waited for; matrix products, arithmetic and copies ran while one was open for 1% of the time, Pallas kernels for 26%

profile of v6, /device:TPU:0, one launch (start us, length us, event | category | flops | bytes accessed | tf_op | source)
XLA Modules:
  0.0 220.3 jit_solution(15947746247130051460)
XLA Ops:
  0.0 3.0 %collective-permute-start.4 = (bf16[16,2,128,128]{3,2,1,0:T(8,128)(2,1)}, bf16[16,2,128,128]{3,2,1,0:T(8,128)(2,1)S(1)}, u32[]{:S(2)}, u32[]{:S(2)}) collective-permute-start(bf16[16,2,128,128]{3,2,1,0:T(8,128)(2,1)} %bitcast.28), channel_id=1, source_target_pairs={{0,4},{12,8},{4,0},{8,12},{1,5},{13,9},{5,1},{9,13},{2,6},{14,10},... | collective-permute-start | bytes 3145736 | tf_op jit(solution)/shard_map/ppermute | solution.py:352
  3.0 5.5 %extrapolate.3.refs_3_ = bf16[3,512,256]{2,1,0:T(8,128)(2,1)} custom-call(s32[3]{0:T(128)} %constant.38.clone.order, s32[3,16]{1,0:T(4,128)} %bitcast.36, bf16[16384,128]{1,0:T(8,128)(2,1)} %bitcast.33, bf16[16,3,2,128,128]{4,3,2,1,0:T(8,128)(2,1)} %bitcast.30), custom_call_target="tpu_custom_call" | custom-call | flops 1000 | bytes 1000 | tf_op jit(solution)/shard_map/extrapolate/pallas_call | solution.py:204
  9.2 7.2 %collective-permute-start.2 = (bf16[3,512,256]{2,1,0:T(8,128)(2,1)}, bf16[3,512,256]{2,1,0:T(8,128)(2,1)}, u32[]{:S(2)}, u32[]{:S(2)}) collective-permute-start(bf16[3,512,256]{2,1,0:T(8,128)(2,1)} %extrapolate.3.refs_3_), channel_id=1, source_target_pairs={{0,4},{12,8},{1,5},{13,9},{2,6},{14,10},{3,7},{15,11},{16,20},{28,... | collective-permute-start | bytes 2359304 | tf_op jit(solution)/shard_map/ppermute | solution.py:352
  16.4 12.0 %extrapolate.4 = (bf16[6,512,256]{2,1,0:T(8,128)(2,1)}, bf16[7,512,256]{2,1,0:T(8,128)(2,1)}) custom-call(s32[13]{0:T(128)} %constant.39.clone.order, s32[3,16]{1,0:T(4,128)} %bitcast.37, bf16[16384,128]{1,0:T(8,128)(2,1)} %bitcast.34, bf16[16,3,2,128,128]{4,3,2,1,0:T(8,128)(2,1)} %bitcast.31), custom_call_target="tpu_custom_call" | custom-call | flops 1000 | bytes 1000 | tf_op jit(solution)/shard_map/extrapolate/pallas_call | solution.py:204
  28.4 1.8 collective-permute-start.5
  30.2 1.4 collective-permute-start.7
  33.5 1.3 collective-permute-start.8
  34.8 13.9 %extrapolate.5 = (bf16[9,512,256]{2,1,0:T(8,128)(2,1)}, bf16[7,512,256]{2,1,0:T(8,128)(2,1)}) custom-call(s32[16]{0:T(128)} %constant.40.clone.order, s32[3,16]{1,0:T(4,128)} %bitcast.38, bf16[16384,128]{1,0:T(8,128)(2,1)} %bitcast.35, bf16[16,3,2,128,128]{4,3,2,1,0:T(8,128)(2,1)} %bitcast.32), custom_call_target="tpu_custom_call" | custom-call | flops 1000 | bytes 1000 | tf_op jit(solution)/shard_map/extrapolate/pallas_call | solution.py:204
  48.8 1.3 collective-permute-start.3
  50.1 7.4 %collective-permute-start.1 = (bf16[9,512,256]{2,1,0:T(8,128)(2,1)}, bf16[9,512,256]{2,1,0:T(8,128)(2,1)}, u32[]{:S(2)}, u32[]{:S(2)}) collective-permute-start(bf16[9,512,256]{2,1,0:T(8,128)(2,1)} %get-tuple-element.20.near_in), channel_id=1, source_target_pairs={{0,4},{12,8},{1,5},{13,9},{2,6},{14,10},{3,7},{15,11},{16,20},{28,... | collective-permute-start | bytes 7077896 | tf_op jit(solution)/shard_map/ppermute | solution.py:352
  58.2 19.3 %collective-permute-done.7.refs_7_ = bf16[6,512,256]{2,1,0:T(8,128)(2,1)S(1)} collective-permute-done((bf16[6,512,256]{2,1,0:T(8,128)(2,1)}, bf16[6,512,256]{2,1,0:T(8,128)(2,1)S(1)}, u32[]{:S(2)}, u32[]{:S(2)}) %collective-permute-start.7) | collective-permute-done | bytes 1572896 | tf_op jit(solution)/shard_map/ppermute | solution.py:352
  77.5 4.4 %collective-permute-start.11 = (bf16[7,512,256]{2,1,0:T(8,128)(2,1)S(1)}, bf16[7,512,256]{2,1,0:T(8,128)(2,1)}, u32[]{:S(2)}, u32[]{:S(2)}) collective-permute-start(bf16[7,512,256]{2,1,0:T(8,128)(2,1)S(1)} %copy-done), channel_id=1, source_target_pairs={{0,12},{12,0},{1,13},{13,1},{2,14},{14,2},{3,15},{15,3},{16,28},{2... | collective-permute-start | bytes 5505032 | tf_op jit(solution)/shard_map/ppermute | solution.py:352
  83.5 32.3 %collective-permute-done.3.far_out = bf16[7,512,256]{2,1,0:T(8,128)(2,1)S(1)} collective-permute-done((bf16[7,512,256]{2,1,0:T(8,128)(2,1)}, bf16[7,512,256]{2,1,0:T(8,128)(2,1)S(1)}, u32[]{:S(2)}, u32[]{:S(2)}) %collective-permute-start.3) | collective-permute-done | bytes 1835040 | tf_op jit(solution)/shard_map/ppermute | solution.py:352
  115.9 1.2 copy-done.6
  118.3 1.3 collective-permute-start.10
  120.4 1.3 collective-permute-start.12
  121.9 6.1 %collective-permute-done.1.far_in = bf16[9,512,256]{2,1,0:T(8,128)(2,1)} collective-permute-done((bf16[9,512,256]{2,1,0:T(8,128)(2,1)}, bf16[9,512,256]{2,1,0:T(8,128)(2,1)}, u32[]{:S(2)}, u32[]{:S(2)}) %collective-permute-start.1) | collective-permute-done | bytes 2359328 | tf_op jit(solution)/shard_map/ppermute | solution.py:352
  128.0 1.7 copy-done.4
  129.7 1.5 copy-done.5
  131.2 1.5 copy-done.7
  135.2 14.1 %product.1.refs_0_.refs_1_.refs_2_ = bf16[9,256,2048]{2,1,0:T(8,128)(2,1)S(1)} custom-call(s32[16]{0:T(128)S(1)} %get-tuple-element.32.near_ids, s32[16]{0:T(128)S(1)} %get-tuple-element.31.far_ids, s32[1]{0:T(128)} %bitcast.1.inner, bf16[9,512,256]{2,1,0:T(8,128)(2,1)S(1)} %copy-done.4, bf16[7,512,256]{2,1,0:T(8,128)(2,1)S(1)} %copy-done.5, ...), custom_call_target="tpu_custom_call" | custom-call | flops 1000 | bytes 1000 | tf_op jit(solution)/shard_map/product/pallas_call | solution.py:274
  149.2 20.0 %collective-permute-done.11.refs_11_ = bf16[7,512,256]{2,1,0:T(8,128)(2,1)} collective-permute-done((bf16[7,512,256]{2,1,0:T(8,128)(2,1)S(1)}, bf16[7,512,256]{2,1,0:T(8,128)(2,1)}, u32[]{:S(2)}, u32[]{:S(2)}) %collective-permute-start.11) | collective-permute-done | bytes 1835040 | tf_op jit(solution)/shard_map/ppermute | solution.py:352
  169.3 8.0 %image.3.refs_4_ = f32[9,2,128,128]{3,2,1,0:T(8,128)S(1)} custom-call(s32[3]{0:T(128)S(1)} %pad_add_fusion.places.unused, s32[3]{0:T(128)S(1)} %pad_add_fusion.places.unused, s32[1]{0:T(128)} %bitcast.1.inner, bf16[9,256,2048]{2,1,0:T(8,128)(2,1)S(1)} %product.1.refs_0_.refs_1_.refs_2_, bf16[9,256,2048]{2,1,0:T(8,128)(2,1)S(1)} %product.1.refs_0_.refs_1_.refs_2_, ...), custom_call_target="tpu_custom_call" | custom-call | flops 1000 | bytes 1000 | tf_op jit(solution)/shard_map/image/pallas_call | solution.py:335
  177.3 15.1 %collective-permute-done.10.refs_3_ = bf16[5,512,256]{2,1,0:T(8,128)(2,1)} collective-permute-done((bf16[5,512,256]{2,1,0:T(8,128)(2,1)}, bf16[5,512,256]{2,1,0:T(8,128)(2,1)}, u32[]{:S(2)}, u32[]{:S(2)}) %collective-permute-start.10) | collective-permute-done | bytes 1310752 | tf_op jit(solution)/shard_map/ppermute | solution.py:352
  192.4 4.0 %image.4 = f32[6,2,128,128]{3,2,1,0:T(8,128)S(1)} custom-call(s32[1]{0:T(128)} %bitcast.places.unused, s32[1]{0:T(128)} %bitcast.places.unused, s32[1]{0:T(128)} %bitcast.1.inner, bf16[9,256,2048]{2,1,0:T(8,128)(2,1)S(1)} %product.1.refs_0_.refs_1_.refs_2_, bf16[3,512,256]{2,1,0:T(8,128)(2,1)S(1)} %copy-done.2, ...), custom_call_target="tpu_custom_call" | custom-call | flops 1000 | bytes 1000 | tf_op jit(solution)/shard_map/image/pallas_call | solution.py:335
  196.5 4.2 %collective-permute-done.12.refs_3_ = bf16[2,512,256]{2,1,0:T(8,128)(2,1)} collective-permute-done((bf16[2,512,256]{2,1,0:T(8,128)(2,1)}, bf16[2,512,256]{2,1,0:T(8,128)(2,1)}, u32[]{:S(2)}, u32[]{:S(2)}) %collective-permute-start.12) | collective-permute-done | bytes 524320 | tf_op jit(solution)/shard_map/ppermute | solution.py:352
  200.7 1.8 image.5
  202.7 1.6 collective-permute-done.13
  206.0 1.5 collective-permute-start.17
  208.9 2.7 %collective-permute-done.17 = bf16[2,2,128,128]{3,2,1,0:T(8,128)(2,1)S(1)} collective-permute-done((bf16[2,2,128,128]{3,2,1,0:T(8,128)(2,1)S(1)}, bf16[2,2,128,128]{3,2,1,0:T(8,128)(2,1)S(1)}, u32[]{:S(2)}, u32[]{:S(2)}) %collective-permute-start.17) | collective-permute-done | bytes 131104 | tf_op jit(solution)/shard_map/ppermute | solution.py:357
  211.7 3.5 %collective-permute-start.18 = (bf16[2,128,128]{2,1,0:T(8,128)(2,1)S(1)}, bf16[2,128,128]{2,1,0:T(8,128)(2,1)S(1)}, u32[]{:S(2)}, u32[]{:S(2)}) collective-permute-start(bf16[2,128,128]{2,1,0:T(8,128)(2,1)S(1)} %fusion.3), channel_id=1, source_target_pairs={{0,12},{1,13},{2,14},{4,8},{5,9},{6,10},{7,11},{8,4},{9,5},{10,6},... | collective-permute-start | bytes 196616 | tf_op jit(solution)/shard_map/ppermute | solution.py:357
  215.2 4.5 %collective-permute-done.18 = bf16[2,128,128]{2,1,0:T(8,128)(2,1)S(1)} collective-permute-done((bf16[2,128,128]{2,1,0:T(8,128)(2,1)S(1)}, bf16[2,128,128]{2,1,0:T(8,128)(2,1)S(1)}, u32[]{:S(2)}, u32[]{:S(2)}) %collective-permute-start.18) | collective-permute-done | bytes 65568 | tf_op jit(solution)/shard_map/ppermute | solution.py:357
  (63 shorter events, 13.6 us)
Async XLA Ops:
  0.0 32.5 %collective-permute-start.4 = (bf16[16,2,128,128]{3,2,1,0:T(8,128)(2,1)}, bf16[16,2,128,128]{3,2,1,0:T(8,128)(2,1)S(1)}, u32[]{:S(2)}, u32[]{:S(2)}) collective-permute-start(bf16[16,2,128,128]{3,2,1,0:T(8,128)(2,1)} %bitcast.28), channel_id=1, source_target_pairs={{0,4},{12,8},{4,0},{8,12},{1,5},{13,9},{5,1},{9,13},{2,6},{14,10},... | collective-permute-start | bytes 3145736 | tf_op jit(solution)/shard_map/ppermute | solution.py:352
  8.5 23.1 %collective-permute-start = (bf16[3,512,256]{2,1,0:T(8,128)(2,1)}, bf16[3,512,256]{2,1,0:T(8,128)(2,1)S(1)}, u32[]{:S(2)}, u32[]{:S(2)}) collective-permute-start(bf16[3,512,256]{2,1,0:T(8,128)(2,1)} %extrapolate.3.refs_3_), channel_id=1, source_target_pairs={{4,8},{8,4},{5,9},{9,5},{6,10},{10,6},{7,11},{11,7},{20,24},{24,20... | collective-permute-start | bytes 2359304 | tf_op jit(solution)/shard_map/ppermute | solution.py:352
  9.2 39.5 %collective-permute-start.2 = (bf16[3,512,256]{2,1,0:T(8,128)(2,1)}, bf16[3,512,256]{2,1,0:T(8,128)(2,1)}, u32[]{:S(2)}, u32[]{:S(2)}) collective-permute-start(bf16[3,512,256]{2,1,0:T(8,128)(2,1)} %extrapolate.3.refs_3_), channel_id=1, source_target_pairs={{0,4},{12,8},{1,5},{13,9},{2,6},{14,10},{3,7},{15,11},{16,20},{28,... | collective-permute-start | bytes 2359304 | tf_op jit(solution)/shard_map/ppermute | solution.py:352
  28.4 29.0 %collective-permute-start.5 = (bf16[6,512,256]{2,1,0:T(8,128)(2,1)}, bf16[6,512,256]{2,1,0:T(8,128)(2,1)}, u32[]{:S(2)}, u32[]{:S(2)}) collective-permute-start(bf16[6,512,256]{2,1,0:T(8,128)(2,1)} %get-tuple-element.23.refs_4_), channel_id=1, source_target_pairs={{4,8},{8,4},{5,9},{9,5},{6,10},{10,6},{7,11},{11,7},{20,24},{24,20... | collective-permute-start | bytes 4718600 | tf_op jit(solution)/shard_map/ppermute | solution.py:352
  30.2 47.2 %collective-permute-start.7 = (bf16[6,512,256]{2,1,0:T(8,128)(2,1)}, bf16[6,512,256]{2,1,0:T(8,128)(2,1)S(1)}, u32[]{:S(2)}, u32[]{:S(2)}) collective-permute-start(bf16[6,512,256]{2,1,0:T(8,128)(2,1)} %get-tuple-element.23.refs_4_), channel_id=1, source_target_pairs={{0,4},{12,8},{1,5},{13,9},{2,6},{14,10},{3,7},{15,11},{16,20},{28,... | collective-permute-start | bytes 4718600 | tf_op jit(solution)/shard_map/ppermute | solution.py:352
  33.5 48.3 %collective-permute-start.8 = (bf16[7,512,256]{2,1,0:T(8,128)(2,1)}, bf16[7,512,256]{2,1,0:T(8,128)(2,1)}, u32[]{:S(2)}, u32[]{:S(2)}) collective-permute-start(bf16[7,512,256]{2,1,0:T(8,128)(2,1)} %get-tuple-element.27.refs_5_), channel_id=1, source_target_pairs={{4,0},{8,12},{5,1},{9,13},{6,2},{10,14},{7,3},{11,15},{20,16},{24,... | collective-permute-start | bytes 5505032 | tf_op jit(solution)/shard_map/ppermute | solution.py:352
  34.8 42.6 %copy-start = (bf16[7,512,256]{2,1,0:T(8,128)(2,1)S(1)}, bf16[7,512,256]{2,1,0:T(8,128)(2,1)}, u32[]{:S(2)}) copy-start(bf16[7,512,256]{2,1,0:T(8,128)(2,1)} %get-tuple-element.27.refs_5_) | copy-start | bytes 5505028
  48.8 67.1 %collective-permute-start.3 = (bf16[7,512,256]{2,1,0:T(8,128)(2,1)}, bf16[7,512,256]{2,1,0:T(8,128)(2,1)S(1)}, u32[]{:S(2)}, u32[]{:S(2)}) collective-permute-start(bf16[7,512,256]{2,1,0:T(8,128)(2,1)} %get-tuple-element.22.near_out), channel_id=1, source_target_pairs={{4,0},{8,12},{5,1},{9,13},{6,2},{10,14},{7,3},{11,15},{20,16},{24,... | collective-permute-start | bytes 5505032 | tf_op jit(solution)/shard_map/ppermute | solution.py:352
  50.1 71.6 %copy-start.17 = (s32[64,2]{0,1:T(2,128)S(1)}, s32[64,2]{0,1:T(2,128)}, u32[]{:S(2)}) copy-start(s32[64,2]{0,1:T(2,128)} %param.13) | copy-start | bytes 1540
  50.1 77.9 %collective-permute-start.1 = (bf16[9,512,256]{2,1,0:T(8,128)(2,1)}, bf16[9,512,256]{2,1,0:T(8,128)(2,1)}, u32[]{:S(2)}, u32[]{:S(2)}) collective-permute-start(bf16[9,512,256]{2,1,0:T(8,128)(2,1)} %get-tuple-element.20.near_in), channel_id=1, source_target_pairs={{0,4},{12,8},{1,5},{13,9},{2,6},{14,10},{3,7},{15,11},{16,20},{28,... | collective-permute-start | bytes 7077896 | tf_op jit(solution)/shard_map/ppermute | solution.py:352
  57.4 25.2 %collective-permute-start.6 = (bf16[3,512,256]{2,1,0:T(8,128)(2,1)}, bf16[3,512,256]{2,1,0:T(8,128)(2,1)S(1)}, u32[]{:S(2)}, u32[]{:S(2)}) collective-permute-start(bf16[3,512,256]{2,1,0:T(8,128)(2,1)} %collective-permute-done.2.refs_6_), channel_id=1, source_target_pairs={{4,8},{8,4},{5,9},{9,5},{6,10},{10,6},{7,11},{11,7},{20,24},{24,20... | collective-permute-start | bytes 2359304 | tf_op jit(solution)/shard_map/ppermute | solution.py:352
  77.5 4.4 %copy-start.9 = (bf16[6,512,256]{2,1,0:T(8,128)(2,1)}, bf16[6,512,256]{2,1,0:T(8,128)(2,1)S(1)}, u32[]{:S(2)}) copy-start(bf16[6,512,256]{2,1,0:T(8,128)(2,1)S(1)} %collective-permute-done.7.refs_7_) | copy-start | bytes 4718596
  77.5 91.8 %collective-permute-start.11 = (bf16[7,512,256]{2,1,0:T(8,128)(2,1)S(1)}, bf16[7,512,256]{2,1,0:T(8,128)(2,1)}, u32[]{:S(2)}, u32[]{:S(2)}) collective-permute-start(bf16[7,512,256]{2,1,0:T(8,128)(2,1)S(1)} %copy-done), channel_id=1, source_target_pairs={{0,12},{12,0},{1,13},{13,1},{2,14},{14,2},{3,15},{15,3},{16,28},{2... | collective-permute-start | bytes 5505032 | tf_op jit(solution)/shard_map/ppermute | solution.py:352
  81.9 110.5 %collective-permute-start.9 = (bf16[6,512,256]{2,1,0:T(8,128)(2,1)}, bf16[6,512,256]{2,1,0:T(8,128)(2,1)S(1)}, u32[]{:S(2)}, u32[]{:S(2)}) collective-permute-start(bf16[6,512,256]{2,1,0:T(8,128)(2,1)} %copy-done.9), channel_id=1, source_target_pairs={{4,8},{8,4},{5,9},{9,5},{6,10},{10,6},{7,11},{11,7},{20,24},{24,20... | collective-permute-start | bytes 4718600 | tf_op jit(solution)/shard_map/ppermute | solution.py:352
  115.9 1.2 copy-start.6
  118.3 74.1 %collective-permute-start.10 = (bf16[5,512,256]{2,1,0:T(8,128)(2,1)}, bf16[5,512,256]{2,1,0:T(8,128)(2,1)}, u32[]{:S(2)}, u32[]{:S(2)}) collective-permute-start(bf16[5,512,256]{2,1,0:T(8,128)(2,1)} %slice.41), channel_id=1, source_target_pairs={{4,12},{8,0},{5,13},{9,1},{6,14},{10,2},{7,15},{11,3},{20,28},{24,... | collective-permute-start | bytes 3932168 | tf_op jit(solution)/shard_map/ppermute | solution.py:352
  120.4 80.3 %collective-permute-start.12 = (bf16[2,512,256]{2,1,0:T(8,128)(2,1)}, bf16[2,512,256]{2,1,0:T(8,128)(2,1)}, u32[]{:S(2)}, u32[]{:S(2)}) collective-permute-start(bf16[2,512,256]{2,1,0:T(8,128)(2,1)} %slice.43), channel_id=1, source_target_pairs={{4,12},{8,0},{5,13},{9,1},{6,14},{10,2},{7,15},{11,3},{20,28},{24,... | collective-permute-start | bytes 1572872 | tf_op jit(solution)/shard_map/ppermute | solution.py:352
  128.0 1.7 copy-start.4
  129.7 1.5 copy-start.5
  131.2 1.5 copy-start.7
  135.1 34.1 %copy-start.3 = (bf16[3,512,256]{2,1,0:T(8,128)(2,1)S(1)}, bf16[3,512,256]{2,1,0:T(8,128)(2,1)}, u32[]{:S(2)}) copy-start(bf16[3,512,256]{2,1,0:T(8,128)(2,1)} %extrapolate.3.refs_3_) | copy-start | bytes 2359300
  135.1 34.1 %copy-start.8 = (bf16[6,512,256]{2,1,0:T(8,128)(2,1)S(1)}, bf16[6,512,256]{2,1,0:T(8,128)(2,1)}, u32[]{:S(2)}) copy-start(bf16[6,512,256]{2,1,0:T(8,128)(2,1)} %get-tuple-element.23.refs_4_) | copy-start | bytes 4718596
  135.1 34.1 %copy-start.10 = (bf16[6,512,256]{2,1,0:T(8,128)(2,1)S(1)}, bf16[6,512,256]{2,1,0:T(8,128)(2,1)}, u32[]{:S(2)}) copy-start(bf16[6,512,256]{2,1,0:T(8,128)(2,1)} %copy-done.9) | copy-start | bytes 4718596
  135.1 34.1 %copy-start.15 = (bf16[3,512,256]{2,1,0:T(8,128)(2,1)S(1)}, bf16[3,512,256]{2,1,0:T(8,128)(2,1)}, u32[]{:S(2)}) copy-start(bf16[3,512,256]{2,1,0:T(8,128)(2,1)} %copy-done.14) | copy-start | bytes 2359300
  149.2 43.2 %copy-start.2 = (bf16[3,512,256]{2,1,0:T(8,128)(2,1)S(1)}, bf16[3,512,256]{2,1,0:T(8,128)(2,1)}, u32[]{:S(2)}) copy-start(bf16[3,512,256]{2,1,0:T(8,128)(2,1)} %copy-done.1) | copy-start | bytes 2359300
  196.4 6.0 %copy-start.16 = (f32[1,2,128,128]{3,2,1,0:T(8,128)}, f32[1,2,128,128]{3,2,1,0:T(8,128)S(1)}, u32[]{:S(2)}) copy-start(f32[1,2,128,128]{3,2,1,0:T(8,128)S(1)} %get-tuple-element.30) | copy-start | bytes 393220
  202.6 1.7 collective-permute-start.13
  205.3 2.3 %collective-permute-start.14 = (bf16[2,128,128]{2,1,0:T(8,128)(2,1)S(1)}, bf16[2,128,128]{2,1,0:T(8,128)(2,1)S(1)}, u32[]{:S(2)}, u32[]{:S(2)}) collective-permute-start(bf16[2,128,128]{2,1,0:T(8,128)(2,1)S(1)} %fusion.2), channel_id=1, source_target_pairs={{5,7},{9,11},{21,23},{25,27}} | collective-permute-start | bytes 196616 | tf_op jit(solution)/shard_map/ppermute | solution.py:357
  206.0 5.6 %collective-permute-start.17 = (bf16[2,2,128,128]{3,2,1,0:T(8,128)(2,1)S(1)}, bf16[2,2,128,128]{3,2,1,0:T(8,128)(2,1)S(1)}, u32[]{:S(2)}, u32[]{:S(2)}) collective-permute-start(bf16[2,2,128,128]{3,2,1,0:T(8,128)(2,1)S(1)} %select_convert_fusion.1), channel_id=1, source_target_pairs={{0,2},{1,3},{2,0},{3,1},{4,6},{5,7},{6,4},{7,5},{8,10},{9,11},{10,... | collective-permute-start | bytes 393224 | tf_op jit(solution)/shard_map/ppermute | solution.py:357
  207.6 7.6 %collective-permute-start.15 = (bf16[2,128,128]{2,1,0:T(8,128)(2,1)S(1)}, bf16[2,128,128]{2,1,0:T(8,128)(2,1)S(1)}, u32[]{:S(2)}, u32[]{:S(2)}) collective-permute-start(bf16[2,128,128]{2,1,0:T(8,128)(2,1)S(1)} %add_convert_fusion), channel_id=1, source_target_pairs={{7,15},{23,31}} | collective-permute-start | bytes 196616 | tf_op jit(solution)/shard_map/ppermute | solution.py:357
  208.2 6.9 %collective-permute-start.16 = (bf16[2,128,128]{2,1,0:T(8,128)(2,1)S(1)}, bf16[2,128,128]{2,1,0:T(8,128)(2,1)S(1)}, u32[]{:S(2)}, u32[]{:S(2)}) collective-permute-start(bf16[2,128,128]{2,1,0:T(8,128)(2,1)S(1)} %add_convert_fusion), channel_id=1, source_target_pairs={{11,15},{27,31}} | collective-permute-start | bytes 196616 | tf_op jit(solution)/shard_map/ppermute | solution.py:357
  211.7 8.0 %collective-permute-start.18 = (bf16[2,128,128]{2,1,0:T(8,128)(2,1)S(1)}, bf16[2,128,128]{2,1,0:T(8,128)(2,1)S(1)}, u32[]{:S(2)}, u32[]{:S(2)}) collective-permute-start(bf16[2,128,128]{2,1,0:T(8,128)(2,1)S(1)} %fusion.3), channel_id=1, source_target_pairs={{0,12},{1,13},{2,14},{4,8},{5,9},{6,10},{7,11},{8,4},{9,5},{10,6},... | collective-permute-start | bytes 196616 | tf_op jit(solution)/shard_map/ppermute | solution.py:357
  (5 other events, 5.2 us)

commit v7 on v6

--- a/solution.py
+++ b/solution.py
@@ -105,6 +105,7 @@
 FIRST = 5
 OUTER_FIRST = 4
 LATE = 5
+HALF = 4
 
 
 def outer_place(slot):
@@ -299,8 +300,8 @@
     for n, piece in enumerate(begins):
         field = parts[0][0]
         for part, (begin, is_inner) in zip(parts[1:], piece[1:]):
-            chosen = (inner[0] > 0) & (slot >= begin) if is_inner else inner[0] == 0
-            field = jnp.where(chosen, part[0], field)
+            place = slot if is_inner else outer_place(slot)
+            field = jnp.where(((inner[0] > 0) == is_inner) & (place >= begin), part[0], field)
         parts = parts[len(piece):]
         term = jnp.dot(refs[n][0], field, preferred_element_type=jnp.float32)
         both = term if both is None else both + term
@@ -323,11 +324,10 @@
     values = [product] * len(pieces)
     begins = []
     for _, parts in pieces:
-        inners = [True] * (len(parts) - 1) + [False]
-        for (field, begin), is_inner in zip(parts, inners):
+        for field, begin, is_inner in parts:
             specs.append(part_spec((1, rows, width), first, begin, field.shape[0], is_inner))
             values.append(field)
-        begins.append([(begin, is_inner) for (_, begin), is_inner in zip(parts, inners)])
+        begins.append([(begin, is_inner) for _, begin, is_inner in parts])
     if before is not None:
         specs.append(pl.BlockSpec((1, 2, size, size), lambda j, o, u, i: (first + j, 0, 0, 0)))
         values.append(before)
@@ -405,9 +405,10 @@
     s_out = hand(following(s_outer, r_1_head), *outward)
     s_in = hand(s_inner, *inward)
     forward_head = hand(following(r_1_head, r_3_in), *middle)
-    r_3_out = hand(r_outer, *ends)
     forward = hand(following(r_1_in, r_1_out), *middle)
-    beyond_1 = hand(following(r_outer, s_out, forward_head)[:LATE], *beyond)
+    beyond_1 = hand(r_outer[:LATE], *beyond)
+    r_3_out_1 = hand(following(r_outer, s_out, forward_head)[:HALF], *ends)
+    r_3_out_2 = hand(r_outer[HALF:], *ends)
     beyond_2 = hand(r_outer[LATE:], *beyond)
 
     ids = survey_tiles[:, 1]
@@ -417,15 +418,15 @@
         s_inner, s_outer, s_in, s_out, survey_data[0], far_data, near_ids, far_ids, inner
     )
     early = [
-        (shot, [(r_head, 0), (r_inner, HEAD), (r_outer, 0)]),
-        (shot ^ 1, [(r_1_head, 0), (r_1_in, HEAD), (r_1_out, 0)]),
-        (shot ^ 3, [(r_3_head, 0), (r_3_in, HEAD), (r_3_out, 0)]),
+        (shot, [(r_head, 0, True), (r_inner, HEAD, True), (r_outer, 0, False)]),
+        (shot ^ 1, [(r_1_head, 0, True), (r_1_in, HEAD, True), (r_1_out, 0, False)]),
+        (shot ^ 3, [(r_3_head, 0, True), (r_3_in, HEAD, True), (r_3_out_1, 0, False), (r_3_out_2, HALF, False)]),
     ]
-    forwarded = [(forward_head, 0), (forward, HEAD)]
+    forwarded = [(forward_head, 0, True), (forward, HEAD, True)]
     image = image_blocks(product, 0, len(INNER), early, inner)
-    most = image_blocks(product, 0, LATE + 1, [(shot ^ 2, forwarded + [(beyond_1, 0)])], inner, image)
+    most = image_blocks(product, 0, LATE + 1, [(shot ^ 2, forwarded + [(beyond_1, 0, False)])], inner, image)
     rest = image_blocks(
-        product, LATE + 1, len(INNER) - LATE - 1, [(shot ^ 2, forwarded + [(beyond_2, LATE)])], inner,
+        product, LATE + 1, len(INNER) - LATE - 1, [(shot ^ 2, forwarded + [(beyond_2, LATE, False)])], inner,
         following(image, most),
     )
     one = most[:FIRST]

time: 221 us -> 218 us (0.986)
  waiting for transfers between devices: 106 us -> 93.4 us
  starting transfers between devices: 39.5 us -> 45.9 us
  local copies, waits for them, and re-layouts: 13.2 us -> 17.5 us
    ppermute x13 -> x14, waiting for transfers between devices: 97.1 us -> 85.7 us  [hand(): return lax.ppermute(value, 'shot', pairs)]
    ppermute x13 -> x14, starting transfers between devices: 32.4 us -> 37.8 us  [hand(): return lax.ppermute(value, 'shot', pairs)]
    unnamed x36 -> x38, local copies, waits for them, and re-layouts: 11.2 us -> 13.2 us
  transfers between devices with their start and end apart: 19 -> 20, of which waited for: 9 -> 9; matrix products, arithmetic and copies ran while one was open for 1% -> 2% of each run, Pallas kernels for 26% -> 26%
where the time goes in v7:
time: 218 us; the launch traced here: 217 us
  waiting for transfers between devices  93.4 us (43%)
  Pallas kernels  58.5 us (27%)
  starting transfers between devices  45.9 us (21%)
  local copies, waits for them, and re-layouts  17.5 us (8%)
    ppermute x14, waiting for transfers between devices, hand(): return lax.ppermute(value, 'shot', pairs)  85.7 us
    ppermute x14, starting transfers between devices, hand(): return lax.ppermute(value, 'shot', pairs)  37.8 us
    pallas_call x3, Pallas kernels, extrapolate_blocks(): pl.pallas_call(functools.partial(extrapolate_kernel, sets=sets, rows=rows...  31.4 us
    pallas_call x3, Pallas kernels, image_blocks(): pl.pallas_call(functools.partial(image_kernel, first=first, begins=begins...  14.2 us
    unnamed x38, local copies, waits for them, and re-layouts  13.2 us
    pallas_call x1, Pallas kernels, product_blocks(): pl.pallas_call(product_kernel, grid_spec=pltpu.PrefetchScalarGridSpec(num...  12.9 us
    ppermute x6, starting transfers between devices, send_sum(): lax.ppermute(value.astype(jnp.bfloat16), ('shot', 'freq'), pairs)  8.17 us
    ppermute x6, waiting for transfers between devices, send_sum(): lax.ppermute(value.astype(jnp.bfloat16), ('shot', 'freq'), pairs)  7.65 us
  transfers between devices with their start and end apart: 20, of which 9 were waited for; matrix products, arithmetic and copies ran while one was open for 2% of the time, Pallas kernels for 26%

profile of v7, /device:TPU:0, one launch (start us, length us, event | category | flops | bytes accessed | tf_op | source)
XLA Modules:
  0.0 216.8 jit_solution(9942679589679482919)
XLA Ops:
  0.0 3.0 %collective-permute-start.4 = (bf16[16,2,128,128]{3,2,1,0:T(8,128)(2,1)}, bf16[16,2,128,128]{3,2,1,0:T(8,128)(2,1)S(1)}, u32[]{:S(2)}, u32[]{:S(2)}) collective-permute-start(bf16[16,2,128,128]{3,2,1,0:T(8,128)(2,1)} %bitcast.28), channel_id=1, source_target_pairs={{0,4},{12,8},{4,0},{8,12},{1,5},{13,9},{5,1},{9,13},{2,6},{14,10},... | collective-permute-start | bytes 3145736 | tf_op jit(solution)/shard_map/ppermute | solution.py:352
  3.0 5.5 %extrapolate.3.refs_3_ = bf16[3,512,256]{2,1,0:T(8,128)(2,1)} custom-call(s32[3]{0:T(128)} %constant.38.clone.order, s32[3,16]{1,0:T(4,128)} %bitcast.36, bf16[16384,128]{1,0:T(8,128)(2,1)} %bitcast.33, bf16[16,3,2,128,128]{4,3,2,1,0:T(8,128)(2,1)} %bitcast.30), custom_call_target="tpu_custom_call" | custom-call | flops 1000 | bytes 1000 | tf_op jit(solution)/shard_map/extrapolate/pallas_call | solution.py:205
  9.3 7.1 %collective-permute-start.2 = (bf16[3,512,256]{2,1,0:T(8,128)(2,1)}, bf16[3,512,256]{2,1,0:T(8,128)(2,1)}, u32[]{:S(2)}, u32[]{:S(2)}) collective-permute-start(bf16[3,512,256]{2,1,0:T(8,128)(2,1)} %extrapolate.3.refs_3_), channel_id=1, source_target_pairs={{0,4},{12,8},{1,5},{13,9},{2,6},{14,10},{3,7},{15,11},{16,20},{28,... | collective-permute-start | bytes 2359304 | tf_op jit(solution)/shard_map/ppermute | solution.py:352
  16.4 12.0 %extrapolate.4 = (bf16[6,512,256]{2,1,0:T(8,128)(2,1)}, bf16[7,512,256]{2,1,0:T(8,128)(2,1)}) custom-call(s32[13]{0:T(128)} %constant.39.clone.order, s32[3,16]{1,0:T(4,128)} %bitcast.37, bf16[16384,128]{1,0:T(8,128)(2,1)} %bitcast.34, bf16[16,3,2,128,128]{4,3,2,1,0:T(8,128)(2,1)} %bitcast.31), custom_call_target="tpu_custom_call" | custom-call | flops 1000 | bytes 1000 | tf_op jit(solution)/shard_map/extrapolate/pallas_call | solution.py:205
  31.1 1.3 collective-permute-start.8
  32.4 7.0 %collective-permute-start.7 = (bf16[6,512,256]{2,1,0:T(8,128)(2,1)}, bf16[6,512,256]{2,1,0:T(8,128)(2,1)}, u32[]{:S(2)}, u32[]{:S(2)}) collective-permute-start(bf16[6,512,256]{2,1,0:T(8,128)(2,1)} %get-tuple-element.23.refs_4_), channel_id=1, source_target_pairs={{0,4},{12,8},{1,5},{13,9},{2,6},{14,10},{3,7},{15,11},{16,20},{28,... | collective-permute-start | bytes 4718600 | tf_op jit(solution)/shard_map/ppermute | solution.py:352
  39.3 13.9 %extrapolate.5 = (bf16[9,512,256]{2,1,0:T(8,128)(2,1)}, bf16[7,512,256]{2,1,0:T(8,128)(2,1)}) custom-call(s32[16]{0:T(128)} %constant.40.clone.order, s32[3,16]{1,0:T(4,128)} %bitcast.38, bf16[16384,128]{1,0:T(8,128)(2,1)} %bitcast.35, bf16[16,3,2,128,128]{4,3,2,1,0:T(8,128)(2,1)} %bitcast.32), custom_call_target="tpu_custom_call" | custom-call | flops 1000 | bytes 1000 | tf_op jit(solution)/shard_map/extrapolate/pallas_call | solution.py:205
  53.3 1.3 collective-permute-start.3
  54.6 4.8 %collective-permute-start.1 = (bf16[9,512,256]{2,1,0:T(8,128)(2,1)}, bf16[9,512,256]{2,1,0:T(8,128)(2,1)S(1)}, u32[]{:S(2)}, u32[]{:S(2)}) collective-permute-start(bf16[9,512,256]{2,1,0:T(8,128)(2,1)} %get-tuple-element.20.near_in), channel_id=1, source_target_pairs={{0,4},{12,8},{1,5},{13,9},{2,6},{14,10},{3,7},{15,11},{16,20},{28,... | collective-permute-start | bytes 7077896 | tf_op jit(solution)/shard_map/ppermute | solution.py:352
  61.3 16.2 %collective-permute-done.7.refs_7_ = bf16[6,512,256]{2,1,0:T(8,128)(2,1)} collective-permute-done((bf16[6,512,256]{2,1,0:T(8,128)(2,1)}, bf16[6,512,256]{2,1,0:T(8,128)(2,1)}, u32[]{:S(2)}, u32[]{:S(2)}) %collective-permute-start.7) | collective-permute-done | bytes 1572896 | tf_op jit(solution)/shard_map/ppermute | solution.py:352
  79.4 1.3 collective-permute-start.10
  80.7 32.7 %collective-permute-done.3.far_out = bf16[7,512,256]{2,1,0:T(8,128)(2,1)S(1)} collective-permute-done((bf16[7,512,256]{2,1,0:T(8,128)(2,1)}, bf16[7,512,256]{2,1,0:T(8,128)(2,1)S(1)}, u32[]{:S(2)}, u32[]{:S(2)}) %collective-permute-start.3) | collective-permute-done | bytes 1835040 | tf_op jit(solution)/shard_map/ppermute | solution.py:352
  114.6 3.9 %collective-permute-start.11 = (bf16[4,512,256]{2,1,0:T(8,128)(2,1)}, bf16[4,512,256]{2,1,0:T(8,128)(2,1)}, u32[]{:S(2)}, u32[]{:S(2)}) collective-permute-start(bf16[4,512,256]{2,1,0:T(8,128)(2,1)} %slice.48), channel_id=1, source_target_pairs={{0,12},{12,0},{1,13},{13,1},{2,14},{14,2},{3,15},{15,3},{16,28},{2... | collective-permute-start | bytes 3145736 | tf_op jit(solution)/shard_map/ppermute | solution.py:352
  119.5 3.8 %collective-permute-start.12 = (bf16[3,512,256]{2,1,0:T(8,128)(2,1)}, bf16[3,512,256]{2,1,0:T(8,128)(2,1)}, u32[]{:S(2)}, u32[]{:S(2)}) collective-permute-start(bf16[3,512,256]{2,1,0:T(8,128)(2,1)} %slice.49), channel_id=1, source_target_pairs={{0,12},{12,0},{1,13},{13,1},{2,14},{14,2},{3,15},{15,3},{16,28},{2... | collective-permute-start | bytes 2359304 | tf_op jit(solution)/shard_map/ppermute | solution.py:352
  124.2 3.9 %collective-permute-done.1.far_in = bf16[9,512,256]{2,1,0:T(8,128)(2,1)S(1)} collective-permute-done((bf16[9,512,256]{2,1,0:T(8,128)(2,1)}, bf16[9,512,256]{2,1,0:T(8,128)(2,1)S(1)}, u32[]{:S(2)}, u32[]{:S(2)}) %collective-permute-start.1) | collective-permute-done | bytes 2359328 | tf_op jit(solution)/shard_map/ppermute | solution.py:352
  128.0 1.4 copy-done.5
  131.0 1.7 copy-done.4
  132.6 1.7 copy-done.6
  134.3 1.5 copy-done.7
  135.8 1.5 copy-done.9
  139.8 12.9 %product.1.refs_0_.refs_1_.refs_2_ = bf16[9,256,2048]{2,1,0:T(8,128)(2,1)S(1)} custom-call(s32[16]{0:T(128)S(1)} %get-tuple-element.32.near_ids, s32[16]{0:T(128)S(1)} %get-tuple-element.31.far_ids, s32[1]{0:T(128)} %bitcast.1.inner, bf16[9,512,256]{2,1,0:T(8,128)(2,1)S(1)} %copy-done.4, bf16[7,512,256]{2,1,0:T(8,128)(2,1)S(1)} %copy-done.7, ...), custom_call_target="tpu_custom_call" | custom-call | flops 1000 | bytes 1000 | tf_op jit(solution)/shard_map/product/pallas_call | solution.py:275
  152.7 16.6 %collective-permute-done.12.refs_12_ = bf16[3,512,256]{2,1,0:T(8,128)(2,1)} collective-permute-done((bf16[3,512,256]{2,1,0:T(8,128)(2,1)}, bf16[3,512,256]{2,1,0:T(8,128)(2,1)}, u32[]{:S(2)}, u32[]{:S(2)}) %collective-permute-start.12) | collective-permute-done | bytes 786464 | tf_op jit(solution)/shard_map/ppermute | solution.py:352
  169.3 8.3 %image.3.refs_4_ = f32[9,2,128,128]{3,2,1,0:T(8,128)S(1)} custom-call(s32[3]{0:T(128)S(1)} %pad_add_fusion.places.unused, s32[3]{0:T(128)S(1)} %pad_add_fusion.places.unused, s32[1]{0:T(128)} %bitcast.1.inner, bf16[9,256,2048]{2,1,0:T(8,128)(2,1)S(1)} %product.1.refs_0_.refs_1_.refs_2_, bf16[9,256,2048]{2,1,0:T(8,128)(2,1)S(1)} %product.1.refs_0_.refs_1_.refs_2_, ...), custom_call_target="tpu_custom_call" | custom-call | flops 1000 | bytes 1000 | tf_op jit(solution)/shard_map/image/pallas_call | solution.py:335
  177.6 11.5 %collective-permute-done.10.refs_3_ = bf16[5,512,256]{2,1,0:T(8,128)(2,1)} collective-permute-done((bf16[5,512,256]{2,1,0:T(8,128)(2,1)}, bf16[5,512,256]{2,1,0:T(8,128)(2,1)}, u32[]{:S(2)}, u32[]{:S(2)}) %collective-permute-start.10) | collective-permute-done | bytes 1310752 | tf_op jit(solution)/shard_map/ppermute | solution.py:352
  189.1 4.0 %image.4 = f32[6,2,128,128]{3,2,1,0:T(8,128)S(1)} custom-call(s32[1]{0:T(128)} %bitcast.places.unused, s32[1]{0:T(128)} %bitcast.places.unused, s32[1]{0:T(128)} %bitcast.1.inner, bf16[9,256,2048]{2,1,0:T(8,128)(2,1)S(1)} %product.1.refs_0_.refs_1_.refs_2_, bf16[3,512,256]{2,1,0:T(8,128)(2,1)S(1)} %copy-done.2, ...), custom_call_target="tpu_custom_call" | custom-call | flops 1000 | bytes 1000 | tf_op jit(solution)/shard_map/image/pallas_call | solution.py:335
  193.2 4.9 %collective-permute-done.13.refs_3_ = bf16[2,512,256]{2,1,0:T(8,128)(2,1)} collective-permute-done((bf16[2,512,256]{2,1,0:T(8,128)(2,1)}, bf16[2,512,256]{2,1,0:T(8,128)(2,1)}, u32[]{:S(2)}, u32[]{:S(2)}) %collective-permute-start.13) | collective-permute-done | bytes 524320 | tf_op jit(solution)/shard_map/ppermute | solution.py:352
  198.1 1.8 image.5
  200.1 1.6 collective-permute-done.14
  202.5 1.6 collective-permute-start.18
  205.4 2.7 %collective-permute-done.18 = bf16[2,2,128,128]{3,2,1,0:T(8,128)(2,1)S(1)} collective-permute-done((bf16[2,2,128,128]{3,2,1,0:T(8,128)(2,1)S(1)}, bf16[2,2,128,128]{3,2,1,0:T(8,128)(2,1)S(1)}, u32[]{:S(2)}, u32[]{:S(2)}) %collective-permute-start.18) | collective-permute-done | bytes 131104 | tf_op jit(solution)/shard_map/ppermute | solution.py:357
  208.2 4.5 %collective-permute-start.19 = (bf16[2,128,128]{2,1,0:T(8,128)(2,1)S(1)}, bf16[2,128,128]{2,1,0:T(8,128)(2,1)S(1)}, u32[]{:S(2)}, u32[]{:S(2)}) collective-permute-start(bf16[2,128,128]{2,1,0:T(8,128)(2,1)S(1)} %fusion.3), channel_id=1, source_target_pairs={{0,12},{1,13},{2,14},{4,8},{5,9},{6,10},{7,11},{8,4},{9,5},{10,6},... | collective-permute-start | bytes 196616 | tf_op jit(solution)/shard_map/ppermute | solution.py:357
  212.8 3.4 %collective-permute-done.19 = bf16[2,128,128]{2,1,0:T(8,128)(2,1)S(1)} collective-permute-done((bf16[2,128,128]{2,1,0:T(8,128)(2,1)S(1)}, bf16[2,128,128]{2,1,0:T(8,128)(2,1)S(1)}, u32[]{:S(2)}, u32[]{:S(2)}) %collective-permute-start.19) | collective-permute-done | bytes 65568 | tf_op jit(solution)/shard_map/ppermute | solution.py:357
  (69 shorter events, 17.1 us)
Async XLA Ops:
  0.0 30.1 %collective-permute-start.4 = (bf16[16,2,128,128]{3,2,1,0:T(8,128)(2,1)}, bf16[16,2,128,128]{3,2,1,0:T(8,128)(2,1)S(1)}, u32[]{:S(2)}, u32[]{:S(2)}) collective-permute-start(bf16[16,2,128,128]{3,2,1,0:T(8,128)(2,1)} %bitcast.28), channel_id=1, source_target_pairs={{0,4},{12,8},{4,0},{8,12},{1,5},{13,9},{5,1},{9,13},{2,6},{14,10},... | collective-permute-start | bytes 3145736 | tf_op jit(solution)/shard_map/ppermute | solution.py:352
  8.5 20.7 %collective-permute-start = (bf16[3,512,256]{2,1,0:T(8,128)(2,1)}, bf16[3,512,256]{2,1,0:T(8,128)(2,1)S(1)}, u32[]{:S(2)}, u32[]{:S(2)}) collective-permute-start(bf16[3,512,256]{2,1,0:T(8,128)(2,1)} %extrapolate.3.refs_3_), channel_id=1, source_target_pairs={{4,8},{8,4},{5,9},{9,5},{6,10},{10,6},{7,11},{11,7},{20,24},{24,20... | collective-permute-start | bytes 2359304 | tf_op jit(solution)/shard_map/ppermute | solution.py:352
  9.3 44.0 %collective-permute-start.2 = (bf16[3,512,256]{2,1,0:T(8,128)(2,1)}, bf16[3,512,256]{2,1,0:T(8,128)(2,1)}, u32[]{:S(2)}, u32[]{:S(2)}) collective-permute-start(bf16[3,512,256]{2,1,0:T(8,128)(2,1)} %extrapolate.3.refs_3_), channel_id=1, source_target_pairs={{0,4},{12,8},{1,5},{13,9},{2,6},{14,10},{3,7},{15,11},{16,20},{28,... | collective-permute-start | bytes 2359304 | tf_op jit(solution)/shard_map/ppermute | solution.py:352
  28.4 31.0 %collective-permute-start.5 = (bf16[6,512,256]{2,1,0:T(8,128)(2,1)}, bf16[6,512,256]{2,1,0:T(8,128)(2,1)S(1)}, u32[]{:S(2)}, u32[]{:S(2)}) collective-permute-start(bf16[6,512,256]{2,1,0:T(8,128)(2,1)} %get-tuple-element.23.refs_4_), channel_id=1, source_target_pairs={{4,8},{8,4},{5,9},{9,5},{6,10},{10,6},{7,11},{11,7},{20,24},{24,20... | collective-permute-start | bytes 4718600 | tf_op jit(solution)/shard_map/ppermute | solution.py:352
  31.1 46.4 %collective-permute-start.8 = (bf16[7,512,256]{2,1,0:T(8,128)(2,1)}, bf16[7,512,256]{2,1,0:T(8,128)(2,1)}, u32[]{:S(2)}, u32[]{:S(2)}) collective-permute-start(bf16[7,512,256]{2,1,0:T(8,128)(2,1)} %get-tuple-element.27.refs_5_), channel_id=1, source_target_pairs={{4,0},{8,12},{5,1},{9,13},{6,2},{10,14},{7,3},{11,15},{20,16},{24,... | collective-permute-start | bytes 5505032 | tf_op jit(solution)/shard_map/ppermute | solution.py:352
  32.4 45.1 %collective-permute-start.7 = (bf16[6,512,256]{2,1,0:T(8,128)(2,1)}, bf16[6,512,256]{2,1,0:T(8,128)(2,1)}, u32[]{:S(2)}, u32[]{:S(2)}) collective-permute-start(bf16[6,512,256]{2,1,0:T(8,128)(2,1)} %get-tuple-element.23.refs_4_), channel_id=1, source_target_pairs={{0,4},{12,8},{1,5},{13,9},{2,6},{14,10},{3,7},{15,11},{16,20},{28,... | collective-permute-start | bytes 4718600 | tf_op jit(solution)/shard_map/ppermute | solution.py:352
  39.3 38.9 %copy-start = (bf16[7,512,256]{2,1,0:T(8,128)(2,1)S(1)}, bf16[7,512,256]{2,1,0:T(8,128)(2,1)}, u32[]{:S(2)}) copy-start(bf16[7,512,256]{2,1,0:T(8,128)(2,1)} %get-tuple-element.27.refs_5_) | copy-start | bytes 5505028
  53.3 60.1 %collective-permute-start.3 = (bf16[7,512,256]{2,1,0:T(8,128)(2,1)}, bf16[7,512,256]{2,1,0:T(8,128)(2,1)S(1)}, u32[]{:S(2)}, u32[]{:S(2)}) collective-permute-start(bf16[7,512,256]{2,1,0:T(8,128)(2,1)} %get-tuple-element.22.near_out), channel_id=1, source_target_pairs={{4,0},{8,12},{5,1},{9,13},{6,2},{10,14},{7,3},{11,15},{20,16},{24,... | collective-permute-start | bytes 5505032 | tf_op jit(solution)/shard_map/ppermute | solution.py:352
  54.6 73.4 %collective-permute-start.1 = (bf16[9,512,256]{2,1,0:T(8,128)(2,1)}, bf16[9,512,256]{2,1,0:T(8,128)(2,1)S(1)}, u32[]{:S(2)}, u32[]{:S(2)}) collective-permute-start(bf16[9,512,256]{2,1,0:T(8,128)(2,1)} %get-tuple-element.20.near_in), channel_id=1, source_target_pairs={{0,4},{12,8},{1,5},{13,9},{2,6},{14,10},{3,7},{15,11},{16,20},{28,... | collective-permute-start | bytes 7077896 | tf_op jit(solution)/shard_map/ppermute | solution.py:352
  60.5 20.2 %collective-permute-start.6 = (bf16[3,512,256]{2,1,0:T(8,128)(2,1)}, bf16[3,512,256]{2,1,0:T(8,128)(2,1)S(1)}, u32[]{:S(2)}, u32[]{:S(2)}) collective-permute-start(bf16[3,512,256]{2,1,0:T(8,128)(2,1)} %collective-permute-done.2.refs_6_), channel_id=1, source_target_pairs={{4,8},{8,4},{5,9},{9,5},{6,10},{10,6},{7,11},{11,7},{20,24},{24,20... | collective-permute-start | bytes 2359304 | tf_op jit(solution)/shard_map/ppermute | solution.py:352
  77.5 111.7 %collective-permute-start.9 = (bf16[6,512,256]{2,1,0:T(8,128)(2,1)}, bf16[6,512,256]{2,1,0:T(8,128)(2,1)S(1)}, u32[]{:S(2)}, u32[]{:S(2)}) collective-permute-start(bf16[6,512,256]{2,1,0:T(8,128)(2,1)} %collective-permute-done.7.refs_7_), channel_id=1, source_target_pairs={{4,8},{8,4},{5,9},{9,5},{6,10},{10,6},{7,11},{11,7},{20,24},{24,20... | collective-permute-start | bytes 4718600 | tf_op jit(solution)/shard_map/ppermute | solution.py:352
  79.4 109.7 %collective-permute-start.10 = (bf16[5,512,256]{2,1,0:T(8,128)(2,1)}, bf16[5,512,256]{2,1,0:T(8,128)(2,1)}, u32[]{:S(2)}, u32[]{:S(2)}) collective-permute-start(bf16[5,512,256]{2,1,0:T(8,128)(2,1)} %slice.47), channel_id=1, source_target_pairs={{4,12},{8,0},{5,13},{9,1},{6,14},{10,2},{7,15},{11,3},{20,28},{24,... | collective-permute-start | bytes 3932168 | tf_op jit(solution)/shard_map/ppermute | solution.py:352
  80.7 43.4 %copy-start.1 = (bf16[3,512,256]{2,1,0:T(8,128)(2,1)}, bf16[3,512,256]{2,1,0:T(8,128)(2,1)S(1)}, u32[]{:S(2)}) copy-start(bf16[3,512,256]{2,1,0:T(8,128)(2,1)S(1)} %collective-permute-done.6.refs_1_) | copy-start | bytes 2359300
  113.4 10.8 %copy-start.8 = (bf16[7,512,256]{2,1,0:T(8,128)(2,1)}, bf16[7,512,256]{2,1,0:T(8,128)(2,1)S(1)}, u32[]{:S(2)}) copy-start(bf16[7,512,256]{2,1,0:T(8,128)(2,1)S(1)} %collective-permute-done.3.far_out) | copy-start | bytes 5505028
  114.6 16.2 %copy-start.18 = (s32[64,2]{0,1:T(2,128)S(1)}, s32[64,2]{0,1:T(2,128)}, u32[]{:S(2)}) copy-start(s32[64,2]{0,1:T(2,128)} %param.13) | copy-start | bytes 1540
  114.6 54.7 %collective-permute-start.11 = (bf16[4,512,256]{2,1,0:T(8,128)(2,1)}, bf16[4,512,256]{2,1,0:T(8,128)(2,1)}, u32[]{:S(2)}, u32[]{:S(2)}) collective-permute-start(bf16[4,512,256]{2,1,0:T(8,128)(2,1)} %slice.48), channel_id=1, source_target_pairs={{0,12},{12,0},{1,13},{13,1},{2,14},{14,2},{3,15},{15,3},{16,28},{2... | collective-permute-start | bytes 3145736 | tf_op jit(solution)/shard_map/ppermute | solution.py:352
  119.5 49.7 %collective-permute-start.12 = (bf16[3,512,256]{2,1,0:T(8,128)(2,1)}, bf16[3,512,256]{2,1,0:T(8,128)(2,1)}, u32[]{:S(2)}, u32[]{:S(2)}) collective-permute-start(bf16[3,512,256]{2,1,0:T(8,128)(2,1)} %slice.49), channel_id=1, source_target_pairs={{0,12},{12,0},{1,13},{13,1},{2,14},{14,2},{3,15},{15,3},{16,28},{2... | collective-permute-start | bytes 2359304 | tf_op jit(solution)/shard_map/ppermute | solution.py:352
  129.5 68.6 %collective-permute-start.13 = (bf16[2,512,256]{2,1,0:T(8,128)(2,1)}, bf16[2,512,256]{2,1,0:T(8,128)(2,1)}, u32[]{:S(2)}, u32[]{:S(2)}) collective-permute-start(bf16[2,512,256]{2,1,0:T(8,128)(2,1)} %slice.51), channel_id=1, source_target_pairs={{4,12},{8,0},{5,13},{9,1},{6,14},{10,2},{7,15},{11,3},{20,28},{24,... | collective-permute-start | bytes 1572872 | tf_op jit(solution)/shard_map/ppermute | solution.py:352
  131.0 1.7 copy-start.4
  132.6 1.7 copy-start.6
  134.3 1.5 copy-start.7
  139.7 29.5 %copy-start.3 = (bf16[3,512,256]{2,1,0:T(8,128)(2,1)S(1)}, bf16[3,512,256]{2,1,0:T(8,128)(2,1)}, u32[]{:S(2)}) copy-start(bf16[3,512,256]{2,1,0:T(8,128)(2,1)} %extrapolate.3.refs_3_) | copy-start | bytes 2359300
  139.7 29.5 %copy-start.10 = (bf16[6,512,256]{2,1,0:T(8,128)(2,1)S(1)}, bf16[6,512,256]{2,1,0:T(8,128)(2,1)}, u32[]{:S(2)}) copy-start(bf16[6,512,256]{2,1,0:T(8,128)(2,1)} %get-tuple-element.23.refs_4_) | copy-start | bytes 4718596
  139.8 29.5 %copy-start.12 = (bf16[6,512,256]{2,1,0:T(8,128)(2,1)S(1)}, bf16[6,512,256]{2,1,0:T(8,128)(2,1)}, u32[]{:S(2)}) copy-start(bf16[6,512,256]{2,1,0:T(8,128)(2,1)} %copy-done.11) | copy-start | bytes 4718596
  139.8 29.5 %copy-start.17 = (bf16[3,512,256]{2,1,0:T(8,128)(2,1)S(1)}, bf16[3,512,256]{2,1,0:T(8,128)(2,1)}, u32[]{:S(2)}) copy-start(bf16[3,512,256]{2,1,0:T(8,128)(2,1)} %copy-done.16) | copy-start | bytes 2359300
  152.7 36.5 %copy-start.2 = (bf16[3,512,256]{2,1,0:T(8,128)(2,1)S(1)}, bf16[3,512,256]{2,1,0:T(8,128)(2,1)}, u32[]{:S(2)}) copy-start(bf16[3,512,256]{2,1,0:T(8,128)(2,1)} %copy-done.1) | copy-start | bytes 2359300
  200.0 1.7 collective-permute-start.14
  201.8 2.3 %collective-permute-start.15 = (bf16[2,128,128]{2,1,0:T(8,128)(2,1)S(1)}, bf16[2,128,128]{2,1,0:T(8,128)(2,1)S(1)}, u32[]{:S(2)}, u32[]{:S(2)}) collective-permute-start(bf16[2,128,128]{2,1,0:T(8,128)(2,1)S(1)} %fusion.2), channel_id=1, source_target_pairs={{5,7},{9,11},{21,23},{25,27}} | collective-permute-start | bytes 196616 | tf_op jit(solution)/shard_map/ppermute | solution.py:357
  202.5 5.6 %collective-permute-start.18 = (bf16[2,2,128,128]{3,2,1,0:T(8,128)(2,1)S(1)}, bf16[2,2,128,128]{3,2,1,0:T(8,128)(2,1)S(1)}, u32[]{:S(2)}, u32[]{:S(2)}) collective-permute-start(bf16[2,2,128,128]{3,2,1,0:T(8,128)(2,1)S(1)} %select_convert_fusion.1), channel_id=1, source_target_pairs={{0,2},{1,3},{2,0},{3,1},{4,6},{5,7},{6,4},{7,5},{8,10},{9,11},{10,... | collective-permute-start | bytes 393224 | tf_op jit(solution)/shard_map/ppermute | solution.py:357
  204.1 8.7 %collective-permute-start.16 = (bf16[2,128,128]{2,1,0:T(8,128)(2,1)S(1)}, bf16[2,128,128]{2,1,0:T(8,128)(2,1)S(1)}, u32[]{:S(2)}, u32[]{:S(2)}) collective-permute-start(bf16[2,128,128]{2,1,0:T(8,128)(2,1)S(1)} %add_convert_fusion), channel_id=1, source_target_pairs={{7,15},{23,31}} | collective-permute-start | bytes 196616 | tf_op jit(solution)/shard_map/ppermute | solution.py:357
  204.8 8.0 %collective-permute-start.17 = (bf16[2,128,128]{2,1,0:T(8,128)(2,1)S(1)}, bf16[2,128,128]{2,1,0:T(8,128)(2,1)S(1)}, u32[]{:S(2)}, u32[]{:S(2)}) collective-permute-start(bf16[2,128,128]{2,1,0:T(8,128)(2,1)S(1)} %add_convert_fusion), channel_id=1, source_target_pairs={{11,15},{27,31}} | collective-permute-start | bytes 196616 | tf_op jit(solution)/shard_map/ppermute | solution.py:357
  208.2 8.0 %collective-permute-start.19 = (bf16[2,128,128]{2,1,0:T(8,128)(2,1)S(1)}, bf16[2,128,128]{2,1,0:T(8,128)(2,1)S(1)}, u32[]{:S(2)}, u32[]{:S(2)}) collective-permute-start(bf16[2,128,128]{2,1,0:T(8,128)(2,1)S(1)} %fusion.3), channel_id=1, source_target_pairs={{0,12},{1,13},{2,14},{4,8},{5,9},{6,10},{7,11},{8,4},{9,5},{10,6},... | collective-permute-start | bytes 196616 | tf_op jit(solution)/shard_map/ppermute | solution.py:357
  (7 other events, 8.4 us)

commit v8 on v5

--- a/solution.py
+++ b/solution.py
@@ -105,7 +105,8 @@
 FIRST = 5
 OUTER_FIRST = 4
 LATE = 5
-SWAP = len(INNER) - HEAD
+SWAP = len(OUTER)
+HALF = 4
 
 
 def outer_place(slot):
@@ -237,10 +238,19 @@
     )(order, offsets, inner, flat, operator)
 
 
-def product_kernel(near_ids, far_ids, inner, near_in, near_out, far_in, far_out, near_data, far_data, out, turned, total):
+def chosen(refs, begins, slot, inner):
+    field = refs[0][0]
+    for part, (begin, is_inner) in zip(refs[1:], begins[1:]):
+        place = slot if is_inner else outer_place(slot)
+        field = jnp.where(((inner[0] > 0) == is_inner) & (place >= begin), part[0], field)
+    return field
+
+
+def product_kernel(near_ids, far_ids, inner, *refs, begins):
+    near_data, far_data, out, turned, total = refs[-5:]
     size = near_data.shape[2]
     tiles = near_data.shape[0]
-    sources = near_in.shape[1] // size
+    sources = refs[0].shape[1] // size
     per_source = tiles // sources
 
     @pl.when(pl.program_id(0) == 0)
@@ -251,11 +261,11 @@
                     turned[side * tiles + tile, :, part * size:(part + 1) * size] = data[tile, part].T
 
     total[...] = jnp.zeros_like(total)
-    sides = ((near_in, near_out, near_ids), (far_in, far_out, far_ids))
-    for side, (field_in, field_out, ids) in enumerate(sides):
+    for side, ids in enumerate((near_ids, far_ids)):
+        first = len(begins[0]) * side
+        field = chosen(refs[first:first + len(begins[side])], begins[side], pl.program_id(0), inner)
         for source in range(sources):
-            lines = slice(source * size, (source + 1) * size)
-            upper = jnp.where(inner[0] > 0, field_in[0, lines, :], field_out[0, lines, :])
+            upper = field[source * size:(source + 1) * size, :]
             lower = jnp.concatenate([-upper[:, size:], upper[:, :size]], 1)
             both = jnp.concatenate([upper, lower], 0)
             first = side * tiles + source * per_source
@@ -276,18 +286,22 @@
     return pl.BlockSpec(shape, index)
 
 
-def product_blocks(near_in, near_out, far_in, far_out, near_data, far_data, near_ids, far_ids, inner):
-    blocks, rows, width = near_in.shape
+def product_blocks(near, far, near_data, far_data, near_ids, far_ids, inner):
+    blocks = len(INNER)
+    _, rows, width = near[0][0].shape
     tiles, _, size, _ = near_data.shape
     receivers = NR // size
-    shape = (1, rows, width)
+    parts = near + far
+    begins = [[part[1:] for part in side] for side in (near, far)]
     data_spec = pl.BlockSpec(near_data.shape, lambda j, a, b, i: (0, 0, 0, 0))
     return pl.pallas_call(
-        product_kernel,
+        functools.partial(product_kernel, begins=begins),
         grid_spec=pltpu.PrefetchScalarGridSpec(
             num_scalar_prefetch=3,
             grid=(blocks,),
-            in_specs=[part_spec(shape, 0, 0, len(INNER), True), part_spec(shape, 0, 0, len(OUTER), False)] * 2
+            in_specs=[
+                part_spec((1, rows, width), 0, begin, field.shape[0], is_inner) for field, begin, is_inner in parts
+            ]
             + [data_spec, data_spec],
             out_specs=pl.BlockSpec((1, width, NR), lambda j, a, b, i: (j, 0, 0)),
             scratch_shapes=[
@@ -299,7 +313,7 @@
         compiler_params=params(),
         cost_estimate=SMALL,
         name="product",
-    )(near_ids, far_ids, inner, near_in, near_out, far_in, far_out, near_data, far_data)
+    )(near_ids, far_ids, inner, *[field for field, _, _ in parts], near_data, far_data)
 
 
 def image_kernel(places, unused, inner, *refs, first, begins, size):
@@ -405,33 +419,35 @@
     (r_head,) = make(receiver_field[0], offsets=offsets, sets=[INNER[:HEAD]], listed=True)
     r_1_head = hand(r_head, *inward)
     r_3_head = hand(r_head, *middle)
-    r_inner, r_outer, r_swap = make(
-        receiver_field[0], offsets=following(offsets, r_head), sets=[INNER[HEAD:], OUTER], swap=True
-    )
+    r_inner, r_outer = make(receiver_field[0], offsets=following(offsets, r_head), sets=[INNER[HEAD:], OUTER])
     r_3_in = hand(r_inner, *middle)
-    r_1 = hand(following(r_swap, far_data, r_3_head), *inward, *outward)
-    s_inner, s_outer = make(
-        source_field[0], offsets=following(offsets, r_outer, r_3_head, r_1_head), sets=[INNER, OUTER]
-    )
-    s_out = hand(s_outer, *outward)
-    s_in = hand(s_inner, *inward)
+    r_1_in = hand(r_inner, *inward)
+    r_1_out = hand(following(r_outer, far_data, r_3_head), *outward)
+    s_inner, s_outer, s_rest, s_swap = make(
+        source_field[0],
+        offsets=following(offsets, r_outer, r_3_head),
+        sets=[INNER[:SWAP], OUTER, INNER[SWAP:]],
+        swap=True,
+    )
+    s_far = hand(following(s_swap, r_1_head), *inward, *outward)
     forward_head = hand(r_1_head, *middle)
-    r_3_out = hand(following(r_outer, r_3_in, r_1), *ends)
-    r_1_rest = hand(r_outer[SWAP:], *outward)
-    forward = hand(r_1, *middle)
-    beyond_1 = hand(following(r_outer, s_out, forward_head)[:LATE], *beyond)
-    beyond_2 = hand(following(r_outer, r_1_rest)[LATE:], *beyond)
+    s_rest_far = hand(following(s_rest, r_3_in), *inward)
+    forward = hand(r_1_in, *middle)
+    beyond_1 = hand(following(r_outer, r_1_out)[:LATE], *beyond)
+    r_3_out_1 = hand(following(r_outer, s_far, s_rest_far, forward_head)[:HALF], *ends)
+    r_3_out_2 = hand(r_outer[HALF:], *ends)
+    beyond_2 = hand(r_outer[LATE:], *beyond)
 
     ids = survey_tiles[:, 1]
     near_ids = lax.dynamic_slice_in_dim(ids, shot * tiles, tiles)
     far_ids = lax.dynamic_slice_in_dim(ids, (shot ^ 1) * tiles, tiles)
-    product = product_blocks(
-        s_inner, s_outer, s_in, s_out, survey_data[0], far_data, near_ids, far_ids, inner
-    )
+    near = [(s_inner, 0, True), (s_rest, SWAP, True), (s_outer, 0, False)]
+    far = [(s_far, 0, True), (s_rest_far, SWAP, True), (s_far, 0, False)]
+    product = product_blocks(near, far, survey_data[0], far_data, near_ids, far_ids, inner)
     early = [
         (shot, [(r_head, 0, True), (r_inner, HEAD, True), (r_outer, 0, False)]),
-        (shot ^ 1, [(r_1_head, 0, True), (r_1, HEAD, True), (r_1, 0, False), (r_1_rest, SWAP, False)]),
-        (shot ^ 3, [(r_3_head, 0, True), (r_3_in, HEAD, True), (r_3_out, 0, False)]),
+        (shot ^ 1, [(r_1_head, 0, True), (r_1_in, HEAD, True), (r_1_out, 0, False)]),
+        (shot ^ 3, [(r_3_head, 0, True), (r_3_in, HEAD, True), (r_3_out_1, 0, False), (r_3_out_2, HALF, False)]),
     ]
     forwarded = [(forward_head, 0, True), (forward, HEAD, True)]
     image = image_blocks(product, 0, len(INNER), early, inner)

time: 244 us -> 214 us (0.88)
  waiting for transfers between devices: 125 us -> 82.6 us
  starting transfers between devices: 40.1 us -> 53.3 us
    ppermute x13 -> x14, waiting for transfers between devices: 118 us -> 74.7 us  [hand(): return lax.ppermute(value, 'shot', pairs)]
    ppermute x13 -> x14, starting transfers between devices: 31.4 us -> 45.3 us  [hand(): return lax.ppermute(value, 'shot', pairs)]
    unnamed x38 -> x40, local copies, waits for them, and re-layouts: 12.8 us -> 12.1 us
  transfers between devices with their start and end apart: 19 -> 20, of which waited for: 7 -> 8; matrix products, arithmetic and copies ran while one was open for 1% -> 2% of each run, Pallas kernels for 24% -> 27%
where the time goes in v8:
time: 214 us; the launch traced here: 213 us
  waiting for transfers between devices  82.6 us (39%)
  Pallas kernels  59.5 us (28%)
  starting transfers between devices  53.3 us (25%)
  local copies, waits for them, and re-layouts  16.3 us (8%)
    ppermute x14, waiting for transfers between devices, hand(): return lax.ppermute(value, 'shot', pairs)  74.7 us
    ppermute x14, starting transfers between devices, hand(): return lax.ppermute(value, 'shot', pairs)  45.3 us
    pallas_call x3, Pallas kernels, extrapolate_blocks(): pl.pallas_call(functools.partial(extrapolate_kernel, sets=sets, rows=rows...  32 us
    pallas_call x3, Pallas kernels, image_blocks(): pl.pallas_call(functools.partial(image_kernel, first=first, begins=begins...  14.2 us
    pallas_call x1, Pallas kernels, product_blocks(): pl.pallas_call(functools.partial(product_kernel, begins=begins), grid_spe...  13.3 us
    unnamed x40, local copies, waits for them, and re-layouts  12.1 us
    ppermute x6, starting transfers between devices, send_sum(): lax.ppermute(value.astype(jnp.bfloat16), ('shot', 'freq'), pairs)  7.99 us
    ppermute x6, waiting for transfers between devices, send_sum(): lax.ppermute(value.astype(jnp.bfloat16), ('shot', 'freq'), pairs)  7.84 us
  transfers between devices with their start and end apart: 20, of which 8 were waited for; matrix products, arithmetic and copies ran while one was open for 2% of the time, Pallas kernels for 27%

profile of v8, /device:TPU:0, one launch (start us, length us, event | category | flops | bytes accessed | tf_op | source)
XLA Modules:
  0.0 213.1 jit_solution(13723391562894153359)
XLA Ops:
  0.0 3.0 %collective-permute-start.5 = (bf16[16,2,128,128]{3,2,1,0:T(8,128)(2,1)}, bf16[16,2,128,128]{3,2,1,0:T(8,128)(2,1)S(1)}, u32[]{:S(2)}, u32[]{:S(2)}) collective-permute-start(bf16[16,2,128,128]{3,2,1,0:T(8,128)(2,1)} %bitcast.28), channel_id=1, source_target_pairs={{0,4},{12,8},{4,0},{8,12},{1,5},{13,9},{5,1},{9,13},{2,6},{14,10},... | collective-permute-start | bytes 3145736 | tf_op jit(solution)/shard_map/ppermute | solution.py:376
  3.0 5.5 %extrapolate.3.refs_3_ = bf16[3,512,256]{2,1,0:T(8,128)(2,1)} custom-call(s32[3]{0:T(128)} %constant.38.clone.order, s32[3,16]{1,0:T(4,128)} %bitcast.36, s32[1]{0:T(128)} %bitcast.1.inner, bf16[16384,128]{1,0:T(8,128)(2,1)} %bitcast.33, bf16[16,3,2,128,128]{4,3,2,1,0:T(8,128)(2,1)} %bitcast.30), custom_call_target="tpu_custom_call" | custom-call | flops 1000 | bytes 1000 | tf_op jit(solution)/shard_map/extrapolate/pallas_call | solution.py:216
  9.2 7.2 %collective-permute-start.1 = (bf16[3,512,256]{2,1,0:T(8,128)(2,1)}, bf16[3,512,256]{2,1,0:T(8,128)(2,1)}, u32[]{:S(2)}, u32[]{:S(2)}) collective-permute-start(bf16[3,512,256]{2,1,0:T(8,128)(2,1)} %extrapolate.3.refs_3_), channel_id=1, source_target_pairs={{0,4},{12,8},{1,5},{13,9},{2,6},{14,10},{3,7},{15,11},{16,20},{28,... | collective-permute-start | bytes 2359304 | tf_op jit(solution)/shard_map/ppermute | solution.py:376
  16.4 12.0 %extrapolate.4 = (bf16[6,512,256]{2,1,0:T(8,128)(2,1)}, bf16[7,512,256]{2,1,0:T(8,128)(2,1)}) custom-call(s32[13]{0:T(128)} %constant.39.clone.order, s32[3,16]{1,0:T(4,128)} %bitcast.37, s32[1]{0:T(128)} %bitcast.1.inner, bf16[16384,128]{1,0:T(8,128)(2,1)} %bitcast.34, bf16[16,3,2,128,128]{4,3,2,1,0:T(8,128)(2,1)} %bitcast.31), custom_call_target="tpu_custom_call" | custom-call | flops 1000 | bytes 1000 | tf_op jit(solution)/shard_map/extrapolate/pallas_call | solution.py:216
  31.1 1.3 collective-permute-start.9
  32.4 7.0 %collective-permute-start.7 = (bf16[6,512,256]{2,1,0:T(8,128)(2,1)}, bf16[6,512,256]{2,1,0:T(8,128)(2,1)}, u32[]{:S(2)}, u32[]{:S(2)}) collective-permute-start(bf16[6,512,256]{2,1,0:T(8,128)(2,1)} %get-tuple-element.27.refs_4_), channel_id=1, source_target_pairs={{0,4},{12,8},{1,5},{13,9},{2,6},{14,10},{3,7},{15,11},{16,20},{28,... | collective-permute-start | bytes 4718600 | tf_op jit(solution)/shard_map/ppermute | solution.py:376
  39.4 14.5 %extrapolate.5 = (bf16[7,512,256]{2,1,0:T(8,128)(2,1)}, bf16[7,512,256]{2,1,0:T(8,128)(2,1)}, bf16[2,512,256]{2,1,0:T(8,128)(2,1)}, bf16[7,512,256]{2,1,0:T(8,128)(2,1)}) custom-call(s32[16]{0:T(128)} %constant.40.clone.order, s32[3,16]{1,0:T(4,128)} %bitcast.38, s32[1]{0:T(128)} %bitcast.1.inner, bf16[16384,128]{1,0:T(8,128)(2,1)} %bitcast.35, ...), custom_call_target="tpu_custom_call" | custom-call | flops 1000 | bytes 1000 | tf_op jit(solution)/shard_map/extrapolate/pallas_call | solution.py:216
  54.7 1.2 copy-done.9
  55.9 13.5 %collective-permute-start.4 = (bf16[2,512,256]{2,1,0:T(8,128)(2,1)}, bf16[2,512,256]{2,1,0:T(8,128)(2,1)S(1)}, u32[]{:S(2)}, u32[]{:S(2)}) collective-permute-start(bf16[2,512,256]{2,1,0:T(8,128)(2,1)} %get-tuple-element.28.refs_1_), channel_id=1, source_target_pairs={{0,4},{12,8},{1,5},{13,9},{2,6},{14,10},{3,7},{15,11},{16,20},{28,... | collective-permute-start | bytes 1572872 | tf_op jit(solution)/shard_map/ppermute | solution.py:376
  69.4 8.0 %collective-permute-done.7.refs_7_ = bf16[6,512,256]{2,1,0:T(8,128)(2,1)} collective-permute-done((bf16[6,512,256]{2,1,0:T(8,128)(2,1)}, bf16[6,512,256]{2,1,0:T(8,128)(2,1)}, u32[]{:S(2)}, u32[]{:S(2)}) %collective-permute-start.7) | collective-permute-done | bytes 1572896 | tf_op jit(solution)/shard_map/ppermute | solution.py:376
  79.4 1.3 collective-permute-start.10
  80.7 46.2 %collective-permute-done.4.refs_4_ = bf16[2,512,256]{2,1,0:T(8,128)(2,1)S(1)} collective-permute-done((bf16[2,512,256]{2,1,0:T(8,128)(2,1)}, bf16[2,512,256]{2,1,0:T(8,128)(2,1)S(1)}, u32[]{:S(2)}, u32[]{:S(2)}) %collective-permute-start.4) | collective-permute-done | bytes 524320 | tf_op jit(solution)/shard_map/ppermute | solution.py:376
  128.0 4.5 %collective-permute-start.11 = (bf16[4,512,256]{2,1,0:T(8,128)(2,1)}, bf16[4,512,256]{2,1,0:T(8,128)(2,1)}, u32[]{:S(2)}, u32[]{:S(2)}) collective-permute-start(bf16[4,512,256]{2,1,0:T(8,128)(2,1)} %slice.48), channel_id=1, source_target_pairs={{0,12},{12,0},{1,13},{13,1},{2,14},{14,2},{3,15},{15,3},{16,28},{2... | collective-permute-start | bytes 3145736 | tf_op jit(solution)/shard_map/ppermute | solution.py:376
  133.5 3.3 %collective-permute-start.12 = (bf16[3,512,256]{2,1,0:T(8,128)(2,1)}, bf16[3,512,256]{2,1,0:T(8,128)(2,1)}, u32[]{:S(2)}, u32[]{:S(2)}) collective-permute-start(bf16[3,512,256]{2,1,0:T(8,128)(2,1)} %slice.49), channel_id=1, source_target_pairs={{0,12},{12,0},{1,13},{13,1},{2,14},{14,2},{3,15},{15,3},{16,28},{2... | collective-permute-start | bytes 2359304 | tf_op jit(solution)/shard_map/ppermute | solution.py:376
  137.5 1.3 collective-permute-start.13
  139.0 1.5 copy-done.2
  140.5 1.5 copy-done.6
  142.0 1.5 copy-done.7
  143.5 1.2 copy-done.11
  144.8 1.2 copy-done.13
  148.1 13.3 %product.1.refs_0_.refs_1_.refs_2_ = bf16[9,256,2048]{2,1,0:T(8,128)(2,1)S(1)} custom-call(s32[16]{0:T(128)S(1)} %get-tuple-element.36.near_ids, s32[16]{0:T(128)S(1)} %get-tuple-element.35.far_ids, s32[1]{0:T(128)} %bitcast.1.inner, bf16[7,512,256]{2,1,0:T(8,128)(2,1)S(1)} %copy-done.6, bf16[2,512,256]{2,1,0:T(8,128)(2,1)S(1)} %copy-done.16, ...), custom_call_target="tpu_custom_call" | custom-call | flops 1000 | bytes 1000 | tf_op jit(solution)/shard_map/product/pallas_call | solution.py:297
  161.4 11.7 %collective-permute-done.12.refs_12_ = bf16[3,512,256]{2,1,0:T(8,128)(2,1)} collective-permute-done((bf16[3,512,256]{2,1,0:T(8,128)(2,1)}, bf16[3,512,256]{2,1,0:T(8,128)(2,1)}, u32[]{:S(2)}, u32[]{:S(2)}) %collective-permute-start.12) | collective-permute-done | bytes 786464 | tf_op jit(solution)/shard_map/ppermute | solution.py:376
  173.1 8.3 %image.3.refs_4_ = f32[9,2,128,128]{3,2,1,0:T(8,128)S(1)} custom-call(s32[3]{0:T(128)S(1)} %pad_add_fusion.places.unused, s32[3]{0:T(128)S(1)} %pad_add_fusion.places.unused, s32[1]{0:T(128)} %bitcast.1.inner, bf16[9,256,2048]{2,1,0:T(8,128)(2,1)S(1)} %product.1.refs_0_.refs_1_.refs_2_, bf16[9,256,2048]{2,1,0:T(8,128)(2,1)S(1)} %product.1.refs_0_.refs_1_.refs_2_, ...), custom_call_target="tpu_custom_call" | custom-call | flops 1000 | bytes 1000 | tf_op jit(solution)/shard_map/image/pallas_call | solution.py:359
  181.5 4.8 %collective-permute-done.10.refs_3_ = bf16[5,512,256]{2,1,0:T(8,128)(2,1)} collective-permute-done((bf16[5,512,256]{2,1,0:T(8,128)(2,1)}, bf16[5,512,256]{2,1,0:T(8,128)(2,1)}, u32[]{:S(2)}, u32[]{:S(2)}) %collective-permute-start.10) | collective-permute-done | bytes 1310752 | tf_op jit(solution)/shard_map/ppermute | solution.py:376
  186.3 4.0 %image.4 = f32[6,2,128,128]{3,2,1,0:T(8,128)S(1)} custom-call(s32[1]{0:T(128)} %bitcast.places.unused, s32[1]{0:T(128)} %bitcast.places.unused, s32[1]{0:T(128)} %bitcast.1.inner, bf16[9,256,2048]{2,1,0:T(8,128)(2,1)S(1)} %product.1.refs_0_.refs_1_.refs_2_, bf16[3,512,256]{2,1,0:T(8,128)(2,1)S(1)} %copy-done.4, ...), custom_call_target="tpu_custom_call" | custom-call | flops 1000 | bytes 1000 | tf_op jit(solution)/shard_map/image/pallas_call | solution.py:359
  190.4 4.0 %collective-permute-done.13.refs_3_ = bf16[2,512,256]{2,1,0:T(8,128)(2,1)} collective-permute-done((bf16[2,512,256]{2,1,0:T(8,128)(2,1)}, bf16[2,512,256]{2,1,0:T(8,128)(2,1)}, u32[]{:S(2)}, u32[]{:S(2)}) %collective-permute-start.13) | collective-permute-done | bytes 524320 | tf_op jit(solution)/shard_map/ppermute | solution.py:376
  194.3 1.8 image.5
  196.3 1.6 collective-permute-done.14
  198.8 1.5 collective-permute-start.18
  201.7 2.7 %collective-permute-done.18 = bf16[2,2,128,128]{3,2,1,0:T(8,128)(2,1)S(1)} collective-permute-done((bf16[2,2,128,128]{3,2,1,0:T(8,128)(2,1)S(1)}, bf16[2,2,128,128]{3,2,1,0:T(8,128)(2,1)S(1)}, u32[]{:S(2)}, u32[]{:S(2)}) %collective-permute-start.18) | collective-permute-done | bytes 131104 | tf_op jit(solution)/shard_map/ppermute | solution.py:381
  204.4 4.4 %collective-permute-start.19 = (bf16[2,128,128]{2,1,0:T(8,128)(2,1)S(1)}, bf16[2,128,128]{2,1,0:T(8,128)(2,1)S(1)}, u32[]{:S(2)}, u32[]{:S(2)}) collective-permute-start(bf16[2,128,128]{2,1,0:T(8,128)(2,1)S(1)} %fusion.3), channel_id=1, source_target_pairs={{0,12},{1,13},{2,14},{4,8},{5,9},{6,10},{7,11},{8,4},{9,5},{10,6},... | collective-permute-start | bytes 196616 | tf_op jit(solution)/shard_map/ppermute | solution.py:381
  208.8 3.5 %collective-permute-done.19 = bf16[2,128,128]{2,1,0:T(8,128)(2,1)S(1)} collective-permute-done((bf16[2,128,128]{2,1,0:T(8,128)(2,1)S(1)}, bf16[2,128,128]{2,1,0:T(8,128)(2,1)S(1)}, u32[]{:S(2)}, u32[]{:S(2)}) %collective-permute-start.19) | collective-permute-done | bytes 65568 | tf_op jit(solution)/shard_map/ppermute | solution.py:381
  (71 shorter events, 14.3 us)
Async XLA Ops:
  0.0 30.1 %collective-permute-start.5 = (bf16[16,2,128,128]{3,2,1,0:T(8,128)(2,1)}, bf16[16,2,128,128]{3,2,1,0:T(8,128)(2,1)S(1)}, u32[]{:S(2)}, u32[]{:S(2)}) collective-permute-start(bf16[16,2,128,128]{3,2,1,0:T(8,128)(2,1)} %bitcast.28), channel_id=1, source_target_pairs={{0,4},{12,8},{4,0},{8,12},{1,5},{13,9},{5,1},{9,13},{2,6},{14,10},... | collective-permute-start | bytes 3145736 | tf_op jit(solution)/shard_map/ppermute | solution.py:376
  8.5 20.7 %collective-permute-start = (bf16[3,512,256]{2,1,0:T(8,128)(2,1)}, bf16[3,512,256]{2,1,0:T(8,128)(2,1)S(1)}, u32[]{:S(2)}, u32[]{:S(2)}) collective-permute-start(bf16[3,512,256]{2,1,0:T(8,128)(2,1)} %extrapolate.3.refs_3_), channel_id=1, source_target_pairs={{4,8},{8,4},{5,9},{9,5},{6,10},{10,6},{7,11},{11,7},{20,24},{24,20... | collective-permute-start | bytes 2359304 | tf_op jit(solution)/shard_map/ppermute | solution.py:376
  9.2 44.7 %collective-permute-start.1 = (bf16[3,512,256]{2,1,0:T(8,128)(2,1)}, bf16[3,512,256]{2,1,0:T(8,128)(2,1)}, u32[]{:S(2)}, u32[]{:S(2)}) collective-permute-start(bf16[3,512,256]{2,1,0:T(8,128)(2,1)} %extrapolate.3.refs_3_), channel_id=1, source_target_pairs={{0,4},{12,8},{1,5},{13,9},{2,6},{14,10},{3,7},{15,11},{16,20},{28,... | collective-permute-start | bytes 2359304 | tf_op jit(solution)/shard_map/ppermute | solution.py:376
  28.4 26.3 %collective-permute-start.3 = (bf16[6,512,256]{2,1,0:T(8,128)(2,1)}, bf16[6,512,256]{2,1,0:T(8,128)(2,1)S(1)}, u32[]{:S(2)}, u32[]{:S(2)}) collective-permute-start(bf16[6,512,256]{2,1,0:T(8,128)(2,1)} %get-tuple-element.27.refs_4_), channel_id=1, source_target_pairs={{4,8},{8,4},{5,9},{9,5},{6,10},{10,6},{7,11},{11,7},{20,24},{24,20... | collective-permute-start | bytes 4718600 | tf_op jit(solution)/shard_map/ppermute | solution.py:376
  31.1 47.2 %collective-permute-start.9 = (bf16[7,512,256]{2,1,0:T(8,128)(2,1)}, bf16[7,512,256]{2,1,0:T(8,128)(2,1)}, u32[]{:S(2)}, u32[]{:S(2)}) collective-permute-start(bf16[7,512,256]{2,1,0:T(8,128)(2,1)} %get-tuple-element.31.refs_5_), channel_id=1, source_target_pairs={{4,0},{8,12},{5,1},{9,13},{6,2},{10,14},{7,3},{11,15},{20,16},{24,... | collective-permute-start | bytes 5505032 | tf_op jit(solution)/shard_map/ppermute | solution.py:376
  32.4 45.1 %collective-permute-start.7 = (bf16[6,512,256]{2,1,0:T(8,128)(2,1)}, bf16[6,512,256]{2,1,0:T(8,128)(2,1)}, u32[]{:S(2)}, u32[]{:S(2)}) collective-permute-start(bf16[6,512,256]{2,1,0:T(8,128)(2,1)} %get-tuple-element.27.refs_4_), channel_id=1, source_target_pairs={{0,4},{12,8},{1,5},{13,9},{2,6},{14,10},{3,7},{15,11},{16,20},{28,... | collective-permute-start | bytes 4718600 | tf_op jit(solution)/shard_map/ppermute | solution.py:376
  39.3 38.9 %copy-start = (bf16[7,512,256]{2,1,0:T(8,128)(2,1)S(1)}, bf16[7,512,256]{2,1,0:T(8,128)(2,1)}, u32[]{:S(2)}) copy-start(bf16[7,512,256]{2,1,0:T(8,128)(2,1)} %get-tuple-element.31.refs_5_) | copy-start | bytes 5505028
  53.9 73.0 %collective-permute-start.2 = (bf16[7,512,256]{2,1,0:T(8,128)(2,1)}, bf16[7,512,256]{2,1,0:T(8,128)(2,1)S(1)}, u32[]{:S(2)}, u32[]{:S(2)}) collective-permute-start(bf16[7,512,256]{2,1,0:T(8,128)(2,1)} %get-tuple-element.26), channel_id=1, source_target_pairs={{0,4},{12,8},{4,0},{8,12},{1,5},{13,9},{5,1},{9,13},{2,6},{14,10},... | collective-permute-start | bytes 5505032 | tf_op jit(solution)/shard_map/ppermute | solution.py:376
  54.0 26.7 %collective-permute-start.6 = (bf16[3,512,256]{2,1,0:T(8,128)(2,1)}, bf16[3,512,256]{2,1,0:T(8,128)(2,1)S(1)}, u32[]{:S(2)}, u32[]{:S(2)}) collective-permute-start(bf16[3,512,256]{2,1,0:T(8,128)(2,1)} %collective-permute-done.1.refs_6_), channel_id=1, source_target_pairs={{4,8},{8,4},{5,9},{9,5},{6,10},{10,6},{7,11},{11,7},{20,24},{24,20... | collective-permute-start | bytes 2359304 | tf_op jit(solution)/shard_map/ppermute | solution.py:376
  55.9 71.0 %collective-permute-start.4 = (bf16[2,512,256]{2,1,0:T(8,128)(2,1)}, bf16[2,512,256]{2,1,0:T(8,128)(2,1)S(1)}, u32[]{:S(2)}, u32[]{:S(2)}) collective-permute-start(bf16[2,512,256]{2,1,0:T(8,128)(2,1)} %get-tuple-element.28.refs_1_), channel_id=1, source_target_pairs={{0,4},{12,8},{1,5},{13,9},{2,6},{14,10},{3,7},{15,11},{16,20},{28,... | collective-permute-start | bytes 1572872 | tf_op jit(solution)/shard_map/ppermute | solution.py:376
  77.5 104.0 %collective-permute-start.8 = (bf16[6,512,256]{2,1,0:T(8,128)(2,1)}, bf16[6,512,256]{2,1,0:T(8,128)(2,1)S(1)}, u32[]{:S(2)}, u32[]{:S(2)}) collective-permute-start(bf16[6,512,256]{2,1,0:T(8,128)(2,1)} %collective-permute-done.7.refs_7_), channel_id=1, source_target_pairs={{4,8},{8,4},{5,9},{9,5},{6,10},{10,6},{7,11},{11,7},{20,24},{24,20... | collective-permute-start | bytes 4718600 | tf_op jit(solution)/shard_map/ppermute | solution.py:376
  79.4 106.9 %collective-permute-start.10 = (bf16[5,512,256]{2,1,0:T(8,128)(2,1)}, bf16[5,512,256]{2,1,0:T(8,128)(2,1)}, u32[]{:S(2)}, u32[]{:S(2)}) collective-permute-start(bf16[5,512,256]{2,1,0:T(8,128)(2,1)} %slice.47), channel_id=1, source_target_pairs={{4,12},{8,0},{5,13},{9,1},{6,14},{10,2},{7,15},{11,3},{20,28},{24,... | collective-permute-start | bytes 3932168 | tf_op jit(solution)/shard_map/ppermute | solution.py:376
  80.7 52.8 %copy-start.3 = (bf16[3,512,256]{2,1,0:T(8,128)(2,1)}, bf16[3,512,256]{2,1,0:T(8,128)(2,1)S(1)}, u32[]{:S(2)}) copy-start(bf16[3,512,256]{2,1,0:T(8,128)(2,1)S(1)} %collective-permute-done.6.refs_1_) | copy-start | bytes 2359300
  126.9 6.6 %copy-start.17 = (bf16[2,512,256]{2,1,0:T(8,128)(2,1)}, bf16[2,512,256]{2,1,0:T(8,128)(2,1)S(1)}, u32[]{:S(2)}) copy-start(bf16[2,512,256]{2,1,0:T(8,128)(2,1)S(1)} %collective-permute-done.4.refs_4_) | copy-start | bytes 1572868
  126.9 6.6 %copy-start.1 = (bf16[7,512,256]{2,1,0:T(8,128)(2,1)}, bf16[7,512,256]{2,1,0:T(8,128)(2,1)S(1)}, u32[]{:S(2)}) copy-start(bf16[7,512,256]{2,1,0:T(8,128)(2,1)S(1)} %collective-permute-done.2.refs_3_.refs_5_) | copy-start | bytes 5505028
  128.0 10.9 %copy-start.19 = (s32[64,2]{0,1:T(2,128)S(1)}, s32[64,2]{0,1:T(2,128)}, u32[]{:S(2)}) copy-start(s32[64,2]{0,1:T(2,128)} %param.13) | copy-start | bytes 1540
  128.0 45.1 %collective-permute-start.11 = (bf16[4,512,256]{2,1,0:T(8,128)(2,1)}, bf16[4,512,256]{2,1,0:T(8,128)(2,1)}, u32[]{:S(2)}, u32[]{:S(2)}) collective-permute-start(bf16[4,512,256]{2,1,0:T(8,128)(2,1)} %slice.48), channel_id=1, source_target_pairs={{0,12},{12,0},{1,13},{13,1},{2,14},{14,2},{3,15},{15,3},{16,28},{2... | collective-permute-start | bytes 3145736 | tf_op jit(solution)/shard_map/ppermute | solution.py:376
  133.5 39.7 %collective-permute-start.12 = (bf16[3,512,256]{2,1,0:T(8,128)(2,1)}, bf16[3,512,256]{2,1,0:T(8,128)(2,1)}, u32[]{:S(2)}, u32[]{:S(2)}) collective-permute-start(bf16[3,512,256]{2,1,0:T(8,128)(2,1)} %slice.49), channel_id=1, source_target_pairs={{0,12},{12,0},{1,13},{13,1},{2,14},{14,2},{3,15},{15,3},{16,28},{2... | collective-permute-start | bytes 2359304 | tf_op jit(solution)/shard_map/ppermute | solution.py:376
  137.5 56.8 %collective-permute-start.13 = (bf16[2,512,256]{2,1,0:T(8,128)(2,1)}, bf16[2,512,256]{2,1,0:T(8,128)(2,1)}, u32[]{:S(2)}, u32[]{:S(2)}) collective-permute-start(bf16[2,512,256]{2,1,0:T(8,128)(2,1)} %slice.51), channel_id=1, source_target_pairs={{4,12},{8,0},{5,13},{9,1},{6,14},{10,2},{7,15},{11,3},{20,28},{24,... | collective-permute-start | bytes 1572872 | tf_op jit(solution)/shard_map/ppermute | solution.py:376
  139.0 1.5 copy-start.2
  140.5 1.5 copy-start.6
  148.1 25.0 %copy-start.5 = (bf16[3,512,256]{2,1,0:T(8,128)(2,1)S(1)}, bf16[3,512,256]{2,1,0:T(8,128)(2,1)}, u32[]{:S(2)}) copy-start(bf16[3,512,256]{2,1,0:T(8,128)(2,1)} %extrapolate.3.refs_3_) | copy-start | bytes 2359300
  148.1 25.0 %copy-start.8 = (bf16[6,512,256]{2,1,0:T(8,128)(2,1)S(1)}, bf16[6,512,256]{2,1,0:T(8,128)(2,1)}, u32[]{:S(2)}) copy-start(bf16[6,512,256]{2,1,0:T(8,128)(2,1)} %get-tuple-element.27.refs_4_) | copy-start | bytes 4718596
  148.1 25.0 %copy-start.10 = (bf16[6,512,256]{2,1,0:T(8,128)(2,1)S(1)}, bf16[6,512,256]{2,1,0:T(8,128)(2,1)}, u32[]{:S(2)}) copy-start(bf16[6,512,256]{2,1,0:T(8,128)(2,1)} %copy-done.9) | copy-start | bytes 4718596
  148.1 25.0 %copy-start.15 = (bf16[3,512,256]{2,1,0:T(8,128)(2,1)S(1)}, bf16[3,512,256]{2,1,0:T(8,128)(2,1)}, u32[]{:S(2)}) copy-start(bf16[3,512,256]{2,1,0:T(8,128)(2,1)} %copy-done.14) | copy-start | bytes 2359300
  161.4 24.9 %copy-start.4 = (bf16[3,512,256]{2,1,0:T(8,128)(2,1)S(1)}, bf16[3,512,256]{2,1,0:T(8,128)(2,1)}, u32[]{:S(2)}) copy-start(bf16[3,512,256]{2,1,0:T(8,128)(2,1)} %copy-done.3) | copy-start | bytes 2359300
  196.2 1.7 collective-permute-start.14
  198.0 2.3 %collective-permute-start.15 = (bf16[2,128,128]{2,1,0:T(8,128)(2,1)S(1)}, bf16[2,128,128]{2,1,0:T(8,128)(2,1)S(1)}, u32[]{:S(2)}, u32[]{:S(2)}) collective-permute-start(bf16[2,128,128]{2,1,0:T(8,128)(2,1)S(1)} %fusion.2), channel_id=1, source_target_pairs={{5,7},{9,11},{21,23},{25,27}} | collective-permute-start | bytes 196616 | tf_op jit(solution)/shard_map/ppermute | solution.py:381
  198.8 5.6 %collective-permute-start.18 = (bf16[2,2,128,128]{3,2,1,0:T(8,128)(2,1)S(1)}, bf16[2,2,128,128]{3,2,1,0:T(8,128)(2,1)S(1)}, u32[]{:S(2)}, u32[]{:S(2)}) collective-permute-start(bf16[2,2,128,128]{3,2,1,0:T(8,128)(2,1)S(1)} %select_convert_fusion.1), channel_id=1, source_target_pairs={{0,2},{1,3},{2,0},{3,1},{4,6},{5,7},{6,4},{7,5},{8,10},{9,11},{10,... | collective-permute-start | bytes 393224 | tf_op jit(solution)/shard_map/ppermute | solution.py:381
  200.3 8.5 %collective-permute-start.16 = (bf16[2,128,128]{2,1,0:T(8,128)(2,1)S(1)}, bf16[2,128,128]{2,1,0:T(8,128)(2,1)S(1)}, u32[]{:S(2)}, u32[]{:S(2)}) collective-permute-start(bf16[2,128,128]{2,1,0:T(8,128)(2,1)S(1)} %add_convert_fusion), channel_id=1, source_target_pairs={{7,15},{23,31}} | collective-permute-start | bytes 196616 | tf_op jit(solution)/shard_map/ppermute | solution.py:381
  201.0 7.8 %collective-permute-start.17 = (bf16[2,128,128]{2,1,0:T(8,128)(2,1)S(1)}, bf16[2,128,128]{2,1,0:T(8,128)(2,1)S(1)}, u32[]{:S(2)}, u32[]{:S(2)}) collective-permute-start(bf16[2,128,128]{2,1,0:T(8,128)(2,1)S(1)} %add_convert_fusion), channel_id=1, source_target_pairs={{11,15},{27,31}} | collective-permute-start | bytes 196616 | tf_op jit(solution)/shard_map/ppermute | solution.py:381
  204.4 8.0 %collective-permute-start.19 = (bf16[2,128,128]{2,1,0:T(8,128)(2,1)S(1)}, bf16[2,128,128]{2,1,0:T(8,128)(2,1)S(1)}, u32[]{:S(2)}, u32[]{:S(2)}) collective-permute-start(bf16[2,128,128]{2,1,0:T(8,128)(2,1)S(1)} %fusion.3), channel_id=1, source_target_pairs={{0,12},{1,13},{2,14},{4,8},{5,9},{6,10},{7,11},{8,4},{9,5},{10,6},... | collective-permute-start | bytes 196616 | tf_op jit(solution)/shard_map/ppermute | solution.py:381
  (8 other events, 9.1 us)

commit v9 on v8

--- a/solution.py
+++ b/solution.py
@@ -124,7 +124,7 @@
     step = pl.program_id(0)
     bands = operator.shape[1]
     pitch = 2 * blocks + 1
-    chunk = stage.shape[0] // pitch
+    chunk = stage.shape[0] // pitch - 1
     part_lines = lines.shape[0] // parts
 
     def column(block, band):
@@ -223,7 +223,7 @@
             in_specs=[pl.BlockSpec(memory_space=pltpu.HBM)] * 2,
             out_specs=out_specs,
             scratch_shapes=[
-                pltpu.VMEM((chunk * (2 * blocks + 1), size), jnp.float32),
+                pltpu.VMEM(((chunk + 1) * (2 * blocks + 1), size), jnp.float32),
                 pltpu.VMEM((count * bands if listed else blocks, rows, width), jnp.bfloat16),
                 pltpu.VMEM(flat.shape, jnp.bfloat16),
                 pltpu.VMEM((count,) + operator.shape[1:], jnp.bfloat16),

time: 214 us -> 214 us (level)
  no operation moved by 1% of the time
where the time goes in v9:
time: 214 us; the launch traced here: 213 us
  waiting for transfers between devices  82.6 us (39%)
  Pallas kernels  59.5 us (28%)
  starting transfers between devices  53.3 us (25%)
  local copies, waits for them, and re-layouts  16.3 us (8%)
    ppermute x14, waiting for transfers between devices, hand(): return lax.ppermute(value, 'shot', pairs)  74.7 us
    ppermute x14, starting transfers between devices, hand(): return lax.ppermute(value, 'shot', pairs)  45.3 us
    pallas_call x3, Pallas kernels, extrapolate_blocks(): pl.pallas_call(functools.partial(extrapolate_kernel, sets=sets, rows=rows...  32 us
    pallas_call x3, Pallas kernels, image_blocks(): pl.pallas_call(functools.partial(image_kernel, first=first, begins=begins...  14.2 us
    pallas_call x1, Pallas kernels, product_blocks(): pl.pallas_call(functools.partial(product_kernel, begins=begins), grid_spe...  13.3 us
    unnamed x40, local copies, waits for them, and re-layouts  12.1 us
    ppermute x6, starting transfers between devices, send_sum(): lax.ppermute(value.astype(jnp.bfloat16), ('shot', 'freq'), pairs)  7.99 us
    ppermute x6, waiting for transfers between devices, send_sum(): lax.ppermute(value.astype(jnp.bfloat16), ('shot', 'freq'), pairs)  7.84 us
  transfers between devices with their start and end apart: 20, of which 8 were waited for; matrix products, arithmetic and copies ran while one was open for 2% of the time, Pallas kernels for 27%

profile of v9, /device:TPU:0, one launch (start us, length us, event | category | flops | bytes accessed | tf_op | source)
XLA Modules:
  0.0 213.1 jit_solution(6972190101075801286)
XLA Ops:
  0.0 3.0 %collective-permute-start.5 = (bf16[16,2,128,128]{3,2,1,0:T(8,128)(2,1)}, bf16[16,2,128,128]{3,2,1,0:T(8,128)(2,1)S(1)}, u32[]{:S(2)}, u32[]{:S(2)}) collective-permute-start(bf16[16,2,128,128]{3,2,1,0:T(8,128)(2,1)} %bitcast.28), channel_id=1, source_target_pairs={{0,4},{12,8},{4,0},{8,12},{1,5},{13,9},{5,1},{9,13},{2,6},{14,10},... | collective-permute-start | bytes 3145736 | tf_op jit(solution)/shard_map/ppermute | solution.py:376
  3.0 5.5 %extrapolate.3.refs_3_ = bf16[3,512,256]{2,1,0:T(8,128)(2,1)} custom-call(s32[3]{0:T(128)} %constant.38.clone.order, s32[3,16]{1,0:T(4,128)} %bitcast.36, s32[1]{0:T(128)} %bitcast.1.inner, bf16[16384,128]{1,0:T(8,128)(2,1)} %bitcast.33, bf16[16,3,2,128,128]{4,3,2,1,0:T(8,128)(2,1)} %bitcast.30), custom_call_target="tpu_custom_call" | custom-call | flops 1000 | bytes 1000 | tf_op jit(solution)/shard_map/extrapolate/pallas_call | solution.py:216
  9.2 7.2 %collective-permute-start.1 = (bf16[3,512,256]{2,1,0:T(8,128)(2,1)}, bf16[3,512,256]{2,1,0:T(8,128)(2,1)}, u32[]{:S(2)}, u32[]{:S(2)}) collective-permute-start(bf16[3,512,256]{2,1,0:T(8,128)(2,1)} %extrapolate.3.refs_3_), channel_id=1, source_target_pairs={{0,4},{12,8},{1,5},{13,9},{2,6},{14,10},{3,7},{15,11},{16,20},{28,... | collective-permute-start | bytes 2359304 | tf_op jit(solution)/shard_map/ppermute | solution.py:376
  16.4 12.0 %extrapolate.4 = (bf16[6,512,256]{2,1,0:T(8,128)(2,1)}, bf16[7,512,256]{2,1,0:T(8,128)(2,1)}) custom-call(s32[13]{0:T(128)} %constant.39.clone.order, s32[3,16]{1,0:T(4,128)} %bitcast.37, s32[1]{0:T(128)} %bitcast.1.inner, bf16[16384,128]{1,0:T(8,128)(2,1)} %bitcast.34, bf16[16,3,2,128,128]{4,3,2,1,0:T(8,128)(2,1)} %bitcast.31), custom_call_target="tpu_custom_call" | custom-call | flops 1000 | bytes 1000 | tf_op jit(solution)/shard_map/extrapolate/pallas_call | solution.py:216
  31.1 1.3 collective-permute-start.9
  32.3 7.0 %collective-permute-start.7 = (bf16[6,512,256]{2,1,0:T(8,128)(2,1)}, bf16[6,512,256]{2,1,0:T(8,128)(2,1)}, u32[]{:S(2)}, u32[]{:S(2)}) collective-permute-start(bf16[6,512,256]{2,1,0:T(8,128)(2,1)} %get-tuple-element.27.refs_4_), channel_id=1, source_target_pairs={{0,4},{12,8},{1,5},{13,9},{2,6},{14,10},{3,7},{15,11},{16,20},{28,... | collective-permute-start | bytes 4718600 | tf_op jit(solution)/shard_map/ppermute | solution.py:376
  39.4 14.5 %extrapolate.5 = (bf16[7,512,256]{2,1,0:T(8,128)(2,1)}, bf16[7,512,256]{2,1,0:T(8,128)(2,1)}, bf16[2,512,256]{2,1,0:T(8,128)(2,1)}, bf16[7,512,256]{2,1,0:T(8,128)(2,1)}) custom-call(s32[16]{0:T(128)} %constant.40.clone.order, s32[3,16]{1,0:T(4,128)} %bitcast.38, s32[1]{0:T(128)} %bitcast.1.inner, bf16[16384,128]{1,0:T(8,128)(2,1)} %bitcast.35, ...), custom_call_target="tpu_custom_call" | custom-call | flops 1000 | bytes 1000 | tf_op jit(solution)/shard_map/extrapolate/pallas_call | solution.py:216
  54.7 1.2 copy-done.9
  55.9 13.5 %collective-permute-start.4 = (bf16[2,512,256]{2,1,0:T(8,128)(2,1)}, bf16[2,512,256]{2,1,0:T(8,128)(2,1)S(1)}, u32[]{:S(2)}, u32[]{:S(2)}) collective-permute-start(bf16[2,512,256]{2,1,0:T(8,128)(2,1)} %get-tuple-element.28.refs_1_), channel_id=1, source_target_pairs={{0,4},{12,8},{1,5},{13,9},{2,6},{14,10},{3,7},{15,11},{16,20},{28,... | collective-permute-start | bytes 1572872 | tf_op jit(solution)/shard_map/ppermute | solution.py:376
  69.4 8.0 %collective-permute-done.7.refs_7_ = bf16[6,512,256]{2,1,0:T(8,128)(2,1)} collective-permute-done((bf16[6,512,256]{2,1,0:T(8,128)(2,1)}, bf16[6,512,256]{2,1,0:T(8,128)(2,1)}, u32[]{:S(2)}, u32[]{:S(2)}) %collective-permute-start.7) | collective-permute-done | bytes 1572896 | tf_op jit(solution)/shard_map/ppermute | solution.py:376
  79.4 1.3 collective-permute-start.10
  80.7 46.2 %collective-permute-done.4.refs_4_ = bf16[2,512,256]{2,1,0:T(8,128)(2,1)S(1)} collective-permute-done((bf16[2,512,256]{2,1,0:T(8,128)(2,1)}, bf16[2,512,256]{2,1,0:T(8,128)(2,1)S(1)}, u32[]{:S(2)}, u32[]{:S(2)}) %collective-permute-start.4) | collective-permute-done | bytes 524320 | tf_op jit(solution)/shard_map/ppermute | solution.py:376
  128.0 4.5 %collective-permute-start.11 = (bf16[4,512,256]{2,1,0:T(8,128)(2,1)}, bf16[4,512,256]{2,1,0:T(8,128)(2,1)}, u32[]{:S(2)}, u32[]{:S(2)}) collective-permute-start(bf16[4,512,256]{2,1,0:T(8,128)(2,1)} %slice.48), channel_id=1, source_target_pairs={{0,12},{12,0},{1,13},{13,1},{2,14},{14,2},{3,15},{15,3},{16,28},{2... | collective-permute-start | bytes 3145736 | tf_op jit(solution)/shard_map/ppermute | solution.py:376
  133.5 3.3 %collective-permute-start.12 = (bf16[3,512,256]{2,1,0:T(8,128)(2,1)}, bf16[3,512,256]{2,1,0:T(8,128)(2,1)}, u32[]{:S(2)}, u32[]{:S(2)}) collective-permute-start(bf16[3,512,256]{2,1,0:T(8,128)(2,1)} %slice.49), channel_id=1, source_target_pairs={{0,12},{12,0},{1,13},{13,1},{2,14},{14,2},{3,15},{15,3},{16,28},{2... | collective-permute-start | bytes 2359304 | tf_op jit(solution)/shard_map/ppermute | solution.py:376
  137.5 1.3 collective-permute-start.13
  139.0 1.5 copy-done.2
  140.5 1.5 copy-done.6
  142.0 1.5 copy-done.7
  143.5 1.2 copy-done.11
  144.8 1.2 copy-done.13
  148.1 13.3 %product.1.refs_0_.refs_1_.refs_2_ = bf16[9,256,2048]{2,1,0:T(8,128)(2,1)S(1)} custom-call(s32[16]{0:T(128)S(1)} %get-tuple-element.36.near_ids, s32[16]{0:T(128)S(1)} %get-tuple-element.35.far_ids, s32[1]{0:T(128)} %bitcast.1.inner, bf16[7,512,256]{2,1,0:T(8,128)(2,1)S(1)} %copy-done.6, bf16[2,512,256]{2,1,0:T(8,128)(2,1)S(1)} %copy-done.16, ...), custom_call_target="tpu_custom_call" | custom-call | flops 1000 | bytes 1000 | tf_op jit(solution)/shard_map/product/pallas_call | solution.py:297
  161.4 11.7 %collective-permute-done.12.refs_12_ = bf16[3,512,256]{2,1,0:T(8,128)(2,1)} collective-permute-done((bf16[3,512,256]{2,1,0:T(8,128)(2,1)}, bf16[3,512,256]{2,1,0:T(8,128)(2,1)}, u32[]{:S(2)}, u32[]{:S(2)}) %collective-permute-start.12) | collective-permute-done | bytes 786464 | tf_op jit(solution)/shard_map/ppermute | solution.py:376
  173.1 8.3 %image.3.refs_4_ = f32[9,2,128,128]{3,2,1,0:T(8,128)S(1)} custom-call(s32[3]{0:T(128)S(1)} %pad_add_fusion.places.unused, s32[3]{0:T(128)S(1)} %pad_add_fusion.places.unused, s32[1]{0:T(128)} %bitcast.1.inner, bf16[9,256,2048]{2,1,0:T(8,128)(2,1)S(1)} %product.1.refs_0_.refs_1_.refs_2_, bf16[9,256,2048]{2,1,0:T(8,128)(2,1)S(1)} %product.1.refs_0_.refs_1_.refs_2_, ...), custom_call_target="tpu_custom_call" | custom-call | flops 1000 | bytes 1000 | tf_op jit(solution)/shard_map/image/pallas_call | solution.py:359
  181.5 4.8 %collective-permute-done.10.refs_3_ = bf16[5,512,256]{2,1,0:T(8,128)(2,1)} collective-permute-done((bf16[5,512,256]{2,1,0:T(8,128)(2,1)}, bf16[5,512,256]{2,1,0:T(8,128)(2,1)}, u32[]{:S(2)}, u32[]{:S(2)}) %collective-permute-start.10) | collective-permute-done | bytes 1310752 | tf_op jit(solution)/shard_map/ppermute | solution.py:376
  186.3 4.0 %image.4 = f32[6,2,128,128]{3,2,1,0:T(8,128)S(1)} custom-call(s32[1]{0:T(128)} %bitcast.places.unused, s32[1]{0:T(128)} %bitcast.places.unused, s32[1]{0:T(128)} %bitcast.1.inner, bf16[9,256,2048]{2,1,0:T(8,128)(2,1)S(1)} %product.1.refs_0_.refs_1_.refs_2_, bf16[3,512,256]{2,1,0:T(8,128)(2,1)S(1)} %copy-done.4, ...), custom_call_target="tpu_custom_call" | custom-call | flops 1000 | bytes 1000 | tf_op jit(solution)/shard_map/image/pallas_call | solution.py:359
  190.4 4.0 %collective-permute-done.13.refs_3_ = bf16[2,512,256]{2,1,0:T(8,128)(2,1)} collective-permute-done((bf16[2,512,256]{2,1,0:T(8,128)(2,1)}, bf16[2,512,256]{2,1,0:T(8,128)(2,1)}, u32[]{:S(2)}, u32[]{:S(2)}) %collective-permute-start.13) | collective-permute-done | bytes 524320 | tf_op jit(solution)/shard_map/ppermute | solution.py:376
  194.3 1.8 image.5
  196.3 1.6 collective-permute-done.14
  198.8 1.5 collective-permute-start.18
  201.7 2.7 %collective-permute-done.18 = bf16[2,2,128,128]{3,2,1,0:T(8,128)(2,1)S(1)} collective-permute-done((bf16[2,2,128,128]{3,2,1,0:T(8,128)(2,1)S(1)}, bf16[2,2,128,128]{3,2,1,0:T(8,128)(2,1)S(1)}, u32[]{:S(2)}, u32[]{:S(2)}) %collective-permute-start.18) | collective-permute-done | bytes 131104 | tf_op jit(solution)/shard_map/ppermute | solution.py:381
  204.4 4.4 %collective-permute-start.19 = (bf16[2,128,128]{2,1,0:T(8,128)(2,1)S(1)}, bf16[2,128,128]{2,1,0:T(8,128)(2,1)S(1)}, u32[]{:S(2)}, u32[]{:S(2)}) collective-permute-start(bf16[2,128,128]{2,1,0:T(8,128)(2,1)S(1)} %fusion.3), channel_id=1, source_target_pairs={{0,12},{1,13},{2,14},{4,8},{5,9},{6,10},{7,11},{8,4},{9,5},{10,6},... | collective-permute-start | bytes 196616 | tf_op jit(solution)/shard_map/ppermute | solution.py:381
  208.8 3.5 %collective-permute-done.19 = bf16[2,128,128]{2,1,0:T(8,128)(2,1)S(1)} collective-permute-done((bf16[2,128,128]{2,1,0:T(8,128)(2,1)S(1)}, bf16[2,128,128]{2,1,0:T(8,128)(2,1)S(1)}, u32[]{:S(2)}, u32[]{:S(2)}) %collective-permute-start.19) | collective-permute-done | bytes 65568 | tf_op jit(solution)/shard_map/ppermute | solution.py:381
  (71 shorter events, 14.3 us)
Async XLA Ops:
  0.0 30.1 %collective-permute-start.5 = (bf16[16,2,128,128]{3,2,1,0:T(8,128)(2,1)}, bf16[16,2,128,128]{3,2,1,0:T(8,128)(2,1)S(1)}, u32[]{:S(2)}, u32[]{:S(2)}) collective-permute-start(bf16[16,2,128,128]{3,2,1,0:T(8,128)(2,1)} %bitcast.28), channel_id=1, source_target_pairs={{0,4},{12,8},{4,0},{8,12},{1,5},{13,9},{5,1},{9,13},{2,6},{14,10},... | collective-permute-start | bytes 3145736 | tf_op jit(solution)/shard_map/ppermute | solution.py:376
  8.5 20.6 %collective-permute-start = (bf16[3,512,256]{2,1,0:T(8,128)(2,1)}, bf16[3,512,256]{2,1,0:T(8,128)(2,1)S(1)}, u32[]{:S(2)}, u32[]{:S(2)}) collective-permute-start(bf16[3,512,256]{2,1,0:T(8,128)(2,1)} %extrapolate.3.refs_3_), channel_id=1, source_target_pairs={{4,8},{8,4},{5,9},{9,5},{6,10},{10,6},{7,11},{11,7},{20,24},{24,20... | collective-permute-start | bytes 2359304 | tf_op jit(solution)/shard_map/ppermute | solution.py:376
  9.2 44.7 %collective-permute-start.1 = (bf16[3,512,256]{2,1,0:T(8,128)(2,1)}, bf16[3,512,256]{2,1,0:T(8,128)(2,1)}, u32[]{:S(2)}, u32[]{:S(2)}) collective-permute-start(bf16[3,512,256]{2,1,0:T(8,128)(2,1)} %extrapolate.3.refs_3_), channel_id=1, source_target_pairs={{0,4},{12,8},{1,5},{13,9},{2,6},{14,10},{3,7},{15,11},{16,20},{28,... | collective-permute-start | bytes 2359304 | tf_op jit(solution)/shard_map/ppermute | solution.py:376
  28.4 26.3 %collective-permute-start.3 = (bf16[6,512,256]{2,1,0:T(8,128)(2,1)}, bf16[6,512,256]{2,1,0:T(8,128)(2,1)S(1)}, u32[]{:S(2)}, u32[]{:S(2)}) collective-permute-start(bf16[6,512,256]{2,1,0:T(8,128)(2,1)} %get-tuple-element.27.refs_4_), channel_id=1, source_target_pairs={{4,8},{8,4},{5,9},{9,5},{6,10},{10,6},{7,11},{11,7},{20,24},{24,20... | collective-permute-start | bytes 4718600 | tf_op jit(solution)/shard_map/ppermute | solution.py:376
  31.1 47.2 %collective-permute-start.9 = (bf16[7,512,256]{2,1,0:T(8,128)(2,1)}, bf16[7,512,256]{2,1,0:T(8,128)(2,1)}, u32[]{:S(2)}, u32[]{:S(2)}) collective-permute-start(bf16[7,512,256]{2,1,0:T(8,128)(2,1)} %get-tuple-element.31.refs_5_), channel_id=1, source_target_pairs={{4,0},{8,12},{5,1},{9,13},{6,2},{10,14},{7,3},{11,15},{20,16},{24,... | collective-permute-start | bytes 5505032 | tf_op jit(solution)/shard_map/ppermute | solution.py:376
  32.3 45.1 %collective-permute-start.7 = (bf16[6,512,256]{2,1,0:T(8,128)(2,1)}, bf16[6,512,256]{2,1,0:T(8,128)(2,1)}, u32[]{:S(2)}, u32[]{:S(2)}) collective-permute-start(bf16[6,512,256]{2,1,0:T(8,128)(2,1)} %get-tuple-element.27.refs_4_), channel_id=1, source_target_pairs={{0,4},{12,8},{1,5},{13,9},{2,6},{14,10},{3,7},{15,11},{16,20},{28,... | collective-permute-start | bytes 4718600 | tf_op jit(solution)/shard_map/ppermute | solution.py:376
  39.3 38.9 %copy-start = (bf16[7,512,256]{2,1,0:T(8,128)(2,1)S(1)}, bf16[7,512,256]{2,1,0:T(8,128)(2,1)}, u32[]{:S(2)}) copy-start(bf16[7,512,256]{2,1,0:T(8,128)(2,1)} %get-tuple-element.31.refs_5_) | copy-start | bytes 5505028
  53.9 73.0 %collective-permute-start.2 = (bf16[7,512,256]{2,1,0:T(8,128)(2,1)}, bf16[7,512,256]{2,1,0:T(8,128)(2,1)S(1)}, u32[]{:S(2)}, u32[]{:S(2)}) collective-permute-start(bf16[7,512,256]{2,1,0:T(8,128)(2,1)} %get-tuple-element.26), channel_id=1, source_target_pairs={{0,4},{12,8},{4,0},{8,12},{1,5},{13,9},{5,1},{9,13},{2,6},{14,10},... | collective-permute-start | bytes 5505032 | tf_op jit(solution)/shard_map/ppermute | solution.py:376
  54.0 26.7 %collective-permute-start.6 = (bf16[3,512,256]{2,1,0:T(8,128)(2,1)}, bf16[3,512,256]{2,1,0:T(8,128)(2,1)S(1)}, u32[]{:S(2)}, u32[]{:S(2)}) collective-permute-start(bf16[3,512,256]{2,1,0:T(8,128)(2,1)} %collective-permute-done.1.refs_6_), channel_id=1, source_target_pairs={{4,8},{8,4},{5,9},{9,5},{6,10},{10,6},{7,11},{11,7},{20,24},{24,20... | collective-permute-start | bytes 2359304 | tf_op jit(solution)/shard_map/ppermute | solution.py:376
  55.9 71.0 %collective-permute-start.4 = (bf16[2,512,256]{2,1,0:T(8,128)(2,1)}, bf16[2,512,256]{2,1,0:T(8,128)(2,1)S(1)}, u32[]{:S(2)}, u32[]{:S(2)}) collective-permute-start(bf16[2,512,256]{2,1,0:T(8,128)(2,1)} %get-tuple-element.28.refs_1_), channel_id=1, source_target_pairs={{0,4},{12,8},{1,5},{13,9},{2,6},{14,10},{3,7},{15,11},{16,20},{28,... | collective-permute-start | bytes 1572872 | tf_op jit(solution)/shard_map/ppermute | solution.py:376
  77.5 104.0 %collective-permute-start.8 = (bf16[6,512,256]{2,1,0:T(8,128)(2,1)}, bf16[6,512,256]{2,1,0:T(8,128)(2,1)S(1)}, u32[]{:S(2)}, u32[]{:S(2)}) collective-permute-start(bf16[6,512,256]{2,1,0:T(8,128)(2,1)} %collective-permute-done.7.refs_7_), channel_id=1, source_target_pairs={{4,8},{8,4},{5,9},{9,5},{6,10},{10,6},{7,11},{11,7},{20,24},{24,20... | collective-permute-start | bytes 4718600 | tf_op jit(solution)/shard_map/ppermute | solution.py:376
  79.4 106.9 %collective-permute-start.10 = (bf16[5,512,256]{2,1,0:T(8,128)(2,1)}, bf16[5,512,256]{2,1,0:T(8,128)(2,1)}, u32[]{:S(2)}, u32[]{:S(2)}) collective-permute-start(bf16[5,512,256]{2,1,0:T(8,128)(2,1)} %slice.47), channel_id=1, source_target_pairs={{4,12},{8,0},{5,13},{9,1},{6,14},{10,2},{7,15},{11,3},{20,28},{24,... | collective-permute-start | bytes 3932168 | tf_op jit(solution)/shard_map/ppermute | solution.py:376
  80.7 52.8 %copy-start.3 = (bf16[3,512,256]{2,1,0:T(8,128)(2,1)}, bf16[3,512,256]{2,1,0:T(8,128)(2,1)S(1)}, u32[]{:S(2)}) copy-start(bf16[3,512,256]{2,1,0:T(8,128)(2,1)S(1)} %collective-permute-done.6.refs_1_) | copy-start | bytes 2359300
  126.9 6.6 %copy-start.17 = (bf16[2,512,256]{2,1,0:T(8,128)(2,1)}, bf16[2,512,256]{2,1,0:T(8,128)(2,1)S(1)}, u32[]{:S(2)}) copy-start(bf16[2,512,256]{2,1,0:T(8,128)(2,1)S(1)} %collective-permute-done.4.refs_4_) | copy-start | bytes 1572868
  126.9 6.6 %copy-start.1 = (bf16[7,512,256]{2,1,0:T(8,128)(2,1)}, bf16[7,512,256]{2,1,0:T(8,128)(2,1)S(1)}, u32[]{:S(2)}) copy-start(bf16[7,512,256]{2,1,0:T(8,128)(2,1)S(1)} %collective-permute-done.2.refs_3_.refs_5_) | copy-start | bytes 5505028
  128.0 10.9 %copy-start.19 = (s32[64,2]{0,1:T(2,128)S(1)}, s32[64,2]{0,1:T(2,128)}, u32[]{:S(2)}) copy-start(s32[64,2]{0,1:T(2,128)} %param.13) | copy-start | bytes 1540
  128.0 45.1 %collective-permute-start.11 = (bf16[4,512,256]{2,1,0:T(8,128)(2,1)}, bf16[4,512,256]{2,1,0:T(8,128)(2,1)}, u32[]{:S(2)}, u32[]{:S(2)}) collective-permute-start(bf16[4,512,256]{2,1,0:T(8,128)(2,1)} %slice.48), channel_id=1, source_target_pairs={{0,12},{12,0},{1,13},{13,1},{2,14},{14,2},{3,15},{15,3},{16,28},{2... | collective-permute-start | bytes 3145736 | tf_op jit(solution)/shard_map/ppermute | solution.py:376
  133.5 39.7 %collective-permute-start.12 = (bf16[3,512,256]{2,1,0:T(8,128)(2,1)}, bf16[3,512,256]{2,1,0:T(8,128)(2,1)}, u32[]{:S(2)}, u32[]{:S(2)}) collective-permute-start(bf16[3,512,256]{2,1,0:T(8,128)(2,1)} %slice.49), channel_id=1, source_target_pairs={{0,12},{12,0},{1,13},{13,1},{2,14},{14,2},{3,15},{15,3},{16,28},{2... | collective-permute-start | bytes 2359304 | tf_op jit(solution)/shard_map/ppermute | solution.py:376
  137.5 56.8 %collective-permute-start.13 = (bf16[2,512,256]{2,1,0:T(8,128)(2,1)}, bf16[2,512,256]{2,1,0:T(8,128)(2,1)}, u32[]{:S(2)}, u32[]{:S(2)}) collective-permute-start(bf16[2,512,256]{2,1,0:T(8,128)(2,1)} %slice.51), channel_id=1, source_target_pairs={{4,12},{8,0},{5,13},{9,1},{6,14},{10,2},{7,15},{11,3},{20,28},{24,... | collective-permute-start | bytes 1572872 | tf_op jit(solution)/shard_map/ppermute | solution.py:376
  139.0 1.5 copy-start.2
  140.5 1.5 copy-start.6
  148.1 25.0 %copy-start.5 = (bf16[3,512,256]{2,1,0:T(8,128)(2,1)S(1)}, bf16[3,512,256]{2,1,0:T(8,128)(2,1)}, u32[]{:S(2)}) copy-start(bf16[3,512,256]{2,1,0:T(8,128)(2,1)} %extrapolate.3.refs_3_) | copy-start | bytes 2359300
  148.1 25.0 %copy-start.8 = (bf16[6,512,256]{2,1,0:T(8,128)(2,1)S(1)}, bf16[6,512,256]{2,1,0:T(8,128)(2,1)}, u32[]{:S(2)}) copy-start(bf16[6,512,256]{2,1,0:T(8,128)(2,1)} %get-tuple-element.27.refs_4_) | copy-start | bytes 4718596
  148.1 25.0 %copy-start.10 = (bf16[6,512,256]{2,1,0:T(8,128)(2,1)S(1)}, bf16[6,512,256]{2,1,0:T(8,128)(2,1)}, u32[]{:S(2)}) copy-start(bf16[6,512,256]{2,1,0:T(8,128)(2,1)} %copy-done.9) | copy-start | bytes 4718596
  148.1 25.0 %copy-start.15 = (bf16[3,512,256]{2,1,0:T(8,128)(2,1)S(1)}, bf16[3,512,256]{2,1,0:T(8,128)(2,1)}, u32[]{:S(2)}) copy-start(bf16[3,512,256]{2,1,0:T(8,128)(2,1)} %copy-done.14) | copy-start | bytes 2359300
  161.4 24.9 %copy-start.4 = (bf16[3,512,256]{2,1,0:T(8,128)(2,1)S(1)}, bf16[3,512,256]{2,1,0:T(8,128)(2,1)}, u32[]{:S(2)}) copy-start(bf16[3,512,256]{2,1,0:T(8,128)(2,1)} %copy-done.3) | copy-start | bytes 2359300
  196.2 1.7 collective-permute-start.14
  198.0 2.3 %collective-permute-start.15 = (bf16[2,128,128]{2,1,0:T(8,128)(2,1)S(1)}, bf16[2,128,128]{2,1,0:T(8,128)(2,1)S(1)}, u32[]{:S(2)}, u32[]{:S(2)}) collective-permute-start(bf16[2,128,128]{2,1,0:T(8,128)(2,1)S(1)} %fusion.2), channel_id=1, source_target_pairs={{5,7},{9,11},{21,23},{25,27}} | collective-permute-start | bytes 196616 | tf_op jit(solution)/shard_map/ppermute | solution.py:381
  198.8 5.6 %collective-permute-start.18 = (bf16[2,2,128,128]{3,2,1,0:T(8,128)(2,1)S(1)}, bf16[2,2,128,128]{3,2,1,0:T(8,128)(2,1)S(1)}, u32[]{:S(2)}, u32[]{:S(2)}) collective-permute-start(bf16[2,2,128,128]{3,2,1,0:T(8,128)(2,1)S(1)} %select_convert_fusion.1), channel_id=1, source_target_pairs={{0,2},{1,3},{2,0},{3,1},{4,6},{5,7},{6,4},{7,5},{8,10},{9,11},{10,... | collective-permute-start | bytes 393224 | tf_op jit(solution)/shard_map/ppermute | solution.py:381
  200.3 8.5 %collective-permute-start.16 = (bf16[2,128,128]{2,1,0:T(8,128)(2,1)S(1)}, bf16[2,128,128]{2,1,0:T(8,128)(2,1)S(1)}, u32[]{:S(2)}, u32[]{:S(2)}) collective-permute-start(bf16[2,128,128]{2,1,0:T(8,128)(2,1)S(1)} %add_convert_fusion), channel_id=1, source_target_pairs={{7,15},{23,31}} | collective-permute-start | bytes 196616 | tf_op jit(solution)/shard_map/ppermute | solution.py:381
  201.0 7.8 %collective-permute-start.17 = (bf16[2,128,128]{2,1,0:T(8,128)(2,1)S(1)}, bf16[2,128,128]{2,1,0:T(8,128)(2,1)S(1)}, u32[]{:S(2)}, u32[]{:S(2)}) collective-permute-start(bf16[2,128,128]{2,1,0:T(8,128)(2,1)S(1)} %add_convert_fusion), channel_id=1, source_target_pairs={{11,15},{27,31}} | collective-permute-start | bytes 196616 | tf_op jit(solution)/shard_map/ppermute | solution.py:381
  204.4 8.0 %collective-permute-start.19 = (bf16[2,128,128]{2,1,0:T(8,128)(2,1)S(1)}, bf16[2,128,128]{2,1,0:T(8,128)(2,1)S(1)}, u32[]{:S(2)}, u32[]{:S(2)}) collective-permute-start(bf16[2,128,128]{2,1,0:T(8,128)(2,1)S(1)} %fusion.3), channel_id=1, source_target_pairs={{0,12},{1,13},{2,14},{4,8},{5,9},{6,10},{7,11},{8,4},{9,5},{10,6},... | collective-permute-start | bytes 196616 | tf_op jit(solution)/shard_map/ppermute | solution.py:381
  (8 other events, 9.1 us)

commit v10 on v9

--- a/solution.py
+++ b/solution.py
@@ -118,8 +118,8 @@
 
 
 def extrapolate_kernel(order, offsets, inner, field, operator, *refs, sets, rows, blocks, parts, listed, swap):
-    stage, apart, lines, weights, field_sems, weight_sems = refs[-6:]
-    outs = refs[:-6]
+    stage, spare, apart, lines, weights, field_sems, weight_sems = refs[-7:]
+    outs = refs[:-7]
     sizes = [len(one) for one in sets]
     step = pl.program_id(0)
     bands = operator.shape[1]
@@ -148,18 +148,21 @@
         else:
             wanted = list(range(blocks))
 
-        def split(n, carry):
-            for row in range(chunk):
-                here = pl.ds(pl.multiple_of((n * chunk + row) * 2 * blocks, 2 * blocks), 2 * blocks)
-                stage[pl.ds(row * pitch, 2 * blocks), :] = lines[here, :].astype(jnp.float32)
-            to = pl.ds(pl.multiple_of(n * chunk, chunk), chunk)
-            for slot, block in enumerate(wanted):
-                for half in range(2):
-                    picked = stage[pl.ds(2 * block + half, chunk, stride=pitch), :]
-                    apart[slot, to, half * 128:(half + 1) * 128] = picked.astype(jnp.bfloat16)
+        def split(pair, carry):
+            stages = [(2 * pair, stage), (2 * pair + 1, spare)]
+            for n, held in stages:
+                for row in range(chunk):
+                    here = pl.ds(pl.multiple_of((n * chunk + row) * 2 * blocks, 2 * blocks), 2 * blocks)
+                    held[pl.ds(row * pitch, 2 * blocks), :] = lines[here, :].astype(jnp.float32)
+            for n, held in stages:
+                to = pl.ds(pl.multiple_of(n * chunk, chunk), chunk)
+                for slot, block in enumerate(wanted):
+                    for half in range(2):
+                        picked = held[pl.ds(2 * block + half, chunk, stride=pitch), :]
+                        apart[slot, to, half * 128:(half + 1) * 128] = picked.astype(jnp.bfloat16)
             return carry
 
-        steps = rows // chunk // parts
+        steps = rows // (2 * chunk) // parts
         for part in range(parts):
             field_copy(part).wait()
             lax.fori_loop(part * steps, (part + 1) * steps, split, 0)
@@ -223,6 +226,7 @@
             in_specs=[pl.BlockSpec(memory_space=pltpu.HBM)] * 2,
             out_specs=out_specs,
             scratch_shapes=[
+                pltpu.VMEM(((chunk + 1) * (2 * blocks + 1), size), jnp.float32),
                 pltpu.VMEM(((chunk + 1) * (2 * blocks + 1), size), jnp.float32),
                 pltpu.VMEM((count * bands if listed else blocks, rows, width), jnp.bfloat16),
                 pltpu.VMEM(flat.shape, jnp.bfloat16),

time: 214 us -> 214 us (level)
  no operation moved by 1% of the time
where the time goes in v10:
time: 214 us; the launch traced here: 213 us
  waiting for transfers between devices  82.5 us (39%)
  Pallas kernels  59.5 us (28%)
  starting transfers between devices  53.3 us (25%)
  local copies, waits for them, and re-layouts  16.3 us (8%)
    ppermute x14, waiting for transfers between devices, hand(): return lax.ppermute(value, 'shot', pairs)  74.7 us
    ppermute x14, starting transfers between devices, hand(): return lax.ppermute(value, 'shot', pairs)  45.3 us
    pallas_call x3, Pallas kernels, extrapolate_blocks(): pl.pallas_call(functools.partial(extrapolate_kernel, sets=sets, rows=rows...  32.1 us
    pallas_call x3, Pallas kernels, image_blocks(): pl.pallas_call(functools.partial(image_kernel, first=first, begins=begins...  14.2 us
    pallas_call x1, Pallas kernels, product_blocks(): pl.pallas_call(functools.partial(product_kernel, begins=begins), grid_spe...  13.3 us
    unnamed x40, local copies, waits for them, and re-layouts  12.1 us
    ppermute x6, starting transfers between devices, send_sum(): lax.ppermute(value.astype(jnp.bfloat16), ('shot', 'freq'), pairs)  7.99 us
    ppermute x6, waiting for transfers between devices, send_sum(): lax.ppermute(value.astype(jnp.bfloat16), ('shot', 'freq'), pairs)  7.84 us
  transfers between devices with their start and end apart: 20, of which 8 were waited for; matrix products, arithmetic and copies ran while one was open for 2% of the time, Pallas kernels for 27%

profile of v10, /device:TPU:0, one launch (start us, length us, event | category | flops | bytes accessed | tf_op | source)
XLA Modules:
  0.0 213.1 jit_solution(18292134069830853706)
XLA Ops:
  0.0 3.0 %collective-permute-start.5 = (bf16[16,2,128,128]{3,2,1,0:T(8,128)(2,1)}, bf16[16,2,128,128]{3,2,1,0:T(8,128)(2,1)S(1)}, u32[]{:S(2)}, u32[]{:S(2)}) collective-permute-start(bf16[16,2,128,128]{3,2,1,0:T(8,128)(2,1)} %bitcast.28), channel_id=1, source_target_pairs={{0,4},{12,8},{4,0},{8,12},{1,5},{13,9},{5,1},{9,13},{2,6},{14,10},... | collective-permute-start | bytes 3145736 | tf_op jit(solution)/shard_map/ppermute | solution.py:380
  3.0 5.5 %extrapolate.3.refs_3_ = bf16[3,512,256]{2,1,0:T(8,128)(2,1)} custom-call(s32[3]{0:T(128)} %constant.38.clone.order, s32[3,16]{1,0:T(4,128)} %bitcast.36, s32[1]{0:T(128)} %bitcast.1.inner, bf16[16384,128]{1,0:T(8,128)(2,1)} %bitcast.33, bf16[16,3,2,128,128]{4,3,2,1,0:T(8,128)(2,1)} %bitcast.30), custom_call_target="tpu_custom_call" | custom-call | flops 1000 | bytes 1000 | tf_op jit(solution)/shard_map/extrapolate/pallas_call | solution.py:219
  9.2 7.2 %collective-permute-start.1 = (bf16[3,512,256]{2,1,0:T(8,128)(2,1)}, bf16[3,512,256]{2,1,0:T(8,128)(2,1)}, u32[]{:S(2)}, u32[]{:S(2)}) collective-permute-start(bf16[3,512,256]{2,1,0:T(8,128)(2,1)} %extrapolate.3.refs_3_), channel_id=1, source_target_pairs={{0,4},{12,8},{1,5},{13,9},{2,6},{14,10},{3,7},{15,11},{16,20},{28,... | collective-permute-start | bytes 2359304 | tf_op jit(solution)/shard_map/ppermute | solution.py:380
  16.4 12.0 %extrapolate.4 = (bf16[6,512,256]{2,1,0:T(8,128)(2,1)}, bf16[7,512,256]{2,1,0:T(8,128)(2,1)}) custom-call(s32[13]{0:T(128)} %constant.39.clone.order, s32[3,16]{1,0:T(4,128)} %bitcast.37, s32[1]{0:T(128)} %bitcast.1.inner, bf16[16384,128]{1,0:T(8,128)(2,1)} %bitcast.34, bf16[16,3,2,128,128]{4,3,2,1,0:T(8,128)(2,1)} %bitcast.31), custom_call_target="tpu_custom_call" | custom-call | flops 1000 | bytes 1000 | tf_op jit(solution)/shard_map/extrapolate/pallas_call | solution.py:219
  31.1 1.3 collective-permute-start.9
  32.4 7.0 %collective-permute-start.7 = (bf16[6,512,256]{2,1,0:T(8,128)(2,1)}, bf16[6,512,256]{2,1,0:T(8,128)(2,1)}, u32[]{:S(2)}, u32[]{:S(2)}) collective-permute-start(bf16[6,512,256]{2,1,0:T(8,128)(2,1)} %get-tuple-element.27.refs_4_), channel_id=1, source_target_pairs={{0,4},{12,8},{1,5},{13,9},{2,6},{14,10},{3,7},{15,11},{16,20},{28,... | collective-permute-start | bytes 4718600 | tf_op jit(solution)/shard_map/ppermute | solution.py:380
  39.4 14.6 %extrapolate.5 = (bf16[7,512,256]{2,1,0:T(8,128)(2,1)}, bf16[7,512,256]{2,1,0:T(8,128)(2,1)}, bf16[2,512,256]{2,1,0:T(8,128)(2,1)}, bf16[7,512,256]{2,1,0:T(8,128)(2,1)}) custom-call(s32[16]{0:T(128)} %constant.40.clone.order, s32[3,16]{1,0:T(4,128)} %bitcast.38, s32[1]{0:T(128)} %bitcast.1.inner, bf16[16384,128]{1,0:T(8,128)(2,1)} %bitcast.35, ...), custom_call_target="tpu_custom_call" | custom-call | flops 1000 | bytes 1000 | tf_op jit(solution)/shard_map/extrapolate/pallas_call | solution.py:219
  54.8 1.2 copy-done.9
  55.9 13.5 %collective-permute-start.4 = (bf16[2,512,256]{2,1,0:T(8,128)(2,1)}, bf16[2,512,256]{2,1,0:T(8,128)(2,1)S(1)}, u32[]{:S(2)}, u32[]{:S(2)}) collective-permute-start(bf16[2,512,256]{2,1,0:T(8,128)(2,1)} %get-tuple-element.28.refs_1_), channel_id=1, source_target_pairs={{0,4},{12,8},{1,5},{13,9},{2,6},{14,10},{3,7},{15,11},{16,20},{28,... | collective-permute-start | bytes 1572872 | tf_op jit(solution)/shard_map/ppermute | solution.py:380
  69.5 8.0 %collective-permute-done.7.refs_7_ = bf16[6,512,256]{2,1,0:T(8,128)(2,1)} collective-permute-done((bf16[6,512,256]{2,1,0:T(8,128)(2,1)}, bf16[6,512,256]{2,1,0:T(8,128)(2,1)}, u32[]{:S(2)}, u32[]{:S(2)}) %collective-permute-start.7) | collective-permute-done | bytes 1572896 | tf_op jit(solution)/shard_map/ppermute | solution.py:380
  79.4 1.3 collective-permute-start.10
  80.7 46.2 %collective-permute-done.4.refs_4_ = bf16[2,512,256]{2,1,0:T(8,128)(2,1)S(1)} collective-permute-done((bf16[2,512,256]{2,1,0:T(8,128)(2,1)}, bf16[2,512,256]{2,1,0:T(8,128)(2,1)S(1)}, u32[]{:S(2)}, u32[]{:S(2)}) %collective-permute-start.4) | collective-permute-done | bytes 524320 | tf_op jit(solution)/shard_map/ppermute | solution.py:380
  128.0 4.5 %collective-permute-start.11 = (bf16[4,512,256]{2,1,0:T(8,128)(2,1)}, bf16[4,512,256]{2,1,0:T(8,128)(2,1)}, u32[]{:S(2)}, u32[]{:S(2)}) collective-permute-start(bf16[4,512,256]{2,1,0:T(8,128)(2,1)} %slice.48), channel_id=1, source_target_pairs={{0,12},{12,0},{1,13},{13,1},{2,14},{14,2},{3,15},{15,3},{16,28},{2... | collective-permute-start | bytes 3145736 | tf_op jit(solution)/shard_map/ppermute | solution.py:380
  133.5 3.3 %collective-permute-start.12 = (bf16[3,512,256]{2,1,0:T(8,128)(2,1)}, bf16[3,512,256]{2,1,0:T(8,128)(2,1)}, u32[]{:S(2)}, u32[]{:S(2)}) collective-permute-start(bf16[3,512,256]{2,1,0:T(8,128)(2,1)} %slice.49), channel_id=1, source_target_pairs={{0,12},{12,0},{1,13},{13,1},{2,14},{14,2},{3,15},{15,3},{16,28},{2... | collective-permute-start | bytes 2359304 | tf_op jit(solution)/shard_map/ppermute | solution.py:380
  137.5 1.3 collective-permute-start.13
  139.0 1.5 copy-done.2
  140.5 1.5 copy-done.6
  142.0 1.5 copy-done.7
  143.5 1.2 copy-done.11
  144.8 1.2 copy-done.13
  148.1 13.3 %product.1.refs_0_.refs_1_.refs_2_ = bf16[9,256,2048]{2,1,0:T(8,128)(2,1)S(1)} custom-call(s32[16]{0:T(128)S(1)} %get-tuple-element.36.near_ids, s32[16]{0:T(128)S(1)} %get-tuple-element.35.far_ids, s32[1]{0:T(128)} %bitcast.1.inner, bf16[7,512,256]{2,1,0:T(8,128)(2,1)S(1)} %copy-done.6, bf16[2,512,256]{2,1,0:T(8,128)(2,1)S(1)} %copy-done.16, ...), custom_call_target="tpu_custom_call" | custom-call | flops 1000 | bytes 1000 | tf_op jit(solution)/shard_map/product/pallas_call | solution.py:301
  161.4 11.7 %collective-permute-done.12.refs_12_ = bf16[3,512,256]{2,1,0:T(8,128)(2,1)} collective-permute-done((bf16[3,512,256]{2,1,0:T(8,128)(2,1)}, bf16[3,512,256]{2,1,0:T(8,128)(2,1)}, u32[]{:S(2)}, u32[]{:S(2)}) %collective-permute-start.12) | collective-permute-done | bytes 786464 | tf_op jit(solution)/shard_map/ppermute | solution.py:380
  173.1 8.3 %image.3.refs_4_ = f32[9,2,128,128]{3,2,1,0:T(8,128)S(1)} custom-call(s32[3]{0:T(128)S(1)} %pad_add_fusion.places.unused, s32[3]{0:T(128)S(1)} %pad_add_fusion.places.unused, s32[1]{0:T(128)} %bitcast.1.inner, bf16[9,256,2048]{2,1,0:T(8,128)(2,1)S(1)} %product.1.refs_0_.refs_1_.refs_2_, bf16[9,256,2048]{2,1,0:T(8,128)(2,1)S(1)} %product.1.refs_0_.refs_1_.refs_2_, ...), custom_call_target="tpu_custom_call" | custom-call | flops 1000 | bytes 1000 | tf_op jit(solution)/shard_map/image/pallas_call | solution.py:363
  181.5 4.8 %collective-permute-done.10.refs_3_ = bf16[5,512,256]{2,1,0:T(8,128)(2,1)} collective-permute-done((bf16[5,512,256]{2,1,0:T(8,128)(2,1)}, bf16[5,512,256]{2,1,0:T(8,128)(2,1)}, u32[]{:S(2)}, u32[]{:S(2)}) %collective-permute-start.10) | collective-permute-done | bytes 1310752 | tf_op jit(solution)/shard_map/ppermute | solution.py:380
  186.3 4.0 %image.4 = f32[6,2,128,128]{3,2,1,0:T(8,128)S(1)} custom-call(s32[1]{0:T(128)} %bitcast.places.unused, s32[1]{0:T(128)} %bitcast.places.unused, s32[1]{0:T(128)} %bitcast.1.inner, bf16[9,256,2048]{2,1,0:T(8,128)(2,1)S(1)} %product.1.refs_0_.refs_1_.refs_2_, bf16[3,512,256]{2,1,0:T(8,128)(2,1)S(1)} %copy-done.4, ...), custom_call_target="tpu_custom_call" | custom-call | flops 1000 | bytes 1000 | tf_op jit(solution)/shard_map/image/pallas_call | solution.py:363
  190.4 4.0 %collective-permute-done.13.refs_3_ = bf16[2,512,256]{2,1,0:T(8,128)(2,1)} collective-permute-done((bf16[2,512,256]{2,1,0:T(8,128)(2,1)}, bf16[2,512,256]{2,1,0:T(8,128)(2,1)}, u32[]{:S(2)}, u32[]{:S(2)}) %collective-permute-start.13) | collective-permute-done | bytes 524320 | tf_op jit(solution)/shard_map/ppermute | solution.py:380
  194.3 1.8 image.5
  196.3 1.6 collective-permute-done.14
  198.8 1.5 collective-permute-start.18
  201.7 2.7 %collective-permute-done.18 = bf16[2,2,128,128]{3,2,1,0:T(8,128)(2,1)S(1)} collective-permute-done((bf16[2,2,128,128]{3,2,1,0:T(8,128)(2,1)S(1)}, bf16[2,2,128,128]{3,2,1,0:T(8,128)(2,1)S(1)}, u32[]{:S(2)}, u32[]{:S(2)}) %collective-permute-start.18) | collective-permute-done | bytes 131104 | tf_op jit(solution)/shard_map/ppermute | solution.py:385
  204.4 4.4 %collective-permute-start.19 = (bf16[2,128,128]{2,1,0:T(8,128)(2,1)S(1)}, bf16[2,128,128]{2,1,0:T(8,128)(2,1)S(1)}, u32[]{:S(2)}, u32[]{:S(2)}) collective-permute-start(bf16[2,128,128]{2,1,0:T(8,128)(2,1)S(1)} %fusion.3), channel_id=1, source_target_pairs={{0,12},{1,13},{2,14},{4,8},{5,9},{6,10},{7,11},{8,4},{9,5},{10,6},... | collective-permute-start | bytes 196616 | tf_op jit(solution)/shard_map/ppermute | solution.py:385
  208.8 3.5 %collective-permute-done.19 = bf16[2,128,128]{2,1,0:T(8,128)(2,1)S(1)} collective-permute-done((bf16[2,128,128]{2,1,0:T(8,128)(2,1)S(1)}, bf16[2,128,128]{2,1,0:T(8,128)(2,1)S(1)}, u32[]{:S(2)}, u32[]{:S(2)}) %collective-permute-start.19) | collective-permute-done | bytes 65568 | tf_op jit(solution)/shard_map/ppermute | solution.py:385
  (71 shorter events, 14.3 us)
Async XLA Ops:
  0.0 30.1 %collective-permute-start.5 = (bf16[16,2,128,128]{3,2,1,0:T(8,128)(2,1)}, bf16[16,2,128,128]{3,2,1,0:T(8,128)(2,1)S(1)}, u32[]{:S(2)}, u32[]{:S(2)}) collective-permute-start(bf16[16,2,128,128]{3,2,1,0:T(8,128)(2,1)} %bitcast.28), channel_id=1, source_target_pairs={{0,4},{12,8},{4,0},{8,12},{1,5},{13,9},{5,1},{9,13},{2,6},{14,10},... | collective-permute-start | bytes 3145736 | tf_op jit(solution)/shard_map/ppermute | solution.py:380
  8.5 20.7 %collective-permute-start = (bf16[3,512,256]{2,1,0:T(8,128)(2,1)}, bf16[3,512,256]{2,1,0:T(8,128)(2,1)S(1)}, u32[]{:S(2)}, u32[]{:S(2)}) collective-permute-start(bf16[3,512,256]{2,1,0:T(8,128)(2,1)} %extrapolate.3.refs_3_), channel_id=1, source_target_pairs={{4,8},{8,4},{5,9},{9,5},{6,10},{10,6},{7,11},{11,7},{20,24},{24,20... | collective-permute-start | bytes 2359304 | tf_op jit(solution)/shard_map/ppermute | solution.py:380
  9.2 44.7 %collective-permute-start.1 = (bf16[3,512,256]{2,1,0:T(8,128)(2,1)}, bf16[3,512,256]{2,1,0:T(8,128)(2,1)}, u32[]{:S(2)}, u32[]{:S(2)}) collective-permute-start(bf16[3,512,256]{2,1,0:T(8,128)(2,1)} %extrapolate.3.refs_3_), channel_id=1, source_target_pairs={{0,4},{12,8},{1,5},{13,9},{2,6},{14,10},{3,7},{15,11},{16,20},{28,... | collective-permute-start | bytes 2359304 | tf_op jit(solution)/shard_map/ppermute | solution.py:380
  28.4 26.3 %collective-permute-start.3 = (bf16[6,512,256]{2,1,0:T(8,128)(2,1)}, bf16[6,512,256]{2,1,0:T(8,128)(2,1)S(1)}, u32[]{:S(2)}, u32[]{:S(2)}) collective-permute-start(bf16[6,512,256]{2,1,0:T(8,128)(2,1)} %get-tuple-element.27.refs_4_), channel_id=1, source_target_pairs={{4,8},{8,4},{5,9},{9,5},{6,10},{10,6},{7,11},{11,7},{20,24},{24,20... | collective-permute-start | bytes 4718600 | tf_op jit(solution)/shard_map/ppermute | solution.py:380
  31.1 47.1 %collective-permute-start.9 = (bf16[7,512,256]{2,1,0:T(8,128)(2,1)}, bf16[7,512,256]{2,1,0:T(8,128)(2,1)}, u32[]{:S(2)}, u32[]{:S(2)}) collective-permute-start(bf16[7,512,256]{2,1,0:T(8,128)(2,1)} %get-tuple-element.31.refs_5_), channel_id=1, source_target_pairs={{4,0},{8,12},{5,1},{9,13},{6,2},{10,14},{7,3},{11,15},{20,16},{24,... | collective-permute-start | bytes 5505032 | tf_op jit(solution)/shard_map/ppermute | solution.py:380
  32.4 45.1 %collective-permute-start.7 = (bf16[6,512,256]{2,1,0:T(8,128)(2,1)}, bf16[6,512,256]{2,1,0:T(8,128)(2,1)}, u32[]{:S(2)}, u32[]{:S(2)}) collective-permute-start(bf16[6,512,256]{2,1,0:T(8,128)(2,1)} %get-tuple-element.27.refs_4_), channel_id=1, source_target_pairs={{0,4},{12,8},{1,5},{13,9},{2,6},{14,10},{3,7},{15,11},{16,20},{28,... | collective-permute-start | bytes 4718600 | tf_op jit(solution)/shard_map/ppermute | solution.py:380
  39.4 38.9 %copy-start = (bf16[7,512,256]{2,1,0:T(8,128)(2,1)S(1)}, bf16[7,512,256]{2,1,0:T(8,128)(2,1)}, u32[]{:S(2)}) copy-start(bf16[7,512,256]{2,1,0:T(8,128)(2,1)} %get-tuple-element.31.refs_5_) | copy-start | bytes 5505028
  53.9 72.9 %collective-permute-start.2 = (bf16[7,512,256]{2,1,0:T(8,128)(2,1)}, bf16[7,512,256]{2,1,0:T(8,128)(2,1)S(1)}, u32[]{:S(2)}, u32[]{:S(2)}) collective-permute-start(bf16[7,512,256]{2,1,0:T(8,128)(2,1)} %get-tuple-element.26), channel_id=1, source_target_pairs={{0,4},{12,8},{4,0},{8,12},{1,5},{13,9},{5,1},{9,13},{2,6},{14,10},... | collective-permute-start | bytes 5505032 | tf_op jit(solution)/shard_map/ppermute | solution.py:380
  54.0 26.7 %collective-permute-start.6 = (bf16[3,512,256]{2,1,0:T(8,128)(2,1)}, bf16[3,512,256]{2,1,0:T(8,128)(2,1)S(1)}, u32[]{:S(2)}, u32[]{:S(2)}) collective-permute-start(bf16[3,512,256]{2,1,0:T(8,128)(2,1)} %collective-permute-done.1.refs_6_), channel_id=1, source_target_pairs={{4,8},{8,4},{5,9},{9,5},{6,10},{10,6},{7,11},{11,7},{20,24},{24,20... | collective-permute-start | bytes 2359304 | tf_op jit(solution)/shard_map/ppermute | solution.py:380
  55.9 71.0 %collective-permute-start.4 = (bf16[2,512,256]{2,1,0:T(8,128)(2,1)}, bf16[2,512,256]{2,1,0:T(8,128)(2,1)S(1)}, u32[]{:S(2)}, u32[]{:S(2)}) collective-permute-start(bf16[2,512,256]{2,1,0:T(8,128)(2,1)} %get-tuple-element.28.refs_1_), channel_id=1, source_target_pairs={{0,4},{12,8},{1,5},{13,9},{2,6},{14,10},{3,7},{15,11},{16,20},{28,... | collective-permute-start | bytes 1572872 | tf_op jit(solution)/shard_map/ppermute | solution.py:380
  77.5 104.0 %collective-permute-start.8 = (bf16[6,512,256]{2,1,0:T(8,128)(2,1)}, bf16[6,512,256]{2,1,0:T(8,128)(2,1)S(1)}, u32[]{:S(2)}, u32[]{:S(2)}) collective-permute-start(bf16[6,512,256]{2,1,0:T(8,128)(2,1)} %collective-permute-done.7.refs_7_), channel_id=1, source_target_pairs={{4,8},{8,4},{5,9},{9,5},{6,10},{10,6},{7,11},{11,7},{20,24},{24,20... | collective-permute-start | bytes 4718600 | tf_op jit(solution)/shard_map/ppermute | solution.py:380
  79.4 106.9 %collective-permute-start.10 = (bf16[5,512,256]{2,1,0:T(8,128)(2,1)}, bf16[5,512,256]{2,1,0:T(8,128)(2,1)}, u32[]{:S(2)}, u32[]{:S(2)}) collective-permute-start(bf16[5,512,256]{2,1,0:T(8,128)(2,1)} %slice.47), channel_id=1, source_target_pairs={{4,12},{8,0},{5,13},{9,1},{6,14},{10,2},{7,15},{11,3},{20,28},{24,... | collective-permute-start | bytes 3932168 | tf_op jit(solution)/shard_map/ppermute | solution.py:380
  80.7 52.8 %copy-start.3 = (bf16[3,512,256]{2,1,0:T(8,128)(2,1)}, bf16[3,512,256]{2,1,0:T(8,128)(2,1)S(1)}, u32[]{:S(2)}) copy-start(bf16[3,512,256]{2,1,0:T(8,128)(2,1)S(1)} %collective-permute-done.6.refs_1_) | copy-start | bytes 2359300
  126.9 6.6 %copy-start.17 = (bf16[2,512,256]{2,1,0:T(8,128)(2,1)}, bf16[2,512,256]{2,1,0:T(8,128)(2,1)S(1)}, u32[]{:S(2)}) copy-start(bf16[2,512,256]{2,1,0:T(8,128)(2,1)S(1)} %collective-permute-done.4.refs_4_) | copy-start | bytes 1572868
  126.9 6.6 %copy-start.1 = (bf16[7,512,256]{2,1,0:T(8,128)(2,1)}, bf16[7,512,256]{2,1,0:T(8,128)(2,1)S(1)}, u32[]{:S(2)}) copy-start(bf16[7,512,256]{2,1,0:T(8,128)(2,1)S(1)} %collective-permute-done.2.refs_3_.refs_5_) | copy-start | bytes 5505028
  128.0 10.9 %copy-start.19 = (s32[64,2]{0,1:T(2,128)S(1)}, s32[64,2]{0,1:T(2,128)}, u32[]{:S(2)}) copy-start(s32[64,2]{0,1:T(2,128)} %param.13) | copy-start | bytes 1540
  128.0 45.1 %collective-permute-start.11 = (bf16[4,512,256]{2,1,0:T(8,128)(2,1)}, bf16[4,512,256]{2,1,0:T(8,128)(2,1)}, u32[]{:S(2)}, u32[]{:S(2)}) collective-permute-start(bf16[4,512,256]{2,1,0:T(8,128)(2,1)} %slice.48), channel_id=1, source_target_pairs={{0,12},{12,0},{1,13},{13,1},{2,14},{14,2},{3,15},{15,3},{16,28},{2... | collective-permute-start | bytes 3145736 | tf_op jit(solution)/shard_map/ppermute | solution.py:380
  133.5 39.7 %collective-permute-start.12 = (bf16[3,512,256]{2,1,0:T(8,128)(2,1)}, bf16[3,512,256]{2,1,0:T(8,128)(2,1)}, u32[]{:S(2)}, u32[]{:S(2)}) collective-permute-start(bf16[3,512,256]{2,1,0:T(8,128)(2,1)} %slice.49), channel_id=1, source_target_pairs={{0,12},{12,0},{1,13},{13,1},{2,14},{14,2},{3,15},{15,3},{16,28},{2... | collective-permute-start | bytes 2359304 | tf_op jit(solution)/shard_map/ppermute | solution.py:380
  137.5 56.8 %collective-permute-start.13 = (bf16[2,512,256]{2,1,0:T(8,128)(2,1)}, bf16[2,512,256]{2,1,0:T(8,128)(2,1)}, u32[]{:S(2)}, u32[]{:S(2)}) collective-permute-start(bf16[2,512,256]{2,1,0:T(8,128)(2,1)} %slice.51), channel_id=1, source_target_pairs={{4,12},{8,0},{5,13},{9,1},{6,14},{10,2},{7,15},{11,3},{20,28},{24,... | collective-permute-start | bytes 1572872 | tf_op jit(solution)/shard_map/ppermute | solution.py:380
  139.0 1.5 copy-start.2
  140.5 1.5 copy-start.6
  148.1 25.0 %copy-start.5 = (bf16[3,512,256]{2,1,0:T(8,128)(2,1)S(1)}, bf16[3,512,256]{2,1,0:T(8,128)(2,1)}, u32[]{:S(2)}) copy-start(bf16[3,512,256]{2,1,0:T(8,128)(2,1)} %extrapolate.3.refs_3_) | copy-start | bytes 2359300
  148.1 25.0 %copy-start.8 = (bf16[6,512,256]{2,1,0:T(8,128)(2,1)S(1)}, bf16[6,512,256]{2,1,0:T(8,128)(2,1)}, u32[]{:S(2)}) copy-start(bf16[6,512,256]{2,1,0:T(8,128)(2,1)} %get-tuple-element.27.refs_4_) | copy-start | bytes 4718596
  148.1 25.0 %copy-start.10 = (bf16[6,512,256]{2,1,0:T(8,128)(2,1)S(1)}, bf16[6,512,256]{2,1,0:T(8,128)(2,1)}, u32[]{:S(2)}) copy-start(bf16[6,512,256]{2,1,0:T(8,128)(2,1)} %copy-done.9) | copy-start | bytes 4718596
  148.1 25.0 %copy-start.15 = (bf16[3,512,256]{2,1,0:T(8,128)(2,1)S(1)}, bf16[3,512,256]{2,1,0:T(8,128)(2,1)}, u32[]{:S(2)}) copy-start(bf16[3,512,256]{2,1,0:T(8,128)(2,1)} %copy-done.14) | copy-start | bytes 2359300
  161.4 24.9 %copy-start.4 = (bf16[3,512,256]{2,1,0:T(8,128)(2,1)S(1)}, bf16[3,512,256]{2,1,0:T(8,128)(2,1)}, u32[]{:S(2)}) copy-start(bf16[3,512,256]{2,1,0:T(8,128)(2,1)} %copy-done.3) | copy-start | bytes 2359300
  196.2 1.7 collective-permute-start.14
  198.0 2.3 %collective-permute-start.15 = (bf16[2,128,128]{2,1,0:T(8,128)(2,1)S(1)}, bf16[2,128,128]{2,1,0:T(8,128)(2,1)S(1)}, u32[]{:S(2)}, u32[]{:S(2)}) collective-permute-start(bf16[2,128,128]{2,1,0:T(8,128)(2,1)S(1)} %fusion.2), channel_id=1, source_target_pairs={{5,7},{9,11},{21,23},{25,27}} | collective-permute-start | bytes 196616 | tf_op jit(solution)/shard_map/ppermute | solution.py:385
  198.8 5.6 %collective-permute-start.18 = (bf16[2,2,128,128]{3,2,1,0:T(8,128)(2,1)S(1)}, bf16[2,2,128,128]{3,2,1,0:T(8,128)(2,1)S(1)}, u32[]{:S(2)}, u32[]{:S(2)}) collective-permute-start(bf16[2,2,128,128]{3,2,1,0:T(8,128)(2,1)S(1)} %select_convert_fusion.1), channel_id=1, source_target_pairs={{0,2},{1,3},{2,0},{3,1},{4,6},{5,7},{6,4},{7,5},{8,10},{9,11},{10,... | collective-permute-start | bytes 393224 | tf_op jit(solution)/shard_map/ppermute | solution.py:385
  200.3 8.5 %collective-permute-start.16 = (bf16[2,128,128]{2,1,0:T(8,128)(2,1)S(1)}, bf16[2,128,128]{2,1,0:T(8,128)(2,1)S(1)}, u32[]{:S(2)}, u32[]{:S(2)}) collective-permute-start(bf16[2,128,128]{2,1,0:T(8,128)(2,1)S(1)} %add_convert_fusion), channel_id=1, source_target_pairs={{7,15},{23,31}} | collective-permute-start | bytes 196616 | tf_op jit(solution)/shard_map/ppermute | solution.py:385
  201.0 7.8 %collective-permute-start.17 = (bf16[2,128,128]{2,1,0:T(8,128)(2,1)S(1)}, bf16[2,128,128]{2,1,0:T(8,128)(2,1)S(1)}, u32[]{:S(2)}, u32[]{:S(2)}) collective-permute-start(bf16[2,128,128]{2,1,0:T(8,128)(2,1)S(1)} %add_convert_fusion), channel_id=1, source_target_pairs={{11,15},{27,31}} | collective-permute-start | bytes 196616 | tf_op jit(solution)/shard_map/ppermute | solution.py:385
  204.4 8.0 %collective-permute-start.19 = (bf16[2,128,128]{2,1,0:T(8,128)(2,1)S(1)}, bf16[2,128,128]{2,1,0:T(8,128)(2,1)S(1)}, u32[]{:S(2)}, u32[]{:S(2)}) collective-permute-start(bf16[2,128,128]{2,1,0:T(8,128)(2,1)S(1)} %fusion.3), channel_id=1, source_target_pairs={{0,12},{1,13},{2,14},{4,8},{5,9},{6,10},{7,11},{8,4},{9,5},{10,6},... | collective-permute-start | bytes 196616 | tf_op jit(solution)/shard_map/ppermute | solution.py:385
  (8 other events, 9.1 us)
